TPU v7x, 32 devices: a whole 2x2x4 slice. The times are simulated.
32 devices in a mesh: gx: 4 (over x, core), gy: 4 (over z), gz: 2 (over y).
Axes of the slice: x: 2, y: 2, z: 4, core: 2. Of those that a mesh axis runs over, the one named last changes fastest.
Arguments:
- charges: float32 [64, 128, 512], P('gz', 'gy', 'gx'), may hold values from -8 to 8
- kernel_taps: float32 [3, 2, 17], replicated, may hold values from 0 to 2
Outputs:
- potential: float32 [64, 128, 512], P('gz', 'gy', 'gx')
All inputs are finite; a program needn't handle non-finite values.
Results may differ from a plain program's by a relative error of at most 0.0001.
Values sent between devices are 32-bit elements; how exact they have to be, the bound alone decides.
No kernel may reach another device: no remote copies, remote signals or barrier semaphores. Data moves between devices by JAX's collectives and lax.ppermute only.
A program may use at most 128 MiB of HBM per device.

v0:
```python
import jax
import jax.numpy as jnp
from jax import lax
from jax.sharding import PartitionSpec as P

RADIUS = 8
TAPS = 17


RESTRICT_WEIGHTS = ((-3, -0.0625), (-1, 0.5625), (0, 1.0), (1, 0.5625), (3, -0.0625))


def extended(x, sides, width):
    for axis, dim in sides:
        count, length = (lax.axis_size(axis), x.shape[dim])
        up = [(i, (i + 1) % count) for i in range(count - 1)]
        down = [(j, i) for i, j in up]
        last = lax.slice_in_dim(x, length - width, length, axis=dim)
        initial = lax.slice_in_dim(x, 0, width, axis=dim)
        before = lax.ppermute(last, axis, up)
        after = lax.ppermute(initial, axis, down)
        x = jnp.concatenate([before, x, after], axis=dim)
    return x


def convolve_axis(padded, kernel_rows, axis_dim, length):
    weight_shape = (kernel_rows.shape[0],) + (1,) * (padded.ndim - 1)
    summed = kernel_rows[:, 0].reshape(weight_shape) * lax.slice_in_dim(
        padded, 0, length, axis=axis_dim
    )
    for offset in range(1, TAPS):
        summed = summed + kernel_rows[:, offset].reshape(weight_shape) * lax.slice_in_dim(
            padded, offset, offset + length, axis=axis_dim
        )
    return summed


def stencil_box(padded, kernel_rows, extent_z, extent_y, extent_x):
    smoothed = convolve_axis(padded[None], kernel_rows, 1, extent_z)
    smoothed = convolve_axis(smoothed, kernel_rows, 2, extent_y)
    smoothed = convolve_axis(smoothed, kernel_rows, 3, extent_x)
    return jnp.sum(smoothed, axis=0)


def restrict_axis(padded, axis_dim, margin, count):
    summed = None
    for offset, weight in RESTRICT_WEIGHTS:
        first = margin + offset
        piece = lax.slice_in_dim(padded, first, first + 2 * count - 1, stride=2, axis=axis_dim)
        summed = weight * piece if summed is None else summed + weight * piece
    return summed


def restrict_padded(padded, margin, counts):
    result_field = restrict_axis(padded, 0, margin, counts[0])
    result_field = restrict_axis(result_field, 1, margin, counts[1])
    return restrict_axis(result_field, 2, margin, counts[2])


def prolong_axis(padded, axis_dim, margin, count):

    def take(shift):
        return lax.slice_in_dim(padded, margin + shift, margin + shift + count, axis=axis_dim)

    centre = take(0)
    odd_cells = 0.5625 * (centre + take(1)) - 0.0625 * (take(-1) + take(2))
    stacked = jnp.stack([centre, odd_cells], axis=axis_dim + 1)
    new_shape = list(centre.shape)
    new_shape[axis_dim] = 2 * count
    return stacked.reshape(new_shape)


def prolong_padded(padded, margin, counts):
    result_field = prolong_axis(padded, 0, margin, counts[0])
    result_field = prolong_axis(result_field, 1, margin, counts[1])
    return prolong_axis(result_field, 2, margin, counts[2])


def local(charges, kernel_taps):
    extent_z, extent_y, extent_x = charges.shape
    fine_padded = extended(charges, (("gx", 2), ("gy", 1), ("gz", 0)), RADIUS)
    fine_potential = stencil_box(fine_padded, kernel_taps[0], extent_z, extent_y, extent_x)
    mid_z, mid_y, mid_x = (extent_z // 2, extent_y // 2, extent_x // 2)
    mid_charges = restrict_padded(fine_padded, RADIUS, (mid_z, mid_y, mid_x))
    mid_padded = extended(mid_charges, (("gx", 2), ("gy", 1), ("gz", 0)), RADIUS)
    mid_potential = stencil_box(mid_padded, kernel_taps[1], mid_z, mid_y, mid_x)
    coarse_z, coarse_y, coarse_x = (mid_z // 2, mid_y // 2, mid_x // 2)
    coarse_charges = restrict_padded(mid_padded, RADIUS, (coarse_z, coarse_y, coarse_x))
    coarse_rows = kernel_taps[2]
    plane = extended(coarse_charges, (("gx", 2), ("gy", 1)), RADIUS)
    smoothed = convolve_axis(plane[None], coarse_rows, 2, coarse_y)
    smoothed = convolve_axis(smoothed, coarse_rows, 3, coarse_x)
    own_first = lax.axis_index("gz") * coarse_z
    tap_offsets = jnp.arange(TAPS) - RADIUS
    own_rows = own_first + jnp.arange(coarse_z)
    slab_piece = lax.all_gather(smoothed, "gz", axis=1, tiled=True)
    row_count = slab_piece.shape[1]
    piece_rows = jnp.arange(row_count)
    distance = piece_rows[None, :] - own_rows[:, None]
    selector = (distance[:, :, None] == tap_offsets[None, None, :]).astype(jnp.float32)
    banded = jnp.einsum("krd,td->tkr", selector, coarse_rows, precision=lax.Precision.HIGHEST)
    columns = jnp.einsum("tkr,tryx->tkyx", banded, slab_piece, precision=lax.Precision.HIGHEST)
    coarse_potential = jnp.sum(columns, axis=0)
    coarse_wide = extended(coarse_potential, (("gx", 2), ("gy", 1), ("gz", 0)), 2)
    mid_total = mid_potential + prolong_padded(coarse_wide, 2, (coarse_z, coarse_y, coarse_x))
    mid_wide = extended(mid_total, (("gx", 2), ("gy", 1), ("gz", 0)), 2)
    return fine_potential + prolong_padded(mid_wide, 2, (mid_z, mid_y, mid_x))


def solution(mesh):
    return jax.shard_map(
        local,
        mesh=mesh,
        in_specs=(P("gz", "gy", "gx"), P()),
        out_specs=P("gz", "gy", "gx"),
        check_vma=False,
    )
```

profile of v0, /device:TPU:1, one launch (start us, length us, event | category | flops | bytes accessed | tf_op | source)
XLA Modules:
  0.0 183.9 jit_solution(2447467523783490246)
XLA Ops:
  0.0 1.5 fusion.114
  1.5 4.5 %collective-permute-start = (f32[32,32,8]{2,1,0:T(8,128)S(1)}, f32[32,32,8]{2,1,0:T(8,128)S(1)}, u32[]{:S(2)}, u32[]{:S(2)}) collective-permute-start(f32[32,32,8]{2,1,0:T(8,128)S(1)} %get-tuple-element.96), channel_id=1, source_target_pairs={{0,8},{8,16},{16,24},{1,9},{9,17},{17,25},{2,10},{10,18},{18,26},{... | collective-permute-start | bytes 98312 | tf_op jit(solution)/shard_map/ppermute | solution.py:20
  6.0 1.9 %collective-permute-start.1 = (f32[32,32,8]{2,1,0:T(8,128)S(1)}, f32[32,32,8]{2,1,0:T(8,128)S(1)}, u32[]{:S(2)}, u32[]{:S(2)}) collective-permute-start(f32[32,32,8]{2,1,0:T(8,128)S(1)} %get-tuple-element.97), channel_id=1, source_target_pairs={{8,0},{16,8},{24,16},{9,1},{17,9},{25,17},{10,2},{18,10},{26,18},{... | collective-permute-start | bytes 98312 | tf_op jit(solution)/shard_map/ppermute | solution.py:21
  8.0 1.0 slice_reduce_fusion.16
  9.0 3.1 %collective-permute-done = f32[32,32,8]{2,1,0:T(8,128)S(1)} collective-permute-done((f32[32,32,8]{2,1,0:T(8,128)S(1)}, f32[32,32,8]{2,1,0:T(8,128)S(1)}, u32[]{:S(2)}, u32[]{:S(2)}) %collective-permute-start) | collective-permute-done | bytes 32800 | tf_op jit(solution)/shard_map/ppermute | solution.py:20
  12.1 4.4 %collective-permute-done.1 = f32[32,32,8]{2,1,0:T(8,128)S(1)} collective-permute-done((f32[32,32,8]{2,1,0:T(8,128)S(1)}, f32[32,32,8]{2,1,0:T(8,128)S(1)}, u32[]{:S(2)}, u32[]{:S(2)}) %collective-permute-start.1) | collective-permute-done | bytes 32800 | tf_op jit(solution)/shard_map/ppermute | solution.py:21
  16.8 3.5 %collective-permute-start.2 = (f32[32,8,144]{2,1,0:T(8,128)S(1)}, f32[32,8,144]{2,1,0:T(8,128)S(1)}, u32[]{:S(2)}, u32[]{:S(2)}) collective-permute-start(f32[32,8,144]{2,1,0:T(8,128)S(1)} %get-tuple-element.75), channel_id=1, source_target_pairs={{0,2},{2,4},{4,6},{1,3},{3,5},{5,7},{8,10},{10,12},{12,14},{9,11},... | collective-permute-start | bytes 442376 | tf_op jit(solution)/shard_map/ppermute | solution.py:20
  20.3 1.3 collective-permute-start.3
  21.6 1.0 slice_reduce_fusion.50
  22.6 1.0 collective-permute-done.2
  23.6 3.8 %collective-permute-done.3 = f32[32,8,144]{2,1,0:T(8,128)S(1)} collective-permute-done((f32[32,8,144]{2,1,0:T(8,128)S(1)}, f32[32,8,144]{2,1,0:T(8,128)S(1)}, u32[]{:S(2)}, u32[]{:S(2)}) %collective-permute-start.3) | collective-permute-done | bytes 147488 | tf_op jit(solution)/shard_map/ppermute | solution.py:21
  28.0 3.5 %collective-permute-start.4 = (f32[8,48,144]{2,1,0:T(8,128)S(1)}, f32[8,48,144]{2,1,0:T(8,128)S(1)}, u32[]{:S(2)}, u32[]{:S(2)}) collective-permute-start(f32[8,48,144]{2,1,0:T(8,128)S(1)} %get-tuple-element.73), channel_id=1, source_target_pairs={{0,1},{2,3},{4,5},{6,7},{8,9},{10,11},{12,13},{14,15},{16,17},{18,... | collective-permute-start | bytes 663560 | tf_op jit(solution)/shard_map/ppermute | solution.py:20
  31.4 1.3 collective-permute-start.5
  32.7 1.0 convolution_bitcast_fusion.1
  33.7 2.4 %collective-permute-done.4 = f32[8,48,144]{2,1,0:T(8,128)S(1)} collective-permute-done((f32[8,48,144]{2,1,0:T(8,128)S(1)}, f32[8,48,144]{2,1,0:T(8,128)S(1)}, u32[]{:S(2)}, u32[]{:S(2)}) %collective-permute-start.4) | collective-permute-done | bytes 221216 | tf_op jit(solution)/shard_map/ppermute | solution.py:20
  36.1 3.8 %collective-permute-done.5 = f32[8,48,144]{2,1,0:T(8,128)S(1)} collective-permute-done((f32[8,48,144]{2,1,0:T(8,128)S(1)}, f32[8,48,144]{2,1,0:T(8,128)S(1)}, u32[]{:S(2)}, u32[]{:S(2)}) %collective-permute-start.5) | collective-permute-done | bytes 221216 | tf_op jit(solution)/shard_map/ppermute | solution.py:21
  43.0 2.4 %slice.986 = f32[16,16,64]{2,1,0:T(8,128)S(1)} slice(f32[16,16,144]{2,1,0:T(8,128)S(1)} %multiply_add_fusion.3), slice={[0:16:1], [0:16:1], [11:138:2]} | slice | bytes 131072 | tf_op jit(solution)/shard_map/slice | solution.py:49
  45.3 2.4 %slice.985 = f32[16,16,64]{2,1,0:T(8,128)S(1)} slice(f32[16,16,144]{2,1,0:T(8,128)S(1)} %multiply_add_fusion.3), slice={[0:16:1], [0:16:1], [9:136:2]} | slice | bytes 131072 | tf_op jit(solution)/shard_map/slice | solution.py:49
  47.7 2.4 %slice.984 = f32[16,16,64]{2,1,0:T(8,128)S(1)} slice(f32[16,16,144]{2,1,0:T(8,128)S(1)} %multiply_add_fusion.3), slice={[0:16:1], [0:16:1], [8:135:2]} | slice | bytes 131072 | tf_op jit(solution)/shard_map/slice | solution.py:49
  50.1 2.4 %slice.983 = f32[16,16,64]{2,1,0:T(8,128)S(1)} slice(f32[16,16,144]{2,1,0:T(8,128)S(1)} %multiply_add_fusion.3), slice={[0:16:1], [0:16:1], [7:134:2]} | slice | bytes 131072 | tf_op jit(solution)/shard_map/slice | solution.py:49
  52.5 2.4 %slice.982 = f32[16,16,64]{2,1,0:T(8,128)S(1)} slice(f32[16,16,144]{2,1,0:T(8,128)S(1)} %multiply_add_fusion.3), slice={[0:16:1], [0:16:1], [5:132:2]} | slice | bytes 131072 | tf_op jit(solution)/shard_map/slice | solution.py:49
  55.0 4.0 %collective-permute-start.6 = (f32[16,16,8]{2,1,0:T(8,128)S(1)}, f32[16,16,8]{2,1,0:T(8,128)S(1)}, u32[]{:S(2)}, u32[]{:S(2)}) collective-permute-start(f32[16,16,8]{2,1,0:T(8,128)S(1)} %get-tuple-element.112), channel_id=1, source_target_pairs={{0,8},{8,16},{16,24},{1,9},{9,17},{17,25},{2,10},{10,18},{18,26},{... | collective-permute-start | bytes 24584 | tf_op jit(solution)/shard_map/ppermute | solution.py:20
  59.0 1.9 %collective-permute-start.7 = (f32[16,16,8]{2,1,0:T(8,128)S(1)}, f32[16,16,8]{2,1,0:T(8,128)S(1)}, u32[]{:S(2)}, u32[]{:S(2)}) collective-permute-start(f32[16,16,8]{2,1,0:T(8,128)S(1)} %get-tuple-element.113), channel_id=1, source_target_pairs={{8,0},{16,8},{24,16},{9,1},{17,9},{25,17},{10,2},{18,10},{26,18},{... | collective-permute-start | bytes 24584 | tf_op jit(solution)/shard_map/ppermute | solution.py:21
  60.9 1.0 slice_reduce_fusion.33
  62.0 3.3 %collective-permute-done.7 = f32[16,16,8]{2,1,0:T(8,128)S(1)} collective-permute-done((f32[16,16,8]{2,1,0:T(8,128)S(1)}, f32[16,16,8]{2,1,0:T(8,128)S(1)}, u32[]{:S(2)}, u32[]{:S(2)}) %collective-permute-start.7) | collective-permute-done | bytes 8224 | tf_op jit(solution)/shard_map/ppermute | solution.py:21
  65.5 3.2 %collective-permute-start.8 = (f32[16,8,80]{2,1,0:T(8,128)S(1)}, f32[16,8,80]{2,1,0:T(8,128)S(1)}, u32[]{:S(2)}, u32[]{:S(2)}) collective-permute-start(f32[16,8,80]{2,1,0:T(8,128)S(1)} %get-tuple-element.110), channel_id=1, source_target_pairs={{0,2},{2,4},{4,6},{1,3},{3,5},{5,7},{8,10},{10,12},{12,14},{9,11},... | collective-permute-start | bytes 122888 | tf_op jit(solution)/shard_map/ppermute | solution.py:20
  68.7 1.3 collective-permute-start.9
  70.0 1.9 %fusion.125 = f32[1,48,48,144]{3,2,1,0:T(8,128)S(1)} fusion(f32[8,48,144]{2,1,0:T(8,128)} %copy-done.12, f32[32,8,144]{2,1,0:T(8,128)} %copy-done.5, f32[32,32,8]{2,1,0:T(8,128)} %copy-done.1, f32[32,32,128]{2,1,0:T(8,128)S(1)} %copy-done, f32[32,32,8]{2,1,0:T(8,128)S(1)} %collective-permute-done, f32[32,8,144]{2,1,0:T(8,128)} %copy-done.4, ...), kind=kLoop, calls=%fused_computation.380 | loop fusion | flops 1990656 | bytes 2654208 | tf_op jit(solution)/shard_map/broadcast_in_dim | solution.py:39
  71.9 1.7 collective-permute-done.9
  73.8 1.3 collective-permute-start.10
  75.2 1.6 collective-permute-start.11
  76.8 8.9 %slice_bitcast_fusion.16 = (f32[32,48,144]{2,1,0:T(8,128)}, f32[32,48,144]{2,1,0:T(8,128)}, f32[32,48,144]{2,1,0:T(8,128)}, f32[32,48,144]{2,1,0:T(8,128)}, f32[...) fusion(f32[1,48,48,144]{3,2,1,0:T(8,128)S(1)} %fusion.125), kind=kLoop, calls=%fused_computation.51 | loop fusion | bytes 30081024 | tf_op jit(solution)/shard_map/mul | solution.py:28
  86.4 1.2 pad_maximum_fusion.3
  89.6 3.4 %collective-permute-start.12 = (f32[8,8,8]{2,1,0:T(8,128)S(1)}, f32[8,8,8]{2,1,0:T(8,128)S(1)}, u32[]{:S(2)}, u32[]{:S(2)}) collective-permute-start(f32[8,8,8]{2,1,0:T(8,128)S(1)} %get-tuple-element.139), channel_id=1, source_target_pairs={{0,8},{8,16},{16,24},{1,9},{9,17},{17,25},{2,10},{10,18},{18,26},{... | collective-permute-start | bytes 6152 | tf_op jit(solution)/shard_map/ppermute | solution.py:20
  93.0 1.9 %collective-permute-start.13 = (f32[8,8,8]{2,1,0:T(8,128)S(1)}, f32[8,8,8]{2,1,0:T(8,128)S(1)}, u32[]{:S(2)}, u32[]{:S(2)}) collective-permute-start(f32[8,8,8]{2,1,0:T(8,128)S(1)} %get-tuple-element.140), channel_id=1, source_target_pairs={{8,0},{16,8},{24,16},{9,1},{17,9},{25,17},{10,2},{18,10},{26,18},{... | collective-permute-start | bytes 6152 | tf_op jit(solution)/shard_map/ppermute | solution.py:21
  95.0 1.0 fusion.124
  96.0 2.2 %collective-permute-done.13 = f32[8,8,8]{2,1,0:T(8,128)S(1)} collective-permute-done((f32[8,8,8]{2,1,0:T(8,128)S(1)}, f32[8,8,8]{2,1,0:T(8,128)S(1)}, u32[]{:S(2)}, u32[]{:S(2)}) %collective-permute-start.13) | collective-permute-done | bytes 2080 | tf_op jit(solution)/shard_map/ppermute | solution.py:21
  98.3 1.3 collective-permute-start.15
  99.6 4.0 %collective-permute-start.14 = (f32[8,8,48]{2,1,0:T(8,128)S(1)}, f32[8,8,48]{2,1,0:T(8,128)S(1)}, u32[]{:S(2)}, u32[]{:S(2)}) collective-permute-start(f32[8,8,48]{2,1,0:T(8,128)S(1)} %pad_maximum_fusion.28), channel_id=1, source_target_pairs={{0,2},{2,4},{4,6},{1,3},{3,5},{5,7},{8,10},{10,12},{12,14},{9,11},... | collective-permute-start | bytes 36872 | tf_op jit(solution)/shard_map/ppermute | solution.py:20
  105.9 5.1 %all_gather.3 = f32[2,16,8,32]{3,1,0,2:T(8,128)S(1)} all-gather(f32[2,8,8,32]{3,1,0,2:T(8,128)S(1)} %fusion.86), channel_id=1, replica_groups=mesh['gx'=4,'gy'=4,'gz'=2] {'gz'}, dimensions={1}, use_global_device_ids=true | all-gather | bytes 49152 | tf_op jit(solution)/shard_map/all_gather | solution.py:96
  111.3 3.9 %collective-permute-start.16 = (f32[8,8,2]{2,0,1:T(8,128)S(1)}, f32[8,8,2]{2,0,1:T(8,128)S(1)}, u32[]{:S(2)}, u32[]{:S(2)}) collective-permute-start(f32[8,8,2]{2,0,1:T(8,128)S(1)} %get-tuple-element.137), channel_id=1, source_target_pairs={{0,8},{8,16},{16,24},{1,9},{9,17},{17,25},{2,10},{10,18},{18,26},{... | collective-permute-start | bytes 1544 | tf_op jit(solution)/shard_map/ppermute | solution.py:20
  115.3 1.9 %collective-permute-start.17 = (f32[8,8,2]{2,0,1:T(8,128)S(1)}, f32[8,8,2]{2,0,1:T(8,128)S(1)}, u32[]{:S(2)}, u32[]{:S(2)}) collective-permute-start(f32[8,8,2]{2,0,1:T(8,128)S(1)} %get-tuple-element.138), channel_id=1, source_target_pairs={{8,0},{16,8},{24,16},{9,1},{17,9},{25,17},{10,2},{18,10},{26,18},{... | collective-permute-start | bytes 1544 | tf_op jit(solution)/shard_map/ppermute | solution.py:21
  118.0 2.5 %collective-permute-done.17 = f32[8,8,2]{2,0,1:T(8,128)S(1)} collective-permute-done((f32[8,8,2]{2,0,1:T(8,128)S(1)}, f32[8,8,2]{2,0,1:T(8,128)S(1)}, u32[]{:S(2)}, u32[]{:S(2)}) %collective-permute-start.17) | collective-permute-done | bytes 544 | tf_op jit(solution)/shard_map/ppermute | solution.py:21
  120.6 3.9 %collective-permute-start.18 = (f32[8,2,36]{2,0,1:T(8,128)S(1)}, f32[8,2,36]{2,0,1:T(8,128)S(1)}, u32[]{:S(2)}, u32[]{:S(2)}) collective-permute-start(f32[8,2,36]{2,0,1:T(8,128)S(1)} %get-tuple-element.116), channel_id=1, source_target_pairs={{0,2},{2,4},{4,6},{1,3},{3,5},{5,7},{8,10},{10,12},{12,14},{9,11},... | collective-permute-start | bytes 6920 | tf_op jit(solution)/shard_map/ppermute | solution.py:20
  124.5 1.3 collective-permute-start.19
  126.4 2.5 %collective-permute-done.19 = f32[8,2,36]{2,0,1:T(8,128)S(1)} collective-permute-done((f32[8,2,36]{2,0,1:T(8,128)S(1)}, f32[8,2,36]{2,0,1:T(8,128)S(1)}, u32[]{:S(2)}, u32[]{:S(2)}) %collective-permute-start.19) | collective-permute-done | bytes 2336 | tf_op jit(solution)/shard_map/ppermute | solution.py:21
  129.0 1.3 collective-permute-start.20
  130.3 1.2 fusion.42
  131.5 4.0 %collective-permute-start.21 = (f32[2,12,36]{2,0,1:T(2,128)S(1)}, f32[2,12,36]{2,0,1:T(2,128)S(1)}, u32[]{:S(2)}, u32[]{:S(2)}) collective-permute-start(f32[2,12,36]{2,0,1:T(2,128)S(1)} %get-tuple-element.135), channel_id=1, source_target_pairs={{0,1},{2,3},{4,5},{6,7},{8,9},{10,11},{12,13},{14,15},{16,17},{18,... | collective-permute-start | bytes 10376 | tf_op jit(solution)/shard_map/ppermute | solution.py:20
  136.9 1.2 copy.202
  138.1 1.3 copy.203
  139.5 4.5 %collective-permute-start.22 = (f32[16,16,2]{2,1,0:T(8,128)S(1)}, f32[16,16,2]{2,1,0:T(8,128)S(1)}, u32[]{:S(2)}, u32[]{:S(2)}) collective-permute-start(f32[16,16,2]{2,1,0:T(8,128)S(1)} %get-tuple-element.106), channel_id=1, source_target_pairs={{0,8},{8,16},{16,24},{1,9},{9,17},{17,25},{2,10},{10,18},{18,26},{... | collective-permute-start | bytes 6152 | tf_op jit(solution)/shard_map/ppermute | solution.py:20
  144.0 1.9 %collective-permute-start.23 = (f32[16,16,2]{2,1,0:T(8,128)S(1)}, f32[16,16,2]{2,1,0:T(8,128)S(1)}, u32[]{:S(2)}, u32[]{:S(2)}) collective-permute-start(f32[16,16,2]{2,1,0:T(8,128)S(1)} %get-tuple-element.107), channel_id=1, source_target_pairs={{8,0},{16,8},{24,16},{9,1},{17,9},{25,17},{10,2},{18,10},{26,18},{... | collective-permute-start | bytes 6152 | tf_op jit(solution)/shard_map/ppermute | solution.py:21
  146.1 10.6 %multiply_add_fusion = f32[2,32,48,144]{3,2,1,0:T(8,128)S(1)} fusion(f32[32,48,144]{2,1,0:T(8,128)S(1)} %copy-done.3, f32[2]{0:T(128)S(1)} %copy-done.34, f32[32,48,144]{2,1,0:T(8,128)} %get-tuple-element.58, f32[2]{0:T(128)S(1)} %copy-done.35, f32[32,48,144]{2,1,0:T(8,128)} %get-tuple-element.59, f32[2]{0:T(128)S(1)} %copy-done.36, ...), kind=kLoop, calls=%fused_computation | loop fusion | flops 14598144 | bytes 16810120 | tf_op jit(solution)/shard_map/add | solution.py:32
  156.9 1.3 collective-permute-start.25
  158.2 4.2 %collective-permute-start.24 = (f32[16,2,68]{2,0,1:T(8,128)S(1)}, f32[16,2,68]{2,0,1:T(8,128)S(1)}, u32[]{:S(2)}, u32[]{:S(2)}) collective-permute-start(f32[16,2,68]{2,0,1:T(8,128)S(1)} %copy.204), channel_id=1, source_target_pairs={{0,2},{2,4},{4,6},{1,3},{3,5},{5,7},{8,10},{10,12},{12,14},{9,11},... | collective-permute-start | bytes 26120 | tf_op jit(solution)/shard_map/ppermute | solution.py:20
  162.5 4.3 %fusion = f32[2,32,32,144]{3,2,1,0:T(8,128)S(1)} fusion(f32[2,32,48,144]{3,2,1,0:T(8,128)S(1)} %multiply_add_fusion, f32[2]{0:T(128)S(1)} %copy-done.34, f32[2]{0:T(128)S(1)} %copy-done.35, f32[2]{0:T(128)S(1)} %copy-done.36, f32[2]{0:T(128)S(1)} %copy-done.37, f32[2]{0:T(128)S(1)} %copy-done.38, f32[2]{0:T(128)S(1)} %copy-done.39, f32[2]{0:T(128)S(1)} %copy-done.40, ...), kind=kLoop, calls=%fused_computation.3 | loop fusion | flops 9732096 | bytes 21233800 | tf_op jit(solution)/shard_map/add | solution.py:32
  167.1 1.3 collective-permute-start.26
  168.4 5.3 %fusion.17 = f32[32,32,128]{2,1,0:T(8,128)} fusion(f32[2,32,32,144]{3,2,1,0:T(8,128)S(1)} %fusion, f32[2]{0:T(128)S(1)} %copy-done.34, f32[2]{0:T(128)S(1)} %copy-done.35, f32[2]{0:T(128)S(1)} %copy-done.36, f32[2]{0:T(128)S(1)} %copy-done.37, f32[2]{0:T(128)S(1)} %copy-done.38, f32[2]{0:T(128)S(1)} %copy-done.39, f32[2]{0:T(128)S(1)} %copy-done.40, ...), kind=kLoop, calls=%fused_computation.57 | loop fusion | flops 8781824 | bytes 18350216 | tf_op jit(solution)/shard_map/reduce_sum | solution.py:42
  173.7 4.0 %collective-permute-start.27 = (f32[2,20,68]{2,1,0:T(8,128)S(1)}, f32[2,20,68]{2,1,0:T(8,128)S(1)}, u32[]{:S(2)}, u32[]{:S(2)}) collective-permute-start(f32[2,20,68]{2,1,0:T(8,128)S(1)} %get-tuple-element.104), channel_id=1, source_target_pairs={{0,1},{2,3},{4,5},{6,7},{8,9},{10,11},{12,13},{14,15},{16,17},{18,... | collective-permute-start | bytes 32648 | tf_op jit(solution)/shard_map/ppermute | solution.py:20
  177.9 0.7 collective-permute-done.27
  180.0 1.7 copy.212
  181.7 1.3 copy.213
  183.0 0.9 add.680
  (244 shorter events, 13.8 us)
Async XLA Ops:
  0.0 16.5 %copy-start = (f32[32,32,128]{2,1,0:T(8,128)S(1)}, f32[32,32,128]{2,1,0:T(8,128)}, u32[]{:S(2)}) copy-start(f32[32,32,128]{2,1,0:T(8,128)} %param.2) | copy-start | bytes 1572868
  1.5 10.6 %collective-permute-start = (f32[32,32,8]{2,1,0:T(8,128)S(1)}, f32[32,32,8]{2,1,0:T(8,128)S(1)}, u32[]{:S(2)}, u32[]{:S(2)}) collective-permute-start(f32[32,32,8]{2,1,0:T(8,128)S(1)} %get-tuple-element.96), channel_id=1, source_target_pairs={{0,8},{8,16},{16,24},{1,9},{9,17},{17,25},{2,10},{10,18},{18,26},{... | collective-permute-start | bytes 98312 | tf_op jit(solution)/shard_map/ppermute | solution.py:20
  6.0 10.5 %collective-permute-start.1 = (f32[32,32,8]{2,1,0:T(8,128)S(1)}, f32[32,32,8]{2,1,0:T(8,128)S(1)}, u32[]{:S(2)}, u32[]{:S(2)}) collective-permute-start(f32[32,32,8]{2,1,0:T(8,128)S(1)} %get-tuple-element.97), channel_id=1, source_target_pairs={{8,0},{16,8},{24,16},{9,1},{17,9},{25,17},{10,2},{18,10},{26,18},{... | collective-permute-start | bytes 98312 | tf_op jit(solution)/shard_map/ppermute | solution.py:21
  16.5 23.5 %copy-start.1 = (f32[32,32,8]{2,1,0:T(8,128)}, f32[32,32,8]{2,1,0:T(8,128)S(1)}, u32[]{:S(2)}) copy-start(f32[32,32,8]{2,1,0:T(8,128)S(1)} %collective-permute-done.1) | copy-start | bytes 98308
  16.8 6.8 %collective-permute-start.2 = (f32[32,8,144]{2,1,0:T(8,128)S(1)}, f32[32,8,144]{2,1,0:T(8,128)S(1)}, u32[]{:S(2)}, u32[]{:S(2)}) collective-permute-start(f32[32,8,144]{2,1,0:T(8,128)S(1)} %get-tuple-element.75), channel_id=1, source_target_pairs={{0,2},{2,4},{4,6},{1,3},{3,5},{5,7},{8,10},{10,12},{12,14},{9,11},... | collective-permute-start | bytes 442376 | tf_op jit(solution)/shard_map/ppermute | solution.py:20
  20.3 7.1 %collective-permute-start.3 = (f32[32,8,144]{2,1,0:T(8,128)S(1)}, f32[32,8,144]{2,1,0:T(8,128)S(1)}, u32[]{:S(2)}, u32[]{:S(2)}) collective-permute-start(f32[32,8,144]{2,1,0:T(8,128)S(1)} %get-tuple-element.76), channel_id=1, source_target_pairs={{2,0},{4,2},{6,4},{3,1},{5,3},{7,5},{10,8},{12,10},{14,12},{11,9},... | collective-permute-start | bytes 442376 | tf_op jit(solution)/shard_map/ppermute | solution.py:21
  23.6 16.4 %copy-start.4 = (f32[32,8,144]{2,1,0:T(8,128)}, f32[32,8,144]{2,1,0:T(8,128)S(1)}, u32[]{:S(2)}) copy-start(f32[32,8,144]{2,1,0:T(8,128)S(1)} %collective-permute-done.2) | copy-start | bytes 442372
  27.4 12.5 %copy-start.5 = (f32[32,8,144]{2,1,0:T(8,128)}, f32[32,8,144]{2,1,0:T(8,128)S(1)}, u32[]{:S(2)}) copy-start(f32[32,8,144]{2,1,0:T(8,128)S(1)} %collective-permute-done.3) | copy-start | bytes 442372
  28.0 8.2 %collective-permute-start.4 = (f32[8,48,144]{2,1,0:T(8,128)S(1)}, f32[8,48,144]{2,1,0:T(8,128)S(1)}, u32[]{:S(2)}, u32[]{:S(2)}) collective-permute-start(f32[8,48,144]{2,1,0:T(8,128)S(1)} %get-tuple-element.73), channel_id=1, source_target_pairs={{0,1},{2,3},{4,5},{6,7},{8,9},{10,11},{12,13},{14,15},{16,17},{18,... | collective-permute-start | bytes 663560 | tf_op jit(solution)/shard_map/ppermute | solution.py:20
  31.4 8.5 %collective-permute-start.5 = (f32[8,48,144]{2,1,0:T(8,128)S(1)}, f32[8,48,144]{2,1,0:T(8,128)S(1)}, u32[]{:S(2)}, u32[]{:S(2)}) collective-permute-start(f32[8,48,144]{2,1,0:T(8,128)S(1)} %get-tuple-element.74), channel_id=1, source_target_pairs={{1,0},{3,2},{5,4},{7,6},{9,8},{11,10},{13,12},{15,14},{17,16},{19,... | collective-permute-start | bytes 663560 | tf_op jit(solution)/shard_map/ppermute | solution.py:21
  55.0 7.0 %collective-permute-start.6 = (f32[16,16,8]{2,1,0:T(8,128)S(1)}, f32[16,16,8]{2,1,0:T(8,128)S(1)}, u32[]{:S(2)}, u32[]{:S(2)}) collective-permute-start(f32[16,16,8]{2,1,0:T(8,128)S(1)} %get-tuple-element.112), channel_id=1, source_target_pairs={{0,8},{8,16},{16,24},{1,9},{9,17},{17,25},{2,10},{10,18},{18,26},{... | collective-permute-start | bytes 24584 | tf_op jit(solution)/shard_map/ppermute | solution.py:20
  59.0 6.3 %collective-permute-start.7 = (f32[16,16,8]{2,1,0:T(8,128)S(1)}, f32[16,16,8]{2,1,0:T(8,128)S(1)}, u32[]{:S(2)}, u32[]{:S(2)}) collective-permute-start(f32[16,16,8]{2,1,0:T(8,128)S(1)} %get-tuple-element.113), channel_id=1, source_target_pairs={{8,0},{16,8},{24,16},{9,1},{17,9},{25,17},{10,2},{18,10},{26,18},{... | collective-permute-start | bytes 24584 | tf_op jit(solution)/shard_map/ppermute | solution.py:21
  62.0 11.7 %copy-start.7 = (f32[16,16,8]{2,1,0:T(8,128)}, f32[16,16,8]{2,1,0:T(8,128)S(1)}, u32[]{:S(2)}) copy-start(f32[16,16,8]{2,1,0:T(8,128)S(1)} %collective-permute-done.6) | copy-start | bytes 24580
  65.5 6.5 %collective-permute-start.8 = (f32[16,8,80]{2,1,0:T(8,128)S(1)}, f32[16,8,80]{2,1,0:T(8,128)S(1)}, u32[]{:S(2)}, u32[]{:S(2)}) collective-permute-start(f32[16,8,80]{2,1,0:T(8,128)S(1)} %get-tuple-element.110), channel_id=1, source_target_pairs={{0,2},{2,4},{4,6},{1,3},{3,5},{5,7},{8,10},{10,12},{12,14},{9,11},... | collective-permute-start | bytes 122888 | tf_op jit(solution)/shard_map/ppermute | solution.py:20
  68.7 5.0 %collective-permute-start.9 = (f32[16,8,80]{2,1,0:T(8,128)S(1)}, f32[16,8,80]{2,1,0:T(8,128)S(1)}, u32[]{:S(2)}, u32[]{:S(2)}) collective-permute-start(f32[16,8,80]{2,1,0:T(8,128)S(1)} %get-tuple-element.111), channel_id=1, source_target_pairs={{2,0},{4,2},{6,4},{3,1},{5,3},{7,5},{10,8},{12,10},{14,12},{11,9},... | collective-permute-start | bytes 122888 | tf_op jit(solution)/shard_map/ppermute | solution.py:21
  73.8 11.9 %collective-permute-start.10 = (f32[8,32,80]{2,1,0:T(8,128)S(1)}, f32[8,32,80]{2,1,0:T(8,128)S(1)}, u32[]{:S(2)}, u32[]{:S(2)}) collective-permute-start(f32[8,32,80]{2,1,0:T(8,128)S(1)} %get-tuple-element.102), channel_id=1, source_target_pairs={{0,1},{2,3},{4,5},{6,7},{8,9},{10,11},{12,13},{14,15},{16,17},{18,... | collective-permute-start | bytes 245768 | tf_op jit(solution)/shard_map/ppermute | solution.py:20
  75.2 11.2 %copy-start.8 = (f32[16,16,8]{2,1,0:T(8,128)S(1)}, f32[16,16,8]{2,1,0:T(8,128)}, u32[]{:S(2)}) copy-start(f32[16,16,8]{2,1,0:T(8,128)} %copy-done.7) | copy-start | bytes 24580
  75.2 11.2 %copy-start.10 = (f32[16,16,8]{2,1,0:T(8,128)S(1)}, f32[16,16,8]{2,1,0:T(8,128)}, u32[]{:S(2)}) copy-start(f32[16,16,8]{2,1,0:T(8,128)} %copy-done.9) | copy-start | bytes 24580
  75.2 11.2 %collective-permute-start.11 = (f32[8,32,80]{2,1,0:T(8,128)S(1)}, f32[8,32,80]{2,1,0:T(8,128)}, u32[]{:S(2)}, u32[]{:S(2)}) collective-permute-start(f32[8,32,80]{2,1,0:T(8,128)S(1)} %get-tuple-element.103), channel_id=1, source_target_pairs={{1,0},{3,2},{5,4},{7,6},{9,8},{11,10},{13,12},{15,14},{17,16},{19,... | collective-permute-start | bytes 245768 | tf_op jit(solution)/shard_map/ppermute | solution.py:21
  89.6 6.4 %collective-permute-start.12 = (f32[8,8,8]{2,1,0:T(8,128)S(1)}, f32[8,8,8]{2,1,0:T(8,128)S(1)}, u32[]{:S(2)}, u32[]{:S(2)}) collective-permute-start(f32[8,8,8]{2,1,0:T(8,128)S(1)} %get-tuple-element.139), channel_id=1, source_target_pairs={{0,8},{8,16},{16,24},{1,9},{9,17},{17,25},{2,10},{10,18},{18,26},{... | collective-permute-start | bytes 6152 | tf_op jit(solution)/shard_map/ppermute | solution.py:20
  93.0 5.2 %collective-permute-start.13 = (f32[8,8,8]{2,1,0:T(8,128)S(1)}, f32[8,8,8]{2,1,0:T(8,128)S(1)}, u32[]{:S(2)}, u32[]{:S(2)}) collective-permute-start(f32[8,8,8]{2,1,0:T(8,128)S(1)} %get-tuple-element.140), channel_id=1, source_target_pairs={{8,0},{16,8},{24,16},{9,1},{17,9},{25,17},{10,2},{18,10},{26,18},{... | collective-permute-start | bytes 6152 | tf_op jit(solution)/shard_map/ppermute | solution.py:21
  98.3 6.0 %collective-permute-start.15 = (f32[8,8,48]{2,1,0:T(8,128)S(1)}, f32[8,8,48]{2,1,0:T(8,128)S(1)}, u32[]{:S(2)}, u32[]{:S(2)}) collective-permute-start(f32[8,8,48]{2,1,0:T(8,128)S(1)} %pad_maximum_fusion.28), channel_id=1, source_target_pairs={{2,0},{4,2},{6,4},{3,1},{5,3},{7,5},{10,8},{12,10},{14,12},{11,9},... | collective-permute-start | bytes 36872 | tf_op jit(solution)/shard_map/ppermute | solution.py:21
  99.6 5.0 %collective-permute-start.14 = (f32[8,8,48]{2,1,0:T(8,128)S(1)}, f32[8,8,48]{2,1,0:T(8,128)S(1)}, u32[]{:S(2)}, u32[]{:S(2)}) collective-permute-start(f32[8,8,48]{2,1,0:T(8,128)S(1)} %pad_maximum_fusion.28), channel_id=1, source_target_pairs={{0,2},{2,4},{4,6},{1,3},{3,5},{5,7},{8,10},{10,12},{12,14},{9,11},... | collective-permute-start | bytes 36872 | tf_op jit(solution)/shard_map/ppermute | solution.py:20
  104.7 12.5 %copy-start.19 = (f32[2]{0:T(128)S(1)}, f32[2]{0:T(128)}, u32[]{:S(2)}) copy-start(f32[2]{0:T(128)} %get-tuple-element.26) | copy-start | bytes 28
  104.7 12.5 %copy-start.20 = (f32[2]{0:T(128)S(1)}, f32[2]{0:T(128)}, u32[]{:S(2)}) copy-start(f32[2]{0:T(128)} %get-tuple-element.27) | copy-start | bytes 28
  104.7 12.5 %copy-start.21 = (f32[2]{0:T(128)S(1)}, f32[2]{0:T(128)}, u32[]{:S(2)}) copy-start(f32[2]{0:T(128)} %get-tuple-element.28) | copy-start | bytes 28
  104.7 12.5 %copy-start.22 = (f32[2]{0:T(128)S(1)}, f32[2]{0:T(128)}, u32[]{:S(2)}) copy-start(f32[2]{0:T(128)} %get-tuple-element.29) | copy-start | bytes 28
  104.8 12.5 %copy-start.23 = (f32[2]{0:T(128)S(1)}, f32[2]{0:T(128)}, u32[]{:S(2)}) copy-start(f32[2]{0:T(128)} %get-tuple-element.30) | copy-start | bytes 28
  104.8 12.5 %copy-start.24 = (f32[2]{0:T(128)S(1)}, f32[2]{0:T(128)}, u32[]{:S(2)}) copy-start(f32[2]{0:T(128)} %get-tuple-element.31) | copy-start | bytes 28
  104.8 12.5 %copy-start.25 = (f32[2]{0:T(128)S(1)}, f32[2]{0:T(128)}, u32[]{:S(2)}) copy-start(f32[2]{0:T(128)} %get-tuple-element.32) | copy-start | bytes 28
  104.8 12.5 %copy-start.26 = (f32[2]{0:T(128)S(1)}, f32[2]{0:T(128)}, u32[]{:S(2)}) copy-start(f32[2]{0:T(128)} %get-tuple-element.33) | copy-start | bytes 28
  104.8 12.5 %copy-start.27 = (f32[2]{0:T(128)S(1)}, f32[2]{0:T(128)}, u32[]{:S(2)}) copy-start(f32[2]{0:T(128)} %get-tuple-element.34) | copy-start | bytes 28
  104.8 12.5 %copy-start.28 = (f32[2]{0:T(128)S(1)}, f32[2]{0:T(128)}, u32[]{:S(2)}) copy-start(f32[2]{0:T(128)} %get-tuple-element.35) | copy-start | bytes 28
  104.8 12.5 %copy-start.29 = (f32[2]{0:T(128)S(1)}, f32[2]{0:T(128)}, u32[]{:S(2)}) copy-start(f32[2]{0:T(128)} %get-tuple-element.36) | copy-start | bytes 28
  104.8 12.5 %copy-start.30 = (f32[2]{0:T(128)S(1)}, f32[2]{0:T(128)}, u32[]{:S(2)}) copy-start(f32[2]{0:T(128)} %get-tuple-element.37) | copy-start | bytes 28
  104.8 12.5 %copy-start.31 = (f32[2]{0:T(128)S(1)}, f32[2]{0:T(128)}, u32[]{:S(2)}) copy-start(f32[2]{0:T(128)} %get-tuple-element.38) | copy-start | bytes 28
  111.3 6.7 %collective-permute-start.16 = (f32[8,8,2]{2,0,1:T(8,128)S(1)}, f32[8,8,2]{2,0,1:T(8,128)S(1)}, u32[]{:S(2)}, u32[]{:S(2)}) collective-permute-start(f32[8,8,2]{2,0,1:T(8,128)S(1)} %get-tuple-element.137), channel_id=1, source_target_pairs={{0,8},{8,16},{16,24},{1,9},{9,17},{17,25},{2,10},{10,18},{18,26},{... | collective-permute-start | bytes 1544 | tf_op jit(solution)/shard_map/ppermute | solution.py:20
  115.3 5.2 %collective-permute-start.17 = (f32[8,8,2]{2,0,1:T(8,128)S(1)}, f32[8,8,2]{2,0,1:T(8,128)S(1)}, u32[]{:S(2)}, u32[]{:S(2)}) collective-permute-start(f32[8,8,2]{2,0,1:T(8,128)S(1)} %get-tuple-element.138), channel_id=1, source_target_pairs={{8,0},{16,8},{24,16},{9,1},{17,9},{25,17},{10,2},{18,10},{26,18},{... | collective-permute-start | bytes 1544 | tf_op jit(solution)/shard_map/ppermute | solution.py:21
  120.6 5.8 %collective-permute-start.18 = (f32[8,2,36]{2,0,1:T(8,128)S(1)}, f32[8,2,36]{2,0,1:T(8,128)S(1)}, u32[]{:S(2)}, u32[]{:S(2)}) collective-permute-start(f32[8,2,36]{2,0,1:T(8,128)S(1)} %get-tuple-element.116), channel_id=1, source_target_pairs={{0,2},{2,4},{4,6},{1,3},{3,5},{5,7},{8,10},{10,12},{12,14},{9,11},... | collective-permute-start | bytes 6920 | tf_op jit(solution)/shard_map/ppermute | solution.py:20
  124.5 4.4 %collective-permute-start.19 = (f32[8,2,36]{2,0,1:T(8,128)S(1)}, f32[8,2,36]{2,0,1:T(8,128)S(1)}, u32[]{:S(2)}, u32[]{:S(2)}) collective-permute-start(f32[8,2,36]{2,0,1:T(8,128)S(1)} %get-tuple-element.117), channel_id=1, source_target_pairs={{2,0},{4,2},{6,4},{3,1},{5,3},{7,5},{10,8},{12,10},{14,12},{11,9},... | collective-permute-start | bytes 6920 | tf_op jit(solution)/shard_map/ppermute | solution.py:21
  129.0 6.5 %collective-permute-start.20 = (f32[2,12,36]{2,0,1:T(2,128)S(1)}, f32[2,12,36]{2,0,1:T(2,128)S(1)}, u32[]{:S(2)}, u32[]{:S(2)}) collective-permute-start(f32[2,12,36]{2,0,1:T(2,128)S(1)} %get-tuple-element.136), channel_id=1, source_target_pairs={{1,0},{3,2},{5,4},{7,6},{9,8},{11,10},{13,12},{15,14},{17,16},{19,... | collective-permute-start | bytes 10376 | tf_op jit(solution)/shard_map/ppermute | solution.py:21
  131.5 4.8 %collective-permute-start.21 = (f32[2,12,36]{2,0,1:T(2,128)S(1)}, f32[2,12,36]{2,0,1:T(2,128)S(1)}, u32[]{:S(2)}, u32[]{:S(2)}) collective-permute-start(f32[2,12,36]{2,0,1:T(2,128)S(1)} %get-tuple-element.135), channel_id=1, source_target_pairs={{0,1},{2,3},{4,5},{6,7},{8,9},{10,11},{12,13},{14,15},{16,17},{18,... | collective-permute-start | bytes 10376 | tf_op jit(solution)/shard_map/ppermute | solution.py:20
  136.5 9.4 %copy-start.2 = (f32[32,48,144]{2,1,0:T(8,128)S(1)}, f32[32,48,144]{2,1,0:T(8,128)}, u32[]{:S(2)}) copy-start(f32[32,48,144]{2,1,0:T(8,128)} %get-tuple-element.56) | copy-start | bytes 2654212
  136.5 9.4 %copy-start.3 = (f32[32,48,144]{2,1,0:T(8,128)S(1)}, f32[32,48,144]{2,1,0:T(8,128)}, u32[]{:S(2)}) copy-start(f32[32,48,144]{2,1,0:T(8,128)} %get-tuple-element.57) | copy-start | bytes 2654212
  136.6 9.4 %copy-start.33 = (f32[2]{0:T(128)S(1)}, f32[2]{0:T(128)}, u32[]{:S(2)}) copy-start(f32[2]{0:T(128)} %get-tuple-element.39) | copy-start | bytes 28
  139.5 17.2 %collective-permute-start.22 = (f32[16,16,2]{2,1,0:T(8,128)S(1)}, f32[16,16,2]{2,1,0:T(8,128)S(1)}, u32[]{:S(2)}, u32[]{:S(2)}) collective-permute-start(f32[16,16,2]{2,1,0:T(8,128)S(1)} %get-tuple-element.106), channel_id=1, source_target_pairs={{0,8},{8,16},{16,24},{1,9},{9,17},{17,25},{2,10},{10,18},{18,26},{... | collective-permute-start | bytes 6152 | tf_op jit(solution)/shard_map/ppermute | solution.py:20
  144.0 12.7 %collective-permute-start.23 = (f32[16,16,2]{2,1,0:T(8,128)S(1)}, f32[16,16,2]{2,1,0:T(8,128)S(1)}, u32[]{:S(2)}, u32[]{:S(2)}) collective-permute-start(f32[16,16,2]{2,1,0:T(8,128)S(1)} %get-tuple-element.107), channel_id=1, source_target_pairs={{8,0},{16,8},{24,16},{9,1},{17,9},{25,17},{10,2},{18,10},{26,18},{... | collective-permute-start | bytes 6152 | tf_op jit(solution)/shard_map/ppermute | solution.py:21
  146.0 16.4 %copy-start.37 = (f32[2]{0:T(128)S(1)}, f32[2]{0:T(128)}, u32[]{:S(2)}) copy-start(f32[2]{0:T(128)} %get-tuple-element.43) | copy-start | bytes 28
  146.0 16.4 %copy-start.38 = (f32[2]{0:T(128)S(1)}, f32[2]{0:T(128)}, u32[]{:S(2)}) copy-start(f32[2]{0:T(128)} %get-tuple-element.44) | copy-start | bytes 28
  146.0 16.4 %copy-start.39 = (f32[2]{0:T(128)S(1)}, f32[2]{0:T(128)}, u32[]{:S(2)}) copy-start(f32[2]{0:T(128)} %get-tuple-element.45) | copy-start | bytes 28
  146.0 16.4 %copy-start.40 = (f32[2]{0:T(128)S(1)}, f32[2]{0:T(128)}, u32[]{:S(2)}) copy-start(f32[2]{0:T(128)} %get-tuple-element.46) | copy-start | bytes 28
  146.0 16.4 %copy-start.41 = (f32[2]{0:T(128)S(1)}, f32[2]{0:T(128)}, u32[]{:S(2)}) copy-start(f32[2]{0:T(128)} %get-tuple-element.47) | copy-start | bytes 28
  146.0 16.4 %copy-start.42 = (f32[2]{0:T(128)S(1)}, f32[2]{0:T(128)}, u32[]{:S(2)}) copy-start(f32[2]{0:T(128)} %get-tuple-element.48) | copy-start | bytes 28
  146.0 16.4 %copy-start.43 = (f32[2]{0:T(128)S(1)}, f32[2]{0:T(128)}, u32[]{:S(2)}) copy-start(f32[2]{0:T(128)} %get-tuple-element.49) | copy-start | bytes 28
  146.0 16.4 %copy-start.44 = (f32[2]{0:T(128)S(1)}, f32[2]{0:T(128)}, u32[]{:S(2)}) copy-start(f32[2]{0:T(128)} %get-tuple-element.50) | copy-start | bytes 28
  146.0 16.4 %copy-start.45 = (f32[2]{0:T(128)S(1)}, f32[2]{0:T(128)}, u32[]{:S(2)}) copy-start(f32[2]{0:T(128)} %get-tuple-element.51) | copy-start | bytes 28
  146.0 16.4 %copy-start.46 = (f32[2]{0:T(128)S(1)}, f32[2]{0:T(128)}, u32[]{:S(2)}) copy-start(f32[2]{0:T(128)} %get-tuple-element.52) | copy-start | bytes 28
  146.1 16.4 %copy-start.47 = (f32[2]{0:T(128)S(1)}, f32[2]{0:T(128)}, u32[]{:S(2)}) copy-start(f32[2]{0:T(128)} %get-tuple-element.53) | copy-start | bytes 28
  146.1 16.4 %copy-start.48 = (f32[2]{0:T(128)S(1)}, f32[2]{0:T(128)}, u32[]{:S(2)}) copy-start(f32[2]{0:T(128)} %get-tuple-element.54) | copy-start | bytes 28
  146.1 16.4 %copy-start.49 = (f32[2]{0:T(128)S(1)}, f32[2]{0:T(128)}, u32[]{:S(2)}) copy-start(f32[2]{0:T(128)} %get-tuple-element.55) | copy-start | bytes 28
  156.9 10.0 %collective-permute-start.25 = (f32[16,2,68]{2,0,1:T(8,128)S(1)}, f32[16,2,68]{2,0,1:T(8,128)S(1)}, u32[]{:S(2)}, u32[]{:S(2)}) collective-permute-start(f32[16,2,68]{2,0,1:T(8,128)S(1)} %copy.205), channel_id=1, source_target_pairs={{2,0},{4,2},{6,4},{3,1},{5,3},{7,5},{10,8},{12,10},{14,12},{11,9},... | collective-permute-start | bytes 26120 | tf_op jit(solution)/shard_map/ppermute | solution.py:21
  158.2 8.7 %collective-permute-start.24 = (f32[16,2,68]{2,0,1:T(8,128)S(1)}, f32[16,2,68]{2,0,1:T(8,128)S(1)}, u32[]{:S(2)}, u32[]{:S(2)}) collective-permute-start(f32[16,2,68]{2,0,1:T(8,128)S(1)} %copy.204), channel_id=1, source_target_pairs={{0,2},{2,4},{4,6},{1,3},{3,5},{5,7},{8,10},{10,12},{12,14},{9,11},... | collective-permute-start | bytes 26120 | tf_op jit(solution)/shard_map/ppermute | solution.py:20
  167.1 10.6 %collective-permute-start.26 = (f32[2,20,68]{2,1,0:T(8,128)S(1)}, f32[2,20,68]{2,1,0:T(8,128)S(1)}, u32[]{:S(2)}, u32[]{:S(2)}) collective-permute-start(f32[2,20,68]{2,1,0:T(8,128)S(1)} %get-tuple-element.105), channel_id=1, source_target_pairs={{1,0},{3,2},{5,4},{7,6},{9,8},{11,10},{13,12},{15,14},{17,16},{19,... | collective-permute-start | bytes 32648 | tf_op jit(solution)/shard_map/ppermute | solution.py:21
  173.7 4.9 %collective-permute-start.27 = (f32[2,20,68]{2,1,0:T(8,128)S(1)}, f32[2,20,68]{2,1,0:T(8,128)S(1)}, u32[]{:S(2)}, u32[]{:S(2)}) collective-permute-start(f32[2,20,68]{2,1,0:T(8,128)S(1)} %get-tuple-element.104), channel_id=1, source_target_pairs={{0,1},{2,3},{4,5},{6,7},{8,9},{10,11},{12,13},{14,15},{16,17},{18,... | collective-permute-start | bytes 32648 | tf_op jit(solution)/shard_map/ppermute | solution.py:20
  (32 other events, 106.5 us)
where the time goes:
time: 186 us; the launch traced here: 184 us
  starting transfers between devices  73.4 us (39%)
  local copies, waits for them, and re-layouts  37 us (20%)
  other arithmetic  32.7 us (18%)
  waiting for transfers between devices  32.5 us (17%)
  blocking collectives  5.11 us (3%)
  between operations  1.94 us (1%)
    ppermute x14, starting transfers between devices, extended(): before = lax.ppermute(last, axis, up)  51.8 us
    ppermute x14, waiting for transfers between devices, extended(): after = lax.ppermute(initial, axis, down)  24.3 us
    ppermute x14, starting transfers between devices, extended(): after = lax.ppermute(initial, axis, down)  21.5 us
    add x6, other arithmetic, convolve_axis(): summed + kernel_rows[:, offset].reshape(weight_shape) * lax.slice_in_dim(...  16.7 us
    slice x20, local copies, waits for them, and re-layouts, restrict_axis(): lax.slice_in_dim(padded, first, first + 2 * count - 1, stride=2, axis=axi...  15.5 us
    mul x4, local copies, waits for them, and re-layouts, convolve_axis(): kernel_rows[:, 0].reshape(weight_shape)  9.51 us
    ppermute x14, waiting for transfers between devices, extended(): before = lax.ppermute(last, axis, up)  8.18 us
    reduce_sum x2, other arithmetic, stencil_box(): return jnp.sum(smoothed, axis=0)  6.53 us
  transfers between devices with their start and end apart: 28, of which 14 were waited for; matrix products, arithmetic and copies ran while one was open for 21% of the time, Pallas kernels for 0%

commit v1 on v0

v1 whole, which is shorter than its diff:
```python
import jax
import jax.numpy as jnp
from jax import lax
from jax.sharding import PartitionSpec as P

RADIUS = 8
TAPS = 17
WEIGHTS = ((-3, -0.0625), (-1, 0.5625), (0, 1.0), (1, 0.5625), (3, -0.0625))
EXACT = lax.Precision.HIGHEST


def interpolation(difference):
    out = jnp.zeros(difference.shape, jnp.float32)
    for offset, weight in WEIGHTS:
        out = jnp.where(difference == offset, weight, out)
    return out


def banded(taps, rows, columns, valid):
    offset = columns[None, :] - rows[:, None] + RADIUS
    out = jnp.zeros((taps.shape[0],) + offset.shape, jnp.float32)
    for tap in range(TAPS):
        out = jnp.where((offset == tap)[None], taps[:, tap, None, None], out)
    return jnp.where(valid[None, None, :], out, 0.0)


class Axis:
    def __init__(self, name, length):
        self.name, self.length = name, length
        self.count, self.index = lax.axis_size(name), lax.axis_index(name)
        mid, coarse = length // 2, length // 4
        self.first = (0, -1, -2)
        self.extent = (length, mid + 3, coarse + 5)
        self.brick = (length, mid, coarse)
        fine_rows = jnp.arange(length)
        mid_rows = jnp.arange(mid + 3) - 1
        coarse_rows = jnp.arange(coarse + 5) - 2
        self.rows = (fine_rows, mid_rows, coarse_rows)

        def inside(rows, brick):
            place = rows + self.index * brick
            return (place >= 0) & (place < brick * self.count)

        to_mid = interpolation(fine_rows[None, :] - 2 * mid_rows[:, None])
        self.to_mid = jnp.where(inside(mid_rows, mid)[:, None], to_mid, 0.0)
        to_coarse = interpolation(mid_rows[None, :] - 2 * coarse_rows[:, None])
        self.to_coarse = jnp.where(inside(coarse_rows, coarse)[:, None], to_coarse, 0.0)
        self.own = [(self.rows[level], jnp.full((self.extent[level],), True)) for level in range(3)]

    def from_brick(self, level, steps, low, size):
        places = self.first[level] + low + jnp.arange(size) + steps * self.brick[level]
        other = self.index + steps
        valid = (other >= 0) & (other < self.count)
        return places, jnp.broadcast_to(valid, (size,))

    def operators(self, taps, places):
        columns = [
            (jnp.concatenate([p for p, _ in level]), jnp.concatenate([v for _, v in level]))
            for level in places
        ]
        bands = [banded(taps[level], self.rows[level], *columns[level]) for level in range(3)]
        mid = jnp.einsum("ko,tkj->toj", self.to_mid, bands[1], precision=EXACT)
        widen = jnp.dot(self.to_coarse, self.to_mid, precision=EXACT)
        coarse = jnp.einsum("ko,tkj->toj", widen, bands[2], precision=EXACT)
        return bands[0], mid, coarse


def edge(x, dim, width, last):
    length = x.shape[dim]
    return lax.slice_in_dim(x, length - width, length, axis=dim) if last else lax.slice_in_dim(x, 0, width, axis=dim)


def hop(arrays, axis, dim, widths, steps, routes):
    gathered = [[] for _ in arrays]
    places = [[] for _ in arrays]
    below = None
    for names, pairs, up, below in routes:
        for level, (x, width) in enumerate(zip(arrays, widths)):
            if not width:
                continue
            size = x.shape[dim]
            message = jnp.where(up, edge(x, dim, width, True), edge(x, dim, width, False))
            gathered[level].append(lax.ppermute(message, names, pairs))
            lower = axis.from_brick(level, -steps, size - width, width)
            higher = axis.from_brick(level, steps, 0, width)
            places[level].append(tuple(jnp.where(below, a, b) for a, b in zip(lower, higher)))
    if len(routes) == 2 and not isinstance(below, bool):
        for level in range(3):
            a, b = gathered[level]
            gathered[level] = [jnp.where(below, b, a), jnp.where(below, a, b)]
            a, b = places[level]
            places[level] = [tuple(jnp.where(below, q, p) for p, q in zip(a, b)), tuple(jnp.where(below, p, q) for p, q in zip(a, b))]
    return gathered, places


def ring(axis):
    n = axis.count
    up = [(i, (i + 1) % n) for i in range(n)]
    return [((axis.name,), up, True, True), ((axis.name,), [(b, a) for a, b in up], False, False)]


def folded(axis, beside):
    n, m = axis.count, lax.axis_size(beside)
    pairs = []
    for c in range(0, m, 2):
        cycle = [c * n + i for i in range(n)] + [(c + 1) * n + i for i in reversed(range(n))]
        pairs += list(zip(cycle, cycle[1:] + cycle[:1]))
    even = lax.axis_index(beside) % 2 == 0
    names = (beside, axis.name)
    return [(names, pairs, even, even), (names, [(b, a) for a, b in pairs], ~even, ~even)]


def swap(axis, steps):
    n = axis.count
    pairs = [(i, i + steps) for i in range(n - steps)]
    up = axis.index + steps < n
    return [((axis.name,), pairs + [(b, a) for a, b in pairs], up, ~up)]


def line(axis, steps):
    n = axis.count
    pairs = [(i, i + steps) for i in range(n - steps)]
    return [((axis.name,), pairs, True, True), ((axis.name,), [(b, a) for a, b in pairs], False, False)]


def near(axis, beside):
    if axis.count <= 2:
        return swap(axis, 1)
    if beside is not None and lax.axis_size(beside) % 2 == 0:
        return folded(axis, beside)
    return ring(axis)


def gather(arrays, axis, dim, beside):
    coarse = axis.brick[2]
    spill = axis.extent[2] - coarse
    widths = (RADIUS, RADIUS + 3, min(axis.extent[2], RADIUS + spill))
    pieces = [[x] for x in arrays]
    places = [[own] for own in axis.own]
    if axis.count > 1:
        got, where = hop(arrays, axis, dim, widths, 1, near(axis, beside))
        for level in range(3):
            pieces[level] += got[level]
            places[level] += where[level]
    steps = 2
    while steps < axis.count and (steps - 1) * coarse <= RADIUS + 4:
        width = min(axis.extent[2], RADIUS + 4 + 1 - (steps - 1) * coarse)
        routes = swap(axis, steps) if axis.count <= 2 * steps else line(axis, steps)
        got, where = hop(arrays, axis, dim, (0, 0, width), steps, routes)
        pieces[2] += got[2]
        places[2] += where[2]
        steps += 1
    return [jnp.concatenate(p, axis=dim) for p in pieces], places


def local(charges, kernel_taps):
    az, ay, ax = (Axis(name, size) for name, size in zip(("gz", "gy", "gx"), charges.shape))

    def shrink(x, z, y, w):
        x = jnp.einsum("zyx,kx->zyk", x, w, precision=EXACT)
        x = jnp.einsum("zyx,ky->zkx", x, y, precision=EXACT)
        return jnp.einsum("zyx,kz->kyx", x, z, precision=EXACT)

    mid = shrink(charges, az.to_mid, ay.to_mid, ax.to_mid)
    coarse = shrink(mid, az.to_coarse, ay.to_coarse, ax.to_coarse)
    grids = [charges, mid, coarse]
    grids, places = gather(grids, az, 0, None)
    oz = az.operators(kernel_taps, places)
    grids, places = gather(grids, ay, 1, "gx")
    oy = ay.operators(kernel_taps, places)
    grids, places = gather(grids, ax, 2, None)
    ox = ax.operators(kernel_taps, places)
    total = 0.0
    for level in range(3):
        x = jnp.einsum("zyx,tkx->tzyk", grids[level], ox[level], precision=EXACT)
        x = jnp.einsum("tzyx,tky->tzkx", x, oy[level], precision=EXACT)
        total = total + jnp.einsum("tzyx,tkz->kyx", x, oz[level], precision=EXACT)
    return total


def solution(mesh):
    return jax.shard_map(
        local,
        mesh=mesh,
        in_specs=(P("gz", "gy", "gx"), P()),
        out_specs=P("gz", "gy", "gx"),
        check_vma=False,
    )
```

time: 186 us -> 93.8 us (0.50)
  starting transfers between devices: 73.4 us -> 19.5 us
  matrix products: 1.25 us -> 25.5 us
  other arithmetic: 32.7 us -> 11.8 us
  waiting for transfers between devices: 32.5 us -> 12.7 us
  local copies, waits for them, and re-layouts: 37 us -> 22.1 us
  blocking collectives: 5.11 us -> 0 us
    ppermute x28 -> x16, starting transfers between devices: 73.4 us -> 19.5 us  [hop(): gathered[level].append(lax.ppermute(message, names, pairs))]
    dot_general x2 -> x24, matrix products: 1.25 us -> 25.5 us  [the longest x3 6.52 us: local(): x = jnp.einsum('zyx,tkx->tzyk', grids[level], ox[level], precision=EXACT)]
    ppermute x28 -> x16, waiting for transfers between devices: 32.5 us -> 12.7 us  [hop(): gathered[level].append(lax.ppermute(message, names, pairs))]
    add x15 -> x3, other arithmetic: 18.1 us -> 0.01 us  [from_brick(): self.first[level] + low + jnp.arange(size) + steps * self.brick[level]]
    slice x35 -> x12, local copies, waits for them, and re-layouts: 20.4 us -> 10.2 us  [the longest x3 4.52 us: edge(): lax.slice_in_dim(x, 0, width, axis=dim)]
    mul x20 -> x0, local copies, waits for them, and re-layouts: 9.64 us -> none  [the longest x4 9.51 us: convolve_axis(): kernel_rows[:, 0].reshape(weight_shape)]
    ppermute x2 -> x6, local copies, waits for them, and re-layouts: 0.02 us -> 8.35 us  [hop(): gathered[level].append(lax.ppermute(message, names, pairs))]
    reduce_sum x2 -> x0, other arithmetic: 6.53 us -> none  [stencil_box(): return jnp.sum(smoothed, axis=0)]
  transfers between devices with their start and end apart: 28 -> 16, of which waited for: 14 -> 4; matrix products, arithmetic and copies ran while one was open for 21% -> 41% of each run, Pallas kernels for 0% -> 0%
where the time goes in v1:
time: 93.8 us; the launch traced here: 93.3 us
  matrix products  25.5 us (27%)
  local copies, waits for them, and re-layouts  22.1 us (24%)
  starting transfers between devices  19.5 us (21%)
  waiting for transfers between devices  12.7 us (14%)
  other arithmetic  11.8 us (13%)
  between operations  1.66 us (2%)
    ppermute x16, starting transfers between devices, hop(): gathered[level].append(lax.ppermute(message, names, pairs))  19.5 us
    ppermute x16, waiting for transfers between devices, hop(): gathered[level].append(lax.ppermute(message, names, pairs))  12.7 us
    ppermute x6, local copies, waits for them, and re-layouts, hop(): gathered[level].append(lax.ppermute(message, names, pairs))  8.35 us
    dot_general x3, matrix products, local(): x = jnp.einsum('zyx,tkx->tzyk', grids[level], ox[level], precision=EXACT)  6.52 us
    dot_general x3, matrix products, local(): x = jnp.einsum('tzyx,tky->tzkx', x, oy[level], precision=EXACT)  4.68 us
    slice x3, local copies, waits for them, and re-layouts, edge(): lax.slice_in_dim(x, 0, width, axis=dim)  4.52 us
    dot_general x3, matrix products, local(): total = total + jnp.einsum('tzyx,tkz->kyx', x, oz[level], precision=EXACT)  3.91 us
    slice x6, local copies, waits for them, and re-layouts, edge(): lax.slice_in_dim(x, length - width, length, axis=dim)  3.7 us
  transfers between devices with their start and end apart: 16, of which 4 were waited for; matrix products, arithmetic and copies ran while one was open for 41% of the time, Pallas kernels for 0%

profile of v1, /device:TPU:1, one launch (start us, length us, event | category | flops | bytes accessed | tf_op | source)
XLA Modules:
  0.0 93.3 jit_solution(2006803883098044591)
XLA Ops:
  0.0 1.6 %slice_select_fusion.3 = f32[8,32,128]{2,1,0:T(8,128)} fusion(f32[32,32,128]{2,1,0:T(8,128)} %param.2, pred[]{:T(512)S(6)} %lt.104), kind=kLoop, calls=%fused_computation.86 | loop fusion | flops 32768 | bytes 393217 | tf_op jit(solution)/shard_map/jit(_where)/select_n | solution.py:82
  1.6 2.1 %collective-permute-start = (f32[8,32,128]{2,1,0:T(8,128)}, f32[8,32,128]{2,1,0:T(8,128)S(1)}, u32[]{:S(2)}, u32[]{:S(2)}) collective-permute-start(f32[8,32,128]{2,1,0:T(8,128)} %slice_select_fusion.3), channel_id=1, source_target_pairs={{0,1},{1,0},{2,3},{3,2},{4,5},{5,4},{6,7},{7,6},{8,9},{9,8},{10,11... | collective-permute-start | bytes 393224 | tf_op jit(solution)/shard_map/ppermute | solution.py:83
  3.8 1.7 %convolution_bitcast_fusion.2 = f32[32,32,67]{2,1,0:T(8,128)S(1)} fusion(f32[32,32,128]{2,1,0:T(8,128)} %param.2, s32[67]{0:T(128)S(1)} %get-tuple-element.241, pred[67]{0:T(512)(128)(4,1)S(1)} %compare_and_fusion.3), kind=kOutput, calls=%fused_computation.21 | convolution fusion | flops 105484800 | bytes 799055 | tf_op jit(solution)/shard_map/zyx,kx->zyk/dot_general | solution.py:160
  5.5 0.5 convolution_bitcast_fusion.5
  6.6 0.6 fusion.35
  7.9 1.5 %collective-permute-start.10 = (f32[13,13,37]{2,0,1:T(8,128)S(1)}, f32[13,13,37]{2,0,1:T(8,128)S(1)}, u32[]{:S(2)}, u32[]{:S(2)}) collective-permute-start(f32[13,13,37]{2,0,1:T(8,128)S(1)} %fusion.38), channel_id=1, source_target_pairs={{0,1},{1,0},{2,3},{3,2},{4,5},{5,4},{6,7},{7,6},{8,9},{9,8},{10,11... | collective-permute-start | bytes 75044 | tf_op jit(solution)/shard_map/ppermute | solution.py:83
  10.3 1.1 %slice_reduce_fusion.50 = (f32[2]{0:T(128)}, f32[2]{0:T(128)}, f32[2]{0:T(128)}, f32[2]{0:T(128)}, f32[2]{0:T(128)}, /*index=5*/f32[2]{0:T(128)}, f32[2]{0:T(128...) fusion(f32[2,17]{1,0:T(2,128)S(1)} %get-tuple-element.73), kind=kLoop, calls=%fused_computation.886 | loop fusion | bytes 272 | tf_op jit(solution)/shard_map/slice | solution.py:23
  11.4 0.9 fusion.114
  12.3 0.7 fusion.409
  13.1 0.7 fusion.444
  13.8 0.5 slice_reduce_fusion.33
  14.9 0.5 slice_reduce_fusion.16
  16.1 0.7 pad_add_fusion.1
  17.1 0.9 %convolution_bitcast_fusion.12 = f32[2,32,30,1]{1,2,0,3:T(8,128)} fusion(f32[2]{0:T(128)S(1)} %get-tuple-element.23, f32[2]{0:T(128)S(1)} %get-tuple-element.24, f32[2]{0:T(128)S(1)} %get-tuple-element.25, f32[2]{0:T(128)S(1)} %get-tuple-element.26, f32[2]{0:T(128)S(1)} %get-tuple-element.27, f32[2]{0:T(128)S(1)} %get-tuple-element.28, ...), kind=kOutput, calls=%fused_computation.33 | convolution fusion | flops 465576 | bytes 17631 | tf_op jit(solution)/shard_map/ko,tkj->toj/dot_general | solution.py:62
  18.0 0.9 convolution_bitcast_fusion.11
  18.9 1.2 %convolution_bitcast_fusion.7 = f32[2,128,89,1]{1,2,3,0:T(8,128)} fusion(f32[2]{0:T(128)S(1)} %get-tuple-element.23, f32[2]{0:T(128)S(1)} %get-tuple-element.24, f32[2]{0:T(128)S(1)} %get-tuple-element.25, f32[2]{0:T(128)S(1)} %get-tuple-element.26, f32[2]{0:T(128)S(1)} %get-tuple-element.27, f32[2]{0:T(128)S(1)} %get-tuple-element.28, ...), kind=kOutput, calls=%fused_computation.28 | convolution fusion | flops 18635916 | bytes 193067 | tf_op jit(solution)/shard_map/ko,tkj->toj/dot_general | solution.py:62
  20.1 0.9 %convolution_bitcast_fusion.10 = f32[2,32,26,1]{1,2,0,3:T(8,128)} fusion(f32[13,32,1]{1,0,2:T(8,128)S(1)} %convolution_bitcast_fusion.15, f32[2]{0:T(128)S(1)} %get-tuple-element.6, f32[2]{0:T(128)S(1)} %get-tuple-element.7, f32[2]{0:T(128)S(1)} %get-tuple-element.8, f32[2]{0:T(128)S(1)} %get-tuple-element.9, f32[2]{0:T(128)S(1)} %get-tuple-element.10, ...), kind=kOutput, calls=%fused_computation.31 | convolution fusion | flops 271752 | bytes 14228 | tf_op jit(solution)/shard_map/ko,tkj->toj/dot_general | solution.py:64
  21.0 0.9 convolution_bitcast_fusion.9
  21.9 1.0 %convolution_bitcast_fusion.8 = f32[2,128,63,1]{1,2,3,0:T(8,128)} fusion(f32[37,128,1]{1,0,2:T(8,128)S(1)} %convolution_bitcast_fusion.13, f32[2]{0:T(128)S(1)} %get-tuple-element.6, f32[2]{0:T(128)S(1)} %get-tuple-element.7, f32[2]{0:T(128)S(1)} %get-tuple-element.8, f32[2]{0:T(128)S(1)} %get-tuple-element.9, f32[2]{0:T(128)S(1)} %get-tuple-element.10, ...), kind=kOutput, calls=%fused_computation.29 | convolution fusion | flops 7244748 | bytes 123282 | tf_op jit(solution)/shard_map/ko,tkj->toj/dot_general | solution.py:64
  23.0 0.7 pad_add_fusion
  23.7 0.5 concatenate.81
  24.2 1.3 %collective-permute-start.11 = (f32[26,13,37]{2,0,1:T(8,128)S(1)}, f32[26,13,37]{2,0,1:T(8,128)S(1)}, u32[]{:S(2)}, u32[]{:S(2)}) collective-permute-start(f32[26,13,37]{2,0,1:T(8,128)S(1)} %pad_maximum_fusion.5), channel_id=1, source_target_pairs={{2,0},{4,2},{6,4},{14,6},{12,14},{10,12},{8,10},{0,8},{18,16},{20,... | collective-permute-start | bytes 150080 | tf_op jit(solution)/shard_map/ppermute | solution.py:83
  25.8 2.3 %collective-permute-start.13 = (f32[26,5,37]{2,0,1:T(8,128)S(1)}, f32[26,5,37]{2,0,1:T(8,128)S(1)}, u32[]{:S(2)}, u32[]{:S(2)}) collective-permute-start(f32[26,5,37]{2,0,1:T(8,128)S(1)} %fusion.60), channel_id=1, source_target_pairs={{0,4},{2,6},{4,0},{6,2},{1,5},{3,7},{5,1},{7,3},{8,12},{10,14},{12... | collective-permute-start | bytes 57728 | tf_op jit(solution)/shard_map/ppermute | solution.py:83
  28.1 0.8 broadcast_select_fusion.5
  28.9 1.4 %collective-permute-start.6 = (f32[30,11,67]{2,0,1:T(8,128)}, f32[30,11,67]{2,0,1:T(8,128)}, u32[]{:S(2)}, u32[]{:S(2)}) collective-permute-start(f32[30,11,67]{2,0,1:T(8,128)} %get-tuple-element.66), channel_id=1, source_target_pairs={{2,0},{4,2},{6,4},{14,6},{12,14},{10,12},{8,10},{0,8},{18,16},{20,... | collective-permute-start | bytes 265328 | tf_op jit(solution)/shard_map/ppermute | solution.py:83
  30.3 2.9 %collective-permute-start.7 = (f32[30,11,67]{2,0,1:T(8,128)}, f32[30,11,67]{2,0,1:T(8,128)}, u32[]{:S(2)}, u32[]{:S(2)}) collective-permute-start(f32[30,11,67]{2,0,1:T(8,128)} %get-tuple-element.67), channel_id=1, source_target_pairs={{0,2},{2,4},{4,6},{6,14},{14,12},{12,10},{10,8},{8,0},{16,18},{18,... | collective-permute-start | bytes 265328 | tf_op jit(solution)/shard_map/ppermute | solution.py:83
  33.2 2.3 %collective-permute-done.13 = f32[26,5,37]{2,0,1:T(8,128)S(1)} collective-permute-done((f32[26,5,37]{2,0,1:T(8,128)S(1)}, f32[26,5,37]{2,0,1:T(8,128)S(1)}, u32[]{:S(2)}, u32[]{:S(2)}) %collective-permute-start.13) | collective-permute-done | bytes 19272 | tf_op jit(solution)/shard_map/ppermute | solution.py:83
  35.9 1.1 %copy.21 = f32[26,44,13]{1,2,0:T(8,128)} copy(f32[26,44,13]{2,0,1:T(8,128)S(1)} %get-tuple-element.59) | data formatting | bytes 118976 | tf_op jit(solution)/shard_map/slice | solution.py:70
  37.0 2.8 %collective-permute-start.15 = (f32[26,44,13]{1,2,0:T(8,128)}, f32[26,44,13]{1,2,0:T(8,128)S(1)}, u32[]{:S(2)}, u32[]{:S(2)}) collective-permute-start(f32[26,44,13]{1,2,0:T(8,128)} %copy.21), channel_id=1, source_target_pairs={{8,0},{16,8},{24,16},{0,24},{9,1},{17,9},{25,17},{1,25},{10,2},{18... | collective-permute-start | bytes 178472 | tf_op jit(solution)/shard_map/ppermute | solution.py:83
  39.8 0.5 copy.20
  40.3 1.3 %collective-permute-start.14 = (f32[26,44,13]{1,2,0:T(8,128)S(1)}, f32[26,44,13]{1,2,0:T(8,128)}, u32[]{:S(2)}, u32[]{:S(2)}) collective-permute-start(f32[26,44,13]{1,2,0:T(8,128)S(1)} %copy.20), channel_id=1, source_target_pairs={{0,8},{8,16},{16,24},{24,0},{1,9},{9,17},{17,25},{25,1},{2,10},{10... | collective-permute-start | bytes 178472 | tf_op jit(solution)/shard_map/ppermute | solution.py:83
  41.6 0.8 slice_select_fusion.2
  42.4 4.6 %collective-permute-done.15 = f32[26,44,13]{1,2,0:T(8,128)S(1)} collective-permute-done((f32[26,44,13]{1,2,0:T(8,128)}, f32[26,44,13]{1,2,0:T(8,128)S(1)}, u32[]{:S(2)}, u32[]{:S(2)}) %collective-permute-start.15) | collective-permute-done | bytes 59520 | tf_op jit(solution)/shard_map/ppermute | solution.py:83
  47.0 0.7 copy.23
  47.8 1.7 %copy.22 = f32[26,44,13]{2,0,1:T(8,128)S(1)} copy(f32[26,44,13]{1,2,0:T(8,128)} %collective-permute-done.14) | data formatting | bytes 118976 | tf_op jit(solution)/shard_map/ppermute | solution.py:83
  49.5 0.4 pad_maximum_fusion.2
  50.3 1.3 %convolution_bitcast_fusion = f32[2,26,44,128]{3,2,1,0:T(8,128)S(1)} fusion(f32[2,128,63,1]{1,2,3,0:T(8,128)S(1)} %copy-done.7, f32[26,44,63]{2,0,1:T(8,128)S(1)} %pad_maximum_fusion.2), kind=kOutput, calls=%fused_computation.15 | convolution fusion | flops 221405184 | bytes 1524256 | tf_op jit(solution)/shard_map/zyx,tkx->tzyk/dot_general | solution.py:175
  51.7 1.0 %broadcast_select_fusion.4 = (f32[30,11,67]{2,0,1:T(8,128)S(1)}, f32[30,11,67]{2,0,1:T(8,128)S(1)}) fusion(f32[30,11,67]{2,0,1:T(8,128)} %collective-permute-done.6, f32[30,11,67]{2,0,1:T(8,128)} %collective-permute-done.7, pred[]{:T(512)S(6)} %not.11), kind=kLoop, calls=%fused_computation.91 | loop fusion | flops 44220 | bytes 353761 | tf_op jit(solution)/shard_map/jit(_where)/select_n | solution.py:90
  53.0 1.2 %copy.12 = f32[30,41,11]{1,0,2:T(8,128)} copy(f32[30,41,11]{2,0,1:T(8,128)S(1)} %get-tuple-element.61) | data formatting | bytes 108240 | tf_op jit(solution)/shard_map/slice | solution.py:70
  54.2 0.5 copy.11
  54.8 1.8 %collective-permute-start.8 = (f32[30,41,11]{1,0,2:T(8,128)S(1)}, f32[30,41,11]{1,0,2:T(8,128)S(1)}, u32[]{:S(2)}, u32[]{:S(2)}) collective-permute-start(f32[30,41,11]{1,0,2:T(8,128)S(1)} %copy.11), channel_id=1, source_target_pairs={{0,8},{8,16},{16,24},{24,0},{1,9},{9,17},{17,25},{25,1},{2,10},{10... | collective-permute-start | bytes 162368 | tf_op jit(solution)/shard_map/ppermute | solution.py:83
  56.6 1.6 %convolution_bitcast_fusion.1 = f32[2,26,32,128]{3,2,1,0:T(8,128)S(1)} fusion(f32[2,44,32,1]{1,2,3,0:T(8,128)} %convolution_bitcast_fusion.9, f32[2,26,44,128]{3,2,1,0:T(8,128)S(1)} %convolution_bitcast_fusion), kind=kOutput, calls=%fused_computation.17 | convolution fusion | flops 112459776 | bytes 2034688 | tf_op jit(solution)/shard_map/tzyx,tky->tzkx/dot_general | solution.py:176
  58.2 2.9 %collective-permute-done.9 = f32[30,41,11]{1,0,2:T(8,128)S(1)} collective-permute-done((f32[30,41,11]{1,0,2:T(8,128)}, f32[30,41,11]{1,0,2:T(8,128)S(1)}, u32[]{:S(2)}, u32[]{:S(2)}) %collective-permute-start.9) | collective-permute-done | bytes 54152 | tf_op jit(solution)/shard_map/ppermute | solution.py:83
  61.0 0.7 copy.14
  61.8 0.7 copy.13
  62.5 0.4 pad_maximum_fusion.4
  63.0 0.5 copy-done.6
  63.4 1.5 %fusion.28 = f32[2,128,30,41]{1,3,2,0:T(8,128)S(1)} fusion(f32[2,128,89,1]{1,2,3,0:T(8,128)S(1)} %copy-done.6, f32[30,41,89]{2,0,1:T(8,128)S(1)} %pad_maximum_fusion.4), kind=kOutput, calls=%fused_computation.40 | convolution fusion | flops 336291840 | bytes 1788536 | tf_op jit(solution)/shard_map/zyx,tkx->tzyk/dot_general | solution.py:175
  64.9 1.0 %broadcast_select_fusion.7 = (f32[40,8,128]{2,1,0:T(8,128)S(1)}, f32[40,8,128]{2,1,0:T(8,128)S(1)}) fusion(f32[40,8,128]{2,1,0:T(8,128)} %collective-permute-done.1, f32[40,8,128]{2,1,0:T(8,128)} %collective-permute-done.2, pred[]{:T(512)S(6)} %not.11), kind=kLoop, calls=%fused_computation.97 | loop fusion | flops 81920 | bytes 655361 | tf_op jit(solution)/shard_map/jit(_where)/select_n | solution.py:90
  66.0 0.6 copy-done.4
  66.7 1.3 %fusion.873 = (f32[40,48,8]{2,1,0:T(8,128)S(1)}, f32[40,48,8]{2,1,0:T(8,128)}) fusion(f32[40,48,128]{2,1,0:T(8,128)S(1)} %pad_maximum_fusion), kind=kLoop, calls=%fused_computation.1044 | loop fusion | bytes 245760 | tf_op jit(solution)/shard_map/slice | solution.py:70
  68.0 2.2 %copy.6 = f32[40,48,8]{1,2,0:T(8,128)} copy(f32[40,48,8]{2,1,0:T(8,128)} %get-tuple-element.57) | data formatting | bytes 122880 | tf_op jit(solution)/shard_map/slice | solution.py:70
  70.1 1.0 %copy.5 = f32[40,48,8]{1,2,0:T(8,128)} copy(f32[40,48,8]{2,1,0:T(8,128)S(1)} %get-tuple-element.56) | data formatting | bytes 122880 | tf_op jit(solution)/shard_map/slice | solution.py:70
  71.1 1.7 %collective-permute-start.3 = (f32[40,48,8]{1,2,0:T(8,128)}, f32[40,48,8]{1,2,0:T(8,128)}, u32[]{:S(2)}, u32[]{:S(2)}) collective-permute-start(f32[40,48,8]{1,2,0:T(8,128)} %copy.5), channel_id=1, source_target_pairs={{0,8},{8,16},{16,24},{24,0},{1,9},{9,17},{17,25},{25,1},{2,10},{10... | collective-permute-start | bytes 184328 | tf_op jit(solution)/shard_map/ppermute | solution.py:83
  72.9 1.0 %fusion.16 = f32[2,30,32,128]{3,2,1,0:T(8,128)S(1)} fusion(f32[2,41,32,1]{1,2,3,0:T(8,128)S(1)} %copy-done.10, f32[2,128,30,41]{1,3,2,0:T(8,128)S(1)} %fusion.28), kind=kOutput, calls=%fused_computation.16 | convolution fusion | flops 120913920 | bytes 2253056 | tf_op jit(solution)/shard_map/tzyx,tky->tzkx/dot_general | solution.py:176
  74.2 2.9 %collective-permute-done.4 = f32[40,48,8]{1,2,0:T(8,128)} collective-permute-done((f32[40,48,8]{1,2,0:T(8,128)}, f32[40,48,8]{1,2,0:T(8,128)}, u32[]{:S(2)}, u32[]{:S(2)}) %collective-permute-start.4) | collective-permute-done | bytes 61472 | tf_op jit(solution)/shard_map/ppermute | solution.py:83
  77.1 2.2 %copy.8 = f32[40,48,8]{2,1,0:T(8,128)} copy(f32[40,48,8]{1,2,0:T(8,128)} %collective-permute-done.4) | data formatting | bytes 122880 | tf_op jit(solution)/shard_map/ppermute | solution.py:83
  79.3 2.2 %copy.7 = f32[40,48,8]{2,1,0:T(8,128)} copy(f32[40,48,8]{1,2,0:T(8,128)} %collective-permute-done.3) | data formatting | bytes 122880 | tf_op jit(solution)/shard_map/ppermute | solution.py:83
  82.0 3.7 %fusion = f32[2,128,40,48]{1,3,2,0:T(8,128)S(1)} fusion(f32[40,48,8]{2,1,0:T(8,128)} %copy.8, f32[40,48,8]{2,1,0:T(8,128)} %copy.7, f32[40,8,128]{2,1,0:T(8,128)S(1)} %copy-done.5, f32[40,8,128]{2,1,0:T(8,128)S(1)} %get-tuple-element.70, f32[40,32,128]{2,1,0:T(8,128)S(1)} %copy-done.2, f32[2]{0:T(128)S(1)} %copy-done.50, f32[2]{0:T(128)S(1)} %copy-done.51, ...), kind=kOutput, calls=%fused_computation.1 | convolution fusion | flops 851116032 | bytes 3385624 | tf_op jit(solution)/shard_map/zyx,tkx->tzyk/dot_general | solution.py:175
  85.9 2.1 %fusion.13 = f32[2,40,32,128]{3,2,1,0:T(8,128)S(1)} fusion(f32[2,128,40,48]{1,3,2,0:T(8,128)S(1)} %fusion, f32[2]{0:T(128)S(1)} %copy-done.50, f32[2]{0:T(128)S(1)} %copy-done.51, f32[2]{0:T(128)S(1)} %copy-done.52, f32[2]{0:T(128)S(1)} %copy-done.53, f32[2]{0:T(128)S(1)} %copy-done.54, f32[2]{0:T(128)S(1)} %copy-done.55, f32[2]{0:T(128)S(1)} %copy-done.56, ...), kind=kOutput, calls=%fused_computation.14 | convolution fusion | flops 188798976 | bytes 3303096 | tf_op jit(solution)/shard_map/tzyx,tky->tzkx/dot_general | solution.py:176
  88.2 1.6 %fusion.21 = f32[32,32,128]{2,0,1:T(8,128)S(1)} fusion(f32[2,40,32,128]{3,2,1,0:T(8,128)S(1)} %fusion.13, f32[2]{0:T(128)S(1)} %copy-done.50, f32[2]{0:T(128)S(1)} %copy-done.51, f32[2]{0:T(128)S(1)} %copy-done.52, f32[2]{0:T(128)S(1)} %copy-done.53, f32[2]{0:T(128)S(1)} %copy-done.54, f32[2]{0:T(128)S(1)} %copy-done.55, f32[2]{0:T(128)S(1)} %copy-done.56, ...), kind=kOutput, calls=%fused_computation.20 | convolution fusion | flops 125875200 | bytes 1856944 | tf_op jit(solution)/shard_map/tzyx,tkz->kyx/dot_general | solution.py:177
  89.8 1.2 %fusion.25 = f32[32,32,128]{2,0,1:T(8,128)S(1)} fusion(f32[32,32,128]{2,0,1:T(8,128)S(1)} %fusion.21, f32[2,32,30,1]{1,2,0,3:T(8,128)S(1)} %copy-done.8, f32[2,30,32,128]{3,2,1,0:T(8,128)S(1)} %fusion.16), kind=kOutput, calls=%fused_computation.25 | convolution fusion | flops 94502912 | bytes 2039296 | tf_op jit(solution)/shard_map/tzyx,tkz->kyx/dot_general | solution.py:177
  91.0 1.1 %fusion.24 = f32[32,32,128]{2,0,1:T(8,128)S(1)} fusion(f32[32,32,128]{2,0,1:T(8,128)S(1)} %fusion.25, f32[2,32,26,1]{1,2,0,3:T(8,128)S(1)} %copy-done.9, f32[2,26,32,128]{3,2,1,0:T(8,128)S(1)} %convolution_bitcast_fusion.1), kind=kOutput, calls=%fused_computation.23 | convolution fusion | flops 81920000 | bytes 1907200 | tf_op jit(solution)/shard_map/tzyx,tkz->kyx/dot_general | solution.py:177
  92.2 1.1 %copy.27 = f32[32,32,128]{2,1,0:T(8,128)} copy(f32[32,32,128]{2,0,1:T(8,128)S(1)} %fusion.24) | data formatting | bytes 1048576 | tf_op jit(solution)/shard_map/add | solution.py:177
  (235 shorter events, 5.6 us)
Async XLA Ops:
  1.6 40.0 %collective-permute-start = (f32[8,32,128]{2,1,0:T(8,128)}, f32[8,32,128]{2,1,0:T(8,128)S(1)}, u32[]{:S(2)}, u32[]{:S(2)}) collective-permute-start(f32[8,32,128]{2,1,0:T(8,128)} %slice_select_fusion.3), channel_id=1, source_target_pairs={{0,1},{1,0},{2,3},{3,2},{4,5},{5,4},{6,7},{7,6},{8,9},{9,8},{10,11... | collective-permute-start | bytes 393224 | tf_op jit(solution)/shard_map/ppermute | solution.py:83
  5.5 3.9 %copy-start.3 = (f32[32,32,128]{2,1,0:T(8,128)S(1)}, f32[32,32,128]{2,1,0:T(8,128)}, u32[]{:S(2)}) copy-start(f32[32,32,128]{2,1,0:T(8,128)} %param.2) | copy-start | bytes 1572868
  6.4 21.7 %collective-permute-start.5 = (f32[11,19,67]{2,0,1:T(8,128)S(1)}, f32[11,19,67]{2,0,1:T(8,128)S(1)}, u32[]{:S(2)}, u32[]{:S(2)}) collective-permute-start(f32[11,19,67]{2,0,1:T(8,128)S(1)} %slice_select_fusion), channel_id=1, source_target_pairs={{0,1},{1,0},{2,3},{3,2},{4,5},{5,4},{6,7},{7,6},{8,9},{9,8},{10,11... | collective-permute-start | bytes 168044 | tf_op jit(solution)/shard_map/ppermute | solution.py:83
  6.6 3.7 %copy-start.66 = (f32[3,2,17]{2,1,0:T(2,128)S(1)}, f32[3,2,17]{2,1,0:T(2,128)}, u32[]{:S(2)}) copy-start(f32[3,2,17]{2,1,0:T(2,128)} %param.3) | copy-start | bytes 1228
  7.9 16.3 %collective-permute-start.10 = (f32[13,13,37]{2,0,1:T(8,128)S(1)}, f32[13,13,37]{2,0,1:T(8,128)S(1)}, u32[]{:S(2)}, u32[]{:S(2)}) collective-permute-start(f32[13,13,37]{2,0,1:T(8,128)S(1)} %fusion.38), channel_id=1, source_target_pairs={{0,1},{1,0},{2,3},{3,2},{4,5},{5,4},{6,7},{7,6},{8,9},{9,8},{10,11... | collective-permute-start | bytes 75044 | tf_op jit(solution)/shard_map/ppermute | solution.py:83
  24.2 6.0 %collective-permute-start.11 = (f32[26,13,37]{2,0,1:T(8,128)S(1)}, f32[26,13,37]{2,0,1:T(8,128)S(1)}, u32[]{:S(2)}, u32[]{:S(2)}) collective-permute-start(f32[26,13,37]{2,0,1:T(8,128)S(1)} %pad_maximum_fusion.5), channel_id=1, source_target_pairs={{2,0},{4,2},{6,4},{14,6},{12,14},{10,12},{8,10},{0,8},{18,16},{20,... | collective-permute-start | bytes 150080 | tf_op jit(solution)/shard_map/ppermute | solution.py:83
  25.5 7.7 %collective-permute-start.12 = (f32[26,13,37]{2,0,1:T(8,128)S(1)}, f32[26,13,37]{2,0,1:T(8,128)S(1)}, u32[]{:S(2)}, u32[]{:S(2)}) collective-permute-start(f32[26,13,37]{2,0,1:T(8,128)S(1)} %pad_maximum_fusion.5), channel_id=1, source_target_pairs={{0,2},{2,4},{4,6},{6,14},{14,12},{12,10},{10,8},{8,0},{16,18},{18,... | collective-permute-start | bytes 150080 | tf_op jit(solution)/shard_map/ppermute | solution.py:83
  25.8 9.7 %collective-permute-start.13 = (f32[26,5,37]{2,0,1:T(8,128)S(1)}, f32[26,5,37]{2,0,1:T(8,128)S(1)}, u32[]{:S(2)}, u32[]{:S(2)}) collective-permute-start(f32[26,5,37]{2,0,1:T(8,128)S(1)} %fusion.60), channel_id=1, source_target_pairs={{0,4},{2,6},{4,0},{6,2},{1,5},{3,7},{5,1},{7,3},{8,12},{10,14},{12... | collective-permute-start | bytes 57728 | tf_op jit(solution)/shard_map/ppermute | solution.py:83
  28.9 22.7 %collective-permute-start.6 = (f32[30,11,67]{2,0,1:T(8,128)}, f32[30,11,67]{2,0,1:T(8,128)}, u32[]{:S(2)}, u32[]{:S(2)}) collective-permute-start(f32[30,11,67]{2,0,1:T(8,128)} %get-tuple-element.66), channel_id=1, source_target_pairs={{2,0},{4,2},{6,4},{14,6},{12,14},{10,12},{8,10},{0,8},{18,16},{20,... | collective-permute-start | bytes 265328 | tf_op jit(solution)/shard_map/ppermute | solution.py:83
  30.3 21.4 %collective-permute-start.7 = (f32[30,11,67]{2,0,1:T(8,128)}, f32[30,11,67]{2,0,1:T(8,128)}, u32[]{:S(2)}, u32[]{:S(2)}) collective-permute-start(f32[30,11,67]{2,0,1:T(8,128)} %get-tuple-element.67), channel_id=1, source_target_pairs={{0,2},{2,4},{4,6},{6,14},{14,12},{12,10},{10,8},{8,0},{16,18},{18,... | collective-permute-start | bytes 265328 | tf_op jit(solution)/shard_map/ppermute | solution.py:83
  37.0 10.0 %collective-permute-start.15 = (f32[26,44,13]{1,2,0:T(8,128)}, f32[26,44,13]{1,2,0:T(8,128)S(1)}, u32[]{:S(2)}, u32[]{:S(2)}) collective-permute-start(f32[26,44,13]{1,2,0:T(8,128)} %copy.21), channel_id=1, source_target_pairs={{8,0},{16,8},{24,16},{0,24},{9,1},{17,9},{25,17},{1,25},{10,2},{18... | collective-permute-start | bytes 178472 | tf_op jit(solution)/shard_map/ppermute | solution.py:83
  40.3 7.5 %collective-permute-start.14 = (f32[26,44,13]{1,2,0:T(8,128)S(1)}, f32[26,44,13]{1,2,0:T(8,128)}, u32[]{:S(2)}, u32[]{:S(2)}) collective-permute-start(f32[26,44,13]{1,2,0:T(8,128)S(1)} %copy.20), channel_id=1, source_target_pairs={{0,8},{8,16},{16,24},{24,0},{1,9},{9,17},{17,25},{25,1},{2,10},{10... | collective-permute-start | bytes 178472 | tf_op jit(solution)/shard_map/ppermute | solution.py:83
  41.6 8.3 %copy-start = (f32[40,32,128]{2,1,0:T(8,128)}, f32[40,32,128]{2,1,0:T(8,128)S(1)}, u32[]{:S(2)}) copy-start(f32[40,32,128]{2,1,0:T(8,128)S(1)} %constant_dynamic-update-slice_fusion) | copy-start | bytes 1966084
  42.4 22.5 %collective-permute-start.1 = (f32[40,8,128]{2,1,0:T(8,128)}, f32[40,8,128]{2,1,0:T(8,128)}, u32[]{:S(2)}, u32[]{:S(2)}) collective-permute-start(f32[40,8,128]{2,1,0:T(8,128)} %get-tuple-element.62), channel_id=1, source_target_pairs={{2,0},{4,2},{6,4},{14,6},{12,14},{10,12},{8,10},{0,8},{18,16},{20,... | collective-permute-start | bytes 491528 | tf_op jit(solution)/shard_map/ppermute | solution.py:83
  47.0 17.9 %collective-permute-start.2 = (f32[40,8,128]{2,1,0:T(8,128)}, f32[40,8,128]{2,1,0:T(8,128)}, u32[]{:S(2)}, u32[]{:S(2)}) collective-permute-start(f32[40,8,128]{2,1,0:T(8,128)} %get-tuple-element.63), channel_id=1, source_target_pairs={{0,2},{2,4},{4,6},{6,14},{14,12},{12,10},{10,8},{8,0},{16,18},{18,... | collective-permute-start | bytes 491528 | tf_op jit(solution)/shard_map/ppermute | solution.py:83
  54.2 6.8 %collective-permute-start.9 = (f32[30,41,11]{1,0,2:T(8,128)}, f32[30,41,11]{1,0,2:T(8,128)S(1)}, u32[]{:S(2)}, u32[]{:S(2)}) collective-permute-start(f32[30,41,11]{1,0,2:T(8,128)} %copy.12), channel_id=1, source_target_pairs={{8,0},{16,8},{24,16},{0,24},{9,1},{17,9},{25,17},{1,25},{10,2},{18... | collective-permute-start | bytes 162368 | tf_op jit(solution)/shard_map/ppermute | solution.py:83
  54.8 7.0 %collective-permute-start.8 = (f32[30,41,11]{1,0,2:T(8,128)S(1)}, f32[30,41,11]{1,0,2:T(8,128)S(1)}, u32[]{:S(2)}, u32[]{:S(2)}) collective-permute-start(f32[30,41,11]{1,0,2:T(8,128)S(1)} %copy.11), channel_id=1, source_target_pairs={{0,8},{8,16},{16,24},{24,0},{1,9},{9,17},{17,25},{25,1},{2,10},{10... | collective-permute-start | bytes 162368 | tf_op jit(solution)/shard_map/ppermute | solution.py:83
  63.4 3.2 %copy-start.1 = (f32[40,32,128]{2,1,0:T(8,128)S(1)}, f32[40,32,128]{2,1,0:T(8,128)}, u32[]{:S(2)}) copy-start(f32[40,32,128]{2,1,0:T(8,128)} %copy-done) | copy-start | bytes 1966084
  68.0 4.9 %copy-start.10 = (f32[2,41,32,1]{1,2,3,0:T(8,128)S(1)}, f32[2,41,32,1]{1,2,3,0:T(8,128)}, u32[]{:S(2)}) copy-start(f32[2,41,32,1]{1,2,3,0:T(8,128)} %convolution_bitcast_fusion.11) | copy-start | bytes 31492
  70.1 7.0 %collective-permute-start.4 = (f32[40,48,8]{1,2,0:T(8,128)}, f32[40,48,8]{1,2,0:T(8,128)}, u32[]{:S(2)}, u32[]{:S(2)}) collective-permute-start(f32[40,48,8]{1,2,0:T(8,128)} %copy.6), channel_id=1, source_target_pairs={{8,0},{16,8},{24,16},{0,24},{9,1},{17,9},{25,17},{1,25},{10,2},{18... | collective-permute-start | bytes 184328 | tf_op jit(solution)/shard_map/ppermute | solution.py:83
  71.1 8.2 %collective-permute-start.3 = (f32[40,48,8]{1,2,0:T(8,128)}, f32[40,48,8]{1,2,0:T(8,128)}, u32[]{:S(2)}, u32[]{:S(2)}) collective-permute-start(f32[40,48,8]{1,2,0:T(8,128)} %copy.5), channel_id=1, source_target_pairs={{0,8},{8,16},{16,24},{24,0},{1,9},{9,17},{17,25},{25,1},{2,10},{10... | collective-permute-start | bytes 184328 | tf_op jit(solution)/shard_map/ppermute | solution.py:83
  73.8 7.8 %copy-start.2 = (f32[40,32,128]{2,1,0:T(8,128)S(1)}, f32[40,32,128]{2,1,0:T(8,128)}, u32[]{:S(2)}) copy-start(f32[40,32,128]{2,1,0:T(8,128)} %copy-done) | copy-start | bytes 1966084
  73.8 7.7 %copy-start.5 = (f32[40,8,128]{2,1,0:T(8,128)S(1)}, f32[40,8,128]{2,1,0:T(8,128)}, u32[]{:S(2)}) copy-start(f32[40,8,128]{2,1,0:T(8,128)} %copy-done.4) | copy-start | bytes 491524
  73.8 7.7 %copy-start.11 = (pred[128,144]{0,1:T(8,128)(4,1)S(1)}, pred[128,144]{0,1:T(8,128)(4,1)}, u32[]{:S(2)}) copy-start(pred[128,144]{0,1:T(8,128)(4,1)} %get-tuple-element.177) | copy-start | bytes 55300
  73.9 7.7 %copy-start.12 = (pred[128,144]{0,1:T(8,128)(4,1)S(1)}, pred[128,144]{0,1:T(8,128)(4,1)}, u32[]{:S(2)}) copy-start(pred[128,144]{0,1:T(8,128)(4,1)} %get-tuple-element.178) | copy-start | bytes 55300
  73.9 7.7 %copy-start.13 = (pred[128,144]{0,1:T(8,128)(4,1)S(1)}, pred[128,144]{0,1:T(8,128)(4,1)}, u32[]{:S(2)}) copy-start(pred[128,144]{0,1:T(8,128)(4,1)} %get-tuple-element.179) | copy-start | bytes 55300
  73.9 7.7 %copy-start.14 = (pred[128,144]{0,1:T(8,128)(4,1)S(1)}, pred[128,144]{0,1:T(8,128)(4,1)}, u32[]{:S(2)}) copy-start(pred[128,144]{0,1:T(8,128)(4,1)} %get-tuple-element.180) | copy-start | bytes 55300
  73.9 7.7 %copy-start.15 = (pred[128,144]{0,1:T(8,128)(4,1)S(1)}, pred[128,144]{0,1:T(8,128)(4,1)}, u32[]{:S(2)}) copy-start(pred[128,144]{0,1:T(8,128)(4,1)} %get-tuple-element.181) | copy-start | bytes 55300
  73.9 7.7 %copy-start.16 = (pred[128,144]{0,1:T(8,128)(4,1)S(1)}, pred[128,144]{0,1:T(8,128)(4,1)}, u32[]{:S(2)}) copy-start(pred[128,144]{0,1:T(8,128)(4,1)} %get-tuple-element.182) | copy-start | bytes 55300
  73.9 7.7 %copy-start.17 = (pred[128,144]{0,1:T(8,128)(4,1)S(1)}, pred[128,144]{0,1:T(8,128)(4,1)}, u32[]{:S(2)}) copy-start(pred[128,144]{0,1:T(8,128)(4,1)} %get-tuple-element.183) | copy-start | bytes 55300
  73.9 7.7 %copy-start.18 = (pred[128,144]{0,1:T(8,128)(4,1)S(1)}, pred[128,144]{0,1:T(8,128)(4,1)}, u32[]{:S(2)}) copy-start(pred[128,144]{0,1:T(8,128)(4,1)} %get-tuple-element.184) | copy-start | bytes 55300
  73.9 7.7 %copy-start.19 = (pred[128,144]{0,1:T(8,128)(4,1)S(1)}, pred[128,144]{0,1:T(8,128)(4,1)}, u32[]{:S(2)}) copy-start(pred[128,144]{0,1:T(8,128)(4,1)} %get-tuple-element.185) | copy-start | bytes 55300
  73.9 7.7 %copy-start.20 = (pred[128,144]{0,1:T(8,128)(4,1)S(1)}, pred[128,144]{0,1:T(8,128)(4,1)}, u32[]{:S(2)}) copy-start(pred[128,144]{0,1:T(8,128)(4,1)} %get-tuple-element.186) | copy-start | bytes 55300
  73.9 7.7 %copy-start.21 = (pred[128,144]{0,1:T(8,128)(4,1)S(1)}, pred[128,144]{0,1:T(8,128)(4,1)}, u32[]{:S(2)}) copy-start(pred[128,144]{0,1:T(8,128)(4,1)} %get-tuple-element.187) | copy-start | bytes 55300
  74.0 7.7 %copy-start.22 = (pred[128,144]{0,1:T(8,128)(4,1)S(1)}, pred[128,144]{0,1:T(8,128)(4,1)}, u32[]{:S(2)}) copy-start(pred[128,144]{0,1:T(8,128)(4,1)} %get-tuple-element.188) | copy-start | bytes 55300
  74.0 7.7 %copy-start.23 = (pred[128,144]{0,1:T(8,128)(4,1)S(1)}, pred[128,144]{0,1:T(8,128)(4,1)}, u32[]{:S(2)}) copy-start(pred[128,144]{0,1:T(8,128)(4,1)} %get-tuple-element.189) | copy-start | bytes 55300
  74.0 7.7 %copy-start.24 = (pred[128,144]{0,1:T(8,128)(4,1)S(1)}, pred[128,144]{0,1:T(8,128)(4,1)}, u32[]{:S(2)}) copy-start(pred[128,144]{0,1:T(8,128)(4,1)} %get-tuple-element.190) | copy-start | bytes 55300
  74.0 7.7 %copy-start.25 = (pred[128,144]{0,1:T(8,128)(4,1)S(1)}, pred[128,144]{0,1:T(8,128)(4,1)}, u32[]{:S(2)}) copy-start(pred[128,144]{0,1:T(8,128)(4,1)} %get-tuple-element.191) | copy-start | bytes 55300
  74.0 7.7 %copy-start.26 = (pred[128,144]{0,1:T(8,128)(4,1)S(1)}, pred[128,144]{0,1:T(8,128)(4,1)}, u32[]{:S(2)}) copy-start(pred[128,144]{0,1:T(8,128)(4,1)} %get-tuple-element.192) | copy-start | bytes 55300
  74.0 7.7 %copy-start.27 = (pred[128,144]{0,1:T(8,128)(4,1)S(1)}, pred[128,144]{0,1:T(8,128)(4,1)}, u32[]{:S(2)}) copy-start(pred[128,144]{0,1:T(8,128)(4,1)} %get-tuple-element.193) | copy-start | bytes 55300
  74.0 7.7 %copy-start.49 = (f32[2]{0:T(128)S(1)}, f32[2]{0:T(128)}, u32[]{:S(2)}) copy-start(f32[2]{0:T(128)} %get-tuple-element.39) | copy-start | bytes 28
  74.0 7.7 %copy-start.50 = (f32[2]{0:T(128)S(1)}, f32[2]{0:T(128)}, u32[]{:S(2)}) copy-start(f32[2]{0:T(128)} %get-tuple-element.40) | copy-start | bytes 28
  74.0 7.7 %copy-start.51 = (f32[2]{0:T(128)S(1)}, f32[2]{0:T(128)}, u32[]{:S(2)}) copy-start(f32[2]{0:T(128)} %get-tuple-element.41) | copy-start | bytes 28
  74.0 7.7 %copy-start.52 = (f32[2]{0:T(128)S(1)}, f32[2]{0:T(128)}, u32[]{:S(2)}) copy-start(f32[2]{0:T(128)} %get-tuple-element.42) | copy-start | bytes 28
  74.1 7.7 %copy-start.53 = (f32[2]{0:T(128)S(1)}, f32[2]{0:T(128)}, u32[]{:S(2)}) copy-start(f32[2]{0:T(128)} %get-tuple-element.43) | copy-start | bytes 28
  74.1 7.7 %copy-start.54 = (f32[2]{0:T(128)S(1)}, f32[2]{0:T(128)}, u32[]{:S(2)}) copy-start(f32[2]{0:T(128)} %get-tuple-element.44) | copy-start | bytes 28
  74.1 7.7 %copy-start.55 = (f32[2]{0:T(128)S(1)}, f32[2]{0:T(128)}, u32[]{:S(2)}) copy-start(f32[2]{0:T(128)} %get-tuple-element.45) | copy-start | bytes 28
  74.1 7.7 %copy-start.56 = (f32[2]{0:T(128)S(1)}, f32[2]{0:T(128)}, u32[]{:S(2)}) copy-start(f32[2]{0:T(128)} %get-tuple-element.46) | copy-start | bytes 28
  74.1 7.7 %copy-start.57 = (f32[2]{0:T(128)S(1)}, f32[2]{0:T(128)}, u32[]{:S(2)}) copy-start(f32[2]{0:T(128)} %get-tuple-element.47) | copy-start | bytes 28
  74.1 7.7 %copy-start.58 = (f32[2]{0:T(128)S(1)}, f32[2]{0:T(128)}, u32[]{:S(2)}) copy-start(f32[2]{0:T(128)} %get-tuple-element.48) | copy-start | bytes 28
  74.1 7.7 %copy-start.59 = (f32[2]{0:T(128)S(1)}, f32[2]{0:T(128)}, u32[]{:S(2)}) copy-start(f32[2]{0:T(128)} %get-tuple-element.49) | copy-start | bytes 28
  74.1 7.7 %copy-start.60 = (f32[2]{0:T(128)S(1)}, f32[2]{0:T(128)}, u32[]{:S(2)}) copy-start(f32[2]{0:T(128)} %get-tuple-element.50) | copy-start | bytes 28
  74.1 7.7 %copy-start.61 = (f32[2]{0:T(128)S(1)}, f32[2]{0:T(128)}, u32[]{:S(2)}) copy-start(f32[2]{0:T(128)} %get-tuple-element.51) | copy-start | bytes 28
  74.1 7.7 %copy-start.62 = (f32[2]{0:T(128)S(1)}, f32[2]{0:T(128)}, u32[]{:S(2)}) copy-start(f32[2]{0:T(128)} %get-tuple-element.52) | copy-start | bytes 28
  74.2 7.7 %copy-start.63 = (f32[2]{0:T(128)S(1)}, f32[2]{0:T(128)}, u32[]{:S(2)}) copy-start(f32[2]{0:T(128)} %get-tuple-element.53) | copy-start | bytes 28
  77.1 4.8 %copy-start.64 = (f32[2]{0:T(128)S(1)}, f32[2]{0:T(128)}, u32[]{:S(2)}) copy-start(f32[2]{0:T(128)} %get-tuple-element.54) | copy-start | bytes 28
  81.9 3.8 %copy-start.44 = (pred[32,48]{1,0:T(8,128)(4,1)S(1)}, pred[32,48]{1,0:T(8,128)(4,1)}, u32[]{:S(2)}) copy-start(pred[32,48]{1,0:T(8,128)(4,1)} %get-tuple-element.211) | copy-start | bytes 4612
  81.9 3.8 %copy-start.45 = (pred[32,48]{1,0:T(8,128)(4,1)S(1)}, pred[32,48]{1,0:T(8,128)(4,1)}, u32[]{:S(2)}) copy-start(pred[32,48]{1,0:T(8,128)(4,1)} %get-tuple-element.212) | copy-start | bytes 4612
  81.9 3.8 %copy-start.46 = (pred[32,48]{1,0:T(8,128)(4,1)S(1)}, pred[32,48]{1,0:T(8,128)(4,1)}, u32[]{:S(2)}) copy-start(pred[32,48]{1,0:T(8,128)(4,1)} %get-tuple-element.213) | copy-start | bytes 4612
  81.9 3.8 %copy-start.47 = (pred[32,48]{1,0:T(8,128)(4,1)S(1)}, pred[32,48]{1,0:T(8,128)(4,1)}, u32[]{:S(2)}) copy-start(pred[32,48]{1,0:T(8,128)(4,1)} %get-tuple-element.214) | copy-start | bytes 4612
  81.9 3.8 %copy-start.48 = (pred[32,48]{1,0:T(8,128)(4,1)S(1)}, pred[32,48]{1,0:T(8,128)(4,1)}, u32[]{:S(2)}) copy-start(pred[32,48]{1,0:T(8,128)(4,1)} %get-tuple-element.215) | copy-start | bytes 4612
  85.7 2.3 %copy-start.28 = (pred[32,40]{1,0:T(8,128)(4,1)S(1)}, pred[32,40]{1,0:T(8,128)(4,1)}, u32[]{:S(2)}) copy-start(pred[32,40]{1,0:T(8,128)(4,1)} %get-tuple-element.195) | copy-start | bytes 3844
  85.7 2.3 %copy-start.29 = (pred[32,40]{1,0:T(8,128)(4,1)S(1)}, pred[32,40]{1,0:T(8,128)(4,1)}, u32[]{:S(2)}) copy-start(pred[32,40]{1,0:T(8,128)(4,1)} %get-tuple-element.196) | copy-start | bytes 3844
  85.7 2.3 %copy-start.30 = (pred[32,40]{1,0:T(8,128)(4,1)S(1)}, pred[32,40]{1,0:T(8,128)(4,1)}, u32[]{:S(2)}) copy-start(pred[32,40]{1,0:T(8,128)(4,1)} %get-tuple-element.197) | copy-start | bytes 3844
  (20 other events, 40.2 us)

commit v2 on v0

v2 whole, which is shorter than its diff:
```python
import jax
import jax.numpy as jnp
from jax import lax
from jax.experimental import pallas as pl
from jax.experimental.pallas import tpu as pltpu
from jax.sharding import PartitionSpec as P

RADIUS = 8
TAPS = 17
TERMS = 2
WEIGHTS = ((-3, -0.0625), (-1, 0.5625), (0, 1.0), (1, 0.5625), (3, -0.0625))
EXACT = lax.Precision.HIGHEST
SPAN = RADIUS + 5
EDGE = RADIUS + 3
F32, BF16 = jnp.float32, jnp.bfloat16
PARAMS = pltpu.CompilerParams(vmem_limit_bytes=48 * 1024 * 1024)
VMEM = pl.BlockSpec(memory_space=pltpu.VMEM)
SMEM = pl.BlockSpec(memory_space=pltpu.SMEM)


def up8(n):
    return -(-n // 8) * 8


def iota(shape, dim):
    return lax.broadcasted_iota(jnp.int32, shape, dim)


def weight_of(difference):
    size = jnp.abs(difference)
    out = jnp.where(size == 1, 0.5625, jnp.where(size == 3, -0.0625, 0.0))
    return jnp.where(size == 0, 1.0, out)


def choose(condition, a, b):
    return jnp.where(condition, jnp.where(a, 1, 0), jnp.where(b, 1, 0)) != 0


class Cut:
    def __init__(self, name, length):
        self.name, self.fine = name, length
        self.count = lax.axis_size(name)
        self.mid, self.coarse = length // 2, length // 4
        self.mid_all, self.coarse_all = self.mid + 3, self.coarse + 5
        self.second = max(SPAN - self.coarse, 0)

    def index(self):
        return lax.axis_index(self.name)

    def holds_mid(self, k):
        k = k + self.index() * self.mid
        return (k >= 0) & (k < self.mid * self.count)

    def holds_coarse(self, k):
        k = k + self.index() * self.coarse
        return (k >= 0) & (k < self.coarse * self.count)


class Route:
    def __init__(self, names, pairs, up, below):
        self.names, self.pairs, self.up, self.below = names, pairs, up, below

    def __call__(self, x):
        return lax.ppermute(x, self.names, self.pairs)


def flip(pairs):
    return [(b, a) for a, b in pairs]


def swap(cut, steps):
    pairs = [(i, i + steps) for i in range(cut.count - steps)]

    def up():
        return cut.index() + steps < cut.count

    return [Route(cut.name, pairs + flip(pairs), up, lambda: ~up())]


def both_ways(cut, steps):
    pairs = [(i, i + steps) for i in range(cut.count - steps)]
    yes, no = (lambda: cut.index() >= 0), (lambda: cut.index() < 0)
    return [Route(cut.name, pairs, yes, yes), Route(cut.name, flip(pairs), no, no)]


def folded(cut, beside, names):
    n, m = cut.count, lax.axis_size(beside)

    def place(c, i):
        return c * n + i if names[0] == beside else i * m + c

    pairs = []
    for c in range(0, m, 2):
        cycle = [place(c, i) for i in range(n)] + [place(c + 1, i) for i in reversed(range(n))]
        pairs += list(zip(cycle, cycle[1:] + cycle[:1]))

    def even():
        return lax.axis_index(beside) % 2 == 0

    def odd():
        return lax.axis_index(beside) % 2 == 1

    return [Route(names, pairs, even, even), Route(names, flip(pairs), odd, odd)]


def split(x):
    high = x.astype(BF16)
    return high, (x - high.astype(F32)).astype(BF16)


def pick(selector, x):
    nt = (((1,), (1,)), ((), ()))
    a = x.astype(BF16)
    rest = x - a.astype(F32)
    b = rest.astype(BF16)
    c = (rest - b.astype(F32)).astype(BF16)
    out = lax.dot_general(selector, c, nt, preferred_element_type=F32)
    out = out + lax.dot_general(selector, b, nt, preferred_element_type=F32)
    return out + lax.dot_general(selector, a, nt, preferred_element_type=F32)


class Sizes:
    def __init__(self, z, y, x):
        self.z, self.y, self.x = z, y, x
        self.z_routes = swap(z, 1) if z.count <= 2 else both_ways(z, 1)
        self.z2_routes = [] if z.count <= 2 else swap(z, 2) if z.count <= 4 else both_ways(z, 2)
        self.y_routes = folded(y, x.name, (x.name, y.name))
        self.y2_routes = swap(y, 2)
        self.x_routes = folded(x, z.name, (x.name, z.name))
        self.z_fine = RADIUS * y.fine
        self.z_rows = up8(self.z_fine + SPAN * y.mid_all)
        self.z2_rows = up8(z.second * y.mid_all)
        self.fine_planes = z.fine + RADIUS * len(self.z_routes)
        self.sum_planes = z.mid_all + SPAN * len(self.z_routes) + z.second * len(self.z2_routes)
        self.y_fine = RADIUS * self.fine_planes
        self.y_rows = up8(self.y_fine + SPAN * self.sum_planes)
        self.y2_rows = up8(y.second * self.sum_planes)
        self.fine_rows = y.fine + 2 * RADIUS
        self.low = up8(y.mid_all)
        self.high = self.low + up8(SPAN)
        self.far = self.high + up8(SPAN)
        self.sum_rows = -(-(self.far + y.second) // 16) * 16
        self.x_sends = RADIUS + EDGE + SPAN
        cells = max(self.fine_planes * self.fine_rows, self.sum_planes * self.sum_rows)
        self.x_cells = -(-cells // 128) * 128
        assert x.mid_all + x.coarse_all <= x.fine and self.x_sends <= 32
        assert z.coarse >= RADIUS and y.coarse >= RADIUS and y.count == 4


def restrict_kernel(s, nz, charges, own, *rest):
    messages, (wide, mid, high, coarse) = rest[:-4], rest[-4:]
    z, y, x = s.z, s.y, s.x
    lanes = (x.fine, x.fine)
    cell, lane = iota(lanes, 0), iota(lanes, 1)
    k = lane - 1
    to_mid = jnp.where((lane < x.mid_all) & x.holds_mid(k), weight_of(cell - 2 * k), 0.0)
    c = lane - x.mid_all - 2
    inside = (lane >= x.mid_all) & (lane < x.mid_all + x.coarse_all) & x.holds_coarse(c)
    to_coarse = jnp.where(inside, weight_of(cell - 1 - 2 * c), 0.0)
    narrow = to_mid + jnp.dot(to_mid, to_coarse, precision=EXACT, preferred_element_type=F32)
    grid = charges[...]
    reduced = jnp.dot(grid.reshape(z.fine * y.fine, x.fine), narrow, precision=EXACT, preferred_element_type=F32)
    wide[...] = jnp.zeros(wide.shape, F32)
    wide[:, 8 : 8 + y.fine, :] = reduced.reshape(z.fine, y.fine, x.fine)
    rows = 0.0
    for offset, weight in WEIGHTS:
        rows = rows + weight * wide[:, pl.ds(6 + offset, y.mid_all, stride=2), :]
    keep = y.holds_mid(iota((y.mid_all, x.fine), 0) - 1)
    mid[...] = jnp.zeros(mid.shape, F32)
    coarse[...] = jnp.zeros(coarse.shape, F32)
    high[...] = jnp.zeros(high.shape, F32)
    for p in range(z.mid_all):
        total = 0.0
        for offset, weight in WEIGHTS:
            at = 2 * (p - 1) + offset
            if 0 <= at < z.fine:
                total = total + weight * rows[at]
        total = jnp.where(keep & z.holds_mid(p - 1), total, 0.0)
        mid[p, : y.mid_all] = total
        high[p, 8 : 8 + y.mid_all] = total
    rows = 0.0
    for offset, weight in WEIGHTS:
        rows = rows + weight * high[:, pl.ds(5 + offset, y.coarse_all, stride=2), :]
    keep = y.holds_coarse(iota((y.coarse_all, x.fine), 0) - 2)
    for p in range(z.coarse_all):
        total = 0.0
        for offset, weight in WEIGHTS:
            at = 2 * (p - 2) + offset + 1
            if 0 <= at < z.mid_all:
                total = total + weight * rows[at]
        coarse[p, : y.coarse_all] = jnp.where(keep & z.holds_coarse(p - 2), total, 0.0)
    is_mid = iota(mid.shape[1:], 1) < x.mid_all
    for p in range(z.mid_all):
        own[p] = jnp.where(is_mid, mid[p], coarse[p]) if p < z.coarse_all else jnp.where(is_mid, mid[p], 0.0)
    for message, route in zip(messages, s.z_routes):
        up = route.up().astype(jnp.int32)
        message[: s.z_fine] = charges[pl.ds(up * (z.fine - RADIUS), RADIUS)].reshape(s.z_fine, x.fine)
        for p in range(SPAN):
            plane = jnp.where(is_mid, mid[up * (z.mid_all - SPAN) + p], coarse[up * (z.coarse_all - SPAN) + p])
            at = s.z_fine + p * y.mid_all
            message[at : at + y.mid_all] = plane[: y.mid_all]
        filled = s.z_fine + SPAN * y.mid_all
        if filled < s.z_rows:
            message[filled:] = jnp.zeros((s.z_rows - filled, x.fine), F32)
    for message, route in zip(messages[nz:], s.z2_routes):
        up = route.up().astype(jnp.int32)
        message[...] = jnp.zeros(message.shape, F32)
        for p in range(z.second):
            plane = jnp.where(is_mid, 0.0, coarse[up * (z.coarse_all - z.second) + p])
            message[p * y.mid_all : (p + 1) * y.mid_all] = plane[: y.mid_all]


def slabs(s, z_messages, z2_messages):
    out = []
    for message in z_messages:
        out += [(message, s.z_fine + p * s.y.mid_all) for p in range(SPAN)]
    for message in z2_messages:
        out += [(message, p * s.y.mid_all) for p in range(s.z.second)]
    return out


def spread_kernel(s, nz, nz2, charges, own, *rest):
    z_messages, z2_messages = rest[:nz], rest[nz : nz + nz2]
    messages = rest[nz + nz2 : -1]
    far = rest[-1]
    z, y, x = s.z, s.y, s.x
    is_mid = iota((SPAN, x.fine), 1) < x.mid_all
    planes = slabs(s, z_messages, z2_messages)

    def rows_of(p, first, count):
        if p < z.mid_all:
            return own[p, first : first + count]
        message, at = planes[p - z.mid_all]
        return message[at + first : at + first + count]

    for message, route in zip(messages, s.y_routes):
        up = route.up()
        message[: RADIUS * z.fine] = jnp.where(
            up, charges[:, y.fine - RADIUS :, :], charges[:, :RADIUS, :]
        ).reshape(RADIUS * z.fine, x.fine)
        at = RADIUS * z.fine
        for z_message in z_messages:
            slab = z_message[: s.z_fine].reshape(RADIUS, y.fine, x.fine)
            edge = jnp.where(up, slab[:, y.fine - RADIUS :], slab[:, :RADIUS])
            message[at : at + RADIUS * RADIUS] = edge.reshape(RADIUS * RADIUS, x.fine)
            at += RADIUS * RADIUS
        for p in range(s.sum_planes):
            last = jnp.where(
                is_mid, rows_of(p, y.mid_all - SPAN, SPAN), rows_of(p, y.coarse_all - SPAN, SPAN)
            )
            message[at : at + SPAN] = jnp.where(up, last, rows_of(p, 0, SPAN))
            at += SPAN
        if at < s.y_rows:
            message[at:] = jnp.zeros((s.y_rows - at, x.fine), F32)
    up = s.y2_routes[0].up()
    count = y.second
    for p in range(s.sum_planes):
        far[p * count : (p + 1) * count] = jnp.where(up, rows_of(p, y.coarse_all - count, count), rows_of(p, 0, count))
    if s.sum_planes * count < s.y2_rows:
        far[s.sum_planes * count :] = jnp.zeros((s.y2_rows - s.sum_planes * count, x.fine), F32)


def collect_kernel(s, nz, nz2, charges, own, *rest):
    z_messages, z2_messages = rest[:nz], rest[nz : nz + nz2]
    ahead, behind, far, fine, sums, first, second = rest[nz + nz2 :]
    z, y, x = s.z, s.y, s.x
    below = s.y_routes[0].below()
    planes = slabs(s, z_messages, z2_messages)

    def sides(start, count):
        a, b = ahead[start : start + count], behind[start : start + count]
        return jnp.where(below, a, b), jnp.where(below, b, a)

    def fine_planes(at, count, body, row):
        low, high = sides(row, RADIUS * count)
        fine[at : at + count, : y.fine] = body
        fine[at : at + count, y.fine : y.fine + RADIUS] = low.reshape(count, RADIUS, x.fine)
        fine[at : at + count, y.fine + RADIUS :] = high.reshape(count, RADIUS, x.fine)

    fine_planes(0, z.fine, charges[...], 0)
    at = z.fine
    for z_message in z_messages:
        fine_planes(at, RADIUS, z_message[: s.z_fine].reshape(RADIUS, y.fine, x.fine), RADIUS * at)
        at += RADIUS
    sums[...] = jnp.zeros(sums.shape, F32)
    for p in range(s.sum_planes):
        if p < z.mid_all:
            sums[p, : s.low] = own[p]
        else:
            message, at = planes[p - z.mid_all]
            sums[p, : y.mid_all] = message[at : at + y.mid_all]
        low, high = sides(s.y_fine + p * SPAN, SPAN)
        sums[p, s.low : s.low + SPAN] = low
        sums[p, s.high : s.high + SPAN] = high
        sums[p, s.far : s.far + y.second] = far[p * y.second : (p + 1) * y.second]
    row, lane = iota((2 * RADIUS, x.fine), 0), iota((2 * RADIUS, x.fine), 1)
    up = s.x_routes[0].up()
    is_first = row < RADIUS
    goes_up = choose(up, is_first, ~is_first)
    slot = jnp.where(is_first, row, row - RADIUS)
    wanted = jnp.where(goes_up, x.fine - RADIUS + slot, slot)
    picked = pick((lane == wanted).astype(BF16), fine[...].reshape(s.fine_planes * s.fine_rows, x.fine))
    width = EDGE + SPAN
    row, lane = iota((2 * width, x.fine), 0), iota((2 * width, x.fine), 1)
    is_first = row < width
    goes_up = choose(up, is_first, ~is_first)
    slot = jnp.where(is_first, row, row - width)
    from_mid = jnp.where(goes_up, x.mid_all - EDGE + slot, slot)
    from_coarse = slot - EDGE + jnp.where(goes_up, x.mid_all + x.coarse_all - SPAN, x.mid_all)
    wanted = jnp.where(slot < EDGE, from_mid, from_coarse)
    picked_sums = pick((lane == wanted).astype(BF16), sums[...].reshape(s.sum_planes * s.sum_rows, x.fine))
    for n, message in enumerate((first, second)):
        cells = s.fine_planes * s.fine_rows
        message[:RADIUS, :cells] = picked[n * RADIUS : (n + 1) * RADIUS]
        if cells < s.x_cells:
            message[:RADIUS, cells:] = jnp.zeros((RADIUS, s.x_cells - cells), F32)
        cells = s.sum_planes * s.sum_rows
        message[RADIUS:, :cells] = picked_sums[n * width : (n + 1) * width]
        if cells < s.x_cells:
            message[RADIUS:, cells:] = jnp.zeros((width, s.x_cells - cells), F32)


def band(taps, level, offset, valid):
    at = jnp.where(valid, offset + RADIUS, -1)
    out = [jnp.zeros(at.shape, F32) for _ in range(TERMS)]
    for tap in range(TAPS):
        here = at == tap
        out = [jnp.where(here, taps[level, term, tap], total) for term, total in enumerate(out)]
    return out


def dot(a, b):
    return jnp.dot(a, b, precision=EXACT, preferred_element_type=F32)


def operator_kernel(s, taps, x_fine, x_sums, y_fine, y_mid, y_coarse):
    y, x = s.y, s.x
    own, edge = x.fine, 2 * 32
    shape = (own + edge, x.fine)
    row, lane = iota(shape, 0), iota(shape, 1)
    t = row - own
    lower, higher = x.index() > 0, x.index() < x.count - 1
    is_own = row < own
    is_low = ~is_own & (t < 32)
    q = jnp.where(is_low, t, t - 32)
    side = choose(is_low, lower, higher)

    def place(own_place, own_valid, first, count, low_place, high_place):
        r = q - first
        there = (r >= 0) & (r < count) & side
        valid = choose(is_own, own_valid, there)
        return jnp.where(is_own, own_place, jnp.where(is_low, low_place + r, high_place + r)), valid

    where, valid = place(row, row >= 0, 0, RADIUS, -RADIUS, x.fine)
    fine = band(taps, 0, where - lane, valid)
    where, valid = place(row - 1, row < x.mid_all, RADIUS, EDGE, 2 - EDGE, x.mid - 1)
    mid = band(taps, 1, where - (lane - 1), valid & (lane < x.mid_all))
    first = x.mid_all
    where, valid = place(
        row - first - 2, (row >= first) & (row < first + x.coarse_all), RADIUS + EDGE, SPAN, 3 - SPAN, x.coarse - 2
    )
    coarse = band(taps, 2, where - (lane - 2), valid & (lane < x.coarse_all))
    a, b = iota((x.fine, x.fine), 0), iota((x.fine, x.fine), 1)
    from_mid = jnp.where((a < x.mid_all) & x.holds_mid(a - 1), weight_of(b - 2 * (a - 1)), 0.0)
    from_coarse = jnp.where((a < x.coarse_all) & x.holds_coarse(a - 2), weight_of(b - 1 - 2 * (a - 2)), 0.0)
    from_coarse = dot(from_coarse, from_mid)
    columns = [(x_fine, 0, fine)]
    columns += [(x_sums, 0, [dot(m, from_mid) for m in mid])]
    columns += [(x_sums, TERMS * x.fine, [dot(c, from_coarse) for c in coarse])]
    for out, at, terms in columns:
        for term, matrix in enumerate(terms):
            high, low = split(matrix)
            cols = slice(at + term * x.fine, at + (term + 1) * x.fine)
            out[0:own, cols] = high[:own]
            out[own : 2 * own, cols] = high[:own]
            out[2 * own : 3 * own, cols] = low[:own]
            out[3 * own : 3 * own + edge, cols] = high[own:]
            out[3 * own + edge : 3 * own + 2 * edge, cols] = high[own:]
            out[3 * own + 2 * edge : 3 * own + 3 * edge, cols] = low[own:]
            out[3 * own + 3 * edge :, cols] = jnp.zeros((edge, x.fine), BF16)

    lower, higher = y.index() > 0, y.index() < y.count - 1
    far_below = s.y2_routes[0].below()
    n = up8(y.mid_all)

    def write(out, size, terms):
        part = iota((y.fine, 3 * size), 1) >= 2 * size
        for term, matrix in enumerate(terms):
            high, low = split(matrix)
            out[term * y.fine : (term + 1) * y.fine] = jnp.where(part, low.astype(F32), high.astype(F32)).astype(BF16)

    def columns_of(rows, size):
        lane = iota((rows, 3 * size), 1)
        return jnp.where(lane >= 2 * size, lane - 2 * size, jnp.where(lane >= size, lane - size, lane))

    c = columns_of(y.fine, s.fine_rows)
    is_low = (c >= y.fine) & (c < y.fine + RADIUS)
    is_high = c >= y.fine + RADIUS
    where = jnp.where(is_low, c - y.fine - RADIUS, jnp.where(is_high, c - RADIUS, c))
    valid = choose(is_low, lower, choose(is_high, higher, c >= 0))
    write(y_fine, s.fine_rows, band(taps, 0, where - iota(c.shape, 0), valid))

    c = columns_of(n, s.sum_rows)
    r = iota(c.shape, 0)
    is_low = (c >= s.low) & (c < s.low + SPAN)
    is_high = (c >= s.high) & (c < s.high + SPAN)
    is_far = (c >= s.far) & (c < s.far + y.second)
    where = jnp.where(is_low, c - s.low + 2 - SPAN, jnp.where(is_high, c - s.high + y.mid - 1, c - 1))
    valid = choose(is_low, lower, choose(is_high, higher, c < y.mid_all))
    mid = band(taps, 1, where - (r - 1), valid & (r < y.mid_all))
    far = jnp.where(far_below, -2 - y.coarse, 2 * y.coarse - 2)
    where = jnp.where(is_low, c - s.low + 3 - SPAN, jnp.where(is_high, c - s.high + y.coarse - 2, c - 2))
    where = jnp.where(is_far, c - s.far + far, where)
    valid = choose(is_low, lower, choose(is_high, higher, (c < y.coarse_all) | is_far))
    coarse = band(taps, 2, where - (r - 2), valid & (r < y.coarse_all))
    o, k = iota((y.fine, n), 0), iota((y.fine, n), 1)
    from_mid = jnp.where((k < y.mid_all) & y.holds_mid(k - 1), weight_of(o - 2 * (k - 1)), 0.0)
    o, k = iota((n, n), 0), iota((n, n), 1)
    from_coarse = jnp.where((k < y.coarse_all) & y.holds_coarse(k - 2), weight_of(o - 1 - 2 * (k - 2)), 0.0)
    from_coarse = dot(from_mid, from_coarse)
    write(y_mid, s.sum_rows, [dot(from_mid, m) for m in mid])
    write(y_coarse, s.sum_rows, [dot(from_coarse, m) for m in coarse])


def sum_kernel(s, taps, fine, sums, first, second, x_fine, x_sums, y_fine, y_mid, y_coarse, out, *scratch):
    turned, t_fine, t_mid, t_coarse, p_mid, p_coarse = scratch
    z, y, x = s.z, s.y, s.x
    below = s.x_routes[0].below()
    low = jnp.where(below, first[...], second[...])
    high = jnp.where(below, second[...], first[...])
    turned[...] = jnp.concatenate([low, high, low, high], axis=0).T

    def along_x(grid, start, rows, weights):
        edge = turned[start : start + rows]
        edge_high, edge_low = split(edge)
        lane = iota(edge.shape, 1) < 64
        packed = jnp.where(lane, edge_high.astype(F32), edge_low.astype(F32)).astype(BF16)
        grid_high, grid_low = split(grid)
        joined = jnp.concatenate([grid_high, grid_low, grid_high, packed, edge_high], axis=1)
        return split(jnp.dot(joined, weights[...], preferred_element_type=F32))

    def along_y(high, low, weights):
        joined = jnp.concatenate([high, low, high], axis=0)
        result = jnp.dot(weights[...], joined, preferred_element_type=F32)
        return [result[t * y.fine : (t + 1) * y.fine, t * x.fine : (t + 1) * x.fine] for t in range(TERMS)]

    def starts(routes, below_at, above_at, cut, steps):
        result = []
        for route in routes:
            lower = route.below()
            i = cut.index()
            valid = choose(lower, i - steps >= 0, i + steps < cut.count)
            result.append((jnp.where(lower, below_at, above_at), valid))
        return result

    t_fine[...] = jnp.zeros(t_fine.shape, F32)
    t_mid[...] = jnp.zeros(t_mid.shape, F32)
    t_coarse[...] = jnp.zeros(t_coarse.shape, F32)
    group = 8
    fine_at = [(RADIUS + p, None) for p in range(z.fine)]
    for start, valid in starts(s.z_routes, 0, z.fine + RADIUS, z, 1):
        fine_at += [(start + p, valid) for p in range(RADIUS)]
    for g in range(0, s.fine_planes, group):
        n = s.fine_rows
        grid = fine[g : g + group].reshape(group * n, x.fine)
        a, b = along_x(grid, g * n, group * n, x_fine)
        for p in range(group):
            at, valid = fine_at[g + p]
            for t, part in enumerate(along_y(a[p * n : (p + 1) * n], b[p * n : (p + 1) * n], y_fine)):
                t_fine[at, t] = part if valid is None else jnp.where(valid, part, 0.0)

    mid_at = [(SPAN - 3 + p, None) for p in range(z.mid_all)]
    coarse_at = [(SPAN - 5 + p if p < z.coarse_all else None, None) for p in range(z.mid_all)]
    for start, valid in starts(s.z_routes, 0, z.mid + SPAN - 3, z, 1):
        mid_at += [(start + p, valid) for p in range(SPAN)]
    for start, valid in starts(s.z_routes, 0, z.coarse + SPAN - 5, z, 1):
        coarse_at += [(start + p, valid) for p in range(SPAN)]
    for start, valid in starts(s.z2_routes, SPAN - 5 - z.coarse, 2 * z.coarse + SPAN - 5, z, 2):
        mid_at += [(None, None)] * z.second
        coarse_at += [(start + p, valid) for p in range(z.second)]
    group = 4
    for g in range(0, s.sum_planes, group):
        n = s.sum_rows
        count = min(group, s.sum_planes - g)
        grid = sums[g : g + count].reshape(count * n, x.fine)
        a, b = along_x(grid, g * n, count * n, x_sums)
        for p in range(count):
            rows = slice(p * n, (p + 1) * n)
            for which, (held, weights) in enumerate(((t_mid, y_mid), (t_coarse, y_coarse))):
                at, valid = (mid_at, coarse_at)[which][g + p]
                if at is None:
                    continue
                cols = slice(which * TERMS * x.fine, (which + 1) * TERMS * x.fine)
                for t, part in enumerate(along_y(a[rows, cols], b[rows, cols], weights)):
                    if valid is None:
                        held[at, t] = part
                    else:
                        held[at, t] = held[at, t] + jnp.where(valid, part, 0.0)

    def along_z(held, level, base, count):
        totals = [None] * count
        for t in range(TERMS):
            for j in range(count + TAPS - 1):
                plane = held[base + j, t]
                for i in range(max(0, j - TAPS + 1), min(count, j + 1)):
                    term = taps[level, t, j - i] * plane
                    totals[i] = term if totals[i] is None else totals[i] + term
        return totals

    block = 4
    for k in range(0, z.coarse_all, block):
        count = min(block, z.coarse_all - k)
        for i, total in enumerate(along_z(t_coarse, 2, k, count)):
            p_coarse[k + i] = jnp.where(z.holds_coarse(k + i - 2), total, 0.0)
    for k in range(0, z.mid_all, block):
        count = min(block, z.mid_all - k)
        for i, total in enumerate(along_z(t_mid, 1, k + SPAN - 11, count)):
            m = k + i - 1
            for offset, weight in WEIGHTS:
                if (m - offset) % 2 == 0 and 0 <= (m - offset) // 2 + 2 < z.coarse_all:
                    total = total + weight * p_coarse[(m - offset) // 2 + 2]
            p_mid[k + i] = jnp.where(z.holds_mid(m), total, 0.0)

    def step(b, carry):
        for i, total in enumerate(along_z(t_fine, 0, b * block, block)):
            for offset, weight in WEIGHTS:
                if (i - offset) % 2 == 0:
                    total = total + weight * p_mid[b * (block // 2) + (i - offset) // 2 + 1]
            out[b * block + i] = total
        return carry

    lax.fori_loop(0, z.fine // block, step, 0)


def call(kernel, outs, ins, scratch=(), flops=10**7):
    specs = [SMEM if a.ndim == 3 and a.shape[-1] == TAPS else VMEM for a in ins]
    size = sum(a.size * a.dtype.itemsize for a in ins) + sum(o.size * o.dtype.itemsize for o in outs)
    return pl.pallas_call(
        kernel,
        out_shape=tuple(outs),
        in_specs=specs,
        out_specs=tuple(VMEM for _ in outs),
        scratch_shapes=list(scratch),
        compiler_params=PARAMS,
        cost_estimate=pl.CostEstimate(flops=flops, bytes_accessed=size, transcendentals=0),
    )(*ins)


def array(*shape, dtype=F32):
    return jax.ShapeDtypeStruct(shape, dtype)


def local(charges, kernel_taps):
    z, y, x = (Cut(name, size) for name, size in zip(("gz", "gy", "gx"), charges.shape))
    s = Sizes(z, y, x)
    n = x.fine
    nz, nz2 = len(s.z_routes), len(s.z2_routes)

    def bound(kernel, *static):
        return lambda *refs: kernel(s, *static, *refs)

    rows = up8(y.mid_all)
    own, *messages = call(
        bound(restrict_kernel, nz),
        [array(z.mid_all, rows, n)] + [array(s.z_rows, n)] * nz + [array(s.z2_rows, n)] * nz2,
        [charges],
        [
            pltpu.VMEM((z.fine, y.fine + 16, n), F32),
            pltpu.VMEM((z.mid_all, rows, n), F32),
            pltpu.VMEM((z.mid_all, up8(y.mid + 24), n), F32),
            pltpu.VMEM((z.mid_all, rows, n), F32),
        ],
    )
    z_got = [route(m) for route, m in zip(s.z_routes + s.z2_routes, messages)]
    operators = call(
        bound(operator_kernel),
        [
            array(5 * n, TERMS * n, dtype=BF16),
            array(5 * n, 2 * TERMS * n, dtype=BF16),
            array(TERMS * y.fine, 3 * s.fine_rows, dtype=BF16),
            array(TERMS * y.fine, 3 * s.sum_rows, dtype=BF16),
            array(TERMS * y.fine, 3 * s.sum_rows, dtype=BF16),
        ],
        [kernel_taps],
    )
    ahead, behind, far = call(
        bound(spread_kernel, nz, nz2),
        [array(s.y_rows, n), array(s.y_rows, n), array(s.y2_rows, n)],
        [charges, own, *z_got],
    )
    ahead, behind = s.y_routes[0](ahead), s.y_routes[1](behind)
    far = s.y2_routes[0](far)
    fine, sums, first, second = call(
        bound(collect_kernel, nz, nz2),
        [
            array(s.fine_planes, s.fine_rows, n),
            array(s.sum_planes, s.sum_rows, n),
            array(s.x_sends, s.x_cells),
            array(s.x_sends, s.x_cells),
        ],
        [charges, own, *z_got, ahead, behind, far],
    )
    first, second = s.x_routes[0](first), s.x_routes[1](second)
    (out,) = call(
        bound(sum_kernel),
        [array(z.fine, y.fine, n)],
        [kernel_taps, fine, sums, first, second, *operators],
        [
            pltpu.VMEM((s.x_cells, n), F32),
            pltpu.VMEM((z.fine + 2 * RADIUS, TERMS, y.fine, n), F32),
            pltpu.VMEM((z.mid + 2 * SPAN - 3, TERMS, y.fine, n), F32),
            pltpu.VMEM((2 * z.coarse + SPAN, TERMS, y.fine, n), F32),
            pltpu.VMEM((z.mid_all, y.fine, n), F32),
            pltpu.VMEM((z.coarse_all, y.fine, n), F32),
        ],
    )
    return out


def solution(mesh):
    return jax.shard_map(
        local,
        mesh=mesh,
        in_specs=(P("gz", "gy", "gx"), P()),
        out_specs=P("gz", "gy", "gx"),
        check_vma=False,
    )
```

time: 186 us -> 44.3 us (0.24); the launches traced: 184 us -> 44.2 us
  starting transfers between devices: 73.4 us -> 12.4 us
  local copies, waits for them, and re-layouts: 37 us -> 1.05 us
  other arithmetic: 32.7 us -> 0 us
  waiting for transfers between devices: 32.5 us -> 16.6 us
  Pallas kernels: 0 us -> 14.2 us
  blocking collectives: 5.11 us -> 0 us
  between operations: 1.94 us -> 0.04 us
    ppermute x28 -> x6, starting transfers between devices: 73.4 us -> 12.4 us  [__call__(): return lax.ppermute(x, self.names, self.pairs)]
    slice x35 -> x0, local copies, waits for them, and re-layouts: 20.4 us -> none  [the longest x20 15.5 us: restrict_axis(): lax.slice_in_dim(padded, first, first + 2 * count - 1, stride=2, axis=axi...]
    add x15 -> x0, other arithmetic: 18.1 us -> none  [the longest x6 16.7 us: convolve_axis(): summed + kernel_rows[:, offset].reshape(weight_shape) * lax.slice_in_dim(...]
    ppermute x28 -> x6, waiting for transfers between devices: 32.5 us -> 16.6 us  [__call__(): return lax.ppermute(x, self.names, self.pairs)]
    pallas_call x0 -> x5, Pallas kernels: none -> 14.2 us  [call(): pl.pallas_call(kernel, out_shape=tuple(outs), in_specs=specs, out_specs=t...]
    mul x20 -> x0, local copies, waits for them, and re-layouts: 9.64 us -> none  [the longest x4 9.51 us: convolve_axis(): kernel_rows[:, 0].reshape(weight_shape)]
    reduce_sum x2 -> x0, other arithmetic: 6.53 us -> none  [stencil_box(): return jnp.sum(smoothed, axis=0)]
    all_gather x1 -> x0, blocking collectives: 5.11 us -> none  [local(): slab_piece = lax.all_gather(smoothed, 'gz', axis=1, tiled=True)]
  transfers between devices with their start and end apart: 28 -> 6, of which waited for: 14 -> 4; matrix products, arithmetic and copies ran while one was open for 21% -> 0% of each run, Pallas kernels for 0% -> 4%
where the time goes in v2:
time: 44.3 us; the launch traced here: 44.2 us
  waiting for transfers between devices  16.6 us (37%)
  Pallas kernels  14.2 us (32%)
  starting transfers between devices  12.4 us (28%)
  local copies, waits for them, and re-layouts  1.05 us (2%)
    ppermute x6, waiting for transfers between devices, __call__(): return lax.ppermute(x, self.names, self.pairs)  16.6 us
    pallas_call x5, Pallas kernels, call(): pl.pallas_call(kernel, out_shape=tuple(outs), in_specs=specs, out_specs=t...  14.2 us
    ppermute x6, starting transfers between devices, __call__(): return lax.ppermute(x, self.names, self.pairs)  12.4 us
    unnamed x4, local copies, waits for them, and re-layouts  1.05 us
  transfers between devices with their start and end apart: 6, of which 4 were waited for; matrix products, arithmetic and copies ran while one was open for 0% of the time, Pallas kernels for 4%

profile of v2, /device:TPU:1, one launch (start us, length us, event | category | flops | bytes accessed | tf_op | source)
XLA Modules:
  0.0 44.2 jit_solution(9704281155882668651)
XLA Ops:
  0.0 0.0 copy-start
  0.0 1.0 %copy-done = f32[32,32,128]{2,1,0:T(8,128)S(1)} copy-done((f32[32,32,128]{2,1,0:T(8,128)S(1)}, f32[32,32,128]{2,1,0:T(8,128)}, u32[]{:S(2)}) %copy-start) | copy-done | bytes 524312
  1.0 1.1 %shard_map.28 = (f32[19,24,128]{2,1,0:T(8,128)S(1)}, f32[504,128]{1,0:T(8,128)S(1)}) custom-call(f32[32,32,128]{2,1,0:T(8,128)S(1)} %copy-done), custom_call_target="tpu_custom_call" | custom-call | flops 10000000 | bytes 1015808 | tf_op jit(solution)/shard_map/pallas_call | solution.py:538
  2.2 2.1 %collective-permute-start = (f32[504,128]{1,0:T(8,128)S(1)}, f32[504,128]{1,0:T(8,128)S(1)}, u32[]{:S(2)}, u32[]{:S(2)}) collective-permute-start(f32[504,128]{1,0:T(8,128)S(1)} %get-tuple-element.20), channel_id=1, source_target_pairs={{0,1},{1,0},{2,3},{3,2},{4,5},{5,4},{6,7},{7,6},{8,9},{9,8},{10,11... | collective-permute-start | bytes 774152 | tf_op jit(solution)/shard_map/ppermute | solution.py:64
  4.3 5.9 %collective-permute-done.refs_2_ = f32[504,128]{1,0:T(8,128)S(1)} collective-permute-done((f32[504,128]{1,0:T(8,128)S(1)}, f32[504,128]{1,0:T(8,128)S(1)}, u32[]{:S(2)}, u32[]{:S(2)}) %collective-permute-start) | collective-permute-done | bytes 258080 | tf_op jit(solution)/shard_map/ppermute | solution.py:64
  10.3 0.1 shard_map.29
  10.4 1.2 %collective-permute-start.1 = (f32[736,128]{1,0:T(8,128)S(1)}, f32[736,128]{1,0:T(8,128)S(1)}, u32[]{:S(2)}, u32[]{:S(2)}) collective-permute-start(f32[736,128]{1,0:T(8,128)S(1)} %get-tuple-element.21), channel_id=1, source_target_pairs={{0,2},{2,4},{4,6},{6,14},{14,12},{12,10},{10,8},{8,0},{16,18},{18,... | collective-permute-start | bytes 1130504 | tf_op jit(solution)/shard_map/ppermute | solution.py:64
  11.6 0.2 collective-permute-start.2
  11.9 2.2 %collective-permute-start.3 = (f32[160,128]{1,0:T(8,128)S(1)}, f32[160,128]{1,0:T(8,128)S(1)}, u32[]{:S(2)}, u32[]{:S(2)}) collective-permute-start(f32[160,128]{1,0:T(8,128)S(1)} %get-tuple-element.23), channel_id=1, source_target_pairs={{0,4},{2,6},{4,0},{6,2},{1,5},{3,7},{5,1},{7,3},{8,12},{10,14},{12... | collective-permute-start | bytes 245768 | tf_op jit(solution)/shard_map/ppermute | solution.py:64
  14.1 6.6 %collective-permute-done.3.refs_5_ = f32[160,128]{1,0:T(8,128)S(1)} collective-permute-done((f32[160,128]{1,0:T(8,128)S(1)}, f32[160,128]{1,0:T(8,128)S(1)}, u32[]{:S(2)}, u32[]{:S(2)}) %collective-permute-start.3) | collective-permute-done | bytes 81952 | tf_op jit(solution)/shard_map/ppermute | solution.py:64
  20.7 0.0 collective-permute-done.1.refs_3_
  20.7 0.0 collective-permute-done.2.refs_4_
  20.7 1.1 %shard_map.30 = (f32[40,48,128]{2,1,0:T(8,128)S(1)}, f32[32,64,128]{2,1,0:T(8,128)S(1)}, f32[32,2048]{1,0:T(8,128)S(1)}, f32[32,2048]{1,0:T(8,128)S(1)}) custom-call(f32[32,32,128]{2,1,0:T(8,128)S(1)} %copy-done, f32[19,24,128]{2,1,0:T(8,128)S(1)} %get-tuple-element.19.refs_1_, f32[504,128]{1,0:T(8,128)S(1)} %collective-permute-done.refs_2_, ...), custom_call_target="tpu_custom_call" | custom-call | flops 10000000 | bytes 4407296 | tf_op jit(solution)/shard_map/pallas_call | solution.py:538
  21.8 0.0 copy-start.1
  21.8 6.5 %collective-permute-start.4 = (f32[32,2048]{1,0:T(8,128)S(1)}, f32[32,2048]{1,0:T(8,128)S(1)}, u32[]{:S(2)}, u32[]{:S(2)}) collective-permute-start(f32[32,2048]{1,0:T(8,128)S(1)} %get-tuple-element.26), channel_id=1, source_target_pairs={{0,8},{8,16},{16,24},{24,25},{25,17},{17,9},{9,1},{1,0},{2,10},{10... | collective-permute-start | bytes 786440 | tf_op jit(solution)/shard_map/ppermute | solution.py:64
  28.3 0.0 collective-permute-start.5
  28.3 0.0 copy-done.1
  28.3 1.7 %shard_map.31 = (bf16[640,256]{1,0:T(8,128)(2,1)S(1)}, bf16[640,512]{1,0:T(8,128)(2,1)S(1)}, bf16[64,144]{1,0:T(8,128)(2,1)S(1)}, bf16[64,192]{1,0:T(8,128)(2,1)S(1)}, bf16[64,192]{1,0:T(8,128)(2,1)S(1)}) custom-call(f32[3,2,17]{2,1,0:T(2,128)S(1)} %copy-done.1), custom_call_target="tpu_custom_call" | custom-call | flops 10000000 | bytes 1051032 | tf_op jit(solution)/shard_map/pallas_call | solution.py:538
  30.1 1.6 %collective-permute-done.4.refs_3_ = f32[32,2048]{1,0:T(8,128)S(1)} collective-permute-done((f32[32,2048]{1,0:T(8,128)S(1)}, f32[32,2048]{1,0:T(8,128)S(1)}, u32[]{:S(2)}, u32[]{:S(2)}) %collective-permute-start.4) | collective-permute-done | bytes 262176 | tf_op jit(solution)/shard_map/ppermute | solution.py:64
  31.7 2.5 %collective-permute-done.5.refs_4_ = f32[32,2048]{1,0:T(8,128)S(1)} collective-permute-done((f32[32,2048]{1,0:T(8,128)S(1)}, f32[32,2048]{1,0:T(8,128)S(1)}, u32[]{:S(2)}, u32[]{:S(2)}) %collective-permute-start.5) | collective-permute-done | bytes 262176 | tf_op jit(solution)/shard_map/ppermute | solution.py:64
  34.1 10.0 %shard_map.32 = f32[32,32,128]{2,1,0:T(8,128)} custom-call(f32[3,2,17]{2,1,0:T(2,128)S(1)} %copy-done.1, f32[40,48,128]{2,1,0:T(8,128)S(1)} %get-tuple-element.24.refs_1_, f32[32,64,128]{2,1,0:T(8,128)S(1)} %get-tuple-element.25.refs_2_, f32[32,2048]{1,0:T(8,128)S(1)} %collective-permute-done.4.refs_3_, f32[32,2048]{1,0:T(8,128)S(1)} %collective-permute-done.5.refs_4_, ...), custom_call_target="tpu_custom_call" | custom-call | flops 10000000 | bytes 4131224 | tf_op jit(solution)/shard_map/pallas_call | solution.py:538
Async XLA Ops:
  0.0 1.0 %copy-start = (f32[32,32,128]{2,1,0:T(8,128)S(1)}, f32[32,32,128]{2,1,0:T(8,128)}, u32[]{:S(2)}) copy-start(f32[32,32,128]{2,1,0:T(8,128)} %refs_0_.7) | copy-start | bytes 1572868
  2.2 8.1 %collective-permute-start = (f32[504,128]{1,0:T(8,128)S(1)}, f32[504,128]{1,0:T(8,128)S(1)}, u32[]{:S(2)}, u32[]{:S(2)}) collective-permute-start(f32[504,128]{1,0:T(8,128)S(1)} %get-tuple-element.20), channel_id=1, source_target_pairs={{0,1},{1,0},{2,3},{3,2},{4,5},{5,4},{6,7},{7,6},{8,9},{9,8},{10,11... | collective-permute-start | bytes 774152 | tf_op jit(solution)/shard_map/ppermute | solution.py:64
  10.4 10.3 %collective-permute-start.1 = (f32[736,128]{1,0:T(8,128)S(1)}, f32[736,128]{1,0:T(8,128)S(1)}, u32[]{:S(2)}, u32[]{:S(2)}) collective-permute-start(f32[736,128]{1,0:T(8,128)S(1)} %get-tuple-element.21), channel_id=1, source_target_pairs={{0,2},{2,4},{4,6},{6,14},{14,12},{12,10},{10,8},{8,0},{16,18},{18,... | collective-permute-start | bytes 1130504 | tf_op jit(solution)/shard_map/ppermute | solution.py:64
  11.6 9.0 %collective-permute-start.2 = (f32[736,128]{1,0:T(8,128)S(1)}, f32[736,128]{1,0:T(8,128)S(1)}, u32[]{:S(2)}, u32[]{:S(2)}) collective-permute-start(f32[736,128]{1,0:T(8,128)S(1)} %get-tuple-element.22), channel_id=1, source_target_pairs={{2,0},{4,2},{6,4},{14,6},{12,14},{10,12},{8,10},{0,8},{18,16},{20,... | collective-permute-start | bytes 1130504 | tf_op jit(solution)/shard_map/ppermute | solution.py:64
  11.9 8.8 %collective-permute-start.3 = (f32[160,128]{1,0:T(8,128)S(1)}, f32[160,128]{1,0:T(8,128)S(1)}, u32[]{:S(2)}, u32[]{:S(2)}) collective-permute-start(f32[160,128]{1,0:T(8,128)S(1)} %get-tuple-element.23), channel_id=1, source_target_pairs={{0,4},{2,6},{4,0},{6,2},{1,5},{3,7},{5,1},{7,3},{8,12},{10,14},{12... | collective-permute-start | bytes 245768 | tf_op jit(solution)/shard_map/ppermute | solution.py:64
  21.8 6.5 %copy-start.1 = (f32[3,2,17]{2,1,0:T(2,128)S(1)}, f32[3,2,17]{2,1,0:T(2,128)}, u32[]{:S(2)}) copy-start(f32[3,2,17]{2,1,0:T(2,128)} %refs_0_.9) | copy-start | bytes 1228
  21.8 9.8 %collective-permute-start.4 = (f32[32,2048]{1,0:T(8,128)S(1)}, f32[32,2048]{1,0:T(8,128)S(1)}, u32[]{:S(2)}, u32[]{:S(2)}) collective-permute-start(f32[32,2048]{1,0:T(8,128)S(1)} %get-tuple-element.26), channel_id=1, source_target_pairs={{0,8},{8,16},{16,24},{24,25},{25,17},{17,9},{9,1},{1,0},{2,10},{10... | collective-permute-start | bytes 786440 | tf_op jit(solution)/shard_map/ppermute | solution.py:64
  28.3 5.8 %collective-permute-start.5 = (f32[32,2048]{1,0:T(8,128)S(1)}, f32[32,2048]{1,0:T(8,128)S(1)}, u32[]{:S(2)}, u32[]{:S(2)}) collective-permute-start(f32[32,2048]{1,0:T(8,128)S(1)} %get-tuple-element.27), channel_id=1, source_target_pairs={{8,0},{16,8},{24,16},{25,24},{17,25},{9,17},{1,9},{0,1},{10,2},{18... | collective-permute-start | bytes 786440 | tf_op jit(solution)/shard_map/ppermute | solution.py:64

commit v3 on v2

--- a/solution.py
+++ b/solution.py
@@ -13,7 +13,7 @@
 SPAN = RADIUS + 5
 EDGE = RADIUS + 3
 F32, BF16 = jnp.float32, jnp.bfloat16
-PARAMS = pltpu.CompilerParams(vmem_limit_bytes=48 * 1024 * 1024)
+PARAMS = pltpu.CompilerParams(vmem_limit_bytes=32 * 1024 * 1024)
 VMEM = pl.BlockSpec(memory_space=pltpu.VMEM)
 SMEM = pl.BlockSpec(memory_space=pltpu.SMEM)
 
@@ -130,24 +130,28 @@
         self.z_fine = RADIUS * y.fine
         self.z_rows = up8(self.z_fine + SPAN * y.mid_all)
         self.z2_rows = up8(z.second * y.mid_all)
+        self.slab_planes = SPAN * len(self.z_routes) + z.second * len(self.z2_routes)
         self.fine_planes = z.fine + RADIUS * len(self.z_routes)
-        self.sum_planes = z.mid_all + SPAN * len(self.z_routes) + z.second * len(self.z2_routes)
-        self.y_fine = RADIUS * self.fine_planes
-        self.y_rows = up8(self.y_fine + SPAN * self.sum_planes)
-        self.y2_rows = up8(y.second * self.sum_planes)
+        self.sum_planes = z.mid_all + RADIUS * len(self.z_routes)
+        self.y_fine = RADIUS * z.fine
+        self.y_rows = up8(self.y_fine + SPAN * z.mid_all)
+        self.slab_fine = RADIUS * RADIUS * len(self.z_routes)
+        self.slab_rows = up8(self.slab_fine + SPAN * self.slab_planes)
+        self.far_rows = up8(y.second * (z.coarse_all + self.slab_planes))
         self.fine_rows = y.fine + 2 * RADIUS
-        self.low = up8(y.mid_all)
-        self.high = self.low + up8(SPAN)
-        self.far = self.high + up8(SPAN)
-        self.sum_rows = -(-(self.far + y.second) // 16) * 16
+        self.far = y.coarse_all
+        self.low = y.mid_all
+        self.high = self.low + SPAN
+        self.sum_rows = -(-(self.high + SPAN) // 16) * 16
         self.x_sends = RADIUS + EDGE + SPAN
         cells = max(self.fine_planes * self.fine_rows, self.sum_planes * self.sum_rows)
         self.x_cells = -(-cells // 128) * 128
         assert x.mid_all + x.coarse_all <= x.fine and self.x_sends <= 32
+        assert self.far + y.second <= self.low
         assert z.coarse >= RADIUS and y.coarse >= RADIUS and y.count == 4
 
 
-def restrict_kernel(s, nz, charges, own, *rest):
+def restrict_kernel(s, nz, charges, held, own, ahead, behind, *rest):
     messages, (wide, mid, high, coarse) = rest[:-4], rest[-4:]
     z, y, x = s.z, s.y, s.x
     lanes = (x.fine, x.fine)
@@ -159,6 +163,7 @@
     to_coarse = jnp.where(inside, weight_of(cell - 1 - 2 * c), 0.0)
     narrow = to_mid + jnp.dot(to_mid, to_coarse, precision=EXACT, preferred_element_type=F32)
     grid = charges[...]
+    held[...] = grid
     reduced = jnp.dot(grid.reshape(z.fine * y.fine, x.fine), narrow, precision=EXACT, preferred_element_type=F32)
     wide[...] = jnp.zeros(wide.shape, F32)
     wide[:, 8 : 8 + y.fine, :] = reduced.reshape(z.fine, y.fine, x.fine)
@@ -192,6 +197,18 @@
     is_mid = iota(mid.shape[1:], 1) < x.mid_all
     for p in range(z.mid_all):
         own[p] = jnp.where(is_mid, mid[p], coarse[p]) if p < z.coarse_all else jnp.where(is_mid, mid[p], 0.0)
+    is_side = iota((SPAN, x.fine), 1) < x.mid_all
+    for message, route in zip((ahead, behind), s.y_routes):
+        up = route.up()
+        edge = jnp.where(up, charges[:, y.fine - RADIUS :, :], charges[:, :RADIUS, :])
+        message[: s.y_fine] = edge.reshape(s.y_fine, x.fine)
+        for p in range(z.mid_all):
+            last = jnp.where(is_side, own[p, y.mid_all - SPAN : y.mid_all], own[p, y.coarse_all - SPAN : y.coarse_all])
+            at = s.y_fine + p * SPAN
+            message[at : at + SPAN] = jnp.where(up, last, own[p, :SPAN])
+        filled = s.y_fine + SPAN * z.mid_all
+        if filled < s.y_rows:
+            message[filled:] = jnp.zeros((s.y_rows - filled, x.fine), F32)
     for message, route in zip(messages, s.z_routes):
         up = route.up().astype(jnp.int32)
         message[: s.z_fine] = charges[pl.ds(up * (z.fine - RADIUS), RADIUS)].reshape(s.z_fine, x.fine)
@@ -219,80 +236,106 @@
     return out
 
 
-def spread_kernel(s, nz, nz2, charges, own, *rest):
+def spread_kernel(s, nz, nz2, _, own, *rest):
     z_messages, z2_messages = rest[:nz], rest[nz : nz + nz2]
-    messages = rest[nz + nz2 : -1]
-    far = rest[-1]
+    ahead, behind, far = rest[-3:]
     z, y, x = s.z, s.y, s.x
     is_mid = iota((SPAN, x.fine), 1) < x.mid_all
     planes = slabs(s, z_messages, z2_messages)
-
-    def rows_of(p, first, count):
-        if p < z.mid_all:
-            return own[p, first : first + count]
-        message, at = planes[p - z.mid_all]
-        return message[at + first : at + first + count]
-
-    for message, route in zip(messages, s.y_routes):
+    for message, route in zip((ahead, behind), s.y_routes):
         up = route.up()
-        message[: RADIUS * z.fine] = jnp.where(
-            up, charges[:, y.fine - RADIUS :, :], charges[:, :RADIUS, :]
-        ).reshape(RADIUS * z.fine, x.fine)
-        at = RADIUS * z.fine
+        at = 0
         for z_message in z_messages:
             slab = z_message[: s.z_fine].reshape(RADIUS, y.fine, x.fine)
             edge = jnp.where(up, slab[:, y.fine - RADIUS :], slab[:, :RADIUS])
             message[at : at + RADIUS * RADIUS] = edge.reshape(RADIUS * RADIUS, x.fine)
             at += RADIUS * RADIUS
-        for p in range(s.sum_planes):
-            last = jnp.where(
-                is_mid, rows_of(p, y.mid_all - SPAN, SPAN), rows_of(p, y.coarse_all - SPAN, SPAN)
-            )
-            message[at : at + SPAN] = jnp.where(up, last, rows_of(p, 0, SPAN))
+        for held, first in planes:
+            top, end = held[first + y.mid_all - SPAN : first + y.mid_all], first + y.coarse_all
+            last = jnp.where(is_mid, top, held[end - SPAN : end])
+            message[at : at + SPAN] = jnp.where(up, last, held[first : first + SPAN])
             at += SPAN
-        if at < s.y_rows:
-            message[at:] = jnp.zeros((s.y_rows - at, x.fine), F32)
+        if at < s.slab_rows:
+            message[at:] = jnp.zeros((s.slab_rows - at, x.fine), F32)
     up = s.y2_routes[0].up()
-    count = y.second
-    for p in range(s.sum_planes):
-        far[p * count : (p + 1) * count] = jnp.where(up, rows_of(p, y.coarse_all - count, count), rows_of(p, 0, count))
-    if s.sum_planes * count < s.y2_rows:
-        far[s.sum_planes * count :] = jnp.zeros((s.y2_rows - s.sum_planes * count, x.fine), F32)
+    count, end = y.second, y.coarse_all
+    at = 0
+    for p in range(z.coarse_all):
+        far[at : at + count] = jnp.where(up, own[p, end - count : end], own[p, :count])
+        at += count
+    for held, first in planes:
+        far[at : at + count] = jnp.where(up, held[first + end - count : first + end], held[first : first + count])
+        at += count
+    if at < s.far_rows:
+        far[at:] = jnp.zeros((s.far_rows - at, x.fine), F32)
 
 
 def collect_kernel(s, nz, nz2, charges, own, *rest):
     z_messages, z2_messages = rest[:nz], rest[nz : nz + nz2]
-    ahead, behind, far, fine, sums, first, second = rest[nz + nz2 :]
+    pairs = rest[nz + nz2 : nz + nz2 + 4]
+    far, fine, sums, first, second, raw = rest[nz + nz2 + 4 :]
     z, y, x = s.z, s.y, s.x
     below = s.y_routes[0].below()
     planes = slabs(s, z_messages, z2_messages)
 
-    def sides(start, count):
-        a, b = ahead[start : start + count], behind[start : start + count]
+    def sides(which, start, count):
+        a, b = (message[start : start + count] for message in pairs[2 * which : 2 * which + 2])
         return jnp.where(below, a, b), jnp.where(below, b, a)
 
-    def fine_planes(at, count, body, row):
-        low, high = sides(row, RADIUS * count)
+    def fine_planes(at, count, body, which, row):
+        low, high = sides(which, row, RADIUS * count)
         fine[at : at + count, : y.fine] = body
         fine[at : at + count, y.fine : y.fine + RADIUS] = low.reshape(count, RADIUS, x.fine)
         fine[at : at + count, y.fine + RADIUS :] = high.reshape(count, RADIUS, x.fine)
 
-    fine_planes(0, z.fine, charges[...], 0)
+    fine_planes(0, z.fine, charges[...], 0, 0)
     at = z.fine
-    for z_message in z_messages:
-        fine_planes(at, RADIUS, z_message[: s.z_fine].reshape(RADIUS, y.fine, x.fine), RADIUS * at)
+    for n, z_message in enumerate(z_messages):
+        slab = z_message[: s.z_fine].reshape(RADIUS, y.fine, x.fine)
+        fine_planes(at, RADIUS, slab, 1, n * RADIUS * RADIUS)
         at += RADIUS
     sums[...] = jnp.zeros(sums.shape, F32)
-    for p in range(s.sum_planes):
-        if p < z.mid_all:
-            sums[p, : s.low] = own[p]
-        else:
-            message, at = planes[p - z.mid_all]
-            sums[p, : y.mid_all] = message[at : at + y.mid_all]
-        low, high = sides(s.y_fine + p * SPAN, SPAN)
-        sums[p, s.low : s.low + SPAN] = low
-        sums[p, s.high : s.high + SPAN] = high
-        sums[p, s.far : s.far + y.second] = far[p * y.second : (p + 1) * y.second]
+    raw[...] = jnp.zeros(raw.shape, F32)
+    is_mid = iota((y.second, x.fine), 1) < x.mid_all
+
+    def rows_of_plane(out, p, body, which, row, far_row):
+        low, high = sides(which, row, SPAN)
+        out[p, : y.mid_all] = body
+        out[p, s.low : s.low + SPAN] = low
+        out[p, s.high : s.high + SPAN] = high
+        if far_row is not None:
+            at = slice(s.far, s.far + y.second)
+            out[p, at] = jnp.where(is_mid, out[p, at], far[far_row : far_row + y.second])
+
+    for p in range(z.mid_all):
+        far_row = p * y.second if p < z.coarse_all else None
+        rows_of_plane(sums, p, own[p, : y.mid_all], 0, s.y_fine + p * SPAN, far_row)
+    for p, (held, at) in enumerate(planes):
+        far_row = (z.coarse_all + p) * y.second
+        rows_of_plane(raw, p, held[at : at + y.mid_all], 1, s.slab_fine + p * SPAN, far_row)
+    is_mid = iota((s.sum_rows, x.fine), 1) < x.mid_all
+
+    def number(condition, a, b):
+        return jnp.where(condition, a, b)
+
+    for n, route in enumerate(s.z_routes):
+        lower, base = route.below(), n * SPAN
+        for j in range(RADIUS):
+            a = raw[base + number(lower, SPAN - 3 - RADIUS, 3) + j]
+            b = raw[base + number(lower, SPAN - 5 - RADIUS, 5) + j]
+            sums[z.mid_all + n * RADIUS + j] = jnp.where(is_mid, a, b)
+        for i in range(3):
+            at = number(lower, 0, z.mid) + i
+            sums[at] = sums[at] + jnp.where(is_mid, raw[base + number(lower, SPAN - 3, 0) + i], 0.0)
+        for i in range(5):
+            at = number(lower, 0, z.coarse) + i
+            sums[at] = sums[at] + jnp.where(is_mid, 0.0, raw[base + number(lower, SPAN - 5, 0) + i])
+    for n, route in enumerate(s.z2_routes):
+        base = len(s.z_routes) * SPAN + n * z.second
+        start = z.mid_all + number(route.below(), RADIUS - z.coarse, RADIUS + z.coarse - 5)
+        for p in range(z.second):
+            sums[start + p] = sums[start + p] + jnp.where(is_mid, 0.0, raw[base + p])
+
     row, lane = iota((2 * RADIUS, x.fine), 0), iota((2 * RADIUS, x.fine), 1)
     up = s.x_routes[0].up()
     is_first = row < RADIUS
@@ -422,6 +465,18 @@
     write(y_coarse, s.sum_rows, [dot(from_coarse, m) for m in coarse])
 
 
+def own_kernel(s, fine, sums, x_fine, x_sums, fine_part, sums_part):
+    def along_x(grid, weights):
+        high, low = split(grid)
+        joined = jnp.concatenate([high, low, high], axis=1)
+        return jnp.dot(joined, weights[: 3 * s.x.fine], preferred_element_type=F32)
+
+    cells = s.fine_planes * s.fine_rows
+    fine_part[...] = along_x(fine[...].reshape(cells, s.x.fine), x_fine)
+    cells = s.sum_planes * s.sum_rows
+    sums_part[...] = along_x(sums[...].reshape(cells, s.x.fine), x_sums)
+
+
 def sum_kernel(s, taps, fine, sums, first, second, x_fine, x_sums, y_fine, y_mid, y_coarse, out, *scratch):
     turned, t_fine, t_mid, t_coarse, p_mid, p_coarse = scratch
     z, y, x = s.z, s.y, s.x
@@ -430,72 +485,65 @@
     high = jnp.where(below, second[...], first[...])
     turned[...] = jnp.concatenate([low, high, low, high], axis=0).T
 
-    def along_x(grid, start, rows, weights):
+    def along_x(held, start, rows, weights):
         edge = turned[start : start + rows]
         edge_high, edge_low = split(edge)
         lane = iota(edge.shape, 1) < 64
         packed = jnp.where(lane, edge_high.astype(F32), edge_low.astype(F32)).astype(BF16)
-        grid_high, grid_low = split(grid)
-        joined = jnp.concatenate([grid_high, grid_low, grid_high, packed, edge_high], axis=1)
-        return split(jnp.dot(joined, weights[...], preferred_element_type=F32))
+        joined = jnp.concatenate([packed, edge_high], axis=1)
+        part = jnp.dot(joined, weights[3 * x.fine :], preferred_element_type=F32)
+        return split(held[start : start + rows] + part)
 
     def along_y(high, low, weights):
         joined = jnp.concatenate([high, low, high], axis=0)
         result = jnp.dot(weights[...], joined, preferred_element_type=F32)
         return [result[t * y.fine : (t + 1) * y.fine, t * x.fine : (t + 1) * x.fine] for t in range(TERMS)]
 
-    def starts(routes, below_at, above_at, cut, steps):
+    def starts(below_at, above_at):
         result = []
-        for route in routes:
-            lower = route.below()
-            i = cut.index()
-            valid = choose(lower, i - steps >= 0, i + steps < cut.count)
+        for route in s.z_routes:
+            lower, i = route.below(), z.index()
+            valid = choose(lower, i >= 1, i + 1 < z.count)
             result.append((jnp.where(lower, below_at, above_at), valid))
         return result
 
     t_fine[...] = jnp.zeros(t_fine.shape, F32)
     t_mid[...] = jnp.zeros(t_mid.shape, F32)
     t_coarse[...] = jnp.zeros(t_coarse.shape, F32)
-    group = 8
-    fine_at = [(RADIUS + p, None) for p in range(z.fine)]
-    for start, valid in starts(s.z_routes, 0, z.fine + RADIUS, z, 1):
-        fine_at += [(start + p, valid) for p in range(RADIUS)]
-    for g in range(0, s.fine_planes, group):
-        n = s.fine_rows
-        grid = fine[g : g + group].reshape(group * n, x.fine)
-        a, b = along_x(grid, g * n, group * n, x_fine)
-        for p in range(group):
-            at, valid = fine_at[g + p]
-            for t, part in enumerate(along_y(a[p * n : (p + 1) * n], b[p * n : (p + 1) * n], y_fine)):
-                t_fine[at, t] = part if valid is None else jnp.where(valid, part, 0.0)
-
-    mid_at = [(SPAN - 3 + p, None) for p in range(z.mid_all)]
-    coarse_at = [(SPAN - 5 + p if p < z.coarse_all else None, None) for p in range(z.mid_all)]
-    for start, valid in starts(s.z_routes, 0, z.mid + SPAN - 3, z, 1):
-        mid_at += [(start + p, valid) for p in range(SPAN)]
-    for start, valid in starts(s.z_routes, 0, z.coarse + SPAN - 5, z, 1):
-        coarse_at += [(start + p, valid) for p in range(SPAN)]
-    for start, valid in starts(s.z2_routes, SPAN - 5 - z.coarse, 2 * z.coarse + SPAN - 5, z, 2):
-        mid_at += [(None, None)] * z.second
-        coarse_at += [(start + p, valid) for p in range(z.second)]
+
+    def store(held, at, valid, parts):
+        for t, part in enumerate(parts):
+            held[at, t] = part if valid is None else jnp.where(valid, part, 0.0)
+
+    mid_at = [(RADIUS + p, None) for p in range(z.mid_all)]
+    coarse_at = [(RADIUS + p if p < z.coarse_all else None, None) for p in range(z.mid_all)]
+    for start, valid in starts(0, z.mid + 3 + RADIUS):
+        mid_at += [(start + p, valid) for p in range(RADIUS)]
+    for start, valid in starts(0, z.coarse + 5 + RADIUS):
+        coarse_at += [(start + p, valid) for p in range(RADIUS)]
     group = 4
     for g in range(0, s.sum_planes, group):
         n = s.sum_rows
         count = min(group, s.sum_planes - g)
-        grid = sums[g : g + count].reshape(count * n, x.fine)
-        a, b = along_x(grid, g * n, count * n, x_sums)
+        a, b = along_x(sums, g * n, count * n, x_sums)
         for p in range(count):
             rows = slice(p * n, (p + 1) * n)
             for which, (held, weights) in enumerate(((t_mid, y_mid), (t_coarse, y_coarse))):
                 at, valid = (mid_at, coarse_at)[which][g + p]
-                if at is None:
-                    continue
-                cols = slice(which * TERMS * x.fine, (which + 1) * TERMS * x.fine)
-                for t, part in enumerate(along_y(a[rows, cols], b[rows, cols], weights)):
-                    if valid is None:
-                        held[at, t] = part
-                    else:
-                        held[at, t] = held[at, t] + jnp.where(valid, part, 0.0)
+                if at is not None:
+                    cols = slice(which * TERMS * x.fine, (which + 1) * TERMS * x.fine)
+                    store(held, at, valid, along_y(a[rows, cols], b[rows, cols], weights))
+
+    group = 8
+    fine_at = [(RADIUS + p, None) for p in range(z.fine)]
+    for start, valid in starts(0, z.fine + RADIUS):
+        fine_at += [(start + p, valid) for p in range(RADIUS)]
+    for g in range(0, s.fine_planes, group):
+        n = s.fine_rows
+        a, b = along_x(fine, g * n, group * n, x_fine)
+        for p in range(group):
+            rows = slice(p * n, (p + 1) * n)
+            store(t_fine, *fine_at[g + p], along_y(a[rows], b[rows], y_fine))
 
     def along_z(held, level, base, count):
         totals = [None] * count
@@ -514,7 +562,7 @@
             p_coarse[k + i] = jnp.where(z.holds_coarse(k + i - 2), total, 0.0)
     for k in range(0, z.mid_all, block):
         count = min(block, z.mid_all - k)
-        for i, total in enumerate(along_z(t_mid, 1, k + SPAN - 11, count)):
+        for i, total in enumerate(along_z(t_mid, 1, k, count)):
             m = k + i - 1
             for offset, weight in WEIGHTS:
                 if (m - offset) % 2 == 0 and 0 <= (m - offset) // 2 + 2 < z.coarse_all:
@@ -560,9 +608,9 @@
         return lambda *refs: kernel(s, *static, *refs)
 
     rows = up8(y.mid_all)
-    own, *messages = call(
+    held, own, ahead, behind, *messages = call(
         bound(restrict_kernel, nz),
-        [array(z.mid_all, rows, n)] + [array(s.z_rows, n)] * nz + [array(s.z2_rows, n)] * nz2,
+        [array(*charges.shape), array(z.mid_all, rows, n)] + [array(s.y_rows, n)] * 2 + [array(s.z_rows, n)] * nz + [array(s.z2_rows, n)] * nz2,
         [charges],
         [
             pltpu.VMEM((z.fine, y.fine + 16, n), F32),
@@ -572,6 +620,7 @@
         ],
     )
     z_got = [route(m) for route, m in zip(s.z_routes + s.z2_routes, messages)]
+    sides = [s.y_routes[0](ahead), s.y_routes[1](behind)]
     operators = call(
         bound(operator_kernel),
         [
@@ -585,10 +634,10 @@
     )
     ahead, behind, far = call(
         bound(spread_kernel, nz, nz2),
-        [array(s.y_rows, n), array(s.y_rows, n), array(s.y2_rows, n)],
-        [charges, own, *z_got],
-    )
-    ahead, behind = s.y_routes[0](ahead), s.y_routes[1](behind)
+        [array(s.slab_rows, n), array(s.slab_rows, n), array(s.far_rows, n)],
+        [operators[-1], own, *z_got],
+    )
+    sides += [s.y_routes[0](ahead), s.y_routes[1](behind)]
     far = s.y2_routes[0](far)
     fine, sums, first, second = call(
         bound(collect_kernel, nz, nz2),
@@ -598,9 +647,15 @@
             array(s.x_sends, s.x_cells),
             array(s.x_sends, s.x_cells),
         ],
-        [charges, own, *z_got, ahead, behind, far],
+        [held, own, *z_got, *sides, far],
+        [pltpu.VMEM((s.slab_planes, s.sum_rows, n), F32)],
     )
     first, second = s.x_routes[0](first), s.x_routes[1](second)
+    fine, sums = call(
+        bound(own_kernel),
+        [array(s.fine_planes * s.fine_rows, TERMS * n), array(s.sum_planes * s.sum_rows, 2 * TERMS * n)],
+        [fine, sums, *operators[:2]],
+    )
     (out,) = call(
         bound(sum_kernel),
         [array(z.fine, y.fine, n)],
@@ -608,8 +663,8 @@
         [
             pltpu.VMEM((s.x_cells, n), F32),
             pltpu.VMEM((z.fine + 2 * RADIUS, TERMS, y.fine, n), F32),
-            pltpu.VMEM((z.mid + 2 * SPAN - 3, TERMS, y.fine, n), F32),
-            pltpu.VMEM((2 * z.coarse + SPAN, TERMS, y.fine, n), F32),
+            pltpu.VMEM((z.mid + 2 * RADIUS + 3, TERMS, y.fine, n), F32),
+            pltpu.VMEM((z.coarse + 2 * RADIUS + 5, TERMS, y.fine, n), F32),
             pltpu.VMEM((z.mid_all, y.fine, n), F32),
             pltpu.VMEM((z.coarse_all, y.fine, n), F32),
         ],

time: 44.3 us -> 35.6 us (0.80)
  waiting for transfers between devices: 16.6 us -> 8.18 us
  Pallas kernels: 14.2 us -> 13 us
  local copies, waits for them, and re-layouts: 1.05 us -> 1.72 us
    ppermute x6 -> x8, waiting for transfers between devices: 16.6 us -> 8.18 us  [__call__(): return lax.ppermute(x, self.names, self.pairs)]
    pallas_call x5 -> x6, Pallas kernels: 14.2 us -> 13 us  [call(): pl.pallas_call(kernel, out_shape=tuple(outs), in_specs=specs, out_specs=t...]
    unnamed x4, local copies, waits for them, and re-layouts: 1.05 us -> 1.72 us
    ppermute x6 -> x8, starting transfers between devices: 12.4 us -> 12.5 us  [__call__(): return lax.ppermute(x, self.names, self.pairs)]
  transfers between devices with their start and end apart: 6 -> 8, of which waited for: 4 -> 4; matrix products, arithmetic and copies ran while one was open for 0% -> 0% of each run, Pallas kernels for 4% -> 9%
where the time goes in v3:
time: 35.6 us; the launch traced here: 35.4 us
  Pallas kernels  13 us (37%)
  starting transfers between devices  12.5 us (35%)
  waiting for transfers between devices  8.18 us (23%)
  local copies, waits for them, and re-layouts  1.72 us (5%)
    pallas_call x6, Pallas kernels, call(): pl.pallas_call(kernel, out_shape=tuple(outs), in_specs=specs, out_specs=t...  13 us
    ppermute x8, starting transfers between devices, __call__(): return lax.ppermute(x, self.names, self.pairs)  12.5 us
    ppermute x8, waiting for transfers between devices, __call__(): return lax.ppermute(x, self.names, self.pairs)  8.18 us
    unnamed x4, local copies, waits for them, and re-layouts  1.72 us
  transfers between devices with their start and end apart: 8, of which 4 were waited for; matrix products, arithmetic and copies ran while one was open for 0% of the time, Pallas kernels for 9%

profile of v3, /device:TPU:1, one launch (start us, length us, event | category | flops | bytes accessed | tf_op | source)
XLA Modules:
  0.0 35.4 jit_solution(16976128679912149104)
XLA Ops:
  0.0 0.0 copy-start
  0.0 1.0 %copy-done = f32[32,32,128]{2,1,0:T(8,128)S(1)} copy-done((f32[32,32,128]{2,1,0:T(8,128)S(1)}, f32[32,32,128]{2,1,0:T(8,128)}, u32[]{:S(2)}) %copy-start) | copy-done | bytes 524312
  1.0 1.2 %shard_map.28 = (f32[32,32,128]{2,1,0:T(8,128)S(1)}, f32[19,24,128]{2,1,0:T(8,128)S(1)}, f32[504,128]{1,0:T(8,128)S(1)}, f32[504,128]{1,0:T(8,128)S(1)}, f32[504,128]{1,0:T(8,128)S(1)}) custom-call(f32[32,32,128]{2,1,0:T(8,128)S(1)} %copy-done), custom_call_target="tpu_custom_call" | custom-call | flops 10000000 | bytes 2056192 | tf_op jit(solution)/shard_map/pallas_call | solution.py:586
  2.3 2.1 %collective-permute-start = (f32[504,128]{1,0:T(8,128)S(1)}, f32[504,128]{1,0:T(8,128)S(1)}, u32[]{:S(2)}, u32[]{:S(2)}) collective-permute-start(f32[504,128]{1,0:T(8,128)S(1)} %get-tuple-element.26), channel_id=1, source_target_pairs={{0,1},{1,0},{2,3},{3,2},{4,5},{5,4},{6,7},{7,6},{8,9},{9,8},{10,11... | collective-permute-start | bytes 774152 | tf_op jit(solution)/shard_map/ppermute | solution.py:64
  4.4 1.0 %collective-permute-start.1 = (f32[504,128]{1,0:T(8,128)S(1)}, f32[504,128]{1,0:T(8,128)S(1)}, u32[]{:S(2)}, u32[]{:S(2)}) collective-permute-start(f32[504,128]{1,0:T(8,128)S(1)} %get-tuple-element.27), channel_id=1, source_target_pairs={{0,2},{2,4},{4,6},{6,14},{14,12},{12,10},{10,8},{8,0},{16,18},{18,... | collective-permute-start | bytes 774152 | tf_op jit(solution)/shard_map/ppermute | solution.py:64
  5.3 0.5 %collective-permute-start.2 = (f32[504,128]{1,0:T(8,128)S(1)}, f32[504,128]{1,0:T(8,128)S(1)}, u32[]{:S(2)}, u32[]{:S(2)}) collective-permute-start(f32[504,128]{1,0:T(8,128)S(1)} %get-tuple-element.28), channel_id=1, source_target_pairs={{2,0},{4,2},{6,4},{14,6},{12,14},{10,12},{8,10},{0,8},{18,16},{20,... | collective-permute-start | bytes 774152 | tf_op jit(solution)/shard_map/ppermute | solution.py:64
  5.8 0.0 copy-start.1
  5.8 0.7 %copy-done.1 = f32[3,2,17]{2,1,0:T(2,128)S(1)} copy-done((f32[3,2,17]{2,1,0:T(2,128)S(1)}, f32[3,2,17]{2,1,0:T(2,128)}, u32[]{:S(2)}) %copy-start.1) | copy-done | bytes 432
  6.5 1.7 %shard_map.29 = (bf16[640,256]{1,0:T(8,128)(2,1)S(1)}, bf16[640,512]{1,0:T(8,128)(2,1)S(1)}, bf16[64,144]{1,0:T(8,128)(2,1)S(1)}, bf16[64,144]{1,0:T(8,128)(2,1)S(1)}, bf16[64,144]{1,0:T(8,128)(2,1)S(1)}) custom-call(f32[3,2,17]{2,1,0:T(2,128)S(1)} %copy-done.1), custom_call_target="tpu_custom_call" | custom-call | flops 10000000 | bytes 1038744 | tf_op jit(solution)/shard_map/pallas_call | solution.py:586
  8.3 2.0 %collective-permute-done.refs_2_ = f32[504,128]{1,0:T(8,128)S(1)} collective-permute-done((f32[504,128]{1,0:T(8,128)S(1)}, f32[504,128]{1,0:T(8,128)S(1)}, u32[]{:S(2)}, u32[]{:S(2)}) %collective-permute-start) | collective-permute-done | bytes 258080 | tf_op jit(solution)/shard_map/ppermute | solution.py:64
  10.4 1.2 %collective-permute-start.3 = (f32[240,128]{1,0:T(8,128)S(1)}, f32[240,128]{1,0:T(8,128)S(1)}, u32[]{:S(2)}, u32[]{:S(2)}) collective-permute-start(f32[240,128]{1,0:T(8,128)S(1)} %get-tuple-element.30), channel_id=1, source_target_pairs={{0,2},{2,4},{4,6},{6,14},{14,12},{12,10},{10,8},{8,0},{16,18},{18,... | collective-permute-start | bytes 368648 | tf_op jit(solution)/shard_map/ppermute | solution.py:64
  11.6 0.2 collective-permute-start.4
  11.9 2.2 %collective-permute-start.5 = (f32[136,128]{1,0:T(8,128)S(1)}, f32[136,128]{1,0:T(8,128)S(1)}, u32[]{:S(2)}, u32[]{:S(2)}) collective-permute-start(f32[136,128]{1,0:T(8,128)S(1)} %get-tuple-element.32), channel_id=1, source_target_pairs={{0,4},{2,6},{4,0},{6,2},{1,5},{3,7},{5,1},{7,3},{8,12},{10,14},{12... | collective-permute-start | bytes 208904 | tf_op jit(solution)/shard_map/ppermute | solution.py:64
  14.1 0.0 collective-permute-done.1.refs_3_
  14.1 0.0 collective-permute-done.2.refs_4_
  14.1 1.9 %collective-permute-done.5.refs_7_ = f32[136,128]{1,0:T(8,128)S(1)} collective-permute-done((f32[136,128]{1,0:T(8,128)S(1)}, f32[136,128]{1,0:T(8,128)S(1)}, u32[]{:S(2)}, u32[]{:S(2)}) %collective-permute-start.5) | collective-permute-done | bytes 69664 | tf_op jit(solution)/shard_map/ppermute | solution.py:64
  16.0 0.0 collective-permute-done.3.refs_5_
  16.0 0.0 collective-permute-done.4.refs_6_
  16.0 1.1 %shard_map.31 = (f32[40,48,128]{2,1,0:T(8,128)S(1)}, f32[27,48,128]{2,1,0:T(8,128)S(1)}, f32[32,1920]{1,0:T(8,128)S(1)}, f32[32,1920]{1,0:T(8,128)S(1)}) custom-call(f32[32,32,128]{2,1,0:T(8,128)S(1)} %get-tuple-element.24.refs_0_, f32[19,24,128]{2,1,0:T(8,128)S(1)} %get-tuple-element.25.refs_1_, f32[504,128]{1,0:T(8,128)S(1)} %collective-permute-done.refs_2_, ...), custom_call_target="tpu_custom_call" | custom-call | flops 10000000 | bytes 3985408 | tf_op jit(solution)/shard_map/pallas_call | solution.py:586
  17.1 5.2 %collective-permute-start.6 = (f32[32,1920]{1,0:T(8,128)S(1)}, f32[32,1920]{1,0:T(8,128)S(1)}, u32[]{:S(2)}, u32[]{:S(2)}) collective-permute-start(f32[32,1920]{1,0:T(8,128)S(1)} %get-tuple-element.39), channel_id=1, source_target_pairs={{0,8},{8,16},{16,24},{24,25},{25,17},{17,9},{9,1},{1,0},{2,10},{10... | collective-permute-start | bytes 737288 | tf_op jit(solution)/shard_map/ppermute | solution.py:64
  22.3 0.0 collective-permute-start.7
  22.3 1.4 %shard_map.32 = (f32[1920,256]{1,0:T(8,128)S(1)}, f32[1296,512]{1,0:T(8,128)S(1)}) custom-call(f32[40,48,128]{2,1,0:T(8,128)S(1)} %get-tuple-element.33.refs_0_, f32[27,48,128]{2,1,0:T(8,128)S(1)} %get-tuple-element.34.refs_1_, bf16[640,256]{1,0:T(8,128)(2,1)S(1)} %get-tuple-element.35.refs_2_.refs_5_, bf16[640,512]{1,0:T(8,128)(2,1)S(1)} %get-tuple-element.36.refs_3_.refs_6_), custom_call_target="tpu_custom_call" | custom-call | flops 10000000 | bytes 7249920 | tf_op jit(solution)/shard_map/pallas_call | solution.py:586
  23.7 1.7 %collective-permute-done.6.refs_3_ = f32[32,1920]{1,0:T(8,128)S(1)} collective-permute-done((f32[32,1920]{1,0:T(8,128)S(1)}, f32[32,1920]{1,0:T(8,128)S(1)}, u32[]{:S(2)}, u32[]{:S(2)}) %collective-permute-start.6) | collective-permute-done | bytes 245792 | tf_op jit(solution)/shard_map/ppermute | solution.py:64
  25.4 2.5 %collective-permute-done.7.refs_4_ = f32[32,1920]{1,0:T(8,128)S(1)} collective-permute-done((f32[32,1920]{1,0:T(8,128)S(1)}, f32[32,1920]{1,0:T(8,128)S(1)}, u32[]{:S(2)}, u32[]{:S(2)}) %collective-permute-start.7) | collective-permute-done | bytes 245792 | tf_op jit(solution)/shard_map/ppermute | solution.py:64
  27.9 7.5 %shard_map.33 = f32[32,32,128]{2,1,0:T(8,128)} custom-call(f32[3,2,17]{2,1,0:T(2,128)S(1)} %copy-done.1, f32[1920,256]{1,0:T(8,128)S(1)} %get-tuple-element.37.refs_1_, f32[1296,512]{1,0:T(8,128)S(1)} %get-tuple-element.38.refs_2_, f32[32,1920]{1,0:T(8,128)S(1)} %collective-permute-done.6.refs_3_, f32[32,1920]{1,0:T(8,128)S(1)} %collective-permute-done.7.refs_4_, ...), custom_call_target="tpu_custom_call" | custom-call | flops 10000000 | bytes 6674840 | tf_op jit(solution)/shard_map/pallas_call | solution.py:586
  (1 shorter events, 0.0 us)
Async XLA Ops:
  0.0 1.0 %copy-start = (f32[32,32,128]{2,1,0:T(8,128)S(1)}, f32[32,32,128]{2,1,0:T(8,128)}, u32[]{:S(2)}) copy-start(f32[32,32,128]{2,1,0:T(8,128)} %refs_0_.3) | copy-start | bytes 1572868
  2.3 8.1 %collective-permute-start = (f32[504,128]{1,0:T(8,128)S(1)}, f32[504,128]{1,0:T(8,128)S(1)}, u32[]{:S(2)}, u32[]{:S(2)}) collective-permute-start(f32[504,128]{1,0:T(8,128)S(1)} %get-tuple-element.26), channel_id=1, source_target_pairs={{0,1},{1,0},{2,3},{3,2},{4,5},{5,4},{6,7},{7,6},{8,9},{9,8},{10,11... | collective-permute-start | bytes 774152 | tf_op jit(solution)/shard_map/ppermute | solution.py:64
  4.4 9.7 %collective-permute-start.1 = (f32[504,128]{1,0:T(8,128)S(1)}, f32[504,128]{1,0:T(8,128)S(1)}, u32[]{:S(2)}, u32[]{:S(2)}) collective-permute-start(f32[504,128]{1,0:T(8,128)S(1)} %get-tuple-element.27), channel_id=1, source_target_pairs={{0,2},{2,4},{4,6},{6,14},{14,12},{12,10},{10,8},{8,0},{16,18},{18,... | collective-permute-start | bytes 774152 | tf_op jit(solution)/shard_map/ppermute | solution.py:64
  5.3 8.7 %collective-permute-start.2 = (f32[504,128]{1,0:T(8,128)S(1)}, f32[504,128]{1,0:T(8,128)S(1)}, u32[]{:S(2)}, u32[]{:S(2)}) collective-permute-start(f32[504,128]{1,0:T(8,128)S(1)} %get-tuple-element.28), channel_id=1, source_target_pairs={{2,0},{4,2},{6,4},{14,6},{12,14},{10,12},{8,10},{0,8},{18,16},{20,... | collective-permute-start | bytes 774152 | tf_op jit(solution)/shard_map/ppermute | solution.py:64
  5.8 0.7 %copy-start.1 = (f32[3,2,17]{2,1,0:T(2,128)S(1)}, f32[3,2,17]{2,1,0:T(2,128)}, u32[]{:S(2)}) copy-start(f32[3,2,17]{2,1,0:T(2,128)} %refs_0_.5) | copy-start | bytes 1228
  10.4 5.6 %collective-permute-start.3 = (f32[240,128]{1,0:T(8,128)S(1)}, f32[240,128]{1,0:T(8,128)S(1)}, u32[]{:S(2)}, u32[]{:S(2)}) collective-permute-start(f32[240,128]{1,0:T(8,128)S(1)} %get-tuple-element.30), channel_id=1, source_target_pairs={{0,2},{2,4},{4,6},{6,14},{14,12},{12,10},{10,8},{8,0},{16,18},{18,... | collective-permute-start | bytes 368648 | tf_op jit(solution)/shard_map/ppermute | solution.py:64
  11.6 4.4 %collective-permute-start.4 = (f32[240,128]{1,0:T(8,128)S(1)}, f32[240,128]{1,0:T(8,128)S(1)}, u32[]{:S(2)}, u32[]{:S(2)}) collective-permute-start(f32[240,128]{1,0:T(8,128)S(1)} %get-tuple-element.31), channel_id=1, source_target_pairs={{2,0},{4,2},{6,4},{14,6},{12,14},{10,12},{8,10},{0,8},{18,16},{20,... | collective-permute-start | bytes 368648 | tf_op jit(solution)/shard_map/ppermute | solution.py:64
  11.9 4.1 %collective-permute-start.5 = (f32[136,128]{1,0:T(8,128)S(1)}, f32[136,128]{1,0:T(8,128)S(1)}, u32[]{:S(2)}, u32[]{:S(2)}) collective-permute-start(f32[136,128]{1,0:T(8,128)S(1)} %get-tuple-element.32), channel_id=1, source_target_pairs={{0,4},{2,6},{4,0},{6,2},{1,5},{3,7},{5,1},{7,3},{8,12},{10,14},{12... | collective-permute-start | bytes 208904 | tf_op jit(solution)/shard_map/ppermute | solution.py:64
  17.1 8.4 %collective-permute-start.6 = (f32[32,1920]{1,0:T(8,128)S(1)}, f32[32,1920]{1,0:T(8,128)S(1)}, u32[]{:S(2)}, u32[]{:S(2)}) collective-permute-start(f32[32,1920]{1,0:T(8,128)S(1)} %get-tuple-element.39), channel_id=1, source_target_pairs={{0,8},{8,16},{16,24},{24,25},{25,17},{17,9},{9,1},{1,0},{2,10},{10... | collective-permute-start | bytes 737288 | tf_op jit(solution)/shard_map/ppermute | solution.py:64
  22.3 5.6 %collective-permute-start.7 = (f32[32,1920]{1,0:T(8,128)S(1)}, f32[32,1920]{1,0:T(8,128)S(1)}, u32[]{:S(2)}, u32[]{:S(2)}) collective-permute-start(f32[32,1920]{1,0:T(8,128)S(1)} %get-tuple-element.40), channel_id=1, source_target_pairs={{8,0},{16,8},{24,16},{25,24},{17,25},{9,17},{1,9},{0,1},{10,2},{18... | collective-permute-start | bytes 737288 | tf_op jit(solution)/shard_map/ppermute | solution.py:64

commit v4 on v3

--- a/solution.py
+++ b/solution.py
@@ -137,21 +137,24 @@
         self.y_rows = up8(self.y_fine + SPAN * z.mid_all)
         self.slab_fine = RADIUS * RADIUS * len(self.z_routes)
         self.slab_rows = up8(self.slab_fine + SPAN * self.slab_planes)
-        self.far_rows = up8(y.second * (z.coarse_all + self.slab_planes))
+        self.far_groups = x.fine // x.coarse_all
+        self.far_planes = -(-(z.coarse_all + self.slab_planes) // self.far_groups)
+        self.far_rows = up8(y.second * self.far_planes)
         self.fine_rows = y.fine + 2 * RADIUS
         self.far = y.coarse_all
         self.low = y.mid_all
         self.high = self.low + SPAN
         self.sum_rows = -(-(self.high + SPAN) // 16) * 16
-        self.x_sends = RADIUS + EDGE + SPAN
-        cells = max(self.fine_planes * self.fine_rows, self.sum_planes * self.sum_rows)
-        self.x_cells = -(-cells // 128) * 128
-        assert x.mid_all + x.coarse_all <= x.fine and self.x_sends <= 32
+        self.edge_sums = EDGE + SPAN
+        self.fine_blocks = -(-self.fine_planes * self.fine_rows // 128)
+        self.sum_blocks = -(-self.sum_planes * self.sum_rows // 128)
+        self.x_rows = self.fine_blocks * RADIUS + self.sum_blocks * self.edge_sums
+        assert x.mid_all + x.coarse_all <= x.fine
         assert self.far + y.second <= self.low
         assert z.coarse >= RADIUS and y.coarse >= RADIUS and y.count == 4
 
 
-def restrict_kernel(s, nz, charges, held, own, ahead, behind, *rest):
+def restrict_kernel(s, nz, source, charges, own, ahead, behind, *rest):
     messages, (wide, mid, high, coarse) = rest[:-4], rest[-4:]
     z, y, x = s.z, s.y, s.x
     lanes = (x.fine, x.fine)
@@ -162,10 +165,10 @@
     inside = (lane >= x.mid_all) & (lane < x.mid_all + x.coarse_all) & x.holds_coarse(c)
     to_coarse = jnp.where(inside, weight_of(cell - 1 - 2 * c), 0.0)
     narrow = to_mid + jnp.dot(to_mid, to_coarse, precision=EXACT, preferred_element_type=F32)
-    grid = charges[...]
-    held[...] = grid
-    reduced = jnp.dot(grid.reshape(z.fine * y.fine, x.fine), narrow, precision=EXACT, preferred_element_type=F32)
     wide[...] = jnp.zeros(wide.shape, F32)
+    charges[...] = source[...]
+    cells = source[...].reshape(z.fine * y.fine, x.fine)
+    reduced = jnp.dot(cells, narrow, precision=EXACT, preferred_element_type=F32)
     wide[:, 8 : 8 + y.fine, :] = reduced.reshape(z.fine, y.fine, x.fine)
     rows = 0.0
     for offset, weight in WEIGHTS:
@@ -238,7 +241,7 @@
 
 def spread_kernel(s, nz, nz2, _, own, *rest):
     z_messages, z2_messages = rest[:nz], rest[nz : nz + nz2]
-    ahead, behind, far = rest[-3:]
+    ahead, behind, far, rows = rest[-4:]
     z, y, x = s.z, s.y, s.x
     is_mid = iota((SPAN, x.fine), 1) < x.mid_all
     planes = slabs(s, z_messages, z2_messages)
@@ -259,21 +262,25 @@
             message[at:] = jnp.zeros((s.slab_rows - at, x.fine), F32)
     up = s.y2_routes[0].up()
     count, end = y.second, y.coarse_all
-    at = 0
-    for p in range(z.coarse_all):
-        far[at : at + count] = jnp.where(up, own[p, end - count : end], own[p, :count])
-        at += count
-    for held, first in planes:
-        far[at : at + count] = jnp.where(up, held[first + end - count : first + end], held[first : first + count])
-        at += count
-    if at < s.far_rows:
-        far[at:] = jnp.zeros((s.far_rows - at, x.fine), F32)
+    rows[...] = jnp.zeros(rows.shape, F32)
+    sources = [(own.at[p], 0) for p in range(z.coarse_all)] + planes
+    for p, (held, first) in enumerate(sources):
+        g, at = p // s.far_planes, p % s.far_planes * count
+        last = held[first + end - count : first + end]
+        rows[g, at : at + count] = jnp.where(up, last, held[first : first + count])
+    lane = iota(far.shape, 1)
+    total = jnp.zeros(far.shape, F32)
+    for g in range(s.far_groups):
+        start = g * x.coarse_all
+        turned = pltpu.roll(rows[g], (start - x.mid_all) % x.fine, 1)
+        total = jnp.where((lane >= start) & (lane < start + x.coarse_all), turned, total)
+    far[...] = total
 
 
 def collect_kernel(s, nz, nz2, charges, own, *rest):
     z_messages, z2_messages = rest[:nz], rest[nz : nz + nz2]
     pairs = rest[nz + nz2 : nz + nz2 + 4]
-    far, fine, sums, first, second, raw = rest[nz + nz2 + 4 :]
+    far, fine, sums, first, second, raw, rows = rest[nz + nz2 + 4 :]
     z, y, x = s.z, s.y, s.x
     below = s.y_routes[0].below()
     planes = slabs(s, z_messages, z2_messages)
@@ -296,23 +303,25 @@
         at += RADIUS
     sums[...] = jnp.zeros(sums.shape, F32)
     raw[...] = jnp.zeros(raw.shape, F32)
+    for g in range(s.far_groups):
+        rows[g] = pltpu.roll(far[...], (x.mid_all - g * x.coarse_all) % x.fine, 1)
     is_mid = iota((y.second, x.fine), 1) < x.mid_all
 
-    def rows_of_plane(out, p, body, which, row, far_row):
+    def rows_of_plane(out, p, body, which, row, far_plane):
         low, high = sides(which, row, SPAN)
         out[p, : y.mid_all] = body
         out[p, s.low : s.low + SPAN] = low
         out[p, s.high : s.high + SPAN] = high
-        if far_row is not None:
+        if far_plane is not None:
             at = slice(s.far, s.far + y.second)
-            out[p, at] = jnp.where(is_mid, out[p, at], far[far_row : far_row + y.second])
+            start = far_plane % s.far_planes * y.second
+            out[p, at] = jnp.where(is_mid, out[p, at], rows[far_plane // s.far_planes, start : start + y.second])
 
     for p in range(z.mid_all):
-        far_row = p * y.second if p < z.coarse_all else None
-        rows_of_plane(sums, p, own[p, : y.mid_all], 0, s.y_fine + p * SPAN, far_row)
+        far_plane = p if p < z.coarse_all else None
+        rows_of_plane(sums, p, own[p, : y.mid_all], 0, s.y_fine + p * SPAN, far_plane)
     for p, (held, at) in enumerate(planes):
-        far_row = (z.coarse_all + p) * y.second
-        rows_of_plane(raw, p, held[at : at + y.mid_all], 1, s.slab_fine + p * SPAN, far_row)
+        rows_of_plane(raw, p, held[at : at + y.mid_all], 1, s.slab_fine + p * SPAN, z.coarse_all + p)
     is_mid = iota((s.sum_rows, x.fine), 1) < x.mid_all
 
     def number(condition, a, b):
@@ -352,15 +361,18 @@
     from_coarse = slot - EDGE + jnp.where(goes_up, x.mid_all + x.coarse_all - SPAN, x.mid_all)
     wanted = jnp.where(slot < EDGE, from_mid, from_coarse)
     picked_sums = pick((lane == wanted).astype(BF16), sums[...].reshape(s.sum_planes * s.sum_rows, x.fine))
+    spare = s.sum_blocks * 128 - picked_sums.shape[1]
+    if spare:
+        picked_sums = jnp.concatenate([picked_sums, jnp.zeros((2 * width, spare), F32)], axis=1)
+    spare = s.fine_blocks * 128 - picked.shape[1]
+    if spare:
+        picked = jnp.concatenate([picked, jnp.zeros((2 * RADIUS, spare), F32)], axis=1)
     for n, message in enumerate((first, second)):
-        cells = s.fine_planes * s.fine_rows
-        message[:RADIUS, :cells] = picked[n * RADIUS : (n + 1) * RADIUS]
-        if cells < s.x_cells:
-            message[:RADIUS, cells:] = jnp.zeros((RADIUS, s.x_cells - cells), F32)
-        cells = s.sum_planes * s.sum_rows
-        message[RADIUS:, :cells] = picked_sums[n * width : (n + 1) * width]
-        if cells < s.x_cells:
-            message[RADIUS:, cells:] = jnp.zeros((width, s.x_cells - cells), F32)
+        for b in range(s.fine_blocks):
+            message[b * RADIUS : (b + 1) * RADIUS] = picked[n * RADIUS : (n + 1) * RADIUS, b * 128 : (b + 1) * 128]
+        for b in range(s.sum_blocks):
+            at = s.fine_blocks * RADIUS + b * width
+            message[at : at + width] = picked_sums[n * width : (n + 1) * width, b * 128 : (b + 1) * 128]
 
 
 def band(taps, level, offset, valid):
@@ -378,49 +390,50 @@
 
 def operator_kernel(s, taps, x_fine, x_sums, y_fine, y_mid, y_coarse):
     y, x = s.y, s.x
-    own, edge = x.fine, 2 * 32
+    own, edge = x.fine, 64
     shape = (own + edge, x.fine)
     row, lane = iota(shape, 0), iota(shape, 1)
     t = row - own
     lower, higher = x.index() > 0, x.index() < x.count - 1
     is_own = row < own
-    is_low = ~is_own & (t < 32)
-    q = jnp.where(is_low, t, t - 32)
-    side = choose(is_low, lower, higher)
-
-    def place(own_place, own_valid, first, count, low_place, high_place):
-        r = q - first
-        there = (r >= 0) & (r < count) & side
+
+    def place(half, own_place, own_valid, first, count, low_place, high_place):
+        is_low = t < half
+        r = jnp.where(is_low, t, t - half) - first
+        there = (r >= 0) & (r < count) & (t < 2 * half) & choose(is_low, lower, higher)
         valid = choose(is_own, own_valid, there)
         return jnp.where(is_own, own_place, jnp.where(is_low, low_place + r, high_place + r)), valid
 
-    where, valid = place(row, row >= 0, 0, RADIUS, -RADIUS, x.fine)
+    half = s.edge_sums
+    where, valid = place(RADIUS, row, row >= 0, 0, RADIUS, -RADIUS, x.fine)
     fine = band(taps, 0, where - lane, valid)
-    where, valid = place(row - 1, row < x.mid_all, RADIUS, EDGE, 2 - EDGE, x.mid - 1)
+    where, valid = place(half, row - 1, row < x.mid_all, 0, EDGE, 2 - EDGE, x.mid - 1)
     mid = band(taps, 1, where - (lane - 1), valid & (lane < x.mid_all))
     first = x.mid_all
-    where, valid = place(
-        row - first - 2, (row >= first) & (row < first + x.coarse_all), RADIUS + EDGE, SPAN, 3 - SPAN, x.coarse - 2
-    )
+    inside = (row >= first) & (row < first + x.coarse_all)
+    where, valid = place(half, row - first - 2, inside, EDGE, SPAN, 3 - SPAN, x.coarse - 2)
     coarse = band(taps, 2, where - (lane - 2), valid & (lane < x.coarse_all))
     a, b = iota((x.fine, x.fine), 0), iota((x.fine, x.fine), 1)
     from_mid = jnp.where((a < x.mid_all) & x.holds_mid(a - 1), weight_of(b - 2 * (a - 1)), 0.0)
     from_coarse = jnp.where((a < x.coarse_all) & x.holds_coarse(a - 2), weight_of(b - 1 - 2 * (a - 2)), 0.0)
     from_coarse = dot(from_coarse, from_mid)
-    columns = [(x_fine, 0, fine)]
-    columns += [(x_sums, 0, [dot(m, from_mid) for m in mid])]
-    columns += [(x_sums, TERMS * x.fine, [dot(c, from_coarse) for c in coarse])]
-    for out, at, terms in columns:
+    columns = [(x_fine, RADIUS, 0, fine)]
+    columns += [(x_sums, half, 0, [dot(m, from_mid) for m in mid])]
+    columns += [(x_sums, half, TERMS * x.fine, [dot(c, from_coarse) for c in coarse])]
+    for out, half, at, terms in columns:
         for term, matrix in enumerate(terms):
             high, low = split(matrix)
             cols = slice(at + term * x.fine, at + (term + 1) * x.fine)
+            n = 2 * half
+            ends = high[own : own + n]
             out[0:own, cols] = high[:own]
             out[own : 2 * own, cols] = high[:own]
             out[2 * own : 3 * own, cols] = low[:own]
-            out[3 * own : 3 * own + edge, cols] = high[own:]
-            out[3 * own + edge : 3 * own + 2 * edge, cols] = high[own:]
-            out[3 * own + 2 * edge : 3 * own + 3 * edge, cols] = low[own:]
-            out[3 * own + 3 * edge :, cols] = jnp.zeros((edge, x.fine), BF16)
+            out[3 * own :, cols] = jnp.zeros((out.shape[0] - 3 * own, x.fine), BF16)
+            last = 2 * n if 3 * n <= 128 else 128
+            out[3 * own : 3 * own + n, cols] = ends
+            out[3 * own + n : 3 * own + 2 * n, cols] = ends
+            out[3 * own + last : 3 * own + last + n, cols] = low[own : own + n]
 
     lower, higher = y.index() > 0, y.index() < y.count - 1
     far_below = s.y2_routes[0].below()
@@ -478,19 +491,30 @@
 
 
 def sum_kernel(s, taps, fine, sums, first, second, x_fine, x_sums, y_fine, y_mid, y_coarse, out, *scratch):
-    turned, t_fine, t_mid, t_coarse, p_mid, p_coarse = scratch
+    fine_ends, sums_ends, t_fine, t_mid, t_coarse, p_mid, p_coarse = scratch
     z, y, x = s.z, s.y, s.x
     below = s.x_routes[0].below()
-    low = jnp.where(below, first[...], second[...])
-    high = jnp.where(below, second[...], first[...])
-    turned[...] = jnp.concatenate([low, high, low, high], axis=0).T
-
-    def along_x(held, start, rows, weights):
-        edge = turned[start : start + rows]
+    for out_ends, blocks, start, half in (
+        (fine_ends, s.fine_blocks, 0, RADIUS),
+        (sums_ends, s.sum_blocks, s.fine_blocks * RADIUS, s.edge_sums),
+    ):
+        copies = 128 // (2 * half)
+        copies = min(copies, 3)
+        for b in range(blocks):
+            at = slice(start + b * half, start + (b + 1) * half)
+            one, two = first[at], second[at]
+            rows = [jnp.where(below, one, two), jnp.where(below, two, one)] * copies
+            rows.append(jnp.zeros((128 - 2 * half * copies, 128), F32))
+            out_ends[b * 128 : (b + 1) * 128] = jnp.concatenate(rows, axis=0).T
+
+    def along_x(held, ends, half, start, rows, weights):
+        edge = ends[start : start + rows]
         edge_high, edge_low = split(edge)
-        lane = iota(edge.shape, 1) < 64
-        packed = jnp.where(lane, edge_high.astype(F32), edge_low.astype(F32)).astype(BF16)
-        joined = jnp.concatenate([packed, edge_high], axis=1)
+        lane = iota(edge.shape, 1)
+        is_low = (lane >= 2 * half) & (lane < 4 * half)
+        joined = jnp.where(is_low, edge_low.astype(F32), edge_high.astype(F32)).astype(BF16)
+        if 6 * half > 128:
+            joined = jnp.concatenate([joined, edge_high], axis=1)
         part = jnp.dot(joined, weights[3 * x.fine :], preferred_element_type=F32)
         return split(held[start : start + rows] + part)
 
@@ -521,11 +545,9 @@
         mid_at += [(start + p, valid) for p in range(RADIUS)]
     for start, valid in starts(0, z.coarse + 5 + RADIUS):
         coarse_at += [(start + p, valid) for p in range(RADIUS)]
-    group = 4
-    for g in range(0, s.sum_planes, group):
+    def sum_group(g, count):
         n = s.sum_rows
-        count = min(group, s.sum_planes - g)
-        a, b = along_x(sums, g * n, count * n, x_sums)
+        a, b = along_x(sums, sums_ends, s.edge_sums, g * n, count * n, x_sums)
         for p in range(count):
             rows = slice(p * n, (p + 1) * n)
             for which, (held, weights) in enumerate(((t_mid, y_mid), (t_coarse, y_coarse))):
@@ -534,14 +556,14 @@
                     cols = slice(which * TERMS * x.fine, (which + 1) * TERMS * x.fine)
                     store(held, at, valid, along_y(a[rows, cols], b[rows, cols], weights))
 
-    group = 8
     fine_at = [(RADIUS + p, None) for p in range(z.fine)]
     for start, valid in starts(0, z.fine + RADIUS):
         fine_at += [(start + p, valid) for p in range(RADIUS)]
-    for g in range(0, s.fine_planes, group):
+
+    def fine_group(g, count):
         n = s.fine_rows
-        a, b = along_x(fine, g * n, group * n, x_fine)
-        for p in range(group):
+        a, b = along_x(fine, fine_ends, RADIUS, g * n, count * n, x_fine)
+        for p in range(count):
             rows = slice(p * n, (p + 1) * n)
             store(t_fine, *fine_at[g + p], along_y(a[rows], b[rows], y_fine))
 
@@ -556,11 +578,13 @@
         return totals
 
     block = 4
-    for k in range(0, z.coarse_all, block):
+
+    def coarse_block(k):
         count = min(block, z.coarse_all - k)
         for i, total in enumerate(along_z(t_coarse, 2, k, count)):
             p_coarse[k + i] = jnp.where(z.holds_coarse(k + i - 2), total, 0.0)
-    for k in range(0, z.mid_all, block):
+
+    def mid_block(k):
         count = min(block, z.mid_all - k)
         for i, total in enumerate(along_z(t_mid, 1, k, count)):
             m = k + i - 1
@@ -569,15 +593,30 @@
                     total = total + weight * p_coarse[(m - offset) // 2 + 2]
             p_mid[k + i] = jnp.where(z.holds_mid(m), total, 0.0)
 
-    def step(b, carry):
-        for i, total in enumerate(along_z(t_fine, 0, b * block, block)):
+    def fine_block(k):
+        for i, total in enumerate(along_z(t_fine, 0, k, block)):
             for offset, weight in WEIGHTS:
                 if (i - offset) % 2 == 0:
-                    total = total + weight * p_mid[b * (block // 2) + (i - offset) // 2 + 1]
-            out[b * block + i] = total
-        return carry
-
-    lax.fori_loop(0, z.fine // block, step, 0)
+                    total = total + weight * p_mid[k // 2 + (i - offset) // 2 + 1]
+            out[k + i] = total
+
+    for g in range(0, s.sum_planes, 4):
+        sum_group(g, min(4, s.sum_planes - g))
+    later = [lambda k=k: coarse_block(k) for k in range(0, z.coarse_all, block)]
+    later += [lambda k=k: mid_block(k) for k in range(0, z.mid_all, block)]
+    groups = list(range(z.fine, s.fine_planes, 8)) + list(range(0, z.fine, 8))
+    done = 0
+    for n, g in enumerate(groups):
+        fine_group(g, 8)
+        for _ in range(3):
+            if later:
+                later.pop(0)()
+        if g < z.fine:
+            ready = g if g + 8 < z.fine else z.fine
+            later += [lambda k=k: fine_block(k) for k in range(done, ready, block)]
+            done = max(done, ready)
+    while later:
+        later.pop(0)()
 
 
 def call(kernel, outs, ins, scratch=(), flops=10**7):
@@ -624,8 +663,8 @@
     operators = call(
         bound(operator_kernel),
         [
-            array(5 * n, TERMS * n, dtype=BF16),
-            array(5 * n, 2 * TERMS * n, dtype=BF16),
+            array(3 * n + 128, TERMS * n, dtype=BF16),
+            array(3 * n + 256, 2 * TERMS * n, dtype=BF16),
             array(TERMS * y.fine, 3 * s.fine_rows, dtype=BF16),
             array(TERMS * y.fine, 3 * s.sum_rows, dtype=BF16),
             array(TERMS * y.fine, 3 * s.sum_rows, dtype=BF16),
@@ -636,6 +675,7 @@
         bound(spread_kernel, nz, nz2),
         [array(s.slab_rows, n), array(s.slab_rows, n), array(s.far_rows, n)],
         [operators[-1], own, *z_got],
+        [pltpu.VMEM((s.far_groups, s.far_rows, n), F32)],
     )
     sides += [s.y_routes[0](ahead), s.y_routes[1](behind)]
     far = s.y2_routes[0](far)
@@ -644,11 +684,11 @@
         [
             array(s.fine_planes, s.fine_rows, n),
             array(s.sum_planes, s.sum_rows, n),
-            array(s.x_sends, s.x_cells),
-            array(s.x_sends, s.x_cells),
+            array(s.x_rows, n),
+            array(s.x_rows, n),
         ],
         [held, own, *z_got, *sides, far],
-        [pltpu.VMEM((s.slab_planes, s.sum_rows, n), F32)],
+        [pltpu.VMEM((s.slab_planes, s.sum_rows, n), F32), pltpu.VMEM((s.far_groups, s.far_rows, n), F32)],
     )
     first, second = s.x_routes[0](first), s.x_routes[1](second)
     fine, sums = call(
@@ -661,7 +701,8 @@
         [array(z.fine, y.fine, n)],
         [kernel_taps, fine, sums, first, second, *operators],
         [
-            pltpu.VMEM((s.x_cells, n), F32),
+            pltpu.VMEM((s.fine_blocks * 128, n), F32),
+            pltpu.VMEM((s.sum_blocks * 128, n), F32),
             pltpu.VMEM((z.fine + 2 * RADIUS, TERMS, y.fine, n), F32),
             pltpu.VMEM((z.mid + 2 * RADIUS + 3, TERMS, y.fine, n), F32),
             pltpu.VMEM((z.coarse + 2 * RADIUS + 5, TERMS, y.fine, n), F32),

time: 35.6 us -> 33.9 us (0.952)
  waiting for transfers between devices: 8.18 us -> 7.13 us
  Pallas kernels: 13 us -> 12.3 us
    ppermute x8, waiting for transfers between devices: 8.18 us -> 7.13 us  [__call__(): return lax.ppermute(x, self.names, self.pairs)]
    pallas_call x6, Pallas kernels: 13 us -> 12.3 us  [call(): pl.pallas_call(kernel, out_shape=tuple(outs), in_specs=specs, out_specs=t...]
  transfers between devices with their start and end apart: 8 -> 8, of which waited for: 4 -> 4; matrix products, arithmetic and copies ran while one was open for 0% -> 0% of each run, Pallas kernels for 9% -> 10%
where the time goes in v4:
time: 33.9 us; the launch traced here: 33.8 us
  starting transfers between devices  12.6 us (37%)
  Pallas kernels  12.3 us (36%)
  waiting for transfers between devices  7.13 us (21%)
  local copies, waits for them, and re-layouts  1.72 us (5%)
    ppermute x8, starting transfers between devices, __call__(): return lax.ppermute(x, self.names, self.pairs)  12.6 us
    pallas_call x6, Pallas kernels, call(): pl.pallas_call(kernel, out_shape=tuple(outs), in_specs=specs, out_specs=t...  12.3 us
    ppermute x8, waiting for transfers between devices, __call__(): return lax.ppermute(x, self.names, self.pairs)  7.13 us
    unnamed x4, local copies, waits for them, and re-layouts  1.72 us
  transfers between devices with their start and end apart: 8, of which 4 were waited for; matrix products, arithmetic and copies ran while one was open for 0% of the time, Pallas kernels for 10%

profile of v4, /device:TPU:1, one launch (start us, length us, event | category | flops | bytes accessed | tf_op | source)
XLA Modules:
  0.0 33.8 jit_solution(15292284339807076606)
XLA Ops:
  0.0 0.0 copy-start
  0.0 1.0 %copy-done = f32[32,32,128]{2,1,0:T(8,128)S(1)} copy-done((f32[32,32,128]{2,1,0:T(8,128)S(1)}, f32[32,32,128]{2,1,0:T(8,128)}, u32[]{:S(2)}) %copy-start) | copy-done | bytes 524312
  1.0 1.2 %shard_map.28 = (f32[32,32,128]{2,1,0:T(8,128)S(1)}, f32[19,24,128]{2,1,0:T(8,128)S(1)}, f32[504,128]{1,0:T(8,128)S(1)}, f32[504,128]{1,0:T(8,128)S(1)}, f32[504,128]{1,0:T(8,128)S(1)}) custom-call(f32[32,32,128]{2,1,0:T(8,128)S(1)} %copy-done), custom_call_target="tpu_custom_call" | custom-call | flops 10000000 | bytes 2056192 | tf_op jit(solution)/shard_map/pallas_call | solution.py:625
  2.3 2.1 %collective-permute-start = (f32[504,128]{1,0:T(8,128)S(1)}, f32[504,128]{1,0:T(8,128)S(1)}, u32[]{:S(2)}, u32[]{:S(2)}) collective-permute-start(f32[504,128]{1,0:T(8,128)S(1)} %get-tuple-element.26), channel_id=1, source_target_pairs={{0,1},{1,0},{2,3},{3,2},{4,5},{5,4},{6,7},{7,6},{8,9},{9,8},{10,11... | collective-permute-start | bytes 774152 | tf_op jit(solution)/shard_map/ppermute | solution.py:64
  4.4 1.0 %collective-permute-start.1 = (f32[504,128]{1,0:T(8,128)S(1)}, f32[504,128]{1,0:T(8,128)S(1)}, u32[]{:S(2)}, u32[]{:S(2)}) collective-permute-start(f32[504,128]{1,0:T(8,128)S(1)} %get-tuple-element.27), channel_id=1, source_target_pairs={{0,2},{2,4},{4,6},{6,14},{14,12},{12,10},{10,8},{8,0},{16,18},{18,... | collective-permute-start | bytes 774152 | tf_op jit(solution)/shard_map/ppermute | solution.py:64
  5.4 0.5 %collective-permute-start.2 = (f32[504,128]{1,0:T(8,128)S(1)}, f32[504,128]{1,0:T(8,128)S(1)}, u32[]{:S(2)}, u32[]{:S(2)}) collective-permute-start(f32[504,128]{1,0:T(8,128)S(1)} %get-tuple-element.28), channel_id=1, source_target_pairs={{2,0},{4,2},{6,4},{14,6},{12,14},{10,12},{8,10},{0,8},{18,16},{20,... | collective-permute-start | bytes 774152 | tf_op jit(solution)/shard_map/ppermute | solution.py:64
  5.9 0.0 copy-start.1
  5.9 0.7 %copy-done.1 = f32[3,2,17]{2,1,0:T(2,128)S(1)} copy-done((f32[3,2,17]{2,1,0:T(2,128)S(1)}, f32[3,2,17]{2,1,0:T(2,128)}, u32[]{:S(2)}) %copy-start.1) | copy-done | bytes 432
  6.6 1.7 %shard_map.29 = (bf16[512,256]{1,0:T(8,128)(2,1)S(1)}, bf16[640,512]{1,0:T(8,128)(2,1)S(1)}, bf16[64,144]{1,0:T(8,128)(2,1)S(1)}, bf16[64,144]{1,0:T(8,128)(2,1)S(1)}, bf16[64,144]{1,0:T(8,128)(2,1)S(1)}) custom-call(f32[3,2,17]{2,1,0:T(2,128)S(1)} %copy-done.1), custom_call_target="tpu_custom_call" | custom-call | flops 10000000 | bytes 973208 | tf_op jit(solution)/shard_map/pallas_call | solution.py:625
  8.3 2.1 %collective-permute-done.refs_2_ = f32[504,128]{1,0:T(8,128)S(1)} collective-permute-done((f32[504,128]{1,0:T(8,128)S(1)}, f32[504,128]{1,0:T(8,128)S(1)}, u32[]{:S(2)}, u32[]{:S(2)}) %collective-permute-start) | collective-permute-done | bytes 258080 | tf_op jit(solution)/shard_map/ppermute | solution.py:64
  10.4 0.1 shard_map.30
  10.5 1.2 %collective-permute-start.3 = (f32[240,128]{1,0:T(8,128)S(1)}, f32[240,128]{1,0:T(8,128)S(1)}, u32[]{:S(2)}, u32[]{:S(2)}) collective-permute-start(f32[240,128]{1,0:T(8,128)S(1)} %get-tuple-element.30), channel_id=1, source_target_pairs={{0,2},{2,4},{4,6},{6,14},{14,12},{12,10},{10,8},{8,0},{16,18},{18,... | collective-permute-start | bytes 368648 | tf_op jit(solution)/shard_map/ppermute | solution.py:64
  11.7 0.2 collective-permute-start.4
  12.0 2.2 %collective-permute-start.5 = (f32[48,128]{1,0:T(8,128)S(1)}, f32[48,128]{1,0:T(8,128)S(1)}, u32[]{:S(2)}, u32[]{:S(2)}) collective-permute-start(f32[48,128]{1,0:T(8,128)S(1)} %get-tuple-element.32), channel_id=1, source_target_pairs={{0,4},{2,6},{4,0},{6,2},{1,5},{3,7},{5,1},{7,3},{8,12},{10,14},{12... | collective-permute-start | bytes 73736 | tf_op jit(solution)/shard_map/ppermute | solution.py:64
  14.2 0.0 collective-permute-done.1.refs_3_
  14.2 0.0 collective-permute-done.2.refs_4_
  14.2 1.4 %collective-permute-done.5.refs_7_ = f32[48,128]{1,0:T(8,128)S(1)} collective-permute-done((f32[48,128]{1,0:T(8,128)S(1)}, f32[48,128]{1,0:T(8,128)S(1)}, u32[]{:S(2)}, u32[]{:S(2)}) %collective-permute-start.5) | collective-permute-done | bytes 24608 | tf_op jit(solution)/shard_map/ppermute | solution.py:64
  15.5 0.0 collective-permute-done.3.refs_5_
  15.5 0.0 collective-permute-done.4.refs_6_
  15.5 1.0 %shard_map.31 = (f32[40,48,128]{2,1,0:T(8,128)S(1)}, f32[27,48,128]{2,1,0:T(8,128)S(1)}, f32[384,128]{1,0:T(8,128)S(1)}, f32[384,128]{1,0:T(8,128)S(1)}) custom-call(f32[32,32,128]{2,1,0:T(8,128)S(1)} %get-tuple-element.24.refs_0_, f32[19,24,128]{2,1,0:T(8,128)S(1)} %get-tuple-element.25.refs_1_, f32[504,128]{1,0:T(8,128)S(1)} %collective-permute-done.refs_2_, ...), custom_call_target="tpu_custom_call" | custom-call | flops 10000000 | bytes 3842048 | tf_op jit(solution)/shard_map/pallas_call | solution.py:625
  16.6 5.3 %collective-permute-start.6 = (f32[384,128]{1,0:T(8,128)S(1)}, f32[384,128]{1,0:T(8,128)S(1)}, u32[]{:S(2)}, u32[]{:S(2)}) collective-permute-start(f32[384,128]{1,0:T(8,128)S(1)} %get-tuple-element.39), channel_id=1, source_target_pairs={{0,8},{8,16},{16,24},{24,25},{25,17},{17,9},{9,1},{1,0},{2,10},{10... | collective-permute-start | bytes 589832 | tf_op jit(solution)/shard_map/ppermute | solution.py:64
  21.9 0.0 collective-permute-start.7
  21.9 1.4 %shard_map.32 = (f32[1920,256]{1,0:T(8,128)S(1)}, f32[1296,512]{1,0:T(8,128)S(1)}) custom-call(f32[40,48,128]{2,1,0:T(8,128)S(1)} %get-tuple-element.33.refs_0_, f32[27,48,128]{2,1,0:T(8,128)S(1)} %get-tuple-element.34.refs_1_, bf16[512,256]{1,0:T(8,128)(2,1)S(1)} %get-tuple-element.35.refs_2_.refs_5_, bf16[640,512]{1,0:T(8,128)(2,1)S(1)} %get-tuple-element.36.refs_3_.refs_6_), custom_call_target="tpu_custom_call" | custom-call | flops 10000000 | bytes 7184384 | tf_op jit(solution)/shard_map/pallas_call | solution.py:625
  23.3 1.2 %collective-permute-done.6.refs_3_ = f32[384,128]{1,0:T(8,128)S(1)} collective-permute-done((f32[384,128]{1,0:T(8,128)S(1)}, f32[384,128]{1,0:T(8,128)S(1)}, u32[]{:S(2)}, u32[]{:S(2)}) %collective-permute-start.6) | collective-permute-done | bytes 196640 | tf_op jit(solution)/shard_map/ppermute | solution.py:64
  24.5 2.5 %collective-permute-done.7.refs_4_ = f32[384,128]{1,0:T(8,128)S(1)} collective-permute-done((f32[384,128]{1,0:T(8,128)S(1)}, f32[384,128]{1,0:T(8,128)S(1)}, u32[]{:S(2)}, u32[]{:S(2)}) %collective-permute-start.7) | collective-permute-done | bytes 196640 | tf_op jit(solution)/shard_map/ppermute | solution.py:64
  27.0 6.8 %shard_map.33 = f32[32,32,128]{2,1,0:T(8,128)} custom-call(f32[3,2,17]{2,1,0:T(2,128)S(1)} %copy-done.1, f32[1920,256]{1,0:T(8,128)S(1)} %get-tuple-element.37.refs_1_, f32[1296,512]{1,0:T(8,128)S(1)} %get-tuple-element.38.refs_2_, f32[384,128]{1,0:T(8,128)S(1)} %collective-permute-done.6.refs_3_, f32[384,128]{1,0:T(8,128)S(1)} %collective-permute-done.7.refs_4_, ...), custom_call_target="tpu_custom_call" | custom-call | flops 10000000 | bytes 6511000 | tf_op jit(solution)/shard_map/pallas_call | solution.py:625
Async XLA Ops:
  0.0 1.0 %copy-start = (f32[32,32,128]{2,1,0:T(8,128)S(1)}, f32[32,32,128]{2,1,0:T(8,128)}, u32[]{:S(2)}) copy-start(f32[32,32,128]{2,1,0:T(8,128)} %refs_0_.3) | copy-start | bytes 1572868
  2.3 8.1 %collective-permute-start = (f32[504,128]{1,0:T(8,128)S(1)}, f32[504,128]{1,0:T(8,128)S(1)}, u32[]{:S(2)}, u32[]{:S(2)}) collective-permute-start(f32[504,128]{1,0:T(8,128)S(1)} %get-tuple-element.26), channel_id=1, source_target_pairs={{0,1},{1,0},{2,3},{3,2},{4,5},{5,4},{6,7},{7,6},{8,9},{9,8},{10,11... | collective-permute-start | bytes 774152 | tf_op jit(solution)/shard_map/ppermute | solution.py:64
  4.4 9.8 %collective-permute-start.1 = (f32[504,128]{1,0:T(8,128)S(1)}, f32[504,128]{1,0:T(8,128)S(1)}, u32[]{:S(2)}, u32[]{:S(2)}) collective-permute-start(f32[504,128]{1,0:T(8,128)S(1)} %get-tuple-element.27), channel_id=1, source_target_pairs={{0,2},{2,4},{4,6},{6,14},{14,12},{12,10},{10,8},{8,0},{16,18},{18,... | collective-permute-start | bytes 774152 | tf_op jit(solution)/shard_map/ppermute | solution.py:64
  5.4 8.8 %collective-permute-start.2 = (f32[504,128]{1,0:T(8,128)S(1)}, f32[504,128]{1,0:T(8,128)S(1)}, u32[]{:S(2)}, u32[]{:S(2)}) collective-permute-start(f32[504,128]{1,0:T(8,128)S(1)} %get-tuple-element.28), channel_id=1, source_target_pairs={{2,0},{4,2},{6,4},{14,6},{12,14},{10,12},{8,10},{0,8},{18,16},{20,... | collective-permute-start | bytes 774152 | tf_op jit(solution)/shard_map/ppermute | solution.py:64
  5.9 0.7 %copy-start.1 = (f32[3,2,17]{2,1,0:T(2,128)S(1)}, f32[3,2,17]{2,1,0:T(2,128)}, u32[]{:S(2)}) copy-start(f32[3,2,17]{2,1,0:T(2,128)} %refs_0_.5) | copy-start | bytes 1228
  10.5 5.1 %collective-permute-start.3 = (f32[240,128]{1,0:T(8,128)S(1)}, f32[240,128]{1,0:T(8,128)S(1)}, u32[]{:S(2)}, u32[]{:S(2)}) collective-permute-start(f32[240,128]{1,0:T(8,128)S(1)} %get-tuple-element.30), channel_id=1, source_target_pairs={{0,2},{2,4},{4,6},{6,14},{14,12},{12,10},{10,8},{8,0},{16,18},{18,... | collective-permute-start | bytes 368648 | tf_op jit(solution)/shard_map/ppermute | solution.py:64
  11.7 3.8 %collective-permute-start.4 = (f32[240,128]{1,0:T(8,128)S(1)}, f32[240,128]{1,0:T(8,128)S(1)}, u32[]{:S(2)}, u32[]{:S(2)}) collective-permute-start(f32[240,128]{1,0:T(8,128)S(1)} %get-tuple-element.31), channel_id=1, source_target_pairs={{2,0},{4,2},{6,4},{14,6},{12,14},{10,12},{8,10},{0,8},{18,16},{20,... | collective-permute-start | bytes 368648 | tf_op jit(solution)/shard_map/ppermute | solution.py:64
  12.0 3.6 %collective-permute-start.5 = (f32[48,128]{1,0:T(8,128)S(1)}, f32[48,128]{1,0:T(8,128)S(1)}, u32[]{:S(2)}, u32[]{:S(2)}) collective-permute-start(f32[48,128]{1,0:T(8,128)S(1)} %get-tuple-element.32), channel_id=1, source_target_pairs={{0,4},{2,6},{4,0},{6,2},{1,5},{3,7},{5,1},{7,3},{8,12},{10,14},{12... | collective-permute-start | bytes 73736 | tf_op jit(solution)/shard_map/ppermute | solution.py:64
  16.6 7.9 %collective-permute-start.6 = (f32[384,128]{1,0:T(8,128)S(1)}, f32[384,128]{1,0:T(8,128)S(1)}, u32[]{:S(2)}, u32[]{:S(2)}) collective-permute-start(f32[384,128]{1,0:T(8,128)S(1)} %get-tuple-element.39), channel_id=1, source_target_pairs={{0,8},{8,16},{16,24},{24,25},{25,17},{17,9},{9,1},{1,0},{2,10},{10... | collective-permute-start | bytes 589832 | tf_op jit(solution)/shard_map/ppermute | solution.py:64
  21.9 5.1 %collective-permute-start.7 = (f32[384,128]{1,0:T(8,128)S(1)}, f32[384,128]{1,0:T(8,128)S(1)}, u32[]{:S(2)}, u32[]{:S(2)}) collective-permute-start(f32[384,128]{1,0:T(8,128)S(1)} %get-tuple-element.40), channel_id=1, source_target_pairs={{8,0},{16,8},{24,16},{25,24},{17,25},{9,17},{1,9},{0,1},{10,2},{18... | collective-permute-start | bytes 589832 | tf_op jit(solution)/shard_map/ppermute | solution.py:64

commit v5 on v4

--- a/solution.py
+++ b/solution.py
@@ -146,9 +146,11 @@
         self.high = self.low + SPAN
         self.sum_rows = -(-(self.high + SPAN) // 16) * 16
         self.edge_sums = EDGE + SPAN
-        self.fine_blocks = -(-self.fine_planes * self.fine_rows // 128)
+        self.side = x.fine // RADIUS
+        self.fine_groups = -(-self.fine_planes // self.side)
+        self.fine_ends = self.fine_groups * self.fine_rows
         self.sum_blocks = -(-self.sum_planes * self.sum_rows // 128)
-        self.x_rows = self.fine_blocks * RADIUS + self.sum_blocks * self.edge_sums
+        self.x_rows = self.fine_ends + self.sum_blocks * self.edge_sums
         assert x.mid_all + x.coarse_all <= x.fine
         assert self.far + y.second <= self.low
         assert z.coarse >= RADIUS and y.coarse >= RADIUS and y.count == 4
@@ -345,13 +347,19 @@
         for p in range(z.second):
             sums[start + p] = sums[start + p] + jnp.where(is_mid, 0.0, raw[base + p])
 
-    row, lane = iota((2 * RADIUS, x.fine), 0), iota((2 * RADIUS, x.fine), 1)
     up = s.x_routes[0].up()
-    is_first = row < RADIUS
-    goes_up = choose(up, is_first, ~is_first)
-    slot = jnp.where(is_first, row, row - RADIUS)
-    wanted = jnp.where(goes_up, x.fine - RADIUS + slot, slot)
-    picked = pick((lane == wanted).astype(BF16), fine[...].reshape(s.fine_planes * s.fine_rows, x.fine))
+    lane = iota((s.fine_rows, x.fine), 1)
+    for g in range(s.fine_groups):
+        ends = [jnp.zeros(lane.shape, F32)] * 2
+        for j in range(min(s.side, s.fine_planes - g * s.side)):
+            plane = fine[g * s.side + j]
+            here = (lane >= RADIUS * j) & (lane < RADIUS * (j + 1))
+            for n, start in enumerate((x.fine - RADIUS, 0)):
+                shift = (RADIUS * j - start) % x.fine
+                ends[n] = jnp.where(here, pltpu.roll(plane, shift, 1) if shift else plane, ends[n])
+        rows = slice(g * s.fine_rows, (g + 1) * s.fine_rows)
+        first[rows] = jnp.where(up, ends[0], ends[1])
+        second[rows] = jnp.where(up, ends[1], ends[0])
     width = EDGE + SPAN
     row, lane = iota((2 * width, x.fine), 0), iota((2 * width, x.fine), 1)
     is_first = row < width
@@ -364,14 +372,9 @@
     spare = s.sum_blocks * 128 - picked_sums.shape[1]
     if spare:
         picked_sums = jnp.concatenate([picked_sums, jnp.zeros((2 * width, spare), F32)], axis=1)
-    spare = s.fine_blocks * 128 - picked.shape[1]
-    if spare:
-        picked = jnp.concatenate([picked, jnp.zeros((2 * RADIUS, spare), F32)], axis=1)
     for n, message in enumerate((first, second)):
-        for b in range(s.fine_blocks):
-            message[b * RADIUS : (b + 1) * RADIUS] = picked[n * RADIUS : (n + 1) * RADIUS, b * 128 : (b + 1) * 128]
         for b in range(s.sum_blocks):
-            at = s.fine_blocks * RADIUS + b * width
+            at = s.fine_ends + b * width
             message[at : at + width] = picked_sums[n * width : (n + 1) * width, b * 128 : (b + 1) * 128]
 
 
@@ -388,7 +391,19 @@
     return jnp.dot(a, b, precision=EXACT, preferred_element_type=F32)
 
 
-def operator_kernel(s, taps, x_fine, x_sums, y_fine, y_mid, y_coarse):
+def z_columns(s):
+    return s.z.fine * RADIUS
+
+
+def lower_x(x):
+    return x.index() > 0
+
+
+def higher_x(x):
+    return x.index() < x.count - 1
+
+
+def operator_kernel(s, taps, x_fine, x_sums, ends, y_fine, y_mid, y_coarse):
     y, x = s.y, s.x
     own, edge = x.fine, 64
     shape = (own + edge, x.fine)
@@ -405,8 +420,7 @@
         return jnp.where(is_own, own_place, jnp.where(is_low, low_place + r, high_place + r)), valid
 
     half = s.edge_sums
-    where, valid = place(RADIUS, row, row >= 0, 0, RADIUS, -RADIUS, x.fine)
-    fine = band(taps, 0, where - lane, valid)
+    fine = band(taps, 0, row - lane, is_own)
     where, valid = place(half, row - 1, row < x.mid_all, 0, EDGE, 2 - EDGE, x.mid - 1)
     mid = band(taps, 1, where - (lane - 1), valid & (lane < x.mid_all))
     first = x.mid_all
@@ -417,7 +431,7 @@
     from_mid = jnp.where((a < x.mid_all) & x.holds_mid(a - 1), weight_of(b - 2 * (a - 1)), 0.0)
     from_coarse = jnp.where((a < x.coarse_all) & x.holds_coarse(a - 2), weight_of(b - 1 - 2 * (a - 2)), 0.0)
     from_coarse = dot(from_coarse, from_mid)
-    columns = [(x_fine, RADIUS, 0, fine)]
+    columns = [(x_fine, 0, 0, fine)]
     columns += [(x_sums, half, 0, [dot(m, from_mid) for m in mid])]
     columns += [(x_sums, half, TERMS * x.fine, [dot(c, from_coarse) for c in coarse])]
     for out, half, at, terms in columns:
@@ -425,15 +439,35 @@
             high, low = split(matrix)
             cols = slice(at + term * x.fine, at + (term + 1) * x.fine)
             n = 2 * half
-            ends = high[own : own + n]
             out[0:own, cols] = high[:own]
             out[own : 2 * own, cols] = high[:own]
             out[2 * own : 3 * own, cols] = low[:own]
-            out[3 * own :, cols] = jnp.zeros((out.shape[0] - 3 * own, x.fine), BF16)
-            last = 2 * n if 3 * n <= 128 else 128
-            out[3 * own : 3 * own + n, cols] = ends
-            out[3 * own + n : 3 * own + 2 * n, cols] = ends
-            out[3 * own + last : 3 * own + last + n, cols] = low[own : own + n]
+            if n:
+                out[3 * own :, cols] = jnp.zeros((out.shape[0] - 3 * own, x.fine), BF16)
+                out[3 * own : 3 * own + n, cols] = high[own : own + n]
+                out[3 * own + n : 3 * own + 2 * n, cols] = high[own : own + n]
+                out[3 * own + 128 : 3 * own + 128 + n, cols] = low[own : own + n]
+
+    z, slots, wide = s.z, s.side * s.fine_groups, z_columns(s)
+    slot, column = iota((slots, wide), 0), iota((slots, wide), 1)
+    where, valid = slot, slot < z.fine
+    for n, route in enumerate(s.z_routes):
+        lower, i, first = route.below(), z.index(), z.fine + n * RADIUS
+        here = (slot >= first) & (slot < first + RADIUS)
+        where = jnp.where(here, slot - first + jnp.where(lower, -RADIUS, z.fine), where)
+        valid = choose(here, choose(lower, i >= 1, i + 1 < z.count), valid)
+    planes = band(taps, 0, where - column // RADIUS, valid)
+    r, c = iota((RADIUS, wide), 0), iota((RADIUS, wide), 1) % RADIUS
+    cells = (slots, RADIUS, wide)
+    for side, (offset, valid) in enumerate(((r - c - RADIUS, lower_x(x)), (r - c + RADIUS, higher_x(x)))):
+        columns = band(taps, 0, offset, choose(valid, r >= 0, r < 0))
+        for term in range(TERMS):
+            joint = jnp.broadcast_to(planes[term][:, None, :], cells) * jnp.broadcast_to(columns[term][None], cells)
+            high, low = split(joint.reshape(slots * RADIUS, wide))
+            at = 2 * term + side
+            ends[at, : slots * RADIUS] = high
+            ends[at, slots * RADIUS : 2 * slots * RADIUS] = high
+            ends[at, 2 * slots * RADIUS :] = low
 
     lower, higher = y.index() > 0, y.index() < y.count - 1
     far_below = s.y2_routes[0].below()
@@ -478,145 +512,184 @@
     write(y_coarse, s.sum_rows, [dot(from_coarse, m) for m in coarse])
 
 
-def own_kernel(s, fine, sums, x_fine, x_sums, fine_part, sums_part):
+def contract_y(s, weights, high, low):
+    joined = jnp.concatenate([high, low, high], axis=0)
+    result = jnp.dot(weights[...], joined, preferred_element_type=F32)
+    n, m = s.y.fine, s.x.fine
+    return [result[t * n : (t + 1) * n, t * m : (t + 1) * m] for t in range(TERMS)]
+
+
+def contract_z(taps, held, level, base, count):
+    totals = [None] * count
+    for t in range(TERMS):
+        for j in range(count + TAPS - 1):
+            plane = held[base + j, t]
+            for i in range(max(0, j - TAPS + 1), min(count, j + 1)):
+                term = taps[level, t, j - i] * plane
+                totals[i] = term if totals[i] is None else totals[i] + term
+    return totals
+
+
+def slab_starts(s, below_at, above_at):
+    result = []
+    for route in s.z_routes:
+        lower, i = route.below(), s.z.index()
+        valid = choose(lower, i >= 1, i + 1 < s.z.count)
+        result.append((jnp.where(lower, below_at, above_at), valid))
+    return result
+
+
+def store_terms(held, at, valid, parts):
+    for t, part in enumerate(parts):
+        held[at, t] = part if valid is None else jnp.where(valid, part, 0.0)
+
+
+BLOCK = 4
+
+
+def own_kernel(s, taps, fine, sums, x_fine, x_sums, y_fine, fine_part, sums_part, t_fine):
+    z, x = s.z, s.x
+
     def along_x(grid, weights):
         high, low = split(grid)
         joined = jnp.concatenate([high, low, high], axis=1)
-        return jnp.dot(joined, weights[: 3 * s.x.fine], preferred_element_type=F32)
-
-    cells = s.fine_planes * s.fine_rows
-    fine_part[...] = along_x(fine[...].reshape(cells, s.x.fine), x_fine)
-    cells = s.sum_planes * s.sum_rows
-    sums_part[...] = along_x(sums[...].reshape(cells, s.x.fine), x_sums)
-
-
-def sum_kernel(s, taps, fine, sums, first, second, x_fine, x_sums, y_fine, y_mid, y_coarse, out, *scratch):
-    fine_ends, sums_ends, t_fine, t_mid, t_coarse, p_mid, p_coarse = scratch
+        return jnp.dot(joined, weights[: 3 * x.fine], preferred_element_type=F32)
+
+    t_fine[...] = jnp.zeros(t_fine.shape, F32)
+    fine_at = [(RADIUS + p, None) for p in range(z.fine)]
+    for start, valid in slab_starts(s, 0, z.fine + RADIUS):
+        fine_at += [(start + p, valid) for p in range(RADIUS)]
+
+    def fine_group(g, count):
+        n = s.fine_rows
+        a, b = split(along_x(fine[g : g + count].reshape(count * n, x.fine), x_fine))
+        for p in range(count):
+            rows = slice(p * n, (p + 1) * n)
+            store_terms(t_fine, *fine_at[g + p], contract_y(s, y_fine, a[rows], b[rows]))
+
+    def fine_block(k):
+        for i, total in enumerate(contract_z(taps, t_fine, 0, k, BLOCK)):
+            fine_part[k + i] = total
+
+    def sum_part(g, count):
+        n = s.sum_rows
+        grid = sums[g : g + count].reshape(count * n, x.fine)
+        sums_part[g * n : (g + count) * n] = along_x(grid, x_sums)
+
+    later = []
+    done = 0
+    for g in list(range(z.fine, s.fine_planes, 8)) + list(range(0, z.fine, 8)):
+        fine_group(g, 8)
+        while later:
+            later.pop(0)()
+        if g < z.fine:
+            ready = g if g + 8 < z.fine else z.fine
+            later += [lambda k=k: fine_block(k) for k in range(done, ready, BLOCK)]
+            done = max(done, ready)
+    starts = list(range(0, s.sum_planes, 8))
+    while later or starts:
+        if starts:
+            sum_part(starts[0], min(8, s.sum_planes - starts[0]))
+            starts.pop(0)
+        if later:
+            later.pop(0)()
+
+
+def sum_kernel(s, taps, fine, sums, first, second, x_sums, ends, y_fine, y_mid, y_coarse, out, *scratch):
+    sums_ends, t_mid, t_coarse, p_mid, p_coarse = scratch
     z, y, x = s.z, s.y, s.x
     below = s.x_routes[0].below()
-    for out_ends, blocks, start, half in (
-        (fine_ends, s.fine_blocks, 0, RADIUS),
-        (sums_ends, s.sum_blocks, s.fine_blocks * RADIUS, s.edge_sums),
-    ):
-        copies = 128 // (2 * half)
-        copies = min(copies, 3)
-        for b in range(blocks):
-            at = slice(start + b * half, start + (b + 1) * half)
-            one, two = first[at], second[at]
-            rows = [jnp.where(below, one, two), jnp.where(below, two, one)] * copies
-            rows.append(jnp.zeros((128 - 2 * half * copies, 128), F32))
-            out_ends[b * 128 : (b + 1) * 128] = jnp.concatenate(rows, axis=0).T
-
-    def along_x(held, ends, half, start, rows, weights):
-        edge = ends[start : start + rows]
-        edge_high, edge_low = split(edge)
-        lane = iota(edge.shape, 1)
-        is_low = (lane >= 2 * half) & (lane < 4 * half)
-        joined = jnp.where(is_low, edge_low.astype(F32), edge_high.astype(F32)).astype(BF16)
-        if 6 * half > 128:
-            joined = jnp.concatenate([joined, edge_high], axis=1)
-        part = jnp.dot(joined, weights[3 * x.fine :], preferred_element_type=F32)
-        return split(held[start : start + rows] + part)
-
-    def along_y(high, low, weights):
+    half = s.edge_sums
+    for b in range(s.sum_blocks):
+        at = slice(s.fine_ends + b * half, s.fine_ends + (b + 1) * half)
+        one, two = first[at], second[at]
+        rows = [jnp.where(below, one, two), jnp.where(below, two, one)] * 2
+        rows.append(jnp.zeros((128 - 4 * half, 128), F32))
+        sums_ends[b * 128 : (b + 1) * 128] = jnp.concatenate(rows, axis=0).T
+
+    def along_x(start, rows):
+        edge_high, edge_low = split(sums_ends[start : start + rows])
+        is_high = iota(edge_high.shape, 1) < 2 * half
+        packed = jnp.where(is_high, edge_high.astype(F32), edge_low.astype(F32)).astype(BF16)
+        joined = jnp.concatenate([packed, edge_high], axis=1)
+        part = jnp.dot(joined, x_sums[3 * x.fine :], preferred_element_type=F32)
+        return split(sums[start : start + rows] + part)
+
+    def fine_edges():
+        columns = []
+        for flip in range(2):
+            for g in range(s.fine_groups):
+                at = slice(g * s.fine_rows, (g + 1) * s.fine_rows)
+                pair = (first[at], second[at])
+                columns.append(jnp.where(below, pair[flip], pair[1 - flip]))
+        high, low = split(jnp.concatenate(columns, axis=1))
         joined = jnp.concatenate([high, low, high], axis=0)
-        result = jnp.dot(weights[...], joined, preferred_element_type=F32)
-        return [result[t * y.fine : (t + 1) * y.fine, t * x.fine : (t + 1) * x.fine] for t in range(TERMS)]
-
-    def starts(below_at, above_at):
+        high, low = split(jnp.dot(y_fine[...], joined, preferred_element_type=F32))
+        width = s.fine_groups * x.fine
         result = []
-        for route in s.z_routes:
-            lower, i = route.below(), z.index()
-            valid = choose(lower, i >= 1, i + 1 < z.count)
-            result.append((jnp.where(lower, below_at, above_at), valid))
+        for side in range(2):
+            total = 0.0
+            for t in range(TERMS):
+                rows, cols = slice(t * y.fine, (t + 1) * y.fine), slice(side * width, (side + 1) * width)
+                a, b = high[rows, cols], low[rows, cols]
+                joined = jnp.concatenate([a, b, a], axis=1)
+                total = total + jnp.dot(joined, ends[2 * t + side], preferred_element_type=F32)
+            result.append(total)
         return result
 
-    t_fine[...] = jnp.zeros(t_fine.shape, F32)
     t_mid[...] = jnp.zeros(t_mid.shape, F32)
     t_coarse[...] = jnp.zeros(t_coarse.shape, F32)
-
-    def store(held, at, valid, parts):
-        for t, part in enumerate(parts):
-            held[at, t] = part if valid is None else jnp.where(valid, part, 0.0)
-
     mid_at = [(RADIUS + p, None) for p in range(z.mid_all)]
     coarse_at = [(RADIUS + p if p < z.coarse_all else None, None) for p in range(z.mid_all)]
-    for start, valid in starts(0, z.mid + 3 + RADIUS):
+    for start, valid in slab_starts(s, 0, z.mid + 3 + RADIUS):
         mid_at += [(start + p, valid) for p in range(RADIUS)]
-    for start, valid in starts(0, z.coarse + 5 + RADIUS):
+    for start, valid in slab_starts(s, 0, z.coarse + 5 + RADIUS):
         coarse_at += [(start + p, valid) for p in range(RADIUS)]
     def sum_group(g, count):
         n = s.sum_rows
-        a, b = along_x(sums, sums_ends, s.edge_sums, g * n, count * n, x_sums)
+        a, b = along_x(g * n, count * n)
         for p in range(count):
             rows = slice(p * n, (p + 1) * n)
             for which, (held, weights) in enumerate(((t_mid, y_mid), (t_coarse, y_coarse))):
                 at, valid = (mid_at, coarse_at)[which][g + p]
                 if at is not None:
                     cols = slice(which * TERMS * x.fine, (which + 1) * TERMS * x.fine)
-                    store(held, at, valid, along_y(a[rows, cols], b[rows, cols], weights))
-
-    fine_at = [(RADIUS + p, None) for p in range(z.fine)]
-    for start, valid in starts(0, z.fine + RADIUS):
-        fine_at += [(start + p, valid) for p in range(RADIUS)]
-
-    def fine_group(g, count):
-        n = s.fine_rows
-        a, b = along_x(fine, fine_ends, RADIUS, g * n, count * n, x_fine)
-        for p in range(count):
-            rows = slice(p * n, (p + 1) * n)
-            store(t_fine, *fine_at[g + p], along_y(a[rows], b[rows], y_fine))
-
-    def along_z(held, level, base, count):
-        totals = [None] * count
-        for t in range(TERMS):
-            for j in range(count + TAPS - 1):
-                plane = held[base + j, t]
-                for i in range(max(0, j - TAPS + 1), min(count, j + 1)):
-                    term = taps[level, t, j - i] * plane
-                    totals[i] = term if totals[i] is None else totals[i] + term
-        return totals
-
-    block = 4
+                    store_terms(held, at, valid, contract_y(s, weights, a[rows, cols], b[rows, cols]))
 
     def coarse_block(k):
-        count = min(block, z.coarse_all - k)
-        for i, total in enumerate(along_z(t_coarse, 2, k, count)):
+        count = min(BLOCK, z.coarse_all - k)
+        for i, total in enumerate(contract_z(taps, t_coarse, 2, k, count)):
             p_coarse[k + i] = jnp.where(z.holds_coarse(k + i - 2), total, 0.0)
 
     def mid_block(k):
-        count = min(block, z.mid_all - k)
-        for i, total in enumerate(along_z(t_mid, 1, k, count)):
+        count = min(BLOCK, z.mid_all - k)
+        for i, total in enumerate(contract_z(taps, t_mid, 1, k, count)):
             m = k + i - 1
             for offset, weight in WEIGHTS:
                 if (m - offset) % 2 == 0 and 0 <= (m - offset) // 2 + 2 < z.coarse_all:
                     total = total + weight * p_coarse[(m - offset) // 2 + 2]
             p_mid[k + i] = jnp.where(z.holds_mid(m), total, 0.0)
 
-    def fine_block(k):
-        for i, total in enumerate(along_z(t_fine, 0, k, block)):
-            for offset, weight in WEIGHTS:
-                if (i - offset) % 2 == 0:
-                    total = total + weight * p_mid[k // 2 + (i - offset) // 2 + 1]
-            out[k + i] = total
-
     for g in range(0, s.sum_planes, 4):
         sum_group(g, min(4, s.sum_planes - g))
-    later = [lambda k=k: coarse_block(k) for k in range(0, z.coarse_all, block)]
-    later += [lambda k=k: mid_block(k) for k in range(0, z.mid_all, block)]
-    groups = list(range(z.fine, s.fine_planes, 8)) + list(range(0, z.fine, 8))
-    done = 0
-    for n, g in enumerate(groups):
-        fine_group(g, 8)
-        for _ in range(3):
-            if later:
-                later.pop(0)()
-        if g < z.fine:
-            ready = g if g + 8 < z.fine else z.fine
-            later += [lambda k=k: fine_block(k) for k in range(done, ready, block)]
-            done = max(done, ready)
-    while later:
-        later.pop(0)()
+    edges = fine_edges()
+    for k in range(0, z.coarse_all, BLOCK):
+        coarse_block(k)
+    for k in range(0, z.mid_all, BLOCK):
+        mid_block(k)
+    lane = iota((y.fine, x.fine), 1)
+    for k in range(z.fine):
+        total = fine[k]
+        for offset, weight in WEIGHTS:
+            if (k - offset) % 2 == 0:
+                total = total + weight * p_mid[(k - offset) // 2 + 1]
+        block, at = k // s.side, k % s.side * RADIUS
+        low, high = (edge[:, block * x.fine : (block + 1) * x.fine] for edge in edges)
+        low = pltpu.roll(low, -at % x.fine, 1) if at else low
+        turn = (x.fine - RADIUS - at) % x.fine
+        high = pltpu.roll(high, turn, 1) if turn else high
+        total = total + jnp.where(lane < RADIUS, low, jnp.where(lane >= x.fine - RADIUS, high, 0.0))
+        out[k] = total
 
 
 def call(kernel, outs, ins, scratch=(), flops=10**7):
@@ -663,8 +736,9 @@
     operators = call(
         bound(operator_kernel),
         [
-            array(3 * n + 128, TERMS * n, dtype=BF16),
+            array(3 * n, TERMS * n, dtype=BF16),
             array(3 * n + 256, 2 * TERMS * n, dtype=BF16),
+            array(2 * TERMS, 3 * s.fine_groups * n, z_columns(s), dtype=BF16),
             array(TERMS * y.fine, 3 * s.fine_rows, dtype=BF16),
             array(TERMS * y.fine, 3 * s.sum_rows, dtype=BF16),
             array(TERMS * y.fine, 3 * s.sum_rows, dtype=BF16),
@@ -691,19 +765,19 @@
         [pltpu.VMEM((s.slab_planes, s.sum_rows, n), F32), pltpu.VMEM((s.far_groups, s.far_rows, n), F32)],
     )
     first, second = s.x_routes[0](first), s.x_routes[1](second)
+    x_fine, x_sums, ends, y_fine, y_mid, y_coarse = operators
     fine, sums = call(
         bound(own_kernel),
-        [array(s.fine_planes * s.fine_rows, TERMS * n), array(s.sum_planes * s.sum_rows, 2 * TERMS * n)],
-        [fine, sums, *operators[:2]],
+        [array(z.fine, y.fine, n), array(s.sum_planes * s.sum_rows, 2 * TERMS * n)],
+        [kernel_taps, fine, sums, x_fine, x_sums, y_fine],
+        [pltpu.VMEM((z.fine + 2 * RADIUS, TERMS, y.fine, n), F32)],
     )
     (out,) = call(
         bound(sum_kernel),
         [array(z.fine, y.fine, n)],
-        [kernel_taps, fine, sums, first, second, *operators],
+        [kernel_taps, fine, sums, first, second, x_sums, ends, y_fine, y_mid, y_coarse],
         [
-            pltpu.VMEM((s.fine_blocks * 128, n), F32),
             pltpu.VMEM((s.sum_blocks * 128, n), F32),
-            pltpu.VMEM((z.fine + 2 * RADIUS, TERMS, y.fine, n), F32),
             pltpu.VMEM((z.mid + 2 * RADIUS + 3, TERMS, y.fine, n), F32),
             pltpu.VMEM((z.coarse + 2 * RADIUS + 5, TERMS, y.fine, n), F32),
             pltpu.VMEM((z.mid_all, y.fine, n), F32),

time: 33.9 us -> 32.1 us (0.947)
  waiting for transfers between devices: 7.13 us -> 4.14 us
  Pallas kernels: 12.3 us -> 13.4 us
    ppermute x8, waiting for transfers between devices: 7.13 us -> 4.14 us  [__call__(): return lax.ppermute(x, self.names, self.pairs)]
    pallas_call x6, Pallas kernels: 12.3 us -> 13.4 us  [call(): pl.pallas_call(kernel, out_shape=tuple(outs), in_specs=specs, out_specs=t...]
  transfers between devices with their start and end apart: 8 -> 8, of which waited for: 4 -> 3; matrix products, arithmetic and copies ran while one was open for 0% -> 0% of each run, Pallas kernels for 10% -> 20%
where the time goes in v5:
time: 32.1 us; the launch traced here: 31.9 us
  Pallas kernels  13.4 us (42%)
  starting transfers between devices  12.6 us (39%)
  waiting for transfers between devices  4.14 us (13%)
  local copies, waits for them, and re-layouts  1.72 us (5%)
    pallas_call x6, Pallas kernels, call(): pl.pallas_call(kernel, out_shape=tuple(outs), in_specs=specs, out_specs=t...  13.4 us
    ppermute x8, starting transfers between devices, __call__(): return lax.ppermute(x, self.names, self.pairs)  12.6 us
    ppermute x8, waiting for transfers between devices, __call__(): return lax.ppermute(x, self.names, self.pairs)  4.14 us
    unnamed x4, local copies, waits for them, and re-layouts  1.72 us
  transfers between devices with their start and end apart: 8, of which 3 were waited for; matrix products, arithmetic and copies ran while one was open for 0% of the time, Pallas kernels for 20%

profile of v5, /device:TPU:1, one launch (start us, length us, event | category | flops | bytes accessed | tf_op | source)
XLA Modules:
  0.0 31.9 jit_solution(1425892195926410360)
XLA Ops:
  0.0 0.0 copy-start
  0.0 1.0 %copy-done = f32[32,32,128]{2,1,0:T(8,128)S(1)} copy-done((f32[32,32,128]{2,1,0:T(8,128)S(1)}, f32[32,32,128]{2,1,0:T(8,128)}, u32[]{:S(2)}) %copy-start) | copy-done | bytes 524312
  1.0 1.2 %shard_map.28 = (f32[32,32,128]{2,1,0:T(8,128)S(1)}, f32[19,24,128]{2,1,0:T(8,128)S(1)}, f32[504,128]{1,0:T(8,128)S(1)}, f32[504,128]{1,0:T(8,128)S(1)}, f32[504,128]{1,0:T(8,128)S(1)}) custom-call(f32[32,32,128]{2,1,0:T(8,128)S(1)} %copy-done), custom_call_target="tpu_custom_call" | custom-call | flops 10000000 | bytes 2056192 | tf_op jit(solution)/shard_map/pallas_call | solution.py:698
  2.3 2.1 %collective-permute-start = (f32[504,128]{1,0:T(8,128)S(1)}, f32[504,128]{1,0:T(8,128)S(1)}, u32[]{:S(2)}, u32[]{:S(2)}) collective-permute-start(f32[504,128]{1,0:T(8,128)S(1)} %get-tuple-element.27), channel_id=1, source_target_pairs={{0,1},{1,0},{2,3},{3,2},{4,5},{5,4},{6,7},{7,6},{8,9},{9,8},{10,11... | collective-permute-start | bytes 774152 | tf_op jit(solution)/shard_map/ppermute | solution.py:64
  4.4 1.0 %collective-permute-start.1 = (f32[504,128]{1,0:T(8,128)S(1)}, f32[504,128]{1,0:T(8,128)S(1)}, u32[]{:S(2)}, u32[]{:S(2)}) collective-permute-start(f32[504,128]{1,0:T(8,128)S(1)} %get-tuple-element.28), channel_id=1, source_target_pairs={{0,2},{2,4},{4,6},{6,14},{14,12},{12,10},{10,8},{8,0},{16,18},{18,... | collective-permute-start | bytes 774152 | tf_op jit(solution)/shard_map/ppermute | solution.py:64
  5.4 0.5 %collective-permute-start.2 = (f32[504,128]{1,0:T(8,128)S(1)}, f32[504,128]{1,0:T(8,128)S(1)}, u32[]{:S(2)}, u32[]{:S(2)}) collective-permute-start(f32[504,128]{1,0:T(8,128)S(1)} %get-tuple-element.29), channel_id=1, source_target_pairs={{2,0},{4,2},{6,4},{14,6},{12,14},{10,12},{8,10},{0,8},{18,16},{20,... | collective-permute-start | bytes 774152 | tf_op jit(solution)/shard_map/ppermute | solution.py:64
  5.9 0.0 copy-start.1
  5.9 0.7 %copy-done.1 = f32[3,2,17]{2,1,0:T(2,128)S(1)} copy-done((f32[3,2,17]{2,1,0:T(2,128)S(1)}, f32[3,2,17]{2,1,0:T(2,128)}, u32[]{:S(2)}) %copy-start.1) | copy-done | bytes 432
  6.6 2.3 %shard_map.29 = (bf16[384,256]{1,0:T(8,128)(2,1)S(1)}, bf16[640,512]{1,0:T(8,128)(2,1)S(1)}, bf16[4,1152,256]{2,1,0:T(8,128)(2,1)S(1)}, bf16[64,144]{1,0:T(8,128...) custom-call(f32[3,2,17]{2,1,0:T(2,128)S(1)} %copy-done.1), custom_call_target="tpu_custom_call" | custom-call | flops 10000000 | bytes 3266968 | tf_op jit(solution)/shard_map/pallas_call | solution.py:698
  8.9 1.4 %collective-permute-done.refs_2_ = f32[504,128]{1,0:T(8,128)S(1)} collective-permute-done((f32[504,128]{1,0:T(8,128)S(1)}, f32[504,128]{1,0:T(8,128)S(1)}, u32[]{:S(2)}, u32[]{:S(2)}) %collective-permute-start) | collective-permute-done | bytes 258080 | tf_op jit(solution)/shard_map/ppermute | solution.py:64
  10.4 0.1 shard_map.30
  10.5 1.2 %collective-permute-start.3 = (f32[240,128]{1,0:T(8,128)S(1)}, f32[240,128]{1,0:T(8,128)S(1)}, u32[]{:S(2)}, u32[]{:S(2)}) collective-permute-start(f32[240,128]{1,0:T(8,128)S(1)} %get-tuple-element.31), channel_id=1, source_target_pairs={{0,2},{2,4},{4,6},{6,14},{14,12},{12,10},{10,8},{8,0},{16,18},{18,... | collective-permute-start | bytes 368648 | tf_op jit(solution)/shard_map/ppermute | solution.py:64
  11.7 0.2 collective-permute-start.4
  12.0 2.2 %collective-permute-start.5 = (f32[48,128]{1,0:T(8,128)S(1)}, f32[48,128]{1,0:T(8,128)S(1)}, u32[]{:S(2)}, u32[]{:S(2)}) collective-permute-start(f32[48,128]{1,0:T(8,128)S(1)} %get-tuple-element.33), channel_id=1, source_target_pairs={{0,4},{2,6},{4,0},{6,2},{1,5},{3,7},{5,1},{7,3},{8,12},{10,14},{12... | collective-permute-start | bytes 73736 | tf_op jit(solution)/shard_map/ppermute | solution.py:64
  14.2 0.0 collective-permute-done.1.refs_3_
  14.2 0.0 collective-permute-done.2.refs_4_
  14.2 1.4 %collective-permute-done.5.refs_7_ = f32[48,128]{1,0:T(8,128)S(1)} collective-permute-done((f32[48,128]{1,0:T(8,128)S(1)}, f32[48,128]{1,0:T(8,128)S(1)}, u32[]{:S(2)}, u32[]{:S(2)}) %collective-permute-start.5) | collective-permute-done | bytes 24608 | tf_op jit(solution)/shard_map/ppermute | solution.py:64
  15.5 0.0 collective-permute-done.3.refs_5_
  15.5 0.0 collective-permute-done.4.refs_6_
  15.5 0.8 %shard_map.31 = (f32[40,48,128]{2,1,0:T(8,128)S(1)}, f32[27,48,128]{2,1,0:T(8,128)S(1)}, f32[408,128]{1,0:T(8,128)S(1)}, f32[408,128]{1,0:T(8,128)S(1)}) custom-call(f32[32,32,128]{2,1,0:T(8,128)S(1)} %get-tuple-element.25.refs_0_, f32[19,24,128]{2,1,0:T(8,128)S(1)} %get-tuple-element.26.refs_1_, f32[504,128]{1,0:T(8,128)S(1)} %collective-permute-done.refs_2_, ...), custom_call_target="tpu_custom_call" | custom-call | flops 10000000 | bytes 3866624 | tf_op jit(solution)/shard_map/pallas_call | solution.py:698
  16.4 5.3 %collective-permute-start.6 = (f32[408,128]{1,0:T(8,128)S(1)}, f32[408,128]{1,0:T(8,128)S(1)}, u32[]{:S(2)}, u32[]{:S(2)}) collective-permute-start(f32[408,128]{1,0:T(8,128)S(1)} %get-tuple-element.41), channel_id=1, source_target_pairs={{0,8},{8,16},{16,24},{24,25},{25,17},{17,9},{9,1},{1,0},{2,10},{10... | collective-permute-start | bytes 626696 | tf_op jit(solution)/shard_map/ppermute | solution.py:64
  21.7 0.0 collective-permute-start.7
  21.7 3.9 %shard_map.32 = (f32[32,32,128]{2,1,0:T(8,128)S(1)}, f32[1296,512]{1,0:T(8,128)S(1)}) custom-call(f32[3,2,17]{2,1,0:T(2,128)S(1)} %copy-done.1, f32[40,48,128]{2,1,0:T(8,128)S(1)} %get-tuple-element.34.refs_1_, f32[27,48,128]{2,1,0:T(8,128)S(1)} %get-tuple-element.35.refs_2_, bf16[384,256]{1,0:T(8,128)(2,1)S(1)} %get-tuple-element.36.refs_3_, ...), custom_call_target="tpu_custom_call" | custom-call | flops 10000000 | bytes 5695896 | tf_op jit(solution)/shard_map/pallas_call | solution.py:698
  25.6 0.0 collective-permute-done.6.refs_3_
  25.6 1.3 %collective-permute-done.7.refs_4_ = f32[408,128]{1,0:T(8,128)S(1)} collective-permute-done((f32[408,128]{1,0:T(8,128)S(1)}, f32[408,128]{1,0:T(8,128)S(1)}, u32[]{:S(2)}, u32[]{:S(2)}) %collective-permute-start.7) | collective-permute-done | bytes 208928 | tf_op jit(solution)/shard_map/ppermute | solution.py:64
  26.9 5.0 %shard_map.33 = f32[32,32,128]{2,1,0:T(8,128)} custom-call(f32[3,2,17]{2,1,0:T(2,128)S(1)} %copy-done.1, f32[32,32,128]{2,1,0:T(8,128)S(1)} %get-tuple-element.39.refs_1_, f32[1296,512]{1,0:T(8,128)S(1)} %get-tuple-element.40.refs_2_, f32[408,128]{1,0:T(8,128)S(1)} %collective-permute-done.6.refs_3_, f32[408,128]{1,0:T(8,128)S(1)} %collective-permute-done.7.refs_4_, ...), custom_call_target="tpu_custom_call" | custom-call | flops 10000000 | bytes 7190936 | tf_op jit(solution)/shard_map/pallas_call | solution.py:698
Async XLA Ops:
  0.0 1.0 %copy-start = (f32[32,32,128]{2,1,0:T(8,128)S(1)}, f32[32,32,128]{2,1,0:T(8,128)}, u32[]{:S(2)}) copy-start(f32[32,32,128]{2,1,0:T(8,128)} %refs_0_.4) | copy-start | bytes 1572868
  2.3 8.1 %collective-permute-start = (f32[504,128]{1,0:T(8,128)S(1)}, f32[504,128]{1,0:T(8,128)S(1)}, u32[]{:S(2)}, u32[]{:S(2)}) collective-permute-start(f32[504,128]{1,0:T(8,128)S(1)} %get-tuple-element.27), channel_id=1, source_target_pairs={{0,1},{1,0},{2,3},{3,2},{4,5},{5,4},{6,7},{7,6},{8,9},{9,8},{10,11... | collective-permute-start | bytes 774152 | tf_op jit(solution)/shard_map/ppermute | solution.py:64
  4.4 9.8 %collective-permute-start.1 = (f32[504,128]{1,0:T(8,128)S(1)}, f32[504,128]{1,0:T(8,128)S(1)}, u32[]{:S(2)}, u32[]{:S(2)}) collective-permute-start(f32[504,128]{1,0:T(8,128)S(1)} %get-tuple-element.28), channel_id=1, source_target_pairs={{0,2},{2,4},{4,6},{6,14},{14,12},{12,10},{10,8},{8,0},{16,18},{18,... | collective-permute-start | bytes 774152 | tf_op jit(solution)/shard_map/ppermute | solution.py:64
  5.4 8.8 %collective-permute-start.2 = (f32[504,128]{1,0:T(8,128)S(1)}, f32[504,128]{1,0:T(8,128)S(1)}, u32[]{:S(2)}, u32[]{:S(2)}) collective-permute-start(f32[504,128]{1,0:T(8,128)S(1)} %get-tuple-element.29), channel_id=1, source_target_pairs={{2,0},{4,2},{6,4},{14,6},{12,14},{10,12},{8,10},{0,8},{18,16},{20,... | collective-permute-start | bytes 774152 | tf_op jit(solution)/shard_map/ppermute | solution.py:64
  5.9 0.7 %copy-start.1 = (f32[3,2,17]{2,1,0:T(2,128)S(1)}, f32[3,2,17]{2,1,0:T(2,128)}, u32[]{:S(2)}) copy-start(f32[3,2,17]{2,1,0:T(2,128)} %refs_0_.7) | copy-start | bytes 1228
  10.5 5.1 %collective-permute-start.3 = (f32[240,128]{1,0:T(8,128)S(1)}, f32[240,128]{1,0:T(8,128)S(1)}, u32[]{:S(2)}, u32[]{:S(2)}) collective-permute-start(f32[240,128]{1,0:T(8,128)S(1)} %get-tuple-element.31), channel_id=1, source_target_pairs={{0,2},{2,4},{4,6},{6,14},{14,12},{12,10},{10,8},{8,0},{16,18},{18,... | collective-permute-start | bytes 368648 | tf_op jit(solution)/shard_map/ppermute | solution.py:64
  11.7 3.8 %collective-permute-start.4 = (f32[240,128]{1,0:T(8,128)S(1)}, f32[240,128]{1,0:T(8,128)S(1)}, u32[]{:S(2)}, u32[]{:S(2)}) collective-permute-start(f32[240,128]{1,0:T(8,128)S(1)} %get-tuple-element.32), channel_id=1, source_target_pairs={{2,0},{4,2},{6,4},{14,6},{12,14},{10,12},{8,10},{0,8},{18,16},{20,... | collective-permute-start | bytes 368648 | tf_op jit(solution)/shard_map/ppermute | solution.py:64
  12.0 3.6 %collective-permute-start.5 = (f32[48,128]{1,0:T(8,128)S(1)}, f32[48,128]{1,0:T(8,128)S(1)}, u32[]{:S(2)}, u32[]{:S(2)}) collective-permute-start(f32[48,128]{1,0:T(8,128)S(1)} %get-tuple-element.33), channel_id=1, source_target_pairs={{0,4},{2,6},{4,0},{6,2},{1,5},{3,7},{5,1},{7,3},{8,12},{10,14},{12... | collective-permute-start | bytes 73736 | tf_op jit(solution)/shard_map/ppermute | solution.py:64
  16.4 9.2 %collective-permute-start.6 = (f32[408,128]{1,0:T(8,128)S(1)}, f32[408,128]{1,0:T(8,128)S(1)}, u32[]{:S(2)}, u32[]{:S(2)}) collective-permute-start(f32[408,128]{1,0:T(8,128)S(1)} %get-tuple-element.41), channel_id=1, source_target_pairs={{0,8},{8,16},{16,24},{24,25},{25,17},{17,9},{9,1},{1,0},{2,10},{10... | collective-permute-start | bytes 626696 | tf_op jit(solution)/shard_map/ppermute | solution.py:64
  21.7 5.2 %collective-permute-start.7 = (f32[408,128]{1,0:T(8,128)S(1)}, f32[408,128]{1,0:T(8,128)S(1)}, u32[]{:S(2)}, u32[]{:S(2)}) collective-permute-start(f32[408,128]{1,0:T(8,128)S(1)} %get-tuple-element.42), channel_id=1, source_target_pairs={{8,0},{16,8},{24,16},{25,24},{17,25},{9,17},{1,9},{0,1},{10,2},{18... | collective-permute-start | bytes 626696 | tf_op jit(solution)/shard_map/ppermute | solution.py:64

commit v6 on v5

--- a/solution.py
+++ b/solution.py
@@ -128,11 +128,13 @@
         self.y2_routes = swap(y, 2)
         self.x_routes = folded(x, z.name, (x.name, z.name))
         self.z_fine = RADIUS * y.fine
-        self.z_rows = up8(self.z_fine + SPAN * y.mid_all)
-        self.z2_rows = up8(z.second * y.mid_all)
+        self.z_sums = max(EDGE * y.mid_all, SPAN * y.coarse_all)
+        self.z_rows = up8(self.z_fine + self.z_sums)
+        self.z2_rows = up8(z.second * y.coarse_all)
         self.slab_planes = SPAN * len(self.z_routes) + z.second * len(self.z2_routes)
         self.fine_planes = z.fine + RADIUS * len(self.z_routes)
         self.sum_planes = z.mid_all + RADIUS * len(self.z_routes)
+        self.coarse_rows = -(-y.coarse_all // 16) * 16
         self.y_fine = RADIUS * z.fine
         self.y_rows = up8(self.y_fine + SPAN * z.mid_all)
         self.slab_fine = RADIUS * RADIUS * len(self.z_routes)
@@ -152,12 +154,12 @@
         self.sum_blocks = -(-self.sum_planes * self.sum_rows // 128)
         self.x_rows = self.fine_ends + self.sum_blocks * self.edge_sums
         assert x.mid_all + x.coarse_all <= x.fine
-        assert self.far + y.second <= self.low
+        assert self.far + y.second <= self.low and y.coarse_all == SPAN
         assert z.coarse >= RADIUS and y.coarse >= RADIUS and y.count == 4
 
 
 def restrict_kernel(s, nz, source, charges, own, ahead, behind, *rest):
-    messages, (wide, mid, high, coarse) = rest[:-4], rest[-4:]
+    messages, (wide, mid, high, coarse, packed) = rest[:-5], rest[-5:]
     z, y, x = s.z, s.y, s.x
     lanes = (x.fine, x.fine)
     cell, lane = iota(lanes, 0), iota(lanes, 1)
@@ -170,7 +172,16 @@
     wide[...] = jnp.zeros(wide.shape, F32)
     charges[...] = source[...]
     cells = source[...].reshape(z.fine * y.fine, x.fine)
-    reduced = jnp.dot(cells, narrow, precision=EXACT, preferred_element_type=F32)
+    top, rest = cells.astype(BF16), cells
+    rest = rest - top.astype(F32)
+    middle = rest.astype(BF16)
+    low = (rest - middle.astype(F32)).astype(BF16)
+    weights = jnp.concatenate(split(narrow), axis=1)
+    both = jnp.dot(low, weights, preferred_element_type=F32)
+    both = both + jnp.dot(
+        jnp.concatenate([top, middle], axis=1), jnp.concatenate([weights, weights], axis=0), preferred_element_type=F32
+    )
+    reduced = both[:, : x.fine] + both[:, x.fine :]
     wide[:, 8 : 8 + y.fine, :] = reduced.reshape(z.fine, y.fine, x.fine)
     rows = 0.0
     for offset, weight in WEIGHTS:
@@ -217,27 +228,43 @@
     for message, route in zip(messages, s.z_routes):
         up = route.up().astype(jnp.int32)
         message[: s.z_fine] = charges[pl.ds(up * (z.fine - RADIUS), RADIUS)].reshape(s.z_fine, x.fine)
+        packed[...] = jnp.zeros(packed.shape, F32)
+        for p in range(EDGE):
+            packed[0, p * y.mid_all : (p + 1) * y.mid_all] = mid[up * (z.mid_all - EDGE) + p][: y.mid_all]
         for p in range(SPAN):
-            plane = jnp.where(is_mid, mid[up * (z.mid_all - SPAN) + p], coarse[up * (z.coarse_all - SPAN) + p])
-            at = s.z_fine + p * y.mid_all
-            message[at : at + y.mid_all] = plane[: y.mid_all]
-        filled = s.z_fine + SPAN * y.mid_all
-        if filled < s.z_rows:
-            message[filled:] = jnp.zeros((s.z_rows - filled, x.fine), F32)
+            plane = coarse[up * (z.coarse_all - SPAN) + p]
+            packed[1, p * y.coarse_all : (p + 1) * y.coarse_all] = plane[: y.coarse_all]
+        is_mid = iota(packed.shape[1:], 1) < x.mid_all
+        message[s.z_fine :] = jnp.where(is_mid, packed[0], packed[1])
     for message, route in zip(messages[nz:], s.z2_routes):
         up = route.up().astype(jnp.int32)
         message[...] = jnp.zeros(message.shape, F32)
         for p in range(z.second):
-            plane = jnp.where(is_mid, 0.0, coarse[up * (z.coarse_all - z.second) + p])
-            message[p * y.mid_all : (p + 1) * y.mid_all] = plane[: y.mid_all]
+            plane = coarse[up * (z.coarse_all - z.second) + p]
+            message[p * y.coarse_all : (p + 1) * y.coarse_all] = plane[: y.coarse_all]
+
+
+class Slab:
+    def __init__(self, message, mid, coarse):
+        self.message, self.mid, self.coarse = message, mid, coarse
+
+    def coarse_rows(self, first, count):
+        return self.message[self.coarse + first : self.coarse + first + count]
+
+    def rows(self, is_mid, first_mid, first_coarse, count):
+        coarse = 0.0 if first_coarse is None else self.coarse_rows(first_coarse, count)
+        mid = 0.0 if self.mid is None else self.message[self.mid + first_mid : self.mid + first_mid + count]
+        return jnp.where(is_mid, mid, coarse)
 
 
 def slabs(s, z_messages, z2_messages):
     out = []
     for message in z_messages:
-        out += [(message, s.z_fine + p * s.y.mid_all) for p in range(SPAN)]
+        for p in range(SPAN):
+            mid = s.z_fine + p * s.y.mid_all if p < EDGE else None
+            out.append(Slab(message, mid, s.z_fine + p * s.y.coarse_all))
     for message in z2_messages:
-        out += [(message, p * s.y.mid_all) for p in range(s.z.second)]
+        out += [Slab(message, None, p * s.y.coarse_all) for p in range(s.z.second)]
     return out
 
 
@@ -255,21 +282,20 @@
             edge = jnp.where(up, slab[:, y.fine - RADIUS :], slab[:, :RADIUS])
             message[at : at + RADIUS * RADIUS] = edge.reshape(RADIUS * RADIUS, x.fine)
             at += RADIUS * RADIUS
-        for held, first in planes:
-            top, end = held[first + y.mid_all - SPAN : first + y.mid_all], first + y.coarse_all
-            last = jnp.where(is_mid, top, held[end - SPAN : end])
-            message[at : at + SPAN] = jnp.where(up, last, held[first : first + SPAN])
+        for plane in planes:
+            last = plane.rows(is_mid, y.mid_all - SPAN, y.coarse_all - SPAN, SPAN)
+            message[at : at + SPAN] = jnp.where(up, last, plane.rows(is_mid, 0, 0, SPAN))
             at += SPAN
         if at < s.slab_rows:
             message[at:] = jnp.zeros((s.slab_rows - at, x.fine), F32)
     up = s.y2_routes[0].up()
     count, end = y.second, y.coarse_all
     rows[...] = jnp.zeros(rows.shape, F32)
-    sources = [(own.at[p], 0) for p in range(z.coarse_all)] + planes
-    for p, (held, first) in enumerate(sources):
+    pairs = [(own[p, end - count : end], own[p, :count]) for p in range(z.coarse_all)]
+    pairs += [(plane.coarse_rows(end - count, count), plane.coarse_rows(0, count)) for plane in planes]
+    for p, (last, start) in enumerate(pairs):
         g, at = p // s.far_planes, p % s.far_planes * count
-        last = held[first + end - count : first + end]
-        rows[g, at : at + count] = jnp.where(up, last, held[first : first + count])
+        rows[g, at : at + count] = jnp.where(up, last, start)
     lane = iota(far.shape, 1)
     total = jnp.zeros(far.shape, F32)
     for g in range(s.far_groups):
@@ -281,8 +307,9 @@
 
 def collect_kernel(s, nz, nz2, charges, own, *rest):
     z_messages, z2_messages = rest[:nz], rest[nz : nz + nz2]
-    pairs = rest[nz + nz2 : nz + nz2 + 4]
-    far, fine, sums, first, second, raw, rows = rest[nz + nz2 + 4 :]
+    rest = rest[nz + nz2 :]
+    pairs = rest[:4]
+    far, fine, sums, first, second, raw, rows = rest[4:]
     z, y, x = s.z, s.y, s.x
     below = s.y_routes[0].below()
     planes = slabs(s, z_messages, z2_messages)
@@ -322,8 +349,11 @@
     for p in range(z.mid_all):
         far_plane = p if p < z.coarse_all else None
         rows_of_plane(sums, p, own[p, : y.mid_all], 0, s.y_fine + p * SPAN, far_plane)
-    for p, (held, at) in enumerate(planes):
-        rows_of_plane(raw, p, held[at : at + y.mid_all], 1, s.slab_fine + p * SPAN, z.coarse_all + p)
+    is_mid_row = iota((SPAN, x.fine), 1) < x.mid_all
+    is_mid_rest = iota((y.mid_all - SPAN, x.fine), 1) < x.mid_all
+    for p, plane in enumerate(planes):
+        body = [plane.rows(is_mid_row, 0, 0, SPAN), plane.rows(is_mid_rest, SPAN, None, y.mid_all - SPAN)]
+        rows_of_plane(raw, p, jnp.concatenate(body, axis=0), 1, s.slab_fine + p * SPAN, z.coarse_all + p)
     is_mid = iota((s.sum_rows, x.fine), 1) < x.mid_all
 
     def number(condition, a, b):
@@ -332,12 +362,12 @@
     for n, route in enumerate(s.z_routes):
         lower, base = route.below(), n * SPAN
         for j in range(RADIUS):
-            a = raw[base + number(lower, SPAN - 3 - RADIUS, 3) + j]
+            a = raw[base + number(lower, 0, 3) + j]
             b = raw[base + number(lower, SPAN - 5 - RADIUS, 5) + j]
             sums[z.mid_all + n * RADIUS + j] = jnp.where(is_mid, a, b)
         for i in range(3):
             at = number(lower, 0, z.mid) + i
-            sums[at] = sums[at] + jnp.where(is_mid, raw[base + number(lower, SPAN - 3, 0) + i], 0.0)
+            sums[at] = sums[at] + jnp.where(is_mid, raw[base + number(lower, EDGE - 3, 0) + i], 0.0)
         for i in range(5):
             at = number(lower, 0, z.coarse) + i
             sums[at] = sums[at] + jnp.where(is_mid, 0.0, raw[base + number(lower, SPAN - 5, 0) + i])
@@ -403,7 +433,7 @@
     return x.index() < x.count - 1
 
 
-def operator_kernel(s, taps, x_fine, x_sums, ends, y_fine, y_mid, y_coarse):
+def operator_kernel(s, taps, x_fine, x_sums, ends, y_fine, y_mid, y_coarse, widen_x, widen_y):
     y, x = s.y, s.x
     own, edge = x.fine, 64
     shape = (own + edge, x.fine)
@@ -426,14 +456,23 @@
     first = x.mid_all
     inside = (row >= first) & (row < first + x.coarse_all)
     where, valid = place(half, row - first - 2, inside, EDGE, SPAN, 3 - SPAN, x.coarse - 2)
-    coarse = band(taps, 2, where - (lane - 2), valid & (lane < x.coarse_all))
+    side = x.fine // TERMS
+    column = lane % side
+    terms = band(taps, 2, where - (column - 2), valid & (column < x.coarse_all))
+    coarse = terms[0]
+    for term in range(1, TERMS):
+        coarse = jnp.where(lane >= term * side, terms[term], coarse)
     a, b = iota((x.fine, x.fine), 0), iota((x.fine, x.fine), 1)
     from_mid = jnp.where((a < x.mid_all) & x.holds_mid(a - 1), weight_of(b - 2 * (a - 1)), 0.0)
-    from_coarse = jnp.where((a < x.coarse_all) & x.holds_coarse(a - 2), weight_of(b - 1 - 2 * (a - 2)), 0.0)
-    from_coarse = dot(from_coarse, from_mid)
+    c = a % side
+    from_coarse = jnp.where((c < x.coarse_all) & x.holds_coarse(c - 2), weight_of(b - 1 - 2 * (c - 2)), 0.0)
+    high, low = split(dot(from_coarse, from_mid))
+    widen_x[:own] = high
+    widen_x[own : 2 * own] = high
+    widen_x[2 * own :] = low
     columns = [(x_fine, 0, 0, fine)]
     columns += [(x_sums, half, 0, [dot(m, from_mid) for m in mid])]
-    columns += [(x_sums, half, TERMS * x.fine, [dot(c, from_coarse) for c in coarse])]
+    columns += [(x_sums, half, TERMS * x.fine, [coarse])]
     for out, half, at, terms in columns:
         for term, matrix in enumerate(terms):
             high, low = split(matrix)
@@ -474,10 +513,11 @@
     n = up8(y.mid_all)
 
     def write(out, size, terms):
-        part = iota((y.fine, 3 * size), 1) >= 2 * size
+        part = iota(terms[0].shape, 1) >= 2 * size
         for term, matrix in enumerate(terms):
             high, low = split(matrix)
-            out[term * y.fine : (term + 1) * y.fine] = jnp.where(part, low.astype(F32), high.astype(F32)).astype(BF16)
+            n = matrix.shape[0]
+            out[term * n : (term + 1) * n] = jnp.where(part, low.astype(F32), high.astype(F32)).astype(BF16)
 
     def columns_of(rows, size):
         lane = iota((rows, 3 * size), 1)
@@ -505,11 +545,13 @@
     coarse = band(taps, 2, where - (r - 2), valid & (r < y.coarse_all))
     o, k = iota((y.fine, n), 0), iota((y.fine, n), 1)
     from_mid = jnp.where((k < y.mid_all) & y.holds_mid(k - 1), weight_of(o - 2 * (k - 1)), 0.0)
-    o, k = iota((n, n), 0), iota((n, n), 1)
-    from_coarse = jnp.where((k < y.coarse_all) & y.holds_coarse(k - 2), weight_of(o - 1 - 2 * (k - 2)), 0.0)
-    from_coarse = dot(from_mid, from_coarse)
-    write(y_mid, s.sum_rows, [dot(from_mid, m) for m in mid])
-    write(y_coarse, s.sum_rows, [dot(from_coarse, m) for m in coarse])
+    m = s.coarse_rows
+    c = columns_of(n, m)
+    k = iota(c.shape, 0)
+    from_coarse = jnp.where((c < y.coarse_all) & y.holds_coarse(c - 2), weight_of(k - 1 - 2 * (c - 2)), 0.0)
+    write(y_mid, s.sum_rows, [dot(from_mid, matrix) for matrix in mid])
+    write(y_coarse, s.sum_rows, [matrix[:m] for matrix in coarse])
+    write(widen_y, m, [dot(from_mid, from_coarse)])
 
 
 def contract_y(s, weights, high, low):
@@ -519,13 +561,13 @@
     return [result[t * n : (t + 1) * n, t * m : (t + 1) * m] for t in range(TERMS)]
 
 
-def contract_z(taps, held, level, base, count):
+def contract_z(weight, held, base, count):
     totals = [None] * count
-    for t in range(TERMS):
+    for t in range(held.shape[1]):
         for j in range(count + TAPS - 1):
             plane = held[base + j, t]
             for i in range(max(0, j - TAPS + 1), min(count, j + 1)):
-                term = taps[level, t, j - i] * plane
+                term = weight(t, j - i) * plane
                 totals[i] = term if totals[i] is None else totals[i] + term
     return totals
 
@@ -568,7 +610,7 @@
             store_terms(t_fine, *fine_at[g + p], contract_y(s, y_fine, a[rows], b[rows]))
 
     def fine_block(k):
-        for i, total in enumerate(contract_z(taps, t_fine, 0, k, BLOCK)):
+        for i, total in enumerate(contract_z(lambda t, d: taps[0, t, d], t_fine, k, BLOCK)):
             fine_part[k + i] = total
 
     def sum_part(g, count):
@@ -595,8 +637,8 @@
             later.pop(0)()
 
 
-def sum_kernel(s, taps, fine, sums, first, second, x_sums, ends, y_fine, y_mid, y_coarse, out, *scratch):
-    sums_ends, t_mid, t_coarse, p_mid, p_coarse = scratch
+def sum_kernel(s, taps, fine, sums, first, second, x_sums, ends, y_fine, y_mid, y_coarse, widen_x, widen_y, out, *scratch):
+    sums_ends, t_mid, t_coarse, p_mid, p_coarse, narrow = scratch
     z, y, x = s.z, s.y, s.x
     below = s.x_routes[0].below()
     half = s.edge_sums
@@ -645,36 +687,56 @@
         mid_at += [(start + p, valid) for p in range(RADIUS)]
     for start, valid in slab_starts(s, 0, z.coarse + 5 + RADIUS):
         coarse_at += [(start + p, valid) for p in range(RADIUS)]
+    is_second = iota((s.coarse_rows, x.fine), 1) >= x.fine // TERMS
+    coarse_taps = [jnp.where(is_second, taps[2, 1, d], taps[2, 0, d]) for d in range(TAPS)]
+
     def sum_group(g, count):
         n = s.sum_rows
         a, b = along_x(g * n, count * n)
         for p in range(count):
             rows = slice(p * n, (p + 1) * n)
-            for which, (held, weights) in enumerate(((t_mid, y_mid), (t_coarse, y_coarse))):
-                at, valid = (mid_at, coarse_at)[which][g + p]
-                if at is not None:
-                    cols = slice(which * TERMS * x.fine, (which + 1) * TERMS * x.fine)
-                    store_terms(held, at, valid, contract_y(s, weights, a[rows, cols], b[rows, cols]))
+            at, valid = mid_at[g + p]
+            cols = slice(0, TERMS * x.fine)
+            store_terms(t_mid, at, valid, contract_y(s, y_mid, a[rows, cols], b[rows, cols]))
+            at, valid = coarse_at[g + p]
+            if at is not None:
+                cols = slice(TERMS * x.fine, (TERMS + 1) * x.fine)
+                joined = jnp.concatenate([a[rows, cols], b[rows, cols], a[rows, cols]], axis=0)
+                both = jnp.dot(y_coarse[...], joined, preferred_element_type=F32)
+                m = s.coarse_rows
+                store_terms(t_coarse, at, valid, [jnp.where(is_second, both[m:], both[:m])])
 
     def coarse_block(k):
         count = min(BLOCK, z.coarse_all - k)
-        for i, total in enumerate(contract_z(taps, t_coarse, 2, k, count)):
-            p_coarse[k + i] = jnp.where(z.holds_coarse(k + i - 2), total, 0.0)
+        for i, total in enumerate(contract_z(lambda t, d: coarse_taps[d], t_coarse, k, count)):
+            narrow[k + i] = jnp.where(z.holds_coarse(k + i - 2), total, 0.0)
+
+    def widen():
+        m = s.coarse_rows
+        high, low = split(narrow[...].reshape(z.coarse_all * m, x.fine))
+        joined = jnp.concatenate([high, low, high], axis=1)
+        high, low = split(jnp.dot(joined, widen_x[...], preferred_element_type=F32))
+        for p in range(z.coarse_all):
+            rows = slice(p * m, (p + 1) * m)
+            joined = jnp.concatenate([high[rows], low[rows], high[rows]], axis=0)
+            p_coarse[p] = jnp.dot(widen_y[...], joined, preferred_element_type=F32)
 
     def mid_block(k):
         count = min(BLOCK, z.mid_all - k)
-        for i, total in enumerate(contract_z(taps, t_mid, 1, k, count)):
+        for i, total in enumerate(contract_z(lambda t, d: taps[1, t, d], t_mid, k, count)):
             m = k + i - 1
             for offset, weight in WEIGHTS:
                 if (m - offset) % 2 == 0 and 0 <= (m - offset) // 2 + 2 < z.coarse_all:
                     total = total + weight * p_coarse[(m - offset) // 2 + 2]
             p_mid[k + i] = jnp.where(z.holds_mid(m), total, 0.0)
 
-    for g in range(0, s.sum_planes, 4):
-        sum_group(g, min(4, s.sum_planes - g))
+    groups = list(range(z.mid_all, s.sum_planes, 4)) + list(range(0, z.mid_all, 4))
+    for g in groups:
+        sum_group(g, min(4, s.sum_planes - g if g >= z.mid_all else z.mid_all - g))
     edges = fine_edges()
     for k in range(0, z.coarse_all, BLOCK):
         coarse_block(k)
+    widen()
     for k in range(0, z.mid_all, BLOCK):
         mid_block(k)
     lane = iota((y.fine, x.fine), 1)
@@ -729,6 +791,7 @@
             pltpu.VMEM((z.mid_all, rows, n), F32),
             pltpu.VMEM((z.mid_all, up8(y.mid + 24), n), F32),
             pltpu.VMEM((z.mid_all, rows, n), F32),
+            pltpu.VMEM((2, s.z_rows - s.z_fine, n), F32),
         ],
     )
     z_got = [route(m) for route, m in zip(s.z_routes + s.z2_routes, messages)]
@@ -737,11 +800,13 @@
         bound(operator_kernel),
         [
             array(3 * n, TERMS * n, dtype=BF16),
-            array(3 * n + 256, 2 * TERMS * n, dtype=BF16),
+            array(3 * n + 256, (TERMS + 1) * n, dtype=BF16),
             array(2 * TERMS, 3 * s.fine_groups * n, z_columns(s), dtype=BF16),
             array(TERMS * y.fine, 3 * s.fine_rows, dtype=BF16),
             array(TERMS * y.fine, 3 * s.sum_rows, dtype=BF16),
-            array(TERMS * y.fine, 3 * s.sum_rows, dtype=BF16),
+            array(TERMS * s.coarse_rows, 3 * s.sum_rows, dtype=BF16),
+            array(3 * n, n, dtype=BF16),
+            array(y.fine, 3 * s.coarse_rows, dtype=BF16),
         ],
         [kernel_taps],
     )
@@ -765,23 +830,24 @@
         [pltpu.VMEM((s.slab_planes, s.sum_rows, n), F32), pltpu.VMEM((s.far_groups, s.far_rows, n), F32)],
     )
     first, second = s.x_routes[0](first), s.x_routes[1](second)
-    x_fine, x_sums, ends, y_fine, y_mid, y_coarse = operators
+    x_fine, x_sums, ends, y_fine, y_mid, y_coarse, widen_x, widen_y = operators
     fine, sums = call(
         bound(own_kernel),
-        [array(z.fine, y.fine, n), array(s.sum_planes * s.sum_rows, 2 * TERMS * n)],
+        [array(z.fine, y.fine, n), array(s.sum_planes * s.sum_rows, (TERMS + 1) * n)],
         [kernel_taps, fine, sums, x_fine, x_sums, y_fine],
         [pltpu.VMEM((z.fine + 2 * RADIUS, TERMS, y.fine, n), F32)],
     )
     (out,) = call(
         bound(sum_kernel),
         [array(z.fine, y.fine, n)],
-        [kernel_taps, fine, sums, first, second, x_sums, ends, y_fine, y_mid, y_coarse],
+        [kernel_taps, fine, sums, first, second, x_sums, ends, y_fine, y_mid, y_coarse, widen_x, widen_y],
         [
             pltpu.VMEM((s.sum_blocks * 128, n), F32),
             pltpu.VMEM((z.mid + 2 * RADIUS + 3, TERMS, y.fine, n), F32),
-            pltpu.VMEM((z.coarse + 2 * RADIUS + 5, TERMS, y.fine, n), F32),
+            pltpu.VMEM((z.coarse + 2 * RADIUS + 5, 1, s.coarse_rows, n), F32),
             pltpu.VMEM((z.mid_all, y.fine, n), F32),
             pltpu.VMEM((z.coarse_all, y.fine, n), F32),
+            pltpu.VMEM((z.coarse_all, s.coarse_rows, n), F32),
         ],
     )
     return out

time: 32.1 us -> 30.8 us (0.960)
  Pallas kernels: 13.4 us -> 12.2 us
    pallas_call x6, Pallas kernels: 13.4 us -> 12.2 us  [call(): pl.pallas_call(kernel, out_shape=tuple(outs), in_specs=specs, out_specs=t...]
where the time goes in v6:
time: 30.8 us; the launch traced here: 30.6 us
  starting transfers between devices  12.6 us (41%)
  Pallas kernels  12.2 us (40%)
  waiting for transfers between devices  4.05 us (13%)
  local copies, waits for them, and re-layouts  1.72 us (6%)
    ppermute x8, starting transfers between devices, __call__(): return lax.ppermute(x, self.names, self.pairs)  12.6 us
    pallas_call x6, Pallas kernels, call(): pl.pallas_call(kernel, out_shape=tuple(outs), in_specs=specs, out_specs=t...  12.2 us
    ppermute x8, waiting for transfers between devices, __call__(): return lax.ppermute(x, self.names, self.pairs)  4.05 us
    unnamed x4, local copies, waits for them, and re-layouts  1.72 us
  transfers between devices with their start and end apart: 8, of which 3 were waited for; matrix products, arithmetic and copies ran while one was open for 0% of the time, Pallas kernels for 20%

profile of v6, /device:TPU:1, one launch (start us, length us, event | category | flops | bytes accessed | tf_op | source)
XLA Modules:
  0.0 30.6 jit_solution(11396007958151661824)
XLA Ops:
  0.0 0.0 copy-start
  0.0 1.0 %copy-done = f32[32,32,128]{2,1,0:T(8,128)S(1)} copy-done((f32[32,32,128]{2,1,0:T(8,128)S(1)}, f32[32,32,128]{2,1,0:T(8,128)}, u32[]{:S(2)}) %copy-start) | copy-done | bytes 524312
  1.0 1.1 %shard_map.28 = (f32[32,32,128]{2,1,0:T(8,128)S(1)}, f32[19,24,128]{2,1,0:T(8,128)S(1)}, f32[504,128]{1,0:T(8,128)S(1)}, f32[504,128]{1,0:T(8,128)S(1)}, f32[472,128]{1,0:T(8,128)S(1)}) custom-call(f32[32,32,128]{2,1,0:T(8,128)S(1)} %copy-done), custom_call_target="tpu_custom_call" | custom-call | flops 10000000 | bytes 2039808 | tf_op jit(solution)/shard_map/pallas_call | solution.py:760
  2.1 2.1 %collective-permute-start = (f32[472,128]{1,0:T(8,128)S(1)}, f32[472,128]{1,0:T(8,128)S(1)}, u32[]{:S(2)}, u32[]{:S(2)}) collective-permute-start(f32[472,128]{1,0:T(8,128)S(1)} %get-tuple-element.29), channel_id=1, source_target_pairs={{0,1},{1,0},{2,3},{3,2},{4,5},{5,4},{6,7},{7,6},{8,9},{9,8},{10,11... | collective-permute-start | bytes 725000 | tf_op jit(solution)/shard_map/ppermute | solution.py:64
  4.3 0.9 %collective-permute-start.1 = (f32[504,128]{1,0:T(8,128)S(1)}, f32[504,128]{1,0:T(8,128)S(1)}, u32[]{:S(2)}, u32[]{:S(2)}) collective-permute-start(f32[504,128]{1,0:T(8,128)S(1)} %get-tuple-element.30), channel_id=1, source_target_pairs={{0,2},{2,4},{4,6},{6,14},{14,12},{12,10},{10,8},{8,0},{16,18},{18,... | collective-permute-start | bytes 774152 | tf_op jit(solution)/shard_map/ppermute | solution.py:64
  5.2 0.5 %collective-permute-start.2 = (f32[504,128]{1,0:T(8,128)S(1)}, f32[504,128]{1,0:T(8,128)S(1)}, u32[]{:S(2)}, u32[]{:S(2)}) collective-permute-start(f32[504,128]{1,0:T(8,128)S(1)} %get-tuple-element.31), channel_id=1, source_target_pairs={{2,0},{4,2},{6,4},{14,6},{12,14},{10,12},{8,10},{0,8},{18,16},{20,... | collective-permute-start | bytes 774152 | tf_op jit(solution)/shard_map/ppermute | solution.py:64
  5.7 0.0 copy-start.1
  5.7 0.7 %copy-done.1 = f32[3,2,17]{2,1,0:T(2,128)S(1)} copy-done((f32[3,2,17]{2,1,0:T(2,128)S(1)}, f32[3,2,17]{2,1,0:T(2,128)}, u32[]{:S(2)}) %copy-start.1) | copy-done | bytes 432
  6.4 2.1 %shard_map.29 = (bf16[384,256]{1,0:T(8,128)(2,1)S(1)}, bf16[640,384]{1,0:T(8,128)(2,1)S(1)}, bf16[4,1152,256]{2,1,0:T(8,128)(2,1)S(1)}, bf16[64,144]{1,0:T(8,128...) custom-call(f32[3,2,17]{2,1,0:T(2,128)S(1)} %copy-done.1), custom_call_target="tpu_custom_call" | custom-call | flops 10000000 | bytes 3195288 | tf_op jit(solution)/shard_map/pallas_call | solution.py:760
  8.5 1.3 %collective-permute-done.refs_2_ = f32[472,128]{1,0:T(8,128)S(1)} collective-permute-done((f32[472,128]{1,0:T(8,128)S(1)}, f32[472,128]{1,0:T(8,128)S(1)}, u32[]{:S(2)}, u32[]{:S(2)}) %collective-permute-start) | collective-permute-done | bytes 241696 | tf_op jit(solution)/shard_map/ppermute | solution.py:64
  9.9 0.1 shard_map.30
  10.0 1.2 %collective-permute-start.3 = (f32[240,128]{1,0:T(8,128)S(1)}, f32[240,128]{1,0:T(8,128)S(1)}, u32[]{:S(2)}, u32[]{:S(2)}) collective-permute-start(f32[240,128]{1,0:T(8,128)S(1)} %get-tuple-element.33), channel_id=1, source_target_pairs={{0,2},{2,4},{4,6},{6,14},{14,12},{12,10},{10,8},{8,0},{16,18},{18,... | collective-permute-start | bytes 368648 | tf_op jit(solution)/shard_map/ppermute | solution.py:64
  11.2 0.2 collective-permute-start.4
  11.5 2.2 %collective-permute-start.5 = (f32[48,128]{1,0:T(8,128)S(1)}, f32[48,128]{1,0:T(8,128)S(1)}, u32[]{:S(2)}, u32[]{:S(2)}) collective-permute-start(f32[48,128]{1,0:T(8,128)S(1)} %get-tuple-element.35), channel_id=1, source_target_pairs={{0,4},{2,6},{4,0},{6,2},{1,5},{3,7},{5,1},{7,3},{8,12},{10,14},{12... | collective-permute-start | bytes 73736 | tf_op jit(solution)/shard_map/ppermute | solution.py:64
  13.6 0.0 collective-permute-done.1.refs_3_
  13.7 0.0 collective-permute-done.2.refs_4_
  13.7 1.4 %collective-permute-done.5.refs_7_ = f32[48,128]{1,0:T(8,128)S(1)} collective-permute-done((f32[48,128]{1,0:T(8,128)S(1)}, f32[48,128]{1,0:T(8,128)S(1)}, u32[]{:S(2)}, u32[]{:S(2)}) %collective-permute-start.5) | collective-permute-done | bytes 24608 | tf_op jit(solution)/shard_map/ppermute | solution.py:64
  15.0 0.0 collective-permute-done.3.refs_5_
  15.0 0.0 collective-permute-done.4.refs_6_
  15.0 0.8 %shard_map.31 = (f32[40,48,128]{2,1,0:T(8,128)S(1)}, f32[27,48,128]{2,1,0:T(8,128)S(1)}, f32[408,128]{1,0:T(8,128)S(1)}, f32[408,128]{1,0:T(8,128)S(1)}) custom-call(f32[32,32,128]{2,1,0:T(8,128)S(1)} %get-tuple-element.27.refs_0_, f32[19,24,128]{2,1,0:T(8,128)S(1)} %get-tuple-element.28.refs_1_, f32[472,128]{1,0:T(8,128)S(1)} %collective-permute-done.refs_2_, ...), custom_call_target="tpu_custom_call" | custom-call | flops 10000000 | bytes 3850240 | tf_op jit(solution)/shard_map/pallas_call | solution.py:760
  15.9 5.3 %collective-permute-start.6 = (f32[408,128]{1,0:T(8,128)S(1)}, f32[408,128]{1,0:T(8,128)S(1)}, u32[]{:S(2)}, u32[]{:S(2)}) collective-permute-start(f32[408,128]{1,0:T(8,128)S(1)} %get-tuple-element.43), channel_id=1, source_target_pairs={{0,8},{8,16},{16,24},{24,25},{25,17},{17,9},{9,1},{1,0},{2,10},{10... | collective-permute-start | bytes 626696 | tf_op jit(solution)/shard_map/ppermute | solution.py:64
  21.2 0.0 collective-permute-start.7
  21.2 3.9 %shard_map.32 = (f32[32,32,128]{2,1,0:T(8,128)S(1)}, f32[1296,384]{1,0:T(8,128)S(1)}) custom-call(f32[3,2,17]{2,1,0:T(2,128)S(1)} %copy-done.1, f32[40,48,128]{2,1,0:T(8,128)S(1)} %get-tuple-element.36.refs_1_, f32[27,48,128]{2,1,0:T(8,128)S(1)} %get-tuple-element.37.refs_2_, bf16[384,256]{1,0:T(8,128)(2,1)S(1)} %get-tuple-element.38.refs_3_, ...), custom_call_target="tpu_custom_call" | custom-call | flops 10000000 | bytes 4868504 | tf_op jit(solution)/shard_map/pallas_call | solution.py:760
  25.0 0.0 collective-permute-done.6.refs_3_
  25.1 1.3 %collective-permute-done.7.refs_4_ = f32[408,128]{1,0:T(8,128)S(1)} collective-permute-done((f32[408,128]{1,0:T(8,128)S(1)}, f32[408,128]{1,0:T(8,128)S(1)}, u32[]{:S(2)}, u32[]{:S(2)}) %collective-permute-start.7) | collective-permute-done | bytes 208928 | tf_op jit(solution)/shard_map/ppermute | solution.py:64
  26.4 4.2 %shard_map.33 = f32[32,32,128]{2,1,0:T(8,128)} custom-call(f32[3,2,17]{2,1,0:T(2,128)S(1)} %copy-done.1, f32[32,32,128]{2,1,0:T(8,128)S(1)} %get-tuple-element.41.refs_1_, f32[1296,384]{1,0:T(8,128)S(1)} %get-tuple-element.42.refs_2_, f32[408,128]{1,0:T(8,128)S(1)} %collective-permute-done.6.refs_3_, f32[408,128]{1,0:T(8,128)S(1)} %collective-permute-done.7.refs_4_, ...), custom_call_target="tpu_custom_call" | custom-call | flops 10000000 | bytes 6455704 | tf_op jit(solution)/shard_map/pallas_call | solution.py:760
Async XLA Ops:
  0.0 1.0 %copy-start = (f32[32,32,128]{2,1,0:T(8,128)S(1)}, f32[32,32,128]{2,1,0:T(8,128)}, u32[]{:S(2)}) copy-start(f32[32,32,128]{2,1,0:T(8,128)} %refs_0_.4) | copy-start | bytes 1572868
  2.1 7.7 %collective-permute-start = (f32[472,128]{1,0:T(8,128)S(1)}, f32[472,128]{1,0:T(8,128)S(1)}, u32[]{:S(2)}, u32[]{:S(2)}) collective-permute-start(f32[472,128]{1,0:T(8,128)S(1)} %get-tuple-element.29), channel_id=1, source_target_pairs={{0,1},{1,0},{2,3},{3,2},{4,5},{5,4},{6,7},{7,6},{8,9},{9,8},{10,11... | collective-permute-start | bytes 725000 | tf_op jit(solution)/shard_map/ppermute | solution.py:64
  4.3 9.4 %collective-permute-start.1 = (f32[504,128]{1,0:T(8,128)S(1)}, f32[504,128]{1,0:T(8,128)S(1)}, u32[]{:S(2)}, u32[]{:S(2)}) collective-permute-start(f32[504,128]{1,0:T(8,128)S(1)} %get-tuple-element.30), channel_id=1, source_target_pairs={{0,2},{2,4},{4,6},{6,14},{14,12},{12,10},{10,8},{8,0},{16,18},{18,... | collective-permute-start | bytes 774152 | tf_op jit(solution)/shard_map/ppermute | solution.py:64
  5.2 8.5 %collective-permute-start.2 = (f32[504,128]{1,0:T(8,128)S(1)}, f32[504,128]{1,0:T(8,128)S(1)}, u32[]{:S(2)}, u32[]{:S(2)}) collective-permute-start(f32[504,128]{1,0:T(8,128)S(1)} %get-tuple-element.31), channel_id=1, source_target_pairs={{2,0},{4,2},{6,4},{14,6},{12,14},{10,12},{8,10},{0,8},{18,16},{20,... | collective-permute-start | bytes 774152 | tf_op jit(solution)/shard_map/ppermute | solution.py:64
  5.7 0.7 %copy-start.1 = (f32[3,2,17]{2,1,0:T(2,128)S(1)}, f32[3,2,17]{2,1,0:T(2,128)}, u32[]{:S(2)}) copy-start(f32[3,2,17]{2,1,0:T(2,128)} %refs_0_.7) | copy-start | bytes 1228
  10.0 5.1 %collective-permute-start.3 = (f32[240,128]{1,0:T(8,128)S(1)}, f32[240,128]{1,0:T(8,128)S(1)}, u32[]{:S(2)}, u32[]{:S(2)}) collective-permute-start(f32[240,128]{1,0:T(8,128)S(1)} %get-tuple-element.33), channel_id=1, source_target_pairs={{0,2},{2,4},{4,6},{6,14},{14,12},{12,10},{10,8},{8,0},{16,18},{18,... | collective-permute-start | bytes 368648 | tf_op jit(solution)/shard_map/ppermute | solution.py:64
  11.2 3.8 %collective-permute-start.4 = (f32[240,128]{1,0:T(8,128)S(1)}, f32[240,128]{1,0:T(8,128)S(1)}, u32[]{:S(2)}, u32[]{:S(2)}) collective-permute-start(f32[240,128]{1,0:T(8,128)S(1)} %get-tuple-element.34), channel_id=1, source_target_pairs={{2,0},{4,2},{6,4},{14,6},{12,14},{10,12},{8,10},{0,8},{18,16},{20,... | collective-permute-start | bytes 368648 | tf_op jit(solution)/shard_map/ppermute | solution.py:64
  11.5 3.6 %collective-permute-start.5 = (f32[48,128]{1,0:T(8,128)S(1)}, f32[48,128]{1,0:T(8,128)S(1)}, u32[]{:S(2)}, u32[]{:S(2)}) collective-permute-start(f32[48,128]{1,0:T(8,128)S(1)} %get-tuple-element.35), channel_id=1, source_target_pairs={{0,4},{2,6},{4,0},{6,2},{1,5},{3,7},{5,1},{7,3},{8,12},{10,14},{12... | collective-permute-start | bytes 73736 | tf_op jit(solution)/shard_map/ppermute | solution.py:64
  15.9 9.2 %collective-permute-start.6 = (f32[408,128]{1,0:T(8,128)S(1)}, f32[408,128]{1,0:T(8,128)S(1)}, u32[]{:S(2)}, u32[]{:S(2)}) collective-permute-start(f32[408,128]{1,0:T(8,128)S(1)} %get-tuple-element.43), channel_id=1, source_target_pairs={{0,8},{8,16},{16,24},{24,25},{25,17},{17,9},{9,1},{1,0},{2,10},{10... | collective-permute-start | bytes 626696 | tf_op jit(solution)/shard_map/ppermute | solution.py:64
  21.2 5.2 %collective-permute-start.7 = (f32[408,128]{1,0:T(8,128)S(1)}, f32[408,128]{1,0:T(8,128)S(1)}, u32[]{:S(2)}, u32[]{:S(2)}) collective-permute-start(f32[408,128]{1,0:T(8,128)S(1)} %get-tuple-element.44), channel_id=1, source_target_pairs={{8,0},{16,8},{24,16},{25,24},{17,25},{9,17},{1,9},{0,1},{10,2},{18... | collective-permute-start | bytes 626696 | tf_op jit(solution)/shard_map/ppermute | solution.py:64

commit v7 on v6

--- a/solution.py
+++ b/solution.py
@@ -305,7 +305,44 @@
     far[...] = total
 
 
-def collect_kernel(s, nz, nz2, charges, own, *rest):
+def roll_ends(s, plane_rows, count):
+    x = s.x
+    lane = iota((count, x.fine), 1)
+    for g in range(s.fine_groups):
+        ends = [jnp.zeros(lane.shape, F32)] * 2
+        for j in range(min(s.side, s.fine_planes - g * s.side)):
+            plane = plane_rows(g * s.side + j)
+            here = (lane >= RADIUS * j) & (lane < RADIUS * (j + 1))
+            for n, start in enumerate((x.fine - RADIUS, 0)):
+                shift = (RADIUS * j - start) % x.fine
+                ends[n] = jnp.where(here, pltpu.roll(plane, shift, 1) if shift else plane, ends[n])
+        yield g, ends
+
+
+def early_kernel(s, nz, charges, *rest):
+    z_messages = rest[:nz]
+    x_fine, y_own, t_part, last, start, slab = rest[nz:]
+    z, y, x = s.z, s.y, s.x
+    for n, message in enumerate(z_messages):
+        slab[n * RADIUS : (n + 1) * RADIUS] = message[: s.z_fine].reshape(RADIUS, y.fine, x.fine)
+
+    def rows_of(p):
+        return charges[p] if p < z.fine else slab[p - z.fine]
+
+    t_part[...] = jnp.zeros(t_part.shape, F32)
+    fine_at = fine_places(s)
+    for g in range(0, s.fine_planes, 8):
+        planes = charges[g : g + 8] if g < z.fine else slab[g - z.fine : g - z.fine + 8]
+        a, b = split(contract_x(s, planes.reshape(8 * y.fine, x.fine), x_fine))
+        for p in range(8):
+            rows = slice(p * y.fine, (p + 1) * y.fine)
+            store_terms(t_part, *fine_at[g + p], contract_y(s, y_own, a[rows], b[rows]))
+    for g, ends in roll_ends(s, rows_of, y.fine):
+        rows = slice(g * y.fine, (g + 1) * y.fine)
+        last[rows], start[rows] = ends
+
+
+def collect_kernel(s, nz, nz2, last, start, own, *rest):
     z_messages, z2_messages = rest[:nz], rest[nz : nz + nz2]
     rest = rest[nz + nz2 :]
     pairs = rest[:4]
@@ -318,18 +355,11 @@
         a, b = (message[start : start + count] for message in pairs[2 * which : 2 * which + 2])
         return jnp.where(below, a, b), jnp.where(below, b, a)
 
-    def fine_planes(at, count, body, which, row):
+    parts = [(0, z.fine, 0, 0)] + [(z.fine + n * RADIUS, RADIUS, 1, n * RADIUS * RADIUS) for n in range(nz)]
+    for at, count, which, row in parts:
         low, high = sides(which, row, RADIUS * count)
-        fine[at : at + count, : y.fine] = body
-        fine[at : at + count, y.fine : y.fine + RADIUS] = low.reshape(count, RADIUS, x.fine)
-        fine[at : at + count, y.fine + RADIUS :] = high.reshape(count, RADIUS, x.fine)
-
-    fine_planes(0, z.fine, charges[...], 0, 0)
-    at = z.fine
-    for n, z_message in enumerate(z_messages):
-        slab = z_message[: s.z_fine].reshape(RADIUS, y.fine, x.fine)
-        fine_planes(at, RADIUS, slab, 1, n * RADIUS * RADIUS)
-        at += RADIUS
+        fine[at : at + count, :RADIUS] = low.reshape(count, RADIUS, x.fine)
+        fine[at : at + count, RADIUS:] = high.reshape(count, RADIUS, x.fine)
     sums[...] = jnp.zeros(sums.shape, F32)
     raw[...] = jnp.zeros(raw.shape, F32)
     for g in range(s.far_groups):
@@ -373,23 +403,19 @@
             sums[at] = sums[at] + jnp.where(is_mid, 0.0, raw[base + number(lower, SPAN - 5, 0) + i])
     for n, route in enumerate(s.z2_routes):
         base = len(s.z_routes) * SPAN + n * z.second
-        start = z.mid_all + number(route.below(), RADIUS - z.coarse, RADIUS + z.coarse - 5)
+        at = z.mid_all + number(route.below(), RADIUS - z.coarse, RADIUS + z.coarse - 5)
         for p in range(z.second):
-            sums[start + p] = sums[start + p] + jnp.where(is_mid, 0.0, raw[base + p])
+            sums[at + p] = sums[at + p] + jnp.where(is_mid, 0.0, raw[base + p])
 
     up = s.x_routes[0].up()
-    lane = iota((s.fine_rows, x.fine), 1)
-    for g in range(s.fine_groups):
-        ends = [jnp.zeros(lane.shape, F32)] * 2
-        for j in range(min(s.side, s.fine_planes - g * s.side)):
-            plane = fine[g * s.side + j]
-            here = (lane >= RADIUS * j) & (lane < RADIUS * (j + 1))
-            for n, start in enumerate((x.fine - RADIUS, 0)):
-                shift = (RADIUS * j - start) % x.fine
-                ends[n] = jnp.where(here, pltpu.roll(plane, shift, 1) if shift else plane, ends[n])
-        rows = slice(g * s.fine_rows, (g + 1) * s.fine_rows)
-        first[rows] = jnp.where(up, ends[0], ends[1])
-        second[rows] = jnp.where(up, ends[1], ends[0])
+    for g, ends in roll_ends(s, lambda p: fine[p], 2 * RADIUS):
+        rows = slice(g * y.fine, (g + 1) * y.fine)
+        at = slice(g * s.fine_rows, g * s.fine_rows + y.fine)
+        first[at] = jnp.where(up, last[rows], start[rows])
+        second[at] = jnp.where(up, start[rows], last[rows])
+        at = slice(g * s.fine_rows + y.fine, (g + 1) * s.fine_rows)
+        first[at] = jnp.where(up, ends[0], ends[1])
+        second[at] = jnp.where(up, ends[1], ends[0])
     width = EDGE + SPAN
     row, lane = iota((2 * width, x.fine), 0), iota((2 * width, x.fine), 1)
     is_first = row < width
@@ -433,8 +459,15 @@
     return x.index() < x.count - 1
 
 
-def operator_kernel(s, taps, x_fine, x_sums, ends, y_fine, y_mid, y_coarse, widen_x, widen_y):
+def operator_kernel(s, taps, x_fine, x_sums, ends, y_own, y_edge, y_fine, y_mid, y_coarse, widen_x, widen_y, table):
     y, x = s.y, s.x
+    for level in range(2):
+        for term in range(TERMS):
+            for tap in range(TAPS):
+                table[(level * TERMS + term) * TAPS + tap] = jnp.full((8, x.fine), taps[level, term, tap], F32)
+    is_second = iota((8, x.fine), 1) >= x.fine // TERMS
+    for tap in range(TAPS):
+        table[2 * TERMS * TAPS + tap] = jnp.where(is_second, taps[2, 1, tap], taps[2, 0, tap])
     own, edge = x.fine, 64
     shape = (own + edge, x.fine)
     row, lane = iota(shape, 0), iota(shape, 1)
@@ -529,6 +562,11 @@
     where = jnp.where(is_low, c - y.fine - RADIUS, jnp.where(is_high, c - RADIUS, c))
     valid = choose(is_low, lower, choose(is_high, higher, c >= 0))
     write(y_fine, s.fine_rows, band(taps, 0, where - iota(c.shape, 0), valid))
+    c = columns_of(y.fine, y.fine)
+    write(y_own, y.fine, band(taps, 0, c - iota(c.shape, 0), c >= 0))
+    c = columns_of(y.fine, 2 * RADIUS)
+    where = jnp.where(c < RADIUS, c - RADIUS, c - RADIUS + y.fine)
+    write(y_edge, 2 * RADIUS, band(taps, 0, where - iota(c.shape, 0), choose(c < RADIUS, lower, higher)))
 
     c = columns_of(n, s.sum_rows)
     r = iota(c.shape, 0)
@@ -561,15 +599,16 @@
     return [result[t * n : (t + 1) * n, t * m : (t + 1) * m] for t in range(TERMS)]
 
 
-def contract_z(weight, held, base, count):
+def contract_z(table, level, held, base, count):
+    rows = held.shape[2:]
     totals = [None] * count
     for t in range(held.shape[1]):
         for j in range(count + TAPS - 1):
-            plane = held[base + j, t]
+            plane = held[base + j, t].reshape(rows[0] // 8, 8, rows[1])
             for i in range(max(0, j - TAPS + 1), min(count, j + 1)):
-                term = weight(t, j - i) * plane
+                term = table[(level * TERMS + t) * TAPS + j - i][None] * plane
                 totals[i] = term if totals[i] is None else totals[i] + term
-    return totals
+    return [total.reshape(rows) for total in totals]
 
 
 def slab_starts(s, below_at, above_at):
@@ -589,34 +628,41 @@
 BLOCK = 4
 
 
-def own_kernel(s, taps, fine, sums, x_fine, x_sums, y_fine, fine_part, sums_part, t_fine):
+def fine_places(s):
+    places = [(RADIUS + p, None) for p in range(s.z.fine)]
+    for start, valid in slab_starts(s, 0, s.z.fine + RADIUS):
+        places += [(start + p, valid) for p in range(RADIUS)]
+    return places
+
+
+def contract_x(s, grid, weights):
+    high, low = split(grid)
+    joined = jnp.concatenate([high, low, high], axis=1)
+    return jnp.dot(joined, weights[: 3 * s.x.fine], preferred_element_type=F32)
+
+
+def own_kernel(s, table, t_part, fine, sums, x_fine, x_sums, y_edge, fine_part, sums_part, t_fine):
     z, x = s.z, s.x
-
-    def along_x(grid, weights):
-        high, low = split(grid)
-        joined = jnp.concatenate([high, low, high], axis=1)
-        return jnp.dot(joined, weights[: 3 * x.fine], preferred_element_type=F32)
-
-    t_fine[...] = jnp.zeros(t_fine.shape, F32)
-    fine_at = [(RADIUS + p, None) for p in range(z.fine)]
-    for start, valid in slab_starts(s, 0, z.fine + RADIUS):
-        fine_at += [(start + p, valid) for p in range(RADIUS)]
+    t_fine[...] = t_part[...]
+    fine_at = fine_places(s)
 
     def fine_group(g, count):
-        n = s.fine_rows
-        a, b = split(along_x(fine[g : g + count].reshape(count * n, x.fine), x_fine))
+        n = 2 * RADIUS
+        a, b = split(contract_x(s, fine[g : g + count].reshape(count * n, x.fine), x_fine))
         for p in range(count):
             rows = slice(p * n, (p + 1) * n)
-            store_terms(t_fine, *fine_at[g + p], contract_y(s, y_fine, a[rows], b[rows]))
+            at, valid = fine_at[g + p]
+            for t, part in enumerate(contract_y(s, y_edge, a[rows], b[rows])):
+                t_fine[at, t] = t_fine[at, t] + (part if valid is None else jnp.where(valid, part, 0.0))
 
     def fine_block(k):
-        for i, total in enumerate(contract_z(lambda t, d: taps[0, t, d], t_fine, k, BLOCK)):
+        for i, total in enumerate(contract_z(table, 0, t_fine, k, BLOCK)):
             fine_part[k + i] = total
 
     def sum_part(g, count):
         n = s.sum_rows
         grid = sums[g : g + count].reshape(count * n, x.fine)
-        sums_part[g * n : (g + count) * n] = along_x(grid, x_sums)
+        sums_part[g * n : (g + count) * n] = contract_x(s, grid, x_sums)
 
     later = []
     done = 0
@@ -637,8 +683,8 @@
             later.pop(0)()
 
 
-def sum_kernel(s, taps, fine, sums, first, second, x_sums, ends, y_fine, y_mid, y_coarse, widen_x, widen_y, out, *scratch):
-    sums_ends, t_mid, t_coarse, p_mid, p_coarse, narrow = scratch
+def sum_kernel(s, table, fine, sums, first, second, x_sums, ends, y_fine, y_mid, y_coarse, widen_x, widen_y, result, *scratch):
+    sums_ends, t_mid, t_coarse, p_mid, p_coarse, narrow, out, left = scratch
     z, y, x = s.z, s.y, s.x
     below = s.x_routes[0].below()
     half = s.edge_sums
@@ -688,7 +734,6 @@
     for start, valid in slab_starts(s, 0, z.coarse + 5 + RADIUS):
         coarse_at += [(start + p, valid) for p in range(RADIUS)]
     is_second = iota((s.coarse_rows, x.fine), 1) >= x.fine // TERMS
-    coarse_taps = [jnp.where(is_second, taps[2, 1, d], taps[2, 0, d]) for d in range(TAPS)]
 
     def sum_group(g, count):
         n = s.sum_rows
@@ -708,7 +753,7 @@
 
     def coarse_block(k):
         count = min(BLOCK, z.coarse_all - k)
-        for i, total in enumerate(contract_z(lambda t, d: coarse_taps[d], t_coarse, k, count)):
+        for i, total in enumerate(contract_z(table, 2, t_coarse, k, count)):
             narrow[k + i] = jnp.where(z.holds_coarse(k + i - 2), total, 0.0)
 
     def widen():
@@ -723,7 +768,7 @@
 
     def mid_block(k):
         count = min(BLOCK, z.mid_all - k)
-        for i, total in enumerate(contract_z(lambda t, d: taps[1, t, d], t_mid, k, count)):
+        for i, total in enumerate(contract_z(table, 1, t_mid, k, count)):
             m = k + i - 1
             for offset, weight in WEIGHTS:
                 if (m - offset) % 2 == 0 and 0 <= (m - offset) // 2 + 2 < z.coarse_all:
@@ -737,10 +782,9 @@
     for k in range(0, z.coarse_all, BLOCK):
         coarse_block(k)
     widen()
-    for k in range(0, z.mid_all, BLOCK):
-        mid_block(k)
     lane = iota((y.fine, x.fine), 1)
-    for k in range(z.fine):
+
+    def finish(k):
         total = fine[k]
         for offset, weight in WEIGHTS:
             if (k - offset) % 2 == 0:
@@ -750,18 +794,31 @@
         low = pltpu.roll(low, -at % x.fine, 1) if at else low
         turn = (x.fine - RADIUS - at) % x.fine
         high = pltpu.roll(high, turn, 1) if turn else high
-        total = total + jnp.where(lane < RADIUS, low, jnp.where(lane >= x.fine - RADIUS, high, 0.0))
-        out[k] = total
-
-
-def call(kernel, outs, ins, scratch=(), flops=10**7):
+        out[k] = total + jnp.where(lane < RADIUS, low, jnp.where(lane >= x.fine - RADIUS, high, 0.0))
+
+    done, copies = 0, []
+    for k in range(0, z.mid_all, BLOCK):
+        mid_block(k)
+        ready = z.fine if k + BLOCK >= z.mid_all else 2 * k + 2
+        while done < ready:
+            finish(done)
+            done += 1
+            if done % 8 == 0:
+                part = pl.ds(done - 8, 8)
+                copies.append(pltpu.make_async_copy(out.at[part], result.at[part], left.at[done // 8 - 1]))
+                copies[-1].start()
+    for copy in copies:
+        copy.wait()
+
+
+def call(kernel, outs, ins, scratch=(), flops=10**7, out_space=pltpu.VMEM):
     specs = [SMEM if a.ndim == 3 and a.shape[-1] == TAPS else VMEM for a in ins]
     size = sum(a.size * a.dtype.itemsize for a in ins) + sum(o.size * o.dtype.itemsize for o in outs)
     return pl.pallas_call(
         kernel,
         out_shape=tuple(outs),
         in_specs=specs,
-        out_specs=tuple(VMEM for _ in outs),
+        out_specs=tuple(pl.BlockSpec(memory_space=out_space) for _ in outs),
         scratch_shapes=list(scratch),
         compiler_params=PARAMS,
         cost_estimate=pl.CostEstimate(flops=flops, bytes_accessed=size, transcendentals=0),
@@ -802,11 +859,14 @@
             array(3 * n, TERMS * n, dtype=BF16),
             array(3 * n + 256, (TERMS + 1) * n, dtype=BF16),
             array(2 * TERMS, 3 * s.fine_groups * n, z_columns(s), dtype=BF16),
+            array(TERMS * y.fine, 3 * y.fine, dtype=BF16),
+            array(TERMS * y.fine, 6 * RADIUS, dtype=BF16),
             array(TERMS * y.fine, 3 * s.fine_rows, dtype=BF16),
             array(TERMS * y.fine, 3 * s.sum_rows, dtype=BF16),
             array(TERMS * s.coarse_rows, 3 * s.sum_rows, dtype=BF16),
             array(3 * n, n, dtype=BF16),
             array(y.fine, 3 * s.coarse_rows, dtype=BF16),
+            array((2 * TERMS + 1) * TAPS, 8, n),
         ],
         [kernel_taps],
     )
@@ -818,29 +878,35 @@
     )
     sides += [s.y_routes[0](ahead), s.y_routes[1](behind)]
     far = s.y2_routes[0](far)
+    x_fine, x_sums, ends, y_own, y_edge, y_fine, y_mid, y_coarse, widen_x, widen_y, table = operators
+    t_part, last, start = call(
+        bound(early_kernel, nz),
+        [array(z.fine + 2 * RADIUS, TERMS, y.fine, n)] + [array(s.fine_groups * y.fine, n)] * 2,
+        [held, *z_got[:nz], x_fine, y_own],
+        [pltpu.VMEM((nz * RADIUS, y.fine, n), F32)],
+    )
     fine, sums, first, second = call(
         bound(collect_kernel, nz, nz2),
         [
-            array(s.fine_planes, s.fine_rows, n),
+            array(s.fine_planes, 2 * RADIUS, n),
             array(s.sum_planes, s.sum_rows, n),
             array(s.x_rows, n),
             array(s.x_rows, n),
         ],
-        [held, own, *z_got, *sides, far],
+        [last, start, own, *z_got, *sides, far],
         [pltpu.VMEM((s.slab_planes, s.sum_rows, n), F32), pltpu.VMEM((s.far_groups, s.far_rows, n), F32)],
     )
     first, second = s.x_routes[0](first), s.x_routes[1](second)
-    x_fine, x_sums, ends, y_fine, y_mid, y_coarse, widen_x, widen_y = operators
     fine, sums = call(
         bound(own_kernel),
         [array(z.fine, y.fine, n), array(s.sum_planes * s.sum_rows, (TERMS + 1) * n)],
-        [kernel_taps, fine, sums, x_fine, x_sums, y_fine],
+        [table, t_part, fine, sums, x_fine, x_sums, y_edge],
         [pltpu.VMEM((z.fine + 2 * RADIUS, TERMS, y.fine, n), F32)],
     )
     (out,) = call(
         bound(sum_kernel),
         [array(z.fine, y.fine, n)],
-        [kernel_taps, fine, sums, first, second, x_sums, ends, y_fine, y_mid, y_coarse, widen_x, widen_y],
+        [table, fine, sums, first, second, x_sums, ends, y_fine, y_mid, y_coarse, widen_x, widen_y],
         [
             pltpu.VMEM((s.sum_blocks * 128, n), F32),
             pltpu.VMEM((z.mid + 2 * RADIUS + 3, TERMS, y.fine, n), F32),
@@ -848,7 +914,10 @@
             pltpu.VMEM((z.mid_all, y.fine, n), F32),
             pltpu.VMEM((z.coarse_all, y.fine, n), F32),
             pltpu.VMEM((z.coarse_all, s.coarse_rows, n), F32),
+            pltpu.VMEM((z.fine, y.fine, n), F32),
+            pltpu.SemaphoreType.DMA((z.fine // 8,)),
         ],
+        out_space=pltpu.HBM,
     )
     return out
 

time: 30.8 us -> 30.1 us (0.977)
  waiting for transfers between devices: 4.05 us -> 3.46 us
    ppermute x8, waiting for transfers between devices: 4.05 us -> 3.46 us  [__call__(): return lax.ppermute(x, self.names, self.pairs)]
    pallas_call x6 -> x7, Pallas kernels: 12.2 us -> 12.1 us  [call(): pl.pallas_call(kernel, out_shape=tuple(outs), in_specs=specs, out_specs=t...]
  transfers between devices with their start and end apart: 8 -> 8, of which waited for: 3 -> 3; matrix products, arithmetic and copies ran while one was open for 0% -> 0% of each run, Pallas kernels for 20% -> 22%
where the time goes in v7:
time: 30.1 us; the launch traced here: 30 us
  starting transfers between devices  12.6 us (42%)
  Pallas kernels  12.1 us (40%)
  waiting for transfers between devices  3.46 us (11%)
  local copies, waits for them, and re-layouts  1.72 us (6%)
    ppermute x8, starting transfers between devices, __call__(): return lax.ppermute(x, self.names, self.pairs)  12.6 us
    pallas_call x7, Pallas kernels, call(): pl.pallas_call(kernel, out_shape=tuple(outs), in_specs=specs, out_specs=t...  12.1 us
    ppermute x8, waiting for transfers between devices, __call__(): return lax.ppermute(x, self.names, self.pairs)  3.46 us
    unnamed x4, local copies, waits for them, and re-layouts  1.72 us
  transfers between devices with their start and end apart: 8, of which 3 were waited for; matrix products, arithmetic and copies ran while one was open for 0% of the time, Pallas kernels for 22%

profile of v7, /device:TPU:1, one launch (start us, length us, event | category | flops | bytes accessed | tf_op | source)
XLA Modules:
  0.0 30.0 jit_solution(4932450386343576426)
XLA Ops:
  0.0 0.0 copy-start
  0.0 1.0 %copy-done = f32[32,32,128]{2,1,0:T(8,128)S(1)} copy-done((f32[32,32,128]{2,1,0:T(8,128)S(1)}, f32[32,32,128]{2,1,0:T(8,128)}, u32[]{:S(2)}) %copy-start) | copy-done | bytes 524312
  1.0 1.1 %shard_map.29 = (f32[32,32,128]{2,1,0:T(8,128)S(1)}, f32[19,24,128]{2,1,0:T(8,128)S(1)}, f32[504,128]{1,0:T(8,128)S(1)}, f32[504,128]{1,0:T(8,128)S(1)}, f32[472,128]{1,0:T(8,128)S(1)}) custom-call(f32[32,32,128]{2,1,0:T(8,128)S(1)} %copy-done), custom_call_target="tpu_custom_call" | custom-call | flops 10000000 | bytes 2039808 | tf_op jit(solution)/shard_map/pallas_call | solution.py:817
  2.1 2.1 %collective-permute-start = (f32[472,128]{1,0:T(8,128)S(1)}, f32[472,128]{1,0:T(8,128)S(1)}, u32[]{:S(2)}, u32[]{:S(2)}) collective-permute-start(f32[472,128]{1,0:T(8,128)S(1)} %get-tuple-element.35), channel_id=1, source_target_pairs={{0,1},{1,0},{2,3},{3,2},{4,5},{5,4},{6,7},{7,6},{8,9},{9,8},{10,11... | collective-permute-start | bytes 725000 | tf_op jit(solution)/shard_map/ppermute | solution.py:64
  4.2 1.0 %collective-permute-start.1 = (f32[504,128]{1,0:T(8,128)S(1)}, f32[504,128]{1,0:T(8,128)S(1)}, u32[]{:S(2)}, u32[]{:S(2)}) collective-permute-start(f32[504,128]{1,0:T(8,128)S(1)} %get-tuple-element.42), channel_id=1, source_target_pairs={{0,2},{2,4},{4,6},{6,14},{14,12},{12,10},{10,8},{8,0},{16,18},{18,... | collective-permute-start | bytes 774152 | tf_op jit(solution)/shard_map/ppermute | solution.py:64
  5.2 0.5 %collective-permute-start.2 = (f32[504,128]{1,0:T(8,128)S(1)}, f32[504,128]{1,0:T(8,128)S(1)}, u32[]{:S(2)}, u32[]{:S(2)}) collective-permute-start(f32[504,128]{1,0:T(8,128)S(1)} %get-tuple-element.43), channel_id=1, source_target_pairs={{2,0},{4,2},{6,4},{14,6},{12,14},{10,12},{8,10},{0,8},{18,16},{20,... | collective-permute-start | bytes 774152 | tf_op jit(solution)/shard_map/ppermute | solution.py:64
  5.7 0.0 copy-start.1
  5.7 0.7 %copy-done.1 = f32[3,2,17]{2,1,0:T(2,128)S(1)} copy-done((f32[3,2,17]{2,1,0:T(2,128)S(1)}, f32[3,2,17]{2,1,0:T(2,128)}, u32[]{:S(2)}) %copy-start.1) | copy-done | bytes 432
  6.4 2.2 %shard_map.28 = (bf16[384,256]{1,0:T(8,128)(2,1)S(1)}, bf16[640,384]{1,0:T(8,128)(2,1)S(1)}, bf16[4,1152,256]{2,1,0:T(8,128)(2,1)S(1)}, bf16[64,96]{1,0:T(8,128)...) custom-call(f32[3,2,17]{2,1,0:T(2,128)S(1)} %copy-done.1), custom_call_target="tpu_custom_call" | custom-call | flops 10000000 | bytes 3561880 | tf_op jit(solution)/shard_map/pallas_call | solution.py:817
  8.6 1.3 %collective-permute-done.refs_1_.refs_2_.refs_3_ = f32[472,128]{1,0:T(8,128)S(1)} collective-permute-done((f32[472,128]{1,0:T(8,128)S(1)}, f32[472,128]{1,0:T(8,128)S(1)}, u32[]{:S(2)}, u32[]{:S(2)}) %collective-permute-start) | collective-permute-done | bytes 241696 | tf_op jit(solution)/shard_map/ppermute | solution.py:64
  9.8 0.1 shard_map.31
  9.9 1.3 %collective-permute-start.3 = (f32[240,128]{1,0:T(8,128)S(1)}, f32[240,128]{1,0:T(8,128)S(1)}, u32[]{:S(2)}, u32[]{:S(2)}) collective-permute-start(f32[240,128]{1,0:T(8,128)S(1)} %get-tuple-element.44), channel_id=1, source_target_pairs={{0,2},{2,4},{4,6},{6,14},{14,12},{12,10},{10,8},{8,0},{16,18},{18,... | collective-permute-start | bytes 368648 | tf_op jit(solution)/shard_map/ppermute | solution.py:64
  11.2 0.2 collective-permute-start.4
  11.4 2.2 %collective-permute-start.5 = (f32[48,128]{1,0:T(8,128)S(1)}, f32[48,128]{1,0:T(8,128)S(1)}, u32[]{:S(2)}, u32[]{:S(2)}) collective-permute-start(f32[48,128]{1,0:T(8,128)S(1)} %get-tuple-element.46), channel_id=1, source_target_pairs={{0,4},{2,6},{4,0},{6,2},{1,5},{3,7},{5,1},{7,3},{8,12},{10,14},{12... | collective-permute-start | bytes 73736 | tf_op jit(solution)/shard_map/ppermute | solution.py:64
  13.6 1.3 %shard_map.30 = (f32[48,2,32,128]{3,2,1,0:T(8,128)S(1)}, f32[96,128]{1,0:T(8,128)S(1)}, f32[96,128]{1,0:T(8,128)S(1)}) custom-call(f32[32,32,128]{2,1,0:T(8,128)S(1)} %get-tuple-element.34.refs_0_, f32[472,128]{1,0:T(8,128)S(1)} %collective-permute-done.refs_1_.refs_2_.refs_3_, bf16[384,256]{1,0:T(8,128)(2,1)S(1)} %get-tuple-element.36.refs_2_.refs_4_, ...), custom_call_target="tpu_custom_call" | custom-call | flops 10000000 | bytes 2646016 | tf_op jit(solution)/shard_map/pallas_call | solution.py:817
  14.9 0.0 collective-permute-done.1.refs_4_
  14.9 0.0 collective-permute-done.2.refs_5_
  14.9 0.1 collective-permute-done.5.refs_8_
  15.0 0.0 collective-permute-done.3.refs_6_
  15.0 0.0 collective-permute-done.4.refs_7_
  15.0 0.7 %shard_map.32 = (f32[40,16,128]{2,1,0:T(8,128)S(1)}, f32[27,48,128]{2,1,0:T(8,128)S(1)}, f32[408,128]{1,0:T(8,128)S(1)}, f32[408,128]{1,0:T(8,128)S(1)}) custom-call(f32[96,128]{1,0:T(8,128)S(1)} %get-tuple-element.39.refs_0_, f32[96,128]{1,0:T(8,128)S(1)} %get-tuple-element.40.refs_1_, f32[19,24,128]{2,1,0:T(8,128)S(1)} %get-tuple-element.41.refs_1_.refs_2_, ...), custom_call_target="tpu_custom_call" | custom-call | flops 10000000 | bytes 2768896 | tf_op jit(solution)/shard_map/pallas_call | solution.py:817
  15.7 5.3 %collective-permute-start.6 = (f32[408,128]{1,0:T(8,128)S(1)}, f32[408,128]{1,0:T(8,128)S(1)}, u32[]{:S(2)}, u32[]{:S(2)}) collective-permute-start(f32[408,128]{1,0:T(8,128)S(1)} %get-tuple-element.53), channel_id=1, source_target_pairs={{0,8},{8,16},{16,24},{24,25},{25,17},{17,9},{9,1},{1,0},{2,10},{10... | collective-permute-start | bytes 626696 | tf_op jit(solution)/shard_map/ppermute | solution.py:64
  21.0 0.0 collective-permute-start.7
  21.0 3.1 %shard_map.33 = (f32[32,32,128]{2,1,0:T(8,128)S(1)}, f32[1296,384]{1,0:T(8,128)S(1)}) custom-call(f32[85,8,128]{2,1,0:T(8,128)S(1)} %get-tuple-element.33.refs_0_, f32[48,2,32,128]{3,2,1,0:T(8,128)S(1)} %get-tuple-element.38.refs_1_, f32[40,16,128]{2,1,0:T(8,128)S(1)} %get-tuple-element.47.refs_2_, f32[27,48,128]{2,1,0:T(8,128)S(1)} %get-tuple-element.48.refs_3_, ...), custom_call_target="tpu_custom_call" | custom-call | flops 10000000 | bytes 6121472 | tf_op jit(solution)/shard_map/pallas_call | solution.py:817
  24.1 0.0 collective-permute-done.6.refs_3_
  24.1 2.1 %collective-permute-done.7.refs_4_ = f32[408,128]{1,0:T(8,128)S(1)} collective-permute-done((f32[408,128]{1,0:T(8,128)S(1)}, f32[408,128]{1,0:T(8,128)S(1)}, u32[]{:S(2)}, u32[]{:S(2)}) %collective-permute-start.7) | collective-permute-done | bytes 208928 | tf_op jit(solution)/shard_map/ppermute | solution.py:64
  26.2 3.7 %shard_map.34 = f32[32,32,128]{2,1,0:T(8,128)} custom-call(f32[85,8,128]{2,1,0:T(8,128)S(1)} %get-tuple-element.33.refs_0_, f32[32,32,128]{2,1,0:T(8,128)S(1)} %get-tuple-element.51.refs_1_, f32[1296,384]{1,0:T(8,128)S(1)} %get-tuple-element.52.refs_2_, f32[408,128]{1,0:T(8,128)S(1)} %collective-permute-done.6.refs_3_, ...), custom_call_target="tpu_custom_call" | custom-call | flops 10000000 | bytes 6803456 | tf_op jit(solution)/shard_map/pallas_call | solution.py:817
Async XLA Ops:
  0.0 1.0 %copy-start = (f32[32,32,128]{2,1,0:T(8,128)S(1)}, f32[32,32,128]{2,1,0:T(8,128)}, u32[]{:S(2)}) copy-start(f32[32,32,128]{2,1,0:T(8,128)} %refs_0_.3) | copy-start | bytes 1572868
  2.1 7.7 %collective-permute-start = (f32[472,128]{1,0:T(8,128)S(1)}, f32[472,128]{1,0:T(8,128)S(1)}, u32[]{:S(2)}, u32[]{:S(2)}) collective-permute-start(f32[472,128]{1,0:T(8,128)S(1)} %get-tuple-element.35), channel_id=1, source_target_pairs={{0,1},{1,0},{2,3},{3,2},{4,5},{5,4},{6,7},{7,6},{8,9},{9,8},{10,11... | collective-permute-start | bytes 725000 | tf_op jit(solution)/shard_map/ppermute | solution.py:64
  4.2 10.7 %collective-permute-start.1 = (f32[504,128]{1,0:T(8,128)S(1)}, f32[504,128]{1,0:T(8,128)S(1)}, u32[]{:S(2)}, u32[]{:S(2)}) collective-permute-start(f32[504,128]{1,0:T(8,128)S(1)} %get-tuple-element.42), channel_id=1, source_target_pairs={{0,2},{2,4},{4,6},{6,14},{14,12},{12,10},{10,8},{8,0},{16,18},{18,... | collective-permute-start | bytes 774152 | tf_op jit(solution)/shard_map/ppermute | solution.py:64
  5.2 9.7 %collective-permute-start.2 = (f32[504,128]{1,0:T(8,128)S(1)}, f32[504,128]{1,0:T(8,128)S(1)}, u32[]{:S(2)}, u32[]{:S(2)}) collective-permute-start(f32[504,128]{1,0:T(8,128)S(1)} %get-tuple-element.43), channel_id=1, source_target_pairs={{2,0},{4,2},{6,4},{14,6},{12,14},{10,12},{8,10},{0,8},{18,16},{20,... | collective-permute-start | bytes 774152 | tf_op jit(solution)/shard_map/ppermute | solution.py:64
  5.7 0.7 %copy-start.1 = (f32[3,2,17]{2,1,0:T(2,128)S(1)}, f32[3,2,17]{2,1,0:T(2,128)}, u32[]{:S(2)}) copy-start(f32[3,2,17]{2,1,0:T(2,128)} %refs_0_.2) | copy-start | bytes 1228
  9.9 5.1 %collective-permute-start.3 = (f32[240,128]{1,0:T(8,128)S(1)}, f32[240,128]{1,0:T(8,128)S(1)}, u32[]{:S(2)}, u32[]{:S(2)}) collective-permute-start(f32[240,128]{1,0:T(8,128)S(1)} %get-tuple-element.44), channel_id=1, source_target_pairs={{0,2},{2,4},{4,6},{6,14},{14,12},{12,10},{10,8},{8,0},{16,18},{18,... | collective-permute-start | bytes 368648 | tf_op jit(solution)/shard_map/ppermute | solution.py:64
  11.2 3.8 %collective-permute-start.4 = (f32[240,128]{1,0:T(8,128)S(1)}, f32[240,128]{1,0:T(8,128)S(1)}, u32[]{:S(2)}, u32[]{:S(2)}) collective-permute-start(f32[240,128]{1,0:T(8,128)S(1)} %get-tuple-element.45), channel_id=1, source_target_pairs={{2,0},{4,2},{6,4},{14,6},{12,14},{10,12},{8,10},{0,8},{18,16},{20,... | collective-permute-start | bytes 368648 | tf_op jit(solution)/shard_map/ppermute | solution.py:64
  11.4 3.6 %collective-permute-start.5 = (f32[48,128]{1,0:T(8,128)S(1)}, f32[48,128]{1,0:T(8,128)S(1)}, u32[]{:S(2)}, u32[]{:S(2)}) collective-permute-start(f32[48,128]{1,0:T(8,128)S(1)} %get-tuple-element.46), channel_id=1, source_target_pairs={{0,4},{2,6},{4,0},{6,2},{1,5},{3,7},{5,1},{7,3},{8,12},{10,14},{12... | collective-permute-start | bytes 73736 | tf_op jit(solution)/shard_map/ppermute | solution.py:64
  15.7 8.4 %collective-permute-start.6 = (f32[408,128]{1,0:T(8,128)S(1)}, f32[408,128]{1,0:T(8,128)S(1)}, u32[]{:S(2)}, u32[]{:S(2)}) collective-permute-start(f32[408,128]{1,0:T(8,128)S(1)} %get-tuple-element.53), channel_id=1, source_target_pairs={{0,8},{8,16},{16,24},{24,25},{25,17},{17,9},{9,1},{1,0},{2,10},{10... | collective-permute-start | bytes 626696 | tf_op jit(solution)/shard_map/ppermute | solution.py:64
  21.0 5.2 %collective-permute-start.7 = (f32[408,128]{1,0:T(8,128)S(1)}, f32[408,128]{1,0:T(8,128)S(1)}, u32[]{:S(2)}, u32[]{:S(2)}) collective-permute-start(f32[408,128]{1,0:T(8,128)S(1)} %get-tuple-element.54), channel_id=1, source_target_pairs={{8,0},{16,8},{24,16},{25,24},{17,25},{9,17},{1,9},{0,1},{10,2},{18... | collective-permute-start | bytes 626696 | tf_op jit(solution)/shard_map/ppermute | solution.py:64

commit v8 on v7

--- a/solution.py
+++ b/solution.py
@@ -120,6 +120,9 @@
 
 
 class Sizes:
+    def place_of(self, p):
+        return p if p < self.slab_start else p + self.coarse_planes - self.slab_start
+
     def __init__(self, z, y, x):
         self.z, self.y, self.x = z, y, x
         self.z_routes = swap(z, 1) if z.count <= 2 else both_ways(z, 1)
@@ -142,6 +145,8 @@
         self.far_groups = x.fine // x.coarse_all
         self.far_planes = -(-(z.coarse_all + self.slab_planes) // self.far_groups)
         self.far_rows = up8(y.second * self.far_planes)
+        self.slab_start = z.coarse_all
+        self.coarse_planes = z.coarse_all + RADIUS * len(self.z_routes)
         self.fine_rows = y.fine + 2 * RADIUS
         self.far = y.coarse_all
         self.low = y.mid_all
@@ -150,17 +155,19 @@
         self.edge_sums = EDGE + SPAN
         self.side = x.fine // RADIUS
         self.fine_groups = -(-self.fine_planes // self.side)
-        self.fine_ends = self.fine_groups * self.fine_rows
+        self.folded = 0 < self.fine_planes % self.side <= self.side // 2
+        self.fine_ends = self.fine_groups * self.fine_rows - (self.fine_rows // 2 if self.folded else 0)
         self.sum_blocks = -(-self.sum_planes * self.sum_rows // 128)
-        self.x_rows = self.fine_ends + self.sum_blocks * self.edge_sums
+        self.coarse_blocks = -(-self.coarse_planes * self.sum_rows // 128)
+        self.mid_ends = self.fine_ends + self.coarse_blocks * self.edge_sums
+        self.x_rows = self.mid_ends + (self.sum_blocks - self.coarse_blocks) * up8(EDGE)
         assert x.mid_all + x.coarse_all <= x.fine
         assert self.far + y.second <= self.low and y.coarse_all == SPAN
         assert z.coarse >= RADIUS and y.coarse >= RADIUS and y.count == 4
 
 
-def restrict_kernel(s, nz, source, charges, own, ahead, behind, *rest):
-    messages, (wide, mid, high, coarse, packed) = rest[:-5], rest[-5:]
-    z, y, x = s.z, s.y, s.x
+def narrow_kernel(s, out):
+    x = s.x
     lanes = (x.fine, x.fine)
     cell, lane = iota(lanes, 0), iota(lanes, 1)
     k = lane - 1
@@ -169,6 +176,12 @@
     inside = (lane >= x.mid_all) & (lane < x.mid_all + x.coarse_all) & x.holds_coarse(c)
     to_coarse = jnp.where(inside, weight_of(cell - 1 - 2 * c), 0.0)
     narrow = to_mid + jnp.dot(to_mid, to_coarse, precision=EXACT, preferred_element_type=F32)
+    out[...] = jnp.concatenate(split(narrow), axis=1)
+
+
+def restrict_kernel(s, nz, source, narrow, charges, own, ahead, behind, *rest):
+    messages, (wide, mid, high, coarse, packed) = rest[:-5], rest[-5:]
+    z, y, x = s.z, s.y, s.x
     wide[...] = jnp.zeros(wide.shape, F32)
     charges[...] = source[...]
     cells = source[...].reshape(z.fine * y.fine, x.fine)
@@ -176,7 +189,7 @@
     rest = rest - top.astype(F32)
     middle = rest.astype(BF16)
     low = (rest - middle.astype(F32)).astype(BF16)
-    weights = jnp.concatenate(split(narrow), axis=1)
+    weights = narrow[...]
     both = jnp.dot(low, weights, preferred_element_type=F32)
     both = both + jnp.dot(
         jnp.concatenate([top, middle], axis=1), jnp.concatenate([weights, weights], axis=0), preferred_element_type=F32
@@ -378,7 +391,7 @@
 
     for p in range(z.mid_all):
         far_plane = p if p < z.coarse_all else None
-        rows_of_plane(sums, p, own[p, : y.mid_all], 0, s.y_fine + p * SPAN, far_plane)
+        rows_of_plane(sums, s.place_of(p), own[p, : y.mid_all], 0, s.y_fine + p * SPAN, far_plane)
     is_mid_row = iota((SPAN, x.fine), 1) < x.mid_all
     is_mid_rest = iota((y.mid_all - SPAN, x.fine), 1) < x.mid_all
     for p, plane in enumerate(planes):
@@ -394,28 +407,30 @@
         for j in range(RADIUS):
             a = raw[base + number(lower, 0, 3) + j]
             b = raw[base + number(lower, SPAN - 5 - RADIUS, 5) + j]
-            sums[z.mid_all + n * RADIUS + j] = jnp.where(is_mid, a, b)
+            sums[s.slab_start + n * RADIUS + j] = jnp.where(is_mid, a, b)
         for i in range(3):
-            at = number(lower, 0, z.mid) + i
+            at = number(lower, 0, s.place_of(z.mid)) + i
             sums[at] = sums[at] + jnp.where(is_mid, raw[base + number(lower, EDGE - 3, 0) + i], 0.0)
         for i in range(5):
             at = number(lower, 0, z.coarse) + i
             sums[at] = sums[at] + jnp.where(is_mid, 0.0, raw[base + number(lower, SPAN - 5, 0) + i])
     for n, route in enumerate(s.z2_routes):
         base = len(s.z_routes) * SPAN + n * z.second
-        at = z.mid_all + number(route.below(), RADIUS - z.coarse, RADIUS + z.coarse - 5)
+        at = s.slab_start + number(route.below(), RADIUS - z.coarse, RADIUS + z.coarse - 5)
         for p in range(z.second):
             sums[at + p] = sums[at + p] + jnp.where(is_mid, 0.0, raw[base + p])
 
     up = s.x_routes[0].up()
+    half, shift = s.fine_rows // 2, x.fine // 2
+    is_first_half = iota((half, x.fine), 1) < shift
     for g, ends in roll_ends(s, lambda p: fine[p], 2 * RADIUS):
         rows = slice(g * y.fine, (g + 1) * y.fine)
-        at = slice(g * s.fine_rows, g * s.fine_rows + y.fine)
-        first[at] = jnp.where(up, last[rows], start[rows])
-        second[at] = jnp.where(up, start[rows], last[rows])
-        at = slice(g * s.fine_rows + y.fine, (g + 1) * s.fine_rows)
-        first[at] = jnp.where(up, ends[0], ends[1])
-        second[at] = jnp.where(up, ends[1], ends[0])
+        both = [jnp.concatenate([old[rows], new], axis=0) for old, new in zip((last, start), ends)]
+        if s.folded and g == s.fine_groups - 1:
+            both = [jnp.where(is_first_half, e[:half], pltpu.roll(e[half:], shift, 1)) for e in both]
+        at = slice(g * s.fine_rows, g * s.fine_rows + both[0].shape[0])
+        first[at] = jnp.where(up, both[0], both[1])
+        second[at] = jnp.where(up, both[1], both[0])
     width = EDGE + SPAN
     row, lane = iota((2 * width, x.fine), 0), iota((2 * width, x.fine), 1)
     is_first = row < width
@@ -429,9 +444,13 @@
     if spare:
         picked_sums = jnp.concatenate([picked_sums, jnp.zeros((2 * width, spare), F32)], axis=1)
     for n, message in enumerate((first, second)):
-        for b in range(s.sum_blocks):
+        rows = picked_sums[n * width : (n + 1) * width]
+        for b in range(s.coarse_blocks):
             at = s.fine_ends + b * width
-            message[at : at + width] = picked_sums[n * width : (n + 1) * width, b * 128 : (b + 1) * 128]
+            message[at : at + width] = rows[:, b * 128 : (b + 1) * 128]
+        for b in range(s.coarse_blocks, s.sum_blocks):
+            at = s.mid_ends + (b - s.coarse_blocks) * up8(EDGE)
+            message[at : at + up8(EDGE)] = rows[: up8(EDGE), b * 128 : (b + 1) * 128]
 
 
 def band(taps, level, offset, valid):
@@ -688,12 +707,20 @@
     z, y, x = s.z, s.y, s.x
     below = s.x_routes[0].below()
     half = s.edge_sums
+    def ends_of(start, rows):
+        one, two = first[start : start + rows], second[start : start + rows]
+        return jnp.where(below, one, two), jnp.where(below, two, one)
+
     for b in range(s.sum_blocks):
-        at = slice(s.fine_ends + b * half, s.fine_ends + (b + 1) * half)
-        one, two = first[at], second[at]
-        rows = [jnp.where(below, one, two), jnp.where(below, two, one)] * 2
-        rows.append(jnp.zeros((128 - 4 * half, 128), F32))
-        sums_ends[b * 128 : (b + 1) * 128] = jnp.concatenate(rows, axis=0).T
+        if b < s.coarse_blocks:
+            pair = ends_of(s.fine_ends + b * half, half)
+        else:
+            rest = jnp.zeros((half - up8(EDGE), 128), F32)
+            pair = ends_of(s.mid_ends + (b - s.coarse_blocks) * up8(EDGE), up8(EDGE))
+            pair = [jnp.concatenate([ends, rest], axis=0) for ends in pair]
+        rows = jnp.concatenate(pair, axis=0)
+        zeros = jnp.zeros((128 - 4 * half, 128), F32)
+        sums_ends[b * 128 : (b + 1) * 128] = jnp.concatenate([rows, rows, zeros], axis=0).T
 
     def along_x(start, rows):
         edge_high, edge_low = split(sums_ends[start : start + rows])
@@ -707,9 +734,13 @@
         columns = []
         for flip in range(2):
             for g in range(s.fine_groups):
-                at = slice(g * s.fine_rows, (g + 1) * s.fine_rows)
+                is_folded = s.folded and g == s.fine_groups - 1
+                at = slice(g * s.fine_rows, s.fine_ends if is_folded else (g + 1) * s.fine_rows)
                 pair = (first[at], second[at])
-                columns.append(jnp.where(below, pair[flip], pair[1 - flip]))
+                ends_here = jnp.where(below, pair[flip], pair[1 - flip])
+                if is_folded:
+                    ends_here = jnp.concatenate([ends_here, pltpu.roll(ends_here, x.fine // 2, 1)], axis=0)
+                columns.append(ends_here)
         high, low = split(jnp.concatenate(columns, axis=1))
         joined = jnp.concatenate([high, low, high], axis=0)
         high, low = split(jnp.dot(y_fine[...], joined, preferred_element_type=F32))
@@ -728,11 +759,14 @@
     t_mid[...] = jnp.zeros(t_mid.shape, F32)
     t_coarse[...] = jnp.zeros(t_coarse.shape, F32)
     mid_at = [(RADIUS + p, None) for p in range(z.mid_all)]
-    coarse_at = [(RADIUS + p if p < z.coarse_all else None, None) for p in range(z.mid_all)]
+    mid_at, rest_at = mid_at[: z.coarse_all], mid_at[z.coarse_all :]
+    coarse_at = [(RADIUS + p, None) for p in range(z.coarse_all)]
     for start, valid in slab_starts(s, 0, z.mid + 3 + RADIUS):
         mid_at += [(start + p, valid) for p in range(RADIUS)]
+    mid_at += rest_at
     for start, valid in slab_starts(s, 0, z.coarse + 5 + RADIUS):
         coarse_at += [(start + p, valid) for p in range(RADIUS)]
+    coarse_at += [(None, None)] * len(rest_at)
     is_second = iota((s.coarse_rows, x.fine), 1) >= x.fine // TERMS
 
     def sum_group(g, count):
@@ -775,27 +809,33 @@
                     total = total + weight * p_coarse[(m - offset) // 2 + 2]
             p_mid[k + i] = jnp.where(z.holds_mid(m), total, 0.0)
 
-    groups = list(range(z.mid_all, s.sum_planes, 4)) + list(range(0, z.mid_all, 4))
-    for g in groups:
-        sum_group(g, min(4, s.sum_planes - g if g >= z.mid_all else z.mid_all - g))
     edges = fine_edges()
-    for k in range(0, z.coarse_all, BLOCK):
-        coarse_block(k)
-    widen()
     lane = iota((y.fine, x.fine), 1)
 
-    def finish(k):
-        total = fine[k]
-        for offset, weight in WEIGHTS:
-            if (k - offset) % 2 == 0:
-                total = total + weight * p_mid[(k - offset) // 2 + 1]
+    def begin(k):
         block, at = k // s.side, k % s.side * RADIUS
         low, high = (edge[:, block * x.fine : (block + 1) * x.fine] for edge in edges)
         low = pltpu.roll(low, -at % x.fine, 1) if at else low
         turn = (x.fine - RADIUS - at) % x.fine
         high = pltpu.roll(high, turn, 1) if turn else high
-        out[k] = total + jnp.where(lane < RADIUS, low, jnp.where(lane >= x.fine - RADIUS, high, 0.0))
-
+        out[k] = fine[k] + jnp.where(lane < RADIUS, low, jnp.where(lane >= x.fine - RADIUS, high, 0.0))
+
+    def finish(k):
+        total = out[k]
+        for offset, weight in WEIGHTS:
+            if (k - offset) % 2 == 0:
+                total = total + weight * p_mid[(k - offset) // 2 + 1]
+        out[k] = total
+
+    groups = list(range(0, s.sum_planes, 4))
+    share = -(-z.fine // len(groups))
+    for n, g in enumerate(groups):
+        sum_group(g, min(4, s.sum_planes - g))
+        for k in range(n * share, min((n + 1) * share, z.fine)):
+            begin(k)
+    for k in range(0, z.coarse_all, BLOCK):
+        coarse_block(k)
+    widen()
     done, copies = 0, []
     for k in range(0, z.mid_all, BLOCK):
         mid_block(k)
@@ -839,10 +879,11 @@
         return lambda *refs: kernel(s, *static, *refs)
 
     rows = up8(y.mid_all)
+    (weights,) = call(bound(narrow_kernel), [array(n, 2 * n, dtype=BF16)], [], flops=10**10)
     held, own, ahead, behind, *messages = call(
         bound(restrict_kernel, nz),
         [array(*charges.shape), array(z.mid_all, rows, n)] + [array(s.y_rows, n)] * 2 + [array(s.z_rows, n)] * nz + [array(s.z2_rows, n)] * nz2,
-        [charges],
+        [charges, weights],
         [
             pltpu.VMEM((z.fine, y.fine + 16, n), F32),
             pltpu.VMEM((z.mid_all, rows, n), F32),

time: 30.1 us -> 29.6 us (0.983)
  local copies, waits for them, and re-layouts: 1.72 us -> 0.8 us
  waiting for transfers between devices: 3.46 us -> 3.88 us
    unnamed x4, local copies, waits for them, and re-layouts: 1.72 us -> 0.8 us
    ppermute x8, waiting for transfers between devices: 3.46 us -> 3.88 us  [__call__(): return lax.ppermute(x, self.names, self.pairs)]
    pallas_call x7 -> x8, Pallas kernels: 12.1 us -> 12.1 us  [call(): pl.pallas_call(kernel, out_shape=tuple(outs), in_specs=specs, out_specs=t...]
  transfers between devices with their start and end apart: 8 -> 8, of which waited for: 3 -> 3; matrix products, arithmetic and copies ran while one was open for 0% -> 0% of each run, Pallas kernels for 22% -> 23%
where the time goes in v8:
time: 29.6 us; the launch traced here: 29.4 us
  starting transfers between devices  12.6 us (43%)
  Pallas kernels  12.1 us (41%)
  waiting for transfers between devices  3.88 us (13%)
  local copies, waits for them, and re-layouts  0.8 us (3%)
    ppermute x8, starting transfers between devices, __call__(): return lax.ppermute(x, self.names, self.pairs)  12.6 us
    pallas_call x8, Pallas kernels, call(): pl.pallas_call(kernel, out_shape=tuple(outs), in_specs=specs, out_specs=t...  12.1 us
    ppermute x8, waiting for transfers between devices, __call__(): return lax.ppermute(x, self.names, self.pairs)  3.88 us
    unnamed x4, local copies, waits for them, and re-layouts  0.8 us
  transfers between devices with their start and end apart: 8, of which 3 were waited for; matrix products, arithmetic and copies ran while one was open for 0% of the time, Pallas kernels for 23%

profile of v8, /device:TPU:1, one launch (start us, length us, event | category | flops | bytes accessed | tf_op | source)
XLA Modules:
  0.0 29.4 jit_solution(5232241804455288147)
XLA Ops:
  0.0 0.0 copy-start
  0.0 0.0 copy-start.1
  0.0 0.2 shard_map.29.refs_1_
  0.2 0.8 %copy-done = f32[32,32,128]{2,1,0:T(8,128)S(1)} copy-done((f32[32,32,128]{2,1,0:T(8,128)S(1)}, f32[32,32,128]{2,1,0:T(8,128)}, u32[]{:S(2)}) %copy-start) | copy-done | bytes 524312
  1.0 0.8 %shard_map.30 = (f32[32,32,128]{2,1,0:T(8,128)S(1)}, f32[19,24,128]{2,1,0:T(8,128)S(1)}, f32[504,128]{1,0:T(8,128)S(1)}, f32[504,128]{1,0:T(8,128)S(1)}, f32[472,128]{1,0:T(8,128)S(1)}) custom-call(f32[32,32,128]{2,1,0:T(8,128)S(1)} %copy-done, bf16[128,256]{1,0:T(8,128)(2,1)S(1)} %shard_map.29.refs_1_), custom_call_target="tpu_custom_call" | custom-call | flops 10000000 | bytes 2105344 | tf_op jit(solution)/shard_map/pallas_call | solution.py:857
  1.8 2.1 %collective-permute-start = (f32[472,128]{1,0:T(8,128)S(1)}, f32[472,128]{1,0:T(8,128)S(1)}, u32[]{:S(2)}, u32[]{:S(2)}) collective-permute-start(f32[472,128]{1,0:T(8,128)S(1)} %get-tuple-element.35), channel_id=1, source_target_pairs={{0,1},{1,0},{2,3},{3,2},{4,5},{5,4},{6,7},{7,6},{8,9},{9,8},{10,11... | collective-permute-start | bytes 725000 | tf_op jit(solution)/shard_map/ppermute | solution.py:64
  3.9 1.0 %collective-permute-start.1 = (f32[504,128]{1,0:T(8,128)S(1)}, f32[504,128]{1,0:T(8,128)S(1)}, u32[]{:S(2)}, u32[]{:S(2)}) collective-permute-start(f32[504,128]{1,0:T(8,128)S(1)} %get-tuple-element.42), channel_id=1, source_target_pairs={{0,2},{2,4},{4,6},{6,14},{14,12},{12,10},{10,8},{8,0},{16,18},{18,... | collective-permute-start | bytes 774152 | tf_op jit(solution)/shard_map/ppermute | solution.py:64
  4.9 0.5 %collective-permute-start.2 = (f32[504,128]{1,0:T(8,128)S(1)}, f32[504,128]{1,0:T(8,128)S(1)}, u32[]{:S(2)}, u32[]{:S(2)}) collective-permute-start(f32[504,128]{1,0:T(8,128)S(1)} %get-tuple-element.43), channel_id=1, source_target_pairs={{2,0},{4,2},{6,4},{14,6},{12,14},{10,12},{8,10},{0,8},{18,16},{20,... | collective-permute-start | bytes 774152 | tf_op jit(solution)/shard_map/ppermute | solution.py:64
  5.4 0.0 copy-done.1
  5.4 2.2 %shard_map.28 = (bf16[384,256]{1,0:T(8,128)(2,1)S(1)}, bf16[640,384]{1,0:T(8,128)(2,1)S(1)}, bf16[4,1152,256]{2,1,0:T(8,128)(2,1)S(1)}, bf16[64,96]{1,0:T(8,128)...) custom-call(f32[3,2,17]{2,1,0:T(2,128)S(1)} %copy-done.1), custom_call_target="tpu_custom_call" | custom-call | flops 10000000 | bytes 3561880 | tf_op jit(solution)/shard_map/pallas_call | solution.py:857
  7.6 1.9 %collective-permute-done.refs_1_.refs_2_.refs_3_ = f32[472,128]{1,0:T(8,128)S(1)} collective-permute-done((f32[472,128]{1,0:T(8,128)S(1)}, f32[472,128]{1,0:T(8,128)S(1)}, u32[]{:S(2)}, u32[]{:S(2)}) %collective-permute-start) | collective-permute-done | bytes 241696 | tf_op jit(solution)/shard_map/ppermute | solution.py:64
  9.5 0.1 shard_map.32
  9.6 1.2 %collective-permute-start.3 = (f32[240,128]{1,0:T(8,128)S(1)}, f32[240,128]{1,0:T(8,128)S(1)}, u32[]{:S(2)}, u32[]{:S(2)}) collective-permute-start(f32[240,128]{1,0:T(8,128)S(1)} %get-tuple-element.44), channel_id=1, source_target_pairs={{0,2},{2,4},{4,6},{6,14},{14,12},{12,10},{10,8},{8,0},{16,18},{18,... | collective-permute-start | bytes 368648 | tf_op jit(solution)/shard_map/ppermute | solution.py:64
  10.9 0.2 collective-permute-start.4
  11.1 2.2 %collective-permute-start.5 = (f32[48,128]{1,0:T(8,128)S(1)}, f32[48,128]{1,0:T(8,128)S(1)}, u32[]{:S(2)}, u32[]{:S(2)}) collective-permute-start(f32[48,128]{1,0:T(8,128)S(1)} %get-tuple-element.46), channel_id=1, source_target_pairs={{0,4},{2,6},{4,0},{6,2},{1,5},{3,7},{5,1},{7,3},{8,12},{10,14},{12... | collective-permute-start | bytes 73736 | tf_op jit(solution)/shard_map/ppermute | solution.py:64
  13.3 1.3 %shard_map.31 = (f32[48,2,32,128]{3,2,1,0:T(8,128)S(1)}, f32[96,128]{1,0:T(8,128)S(1)}, f32[96,128]{1,0:T(8,128)S(1)}) custom-call(f32[32,32,128]{2,1,0:T(8,128)S(1)} %get-tuple-element.34.refs_0_, f32[472,128]{1,0:T(8,128)S(1)} %collective-permute-done.refs_1_.refs_2_.refs_3_, bf16[384,256]{1,0:T(8,128)(2,1)S(1)} %get-tuple-element.36.refs_2_.refs_4_, ...), custom_call_target="tpu_custom_call" | custom-call | flops 10000000 | bytes 2646016 | tf_op jit(solution)/shard_map/pallas_call | solution.py:857
  14.6 0.0 collective-permute-done.1.refs_4_
  14.6 0.0 collective-permute-done.2.refs_5_
  14.6 0.1 collective-permute-done.5.refs_8_
  14.7 0.0 collective-permute-done.3.refs_6_
  14.7 0.0 collective-permute-done.4.refs_7_
  14.7 0.7 %shard_map.33 = (f32[40,16,128]{2,1,0:T(8,128)S(1)}, f32[27,48,128]{2,1,0:T(8,128)S(1)}, f32[360,128]{1,0:T(8,128)S(1)}, f32[360,128]{1,0:T(8,128)S(1)}) custom-call(f32[96,128]{1,0:T(8,128)S(1)} %get-tuple-element.39.refs_0_, f32[96,128]{1,0:T(8,128)S(1)} %get-tuple-element.40.refs_1_, f32[19,24,128]{2,1,0:T(8,128)S(1)} %get-tuple-element.41.refs_1_.refs_2_, ...), custom_call_target="tpu_custom_call" | custom-call | flops 10000000 | bytes 2719744 | tf_op jit(solution)/shard_map/pallas_call | solution.py:857
  15.4 5.3 %collective-permute-start.6 = (f32[360,128]{1,0:T(8,128)S(1)}, f32[360,128]{1,0:T(8,128)S(1)}, u32[]{:S(2)}, u32[]{:S(2)}) collective-permute-start(f32[360,128]{1,0:T(8,128)S(1)} %get-tuple-element.53), channel_id=1, source_target_pairs={{0,8},{8,16},{16,24},{24,25},{25,17},{17,9},{9,1},{1,0},{2,10},{10... | collective-permute-start | bytes 552968 | tf_op jit(solution)/shard_map/ppermute | solution.py:64
  20.7 0.0 collective-permute-start.7
  20.7 3.1 %shard_map.34 = (f32[32,32,128]{2,1,0:T(8,128)S(1)}, f32[1296,384]{1,0:T(8,128)S(1)}) custom-call(f32[85,8,128]{2,1,0:T(8,128)S(1)} %get-tuple-element.33.refs_0_, f32[48,2,32,128]{3,2,1,0:T(8,128)S(1)} %get-tuple-element.38.refs_1_, f32[40,16,128]{2,1,0:T(8,128)S(1)} %get-tuple-element.47.refs_2_, f32[27,48,128]{2,1,0:T(8,128)S(1)} %get-tuple-element.48.refs_3_, ...), custom_call_target="tpu_custom_call" | custom-call | flops 10000000 | bytes 6121472 | tf_op jit(solution)/shard_map/pallas_call | solution.py:857
  23.8 0.0 collective-permute-done.6.refs_3_
  23.8 1.9 %collective-permute-done.7.refs_4_ = f32[360,128]{1,0:T(8,128)S(1)} collective-permute-done((f32[360,128]{1,0:T(8,128)S(1)}, f32[360,128]{1,0:T(8,128)S(1)}, u32[]{:S(2)}, u32[]{:S(2)}) %collective-permute-start.7) | collective-permute-done | bytes 184352 | tf_op jit(solution)/shard_map/ppermute | solution.py:64
  25.6 3.8 %shard_map.35 = f32[32,32,128]{2,1,0:T(8,128)} custom-call(f32[85,8,128]{2,1,0:T(8,128)S(1)} %get-tuple-element.33.refs_0_, f32[32,32,128]{2,1,0:T(8,128)S(1)} %get-tuple-element.51.refs_1_, f32[1296,384]{1,0:T(8,128)S(1)} %get-tuple-element.52.refs_2_, f32[360,128]{1,0:T(8,128)S(1)} %collective-permute-done.6.refs_3_, ...), custom_call_target="tpu_custom_call" | custom-call | flops 10000000 | bytes 6754304 | tf_op jit(solution)/shard_map/pallas_call | solution.py:857
Async XLA Ops:
  0.0 1.0 %copy-start = (f32[32,32,128]{2,1,0:T(8,128)S(1)}, f32[32,32,128]{2,1,0:T(8,128)}, u32[]{:S(2)}) copy-start(f32[32,32,128]{2,1,0:T(8,128)} %refs_0_.3) | copy-start | bytes 1572868
  0.0 5.4 %copy-start.1 = (f32[3,2,17]{2,1,0:T(2,128)S(1)}, f32[3,2,17]{2,1,0:T(2,128)}, u32[]{:S(2)}) copy-start(f32[3,2,17]{2,1,0:T(2,128)} %refs_0_.2) | copy-start | bytes 1228
  1.8 7.7 %collective-permute-start = (f32[472,128]{1,0:T(8,128)S(1)}, f32[472,128]{1,0:T(8,128)S(1)}, u32[]{:S(2)}, u32[]{:S(2)}) collective-permute-start(f32[472,128]{1,0:T(8,128)S(1)} %get-tuple-element.35), channel_id=1, source_target_pairs={{0,1},{1,0},{2,3},{3,2},{4,5},{5,4},{6,7},{7,6},{8,9},{9,8},{10,11... | collective-permute-start | bytes 725000 | tf_op jit(solution)/shard_map/ppermute | solution.py:64
  3.9 10.7 %collective-permute-start.1 = (f32[504,128]{1,0:T(8,128)S(1)}, f32[504,128]{1,0:T(8,128)S(1)}, u32[]{:S(2)}, u32[]{:S(2)}) collective-permute-start(f32[504,128]{1,0:T(8,128)S(1)} %get-tuple-element.42), channel_id=1, source_target_pairs={{0,2},{2,4},{4,6},{6,14},{14,12},{12,10},{10,8},{8,0},{16,18},{18,... | collective-permute-start | bytes 774152 | tf_op jit(solution)/shard_map/ppermute | solution.py:64
  4.9 9.8 %collective-permute-start.2 = (f32[504,128]{1,0:T(8,128)S(1)}, f32[504,128]{1,0:T(8,128)S(1)}, u32[]{:S(2)}, u32[]{:S(2)}) collective-permute-start(f32[504,128]{1,0:T(8,128)S(1)} %get-tuple-element.43), channel_id=1, source_target_pairs={{2,0},{4,2},{6,4},{14,6},{12,14},{10,12},{8,10},{0,8},{18,16},{20,... | collective-permute-start | bytes 774152 | tf_op jit(solution)/shard_map/ppermute | solution.py:64
  9.6 5.1 %collective-permute-start.3 = (f32[240,128]{1,0:T(8,128)S(1)}, f32[240,128]{1,0:T(8,128)S(1)}, u32[]{:S(2)}, u32[]{:S(2)}) collective-permute-start(f32[240,128]{1,0:T(8,128)S(1)} %get-tuple-element.44), channel_id=1, source_target_pairs={{0,2},{2,4},{4,6},{6,14},{14,12},{12,10},{10,8},{8,0},{16,18},{18,... | collective-permute-start | bytes 368648 | tf_op jit(solution)/shard_map/ppermute | solution.py:64
  10.9 3.8 %collective-permute-start.4 = (f32[240,128]{1,0:T(8,128)S(1)}, f32[240,128]{1,0:T(8,128)S(1)}, u32[]{:S(2)}, u32[]{:S(2)}) collective-permute-start(f32[240,128]{1,0:T(8,128)S(1)} %get-tuple-element.45), channel_id=1, source_target_pairs={{2,0},{4,2},{6,4},{14,6},{12,14},{10,12},{8,10},{0,8},{18,16},{20,... | collective-permute-start | bytes 368648 | tf_op jit(solution)/shard_map/ppermute | solution.py:64
  11.1 3.6 %collective-permute-start.5 = (f32[48,128]{1,0:T(8,128)S(1)}, f32[48,128]{1,0:T(8,128)S(1)}, u32[]{:S(2)}, u32[]{:S(2)}) collective-permute-start(f32[48,128]{1,0:T(8,128)S(1)} %get-tuple-element.46), channel_id=1, source_target_pairs={{0,4},{2,6},{4,0},{6,2},{1,5},{3,7},{5,1},{7,3},{8,12},{10,14},{12... | collective-permute-start | bytes 73736 | tf_op jit(solution)/shard_map/ppermute | solution.py:64
  15.4 8.4 %collective-permute-start.6 = (f32[360,128]{1,0:T(8,128)S(1)}, f32[360,128]{1,0:T(8,128)S(1)}, u32[]{:S(2)}, u32[]{:S(2)}) collective-permute-start(f32[360,128]{1,0:T(8,128)S(1)} %get-tuple-element.53), channel_id=1, source_target_pairs={{0,8},{8,16},{16,24},{24,25},{25,17},{17,9},{9,1},{1,0},{2,10},{10... | collective-permute-start | bytes 552968 | tf_op jit(solution)/shard_map/ppermute | solution.py:64
  20.7 5.0 %collective-permute-start.7 = (f32[360,128]{1,0:T(8,128)S(1)}, f32[360,128]{1,0:T(8,128)S(1)}, u32[]{:S(2)}, u32[]{:S(2)}) collective-permute-start(f32[360,128]{1,0:T(8,128)S(1)} %get-tuple-element.54), channel_id=1, source_target_pairs={{8,0},{16,8},{24,16},{25,24},{17,25},{9,17},{1,9},{0,1},{10,2},{18... | collective-permute-start | bytes 552968 | tf_op jit(solution)/shard_map/ppermute | solution.py:64

commit v9 on v8

--- a/solution.py
+++ b/solution.py
@@ -143,7 +143,7 @@
         self.slab_fine = RADIUS * RADIUS * len(self.z_routes)
         self.slab_rows = up8(self.slab_fine + SPAN * self.slab_planes)
         self.far_groups = x.fine // x.coarse_all
-        self.far_planes = -(-(z.coarse_all + self.slab_planes) // self.far_groups)
+        self.far_planes = -(-z.coarse_all // self.far_groups)
         self.far_rows = up8(y.second * self.far_planes)
         self.slab_start = z.coarse_all
         self.coarse_planes = z.coarse_all + RADIUS * len(self.z_routes)
@@ -162,7 +162,7 @@
         self.mid_ends = self.fine_ends + self.coarse_blocks * self.edge_sums
         self.x_rows = self.mid_ends + (self.sum_blocks - self.coarse_blocks) * up8(EDGE)
         assert x.mid_all + x.coarse_all <= x.fine
-        assert self.far + y.second <= self.low and y.coarse_all == SPAN
+        assert self.far + y.second <= self.low and y.second <= 8 and y.coarse_all == SPAN and z.coarse_all == SPAN
         assert z.coarse >= RADIUS and y.coarse >= RADIUS and y.count == 4
 
 
@@ -179,8 +179,8 @@
     out[...] = jnp.concatenate(split(narrow), axis=1)
 
 
-def restrict_kernel(s, nz, source, narrow, charges, own, ahead, behind, *rest):
-    messages, (wide, mid, high, coarse, packed) = rest[:-5], rest[-5:]
+def restrict_kernel(s, nz, source, narrow, charges, own, ahead, behind, far, *rest):
+    messages, (wide, mid, high, coarse, packed, groups) = rest[:-6], rest[-6:]
     z, y, x = s.z, s.y, s.x
     wide[...] = jnp.zeros(wide.shape, F32)
     charges[...] = source[...]
@@ -226,6 +226,19 @@
     is_mid = iota(mid.shape[1:], 1) < x.mid_all
     for p in range(z.mid_all):
         own[p] = jnp.where(is_mid, mid[p], coarse[p]) if p < z.coarse_all else jnp.where(is_mid, mid[p], 0.0)
+    up = s.y2_routes[0].up()
+    count, end = y.second, y.coarse_all
+    groups[...] = jnp.zeros(groups.shape, F32)
+    for p in range(z.coarse_all):
+        g, at = p // s.far_planes, p % s.far_planes * count
+        groups[g, at : at + count] = jnp.where(up, own[p, end - count : end], own[p, :count])
+    lane = iota(far.shape, 1)
+    total = jnp.zeros(far.shape, F32)
+    for g in range(s.far_groups):
+        first = g * x.coarse_all
+        turned = pltpu.roll(groups[g], (first - x.mid_all) % x.fine, 1)
+        total = jnp.where((lane >= first) & (lane < first + x.coarse_all), turned, total)
+    far[...] = total
     is_side = iota((SPAN, x.fine), 1) < x.mid_all
     for message, route in zip((ahead, behind), s.y_routes):
         up = route.up()
@@ -281,9 +294,9 @@
     return out
 
 
-def spread_kernel(s, nz, nz2, _, own, *rest):
+def spread_kernel(s, nz, nz2, _, *rest):
     z_messages, z2_messages = rest[:nz], rest[nz : nz + nz2]
-    ahead, behind, far, rows = rest[-4:]
+    ahead, behind = rest[-2:]
     z, y, x = s.z, s.y, s.x
     is_mid = iota((SPAN, x.fine), 1) < x.mid_all
     planes = slabs(s, z_messages, z2_messages)
@@ -301,21 +314,10 @@
             at += SPAN
         if at < s.slab_rows:
             message[at:] = jnp.zeros((s.slab_rows - at, x.fine), F32)
-    up = s.y2_routes[0].up()
-    count, end = y.second, y.coarse_all
-    rows[...] = jnp.zeros(rows.shape, F32)
-    pairs = [(own[p, end - count : end], own[p, :count]) for p in range(z.coarse_all)]
-    pairs += [(plane.coarse_rows(end - count, count), plane.coarse_rows(0, count)) for plane in planes]
-    for p, (last, start) in enumerate(pairs):
-        g, at = p // s.far_planes, p % s.far_planes * count
-        rows[g, at : at + count] = jnp.where(up, last, start)
-    lane = iota(far.shape, 1)
-    total = jnp.zeros(far.shape, F32)
-    for g in range(s.far_groups):
-        start = g * x.coarse_all
-        turned = pltpu.roll(rows[g], (start - x.mid_all) % x.fine, 1)
-        total = jnp.where((lane >= start) & (lane < start + x.coarse_all), turned, total)
-    far[...] = total
+
+
+def pass_kernel(s, far, out):
+    out[...] = far[...]
 
 
 def roll_ends(s, plane_rows, count):
@@ -359,7 +361,8 @@
     z_messages, z2_messages = rest[:nz], rest[nz : nz + nz2]
     rest = rest[nz + nz2 :]
     pairs = rest[:4]
-    far, fine, sums, first, second, raw, rows = rest[4:]
+    fars = rest[4 : 5 + nz + nz2]
+    fine, sums, first, second, raw, rows = rest[5 + nz + nz2 :]
     z, y, x = s.z, s.y, s.x
     below = s.y_routes[0].below()
     planes = slabs(s, z_messages, z2_messages)
@@ -375,8 +378,12 @@
         fine[at : at + count, RADIUS:] = high.reshape(count, RADIUS, x.fine)
     sums[...] = jnp.zeros(sums.shape, F32)
     raw[...] = jnp.zeros(raw.shape, F32)
-    for g in range(s.far_groups):
-        rows[g] = pltpu.roll(far[...], (x.mid_all - g * x.coarse_all) % x.fine, 1)
+    for n, far in enumerate(fars):
+        for g in range(s.far_groups):
+            turned = pltpu.roll(far[...], (x.mid_all - g * x.coarse_all) % x.fine, 1)
+            for p in range(g * s.far_planes, min((g + 1) * s.far_planes, z.coarse_all)):
+                at = p % s.far_planes * y.second
+                rows[n, p, : y.second] = turned[at : at + y.second]
     is_mid = iota((y.second, x.fine), 1) < x.mid_all
 
     def rows_of_plane(out, p, body, which, row, far_plane):
@@ -386,17 +393,20 @@
         out[p, s.high : s.high + SPAN] = high
         if far_plane is not None:
             at = slice(s.far, s.far + y.second)
-            start = far_plane % s.far_planes * y.second
-            out[p, at] = jnp.where(is_mid, out[p, at], rows[far_plane // s.far_planes, start : start + y.second])
+            out[p, at] = jnp.where(is_mid, out[p, at], rows[far_plane][: y.second])
 
     for p in range(z.mid_all):
-        far_plane = p if p < z.coarse_all else None
+        far_plane = (0, p) if p < z.coarse_all else None
         rows_of_plane(sums, s.place_of(p), own[p, : y.mid_all], 0, s.y_fine + p * SPAN, far_plane)
     is_mid_row = iota((SPAN, x.fine), 1) < x.mid_all
     is_mid_rest = iota((y.mid_all - SPAN, x.fine), 1) < x.mid_all
+    slab_far = [(1 + n, p) for n in range(nz) for p in range(SPAN)]
+    for n, route in enumerate(s.z2_routes):
+        at = jnp.where(route.below(), z.coarse_all - z.second, 0)
+        slab_far += [(1 + nz + n, at + p) for p in range(z.second)]
     for p, plane in enumerate(planes):
         body = [plane.rows(is_mid_row, 0, 0, SPAN), plane.rows(is_mid_rest, SPAN, None, y.mid_all - SPAN)]
-        rows_of_plane(raw, p, jnp.concatenate(body, axis=0), 1, s.slab_fine + p * SPAN, z.coarse_all + p)
+        rows_of_plane(raw, p, jnp.concatenate(body, axis=0), 1, s.slab_fine + p * SPAN, slab_far[p])
     is_mid = iota((s.sum_rows, x.fine), 1) < x.mid_all
 
     def number(condition, a, b):
@@ -880,9 +890,9 @@
 
     rows = up8(y.mid_all)
     (weights,) = call(bound(narrow_kernel), [array(n, 2 * n, dtype=BF16)], [], flops=10**10)
-    held, own, ahead, behind, *messages = call(
+    held, own, ahead, behind, far, *messages = call(
         bound(restrict_kernel, nz),
-        [array(*charges.shape), array(z.mid_all, rows, n)] + [array(s.y_rows, n)] * 2 + [array(s.z_rows, n)] * nz + [array(s.z2_rows, n)] * nz2,
+        [array(*charges.shape), array(z.mid_all, rows, n)] + [array(s.y_rows, n)] * 2 + [array(s.far_rows, n)] + [array(s.z_rows, n)] * nz + [array(s.z2_rows, n)] * nz2,
         [charges, weights],
         [
             pltpu.VMEM((z.fine, y.fine + 16, n), F32),
@@ -890,10 +900,13 @@
             pltpu.VMEM((z.mid_all, up8(y.mid + 24), n), F32),
             pltpu.VMEM((z.mid_all, rows, n), F32),
             pltpu.VMEM((2, s.z_rows - s.z_fine, n), F32),
+            pltpu.VMEM((s.far_groups, s.far_rows, n), F32),
         ],
     )
     z_got = [route(m) for route, m in zip(s.z_routes + s.z2_routes, messages)]
     sides = [s.y_routes[0](ahead), s.y_routes[1](behind)]
+    far = s.y2_routes[0](far)
+    (passed,) = call(bound(pass_kernel), [array(s.far_rows, n)], [far], flops=2*10**9)
     operators = call(
         bound(operator_kernel),
         [
@@ -911,14 +924,13 @@
         ],
         [kernel_taps],
     )
-    ahead, behind, far = call(
+    ahead, behind = call(
         bound(spread_kernel, nz, nz2),
-        [array(s.slab_rows, n), array(s.slab_rows, n), array(s.far_rows, n)],
-        [operators[-1], own, *z_got],
-        [pltpu.VMEM((s.far_groups, s.far_rows, n), F32)],
+        [array(s.slab_rows, n), array(s.slab_rows, n)],
+        [passed, *z_got],
     )
     sides += [s.y_routes[0](ahead), s.y_routes[1](behind)]
-    far = s.y2_routes[0](far)
+    fars = [far] + [route(passed) for route in s.z_routes + s.z2_routes]
     x_fine, x_sums, ends, y_own, y_edge, y_fine, y_mid, y_coarse, widen_x, widen_y, table = operators
     t_part, last, start = call(
         bound(early_kernel, nz),
@@ -934,8 +946,8 @@
             array(s.x_rows, n),
             array(s.x_rows, n),
         ],
-        [last, start, own, *z_got, *sides, far],
-        [pltpu.VMEM((s.slab_planes, s.sum_rows, n), F32), pltpu.VMEM((s.far_groups, s.far_rows, n), F32)],
+        [last, start, own, *z_got, *sides, *fars],
+        [pltpu.VMEM((s.slab_planes, s.sum_rows, n), F32), pltpu.VMEM((1 + nz + nz2, z.coarse_all, 8, n), F32)],
     )
     first, second = s.x_routes[0](first), s.x_routes[1](second)
     fine, sums = call(

time: 29.6 us -> 28.8 us (0.973)
  starting transfers between devices: 12.6 us -> 11.9 us
    ppermute x8 -> x9, starting transfers between devices: 12.6 us -> 11.9 us  [__call__(): return lax.ppermute(x, self.names, self.pairs)]
    ppermute x8 -> x9, waiting for transfers between devices: 3.88 us -> 3.65 us  [__call__(): return lax.ppermute(x, self.names, self.pairs)]
    pallas_call x8 -> x9, Pallas kernels: 12.1 us -> 12.2 us  [call(): pl.pallas_call(kernel, out_shape=tuple(outs), in_specs=specs, out_specs=t...]
  transfers between devices with their start and end apart: 8 -> 9, of which waited for: 3 -> 2; matrix products, arithmetic and copies ran while one was open for 0% -> 0% of each run, Pallas kernels for 23% -> 23%
where the time goes in v9:
time: 28.8 us; the launch traced here: 28.6 us
  Pallas kernels  12.2 us (42%)
  starting transfers between devices  11.9 us (41%)
  waiting for transfers between devices  3.65 us (13%)
  local copies, waits for them, and re-layouts  0.8 us (3%)
    pallas_call x9, Pallas kernels, call(): pl.pallas_call(kernel, out_shape=tuple(outs), in_specs=specs, out_specs=t...  12.2 us
    ppermute x9, starting transfers between devices, __call__(): return lax.ppermute(x, self.names, self.pairs)  11.9 us
    ppermute x9, waiting for transfers between devices, __call__(): return lax.ppermute(x, self.names, self.pairs)  3.65 us
    unnamed x4, local copies, waits for them, and re-layouts  0.8 us
  transfers between devices with their start and end apart: 9, of which 2 were waited for; matrix products, arithmetic and copies ran while one was open for 0% of the time, Pallas kernels for 23%

profile of v9, /device:TPU:1, one launch (start us, length us, event | category | flops | bytes accessed | tf_op | source)
XLA Modules:
  0.0 28.6 jit_solution(7131865360087505235)
XLA Ops:
  0.0 0.0 copy-start
  0.0 0.2 shard_map.29.refs_1_
  0.2 0.8 %copy-done = f32[32,32,128]{2,1,0:T(8,128)S(1)} copy-done((f32[32,32,128]{2,1,0:T(8,128)S(1)}, f32[32,32,128]{2,1,0:T(8,128)}, u32[]{:S(2)}) %copy-start) | copy-done | bytes 524312
  1.0 0.8 %shard_map.30 = (f32[32,32,128]{2,1,0:T(8,128)S(1)}, f32[19,24,128]{2,1,0:T(8,128)S(1)}, f32[504,128]{1,0:T(8,128)S(1)}, f32[504,128]{1,0:T(8,128)S(1)}, f32[32,128]{1,0:T(8,128)S(1)}, /*index=5*/f32[472,128]{1,0:T(8,128)S(1)}) custom-call(f32[32,32,128]{2,1,0:T(8,128)S(1)} %copy-done, bf16[128,256]{1,0:T(8,128)(2,1)S(1)} %shard_map.29.refs_1_), custom_call_target="tpu_custom_call" | custom-call | flops 10000000 | bytes 2121728 | tf_op jit(solution)/shard_map/pallas_call | solution.py:867
  1.9 2.1 %collective-permute-start = (f32[472,128]{1,0:T(8,128)S(1)}, f32[472,128]{1,0:T(8,128)S(1)}, u32[]{:S(2)}, u32[]{:S(2)}) collective-permute-start(f32[472,128]{1,0:T(8,128)S(1)} %get-tuple-element.35), channel_id=1, source_target_pairs={{0,1},{1,0},{2,3},{3,2},{4,5},{5,4},{6,7},{7,6},{8,9},{9,8},{10,11... | collective-permute-start | bytes 725000 | tf_op jit(solution)/shard_map/ppermute | solution.py:64
  3.9 2.3 %collective-permute-start.3 = (f32[32,128]{1,0:T(8,128)S(1)}, f32[32,128]{1,0:T(8,128)S(1)}, u32[]{:S(2)}, u32[]{:S(2)}) collective-permute-start(f32[32,128]{1,0:T(8,128)S(1)} %get-tuple-element.44), channel_id=1, source_target_pairs={{0,4},{2,6},{4,0},{6,2},{1,5},{3,7},{5,1},{7,3},{8,12},{10,14},{12... | collective-permute-start | bytes 49160 | tf_op jit(solution)/shard_map/ppermute | solution.py:64
  6.2 1.2 %collective-permute-start.1 = (f32[504,128]{1,0:T(8,128)S(1)}, f32[504,128]{1,0:T(8,128)S(1)}, u32[]{:S(2)}, u32[]{:S(2)}) collective-permute-start(f32[504,128]{1,0:T(8,128)S(1)} %get-tuple-element.42), channel_id=1, source_target_pairs={{0,2},{2,4},{4,6},{6,14},{14,12},{12,10},{10,8},{8,0},{16,18},{18,... | collective-permute-start | bytes 774152 | tf_op jit(solution)/shard_map/ppermute | solution.py:64
  7.5 0.0 copy-start.1
  7.5 0.2 collective-permute-start.2
  7.7 0.0 collective-permute-done.3.refs_0_.refs_8_
  7.7 1.8 %collective-permute-done.refs_1_.refs_3_ = f32[472,128]{1,0:T(8,128)S(1)} collective-permute-done((f32[472,128]{1,0:T(8,128)S(1)}, f32[472,128]{1,0:T(8,128)S(1)}, u32[]{:S(2)}, u32[]{:S(2)}) %collective-permute-start) | collective-permute-done | bytes 241696 | tf_op jit(solution)/shard_map/ppermute | solution.py:64
  9.6 1.2 %collective-permute-start.4 = (f32[240,128]{1,0:T(8,128)S(1)}, f32[240,128]{1,0:T(8,128)S(1)}, u32[]{:S(2)}, u32[]{:S(2)}) collective-permute-start(f32[240,128]{1,0:T(8,128)S(1)} %get-tuple-element.45), channel_id=1, source_target_pairs={{0,2},{2,4},{4,6},{6,14},{14,12},{12,10},{10,8},{8,0},{16,18},{18,... | collective-permute-start | bytes 368648 | tf_op jit(solution)/shard_map/ppermute | solution.py:64
  10.8 0.2 collective-permute-start.5
  11.1 1.2 %collective-permute-start.6 = (f32[32,128]{1,0:T(8,128)S(1)}, f32[32,128]{1,0:T(8,128)S(1)}, u32[]{:S(2)}, u32[]{:S(2)}) collective-permute-start(f32[32,128]{1,0:T(8,128)S(1)} %shard_map.32.refs_0_), channel_id=1, source_target_pairs={{0,1},{1,0},{2,3},{3,2},{4,5},{5,4},{6,7},{7,6},{8,9},{9,8},{10,11... | collective-permute-start | bytes 49160 | tf_op jit(solution)/shard_map/ppermute | solution.py:64
  12.3 0.0 copy-done.1
  12.3 2.2 %shard_map.28 = (bf16[384,256]{1,0:T(8,128)(2,1)S(1)}, bf16[640,384]{1,0:T(8,128)(2,1)S(1)}, bf16[4,1152,256]{2,1,0:T(8,128)(2,1)S(1)}, bf16[64,96]{1,0:T(8,128)...) custom-call(f32[3,2,17]{2,1,0:T(2,128)S(1)} %copy-done.1), custom_call_target="tpu_custom_call" | custom-call | flops 10000000 | bytes 3561880 | tf_op jit(solution)/shard_map/pallas_call | solution.py:867
  14.5 1.3 %shard_map.31 = (f32[48,2,32,128]{3,2,1,0:T(8,128)S(1)}, f32[96,128]{1,0:T(8,128)S(1)}, f32[96,128]{1,0:T(8,128)S(1)}) custom-call(f32[32,32,128]{2,1,0:T(8,128)S(1)} %get-tuple-element.34.refs_0_, f32[472,128]{1,0:T(8,128)S(1)} %collective-permute-done.refs_1_.refs_3_, bf16[384,256]{1,0:T(8,128)(2,1)S(1)} %get-tuple-element.36.refs_2_.refs_4_, ...), custom_call_target="tpu_custom_call" | custom-call | flops 10000000 | bytes 2646016 | tf_op jit(solution)/shard_map/pallas_call | solution.py:867
  15.7 0.0 collective-permute-done.6.refs_9_
  15.8 0.0 collective-permute-done.1.refs_4_
  15.8 0.0 collective-permute-done.2.refs_5_
  15.8 0.0 collective-permute-done.4.refs_6_
  15.8 0.0 collective-permute-done.5.refs_7_
  15.8 0.7 %shard_map.34 = (f32[40,16,128]{2,1,0:T(8,128)S(1)}, f32[27,48,128]{2,1,0:T(8,128)S(1)}, f32[360,128]{1,0:T(8,128)S(1)}, f32[360,128]{1,0:T(8,128)S(1)}) custom-call(f32[96,128]{1,0:T(8,128)S(1)} %get-tuple-element.39.refs_0_, f32[96,128]{1,0:T(8,128)S(1)} %get-tuple-element.40.refs_1_, f32[19,24,128]{2,1,0:T(8,128)S(1)} %get-tuple-element.41.refs_2_, ...), custom_call_target="tpu_custom_call" | custom-call | flops 10000000 | bytes 2727936 | tf_op jit(solution)/shard_map/pallas_call | solution.py:867
  16.5 3.3 %collective-permute-start.7 = (f32[360,128]{1,0:T(8,128)S(1)}, f32[360,128]{1,0:T(8,128)S(1)}, u32[]{:S(2)}, u32[]{:S(2)}) collective-permute-start(f32[360,128]{1,0:T(8,128)S(1)} %get-tuple-element.53), channel_id=1, source_target_pairs={{0,8},{8,16},{16,24},{24,25},{25,17},{17,9},{9,1},{1,0},{2,10},{10... | collective-permute-start | bytes 552968 | tf_op jit(solution)/shard_map/ppermute | solution.py:64
  19.9 0.0 collective-permute-start.8
  19.9 3.1 %shard_map.35 = (f32[32,32,128]{2,1,0:T(8,128)S(1)}, f32[1296,384]{1,0:T(8,128)S(1)}) custom-call(f32[85,8,128]{2,1,0:T(8,128)S(1)} %get-tuple-element.33.refs_0_, f32[48,2,32,128]{3,2,1,0:T(8,128)S(1)} %get-tuple-element.38.refs_1_, f32[40,16,128]{2,1,0:T(8,128)S(1)} %get-tuple-element.47.refs_2_, f32[27,48,128]{2,1,0:T(8,128)S(1)} %get-tuple-element.48.refs_3_, ...), custom_call_target="tpu_custom_call" | custom-call | flops 10000000 | bytes 6121472 | tf_op jit(solution)/shard_map/pallas_call | solution.py:867
  23.0 0.0 collective-permute-done.7.refs_3_
  23.0 1.8 %collective-permute-done.8.refs_4_ = f32[360,128]{1,0:T(8,128)S(1)} collective-permute-done((f32[360,128]{1,0:T(8,128)S(1)}, f32[360,128]{1,0:T(8,128)S(1)}, u32[]{:S(2)}, u32[]{:S(2)}) %collective-permute-start.8) | collective-permute-done | bytes 184352 | tf_op jit(solution)/shard_map/ppermute | solution.py:64
  24.8 3.8 %shard_map.36 = f32[32,32,128]{2,1,0:T(8,128)} custom-call(f32[85,8,128]{2,1,0:T(8,128)S(1)} %get-tuple-element.33.refs_0_, f32[32,32,128]{2,1,0:T(8,128)S(1)} %get-tuple-element.51.refs_1_, f32[1296,384]{1,0:T(8,128)S(1)} %get-tuple-element.52.refs_2_, f32[360,128]{1,0:T(8,128)S(1)} %collective-permute-done.7.refs_3_, ...), custom_call_target="tpu_custom_call" | custom-call | flops 10000000 | bytes 6754304 | tf_op jit(solution)/shard_map/pallas_call | solution.py:867
  (2 shorter events, 0.0 us)
Async XLA Ops:
  0.0 1.0 %copy-start = (f32[32,32,128]{2,1,0:T(8,128)S(1)}, f32[32,32,128]{2,1,0:T(8,128)}, u32[]{:S(2)}) copy-start(f32[32,32,128]{2,1,0:T(8,128)} %refs_0_.3) | copy-start | bytes 1572868
  1.9 7.7 %collective-permute-start = (f32[472,128]{1,0:T(8,128)S(1)}, f32[472,128]{1,0:T(8,128)S(1)}, u32[]{:S(2)}, u32[]{:S(2)}) collective-permute-start(f32[472,128]{1,0:T(8,128)S(1)} %get-tuple-element.35), channel_id=1, source_target_pairs={{0,1},{1,0},{2,3},{3,2},{4,5},{5,4},{6,7},{7,6},{8,9},{9,8},{10,11... | collective-permute-start | bytes 725000 | tf_op jit(solution)/shard_map/ppermute | solution.py:64
  3.9 3.8 %collective-permute-start.3 = (f32[32,128]{1,0:T(8,128)S(1)}, f32[32,128]{1,0:T(8,128)S(1)}, u32[]{:S(2)}, u32[]{:S(2)}) collective-permute-start(f32[32,128]{1,0:T(8,128)S(1)} %get-tuple-element.44), channel_id=1, source_target_pairs={{0,4},{2,6},{4,0},{6,2},{1,5},{3,7},{5,1},{7,3},{8,12},{10,14},{12... | collective-permute-start | bytes 49160 | tf_op jit(solution)/shard_map/ppermute | solution.py:64
  6.2 9.5 %collective-permute-start.1 = (f32[504,128]{1,0:T(8,128)S(1)}, f32[504,128]{1,0:T(8,128)S(1)}, u32[]{:S(2)}, u32[]{:S(2)}) collective-permute-start(f32[504,128]{1,0:T(8,128)S(1)} %get-tuple-element.42), channel_id=1, source_target_pairs={{0,2},{2,4},{4,6},{6,14},{14,12},{12,10},{10,8},{8,0},{16,18},{18,... | collective-permute-start | bytes 774152 | tf_op jit(solution)/shard_map/ppermute | solution.py:64
  7.5 4.8 %copy-start.1 = (f32[3,2,17]{2,1,0:T(2,128)S(1)}, f32[3,2,17]{2,1,0:T(2,128)}, u32[]{:S(2)}) copy-start(f32[3,2,17]{2,1,0:T(2,128)} %refs_0_.2) | copy-start | bytes 1228
  7.5 8.3 %collective-permute-start.2 = (f32[504,128]{1,0:T(8,128)S(1)}, f32[504,128]{1,0:T(8,128)S(1)}, u32[]{:S(2)}, u32[]{:S(2)}) collective-permute-start(f32[504,128]{1,0:T(8,128)S(1)} %get-tuple-element.43), channel_id=1, source_target_pairs={{2,0},{4,2},{6,4},{14,6},{12,14},{10,12},{8,10},{0,8},{18,16},{20,... | collective-permute-start | bytes 774152 | tf_op jit(solution)/shard_map/ppermute | solution.py:64
  9.6 6.2 %collective-permute-start.4 = (f32[240,128]{1,0:T(8,128)S(1)}, f32[240,128]{1,0:T(8,128)S(1)}, u32[]{:S(2)}, u32[]{:S(2)}) collective-permute-start(f32[240,128]{1,0:T(8,128)S(1)} %get-tuple-element.45), channel_id=1, source_target_pairs={{0,2},{2,4},{4,6},{6,14},{14,12},{12,10},{10,8},{8,0},{16,18},{18,... | collective-permute-start | bytes 368648 | tf_op jit(solution)/shard_map/ppermute | solution.py:64
  10.8 5.0 %collective-permute-start.5 = (f32[240,128]{1,0:T(8,128)S(1)}, f32[240,128]{1,0:T(8,128)S(1)}, u32[]{:S(2)}, u32[]{:S(2)}) collective-permute-start(f32[240,128]{1,0:T(8,128)S(1)} %get-tuple-element.46), channel_id=1, source_target_pairs={{2,0},{4,2},{6,4},{14,6},{12,14},{10,12},{8,10},{0,8},{18,16},{20,... | collective-permute-start | bytes 368648 | tf_op jit(solution)/shard_map/ppermute | solution.py:64
  11.1 4.7 %collective-permute-start.6 = (f32[32,128]{1,0:T(8,128)S(1)}, f32[32,128]{1,0:T(8,128)S(1)}, u32[]{:S(2)}, u32[]{:S(2)}) collective-permute-start(f32[32,128]{1,0:T(8,128)S(1)} %shard_map.32.refs_0_), channel_id=1, source_target_pairs={{0,1},{1,0},{2,3},{3,2},{4,5},{5,4},{6,7},{7,6},{8,9},{9,8},{10,11... | collective-permute-start | bytes 49160 | tf_op jit(solution)/shard_map/ppermute | solution.py:64
  16.5 6.5 %collective-permute-start.7 = (f32[360,128]{1,0:T(8,128)S(1)}, f32[360,128]{1,0:T(8,128)S(1)}, u32[]{:S(2)}, u32[]{:S(2)}) collective-permute-start(f32[360,128]{1,0:T(8,128)S(1)} %get-tuple-element.53), channel_id=1, source_target_pairs={{0,8},{8,16},{16,24},{24,25},{25,17},{17,9},{9,1},{1,0},{2,10},{10... | collective-permute-start | bytes 552968 | tf_op jit(solution)/shard_map/ppermute | solution.py:64
  19.9 5.0 %collective-permute-start.8 = (f32[360,128]{1,0:T(8,128)S(1)}, f32[360,128]{1,0:T(8,128)S(1)}, u32[]{:S(2)}, u32[]{:S(2)}) collective-permute-start(f32[360,128]{1,0:T(8,128)S(1)} %get-tuple-element.54), channel_id=1, source_target_pairs={{8,0},{16,8},{24,16},{25,24},{17,25},{9,17},{1,9},{0,1},{10,2},{18... | collective-permute-start | bytes 552968 | tf_op jit(solution)/shard_map/ppermute | solution.py:64

commit v10 on v9

--- a/solution.py
+++ b/solution.py
@@ -139,9 +139,18 @@
         self.sum_planes = z.mid_all + RADIUS * len(self.z_routes)
         self.coarse_rows = -(-y.coarse_all // 16) * 16
         self.y_fine = RADIUS * z.fine
-        self.y_rows = up8(self.y_fine + SPAN * z.mid_all)
+        self.y_sums = max(EDGE * z.mid_all, SPAN * z.coarse_all)
+        self.y_rows = up8(self.y_fine + self.y_sums)
         self.slab_fine = RADIUS * RADIUS * len(self.z_routes)
-        self.slab_rows = up8(self.slab_fine + SPAN * self.slab_planes)
+        self.slab_mid = EDGE * EDGE * len(self.z_routes)
+        self.slab_coarse = SPAN * self.slab_planes
+        self.extra = max(self.slab_coarse - self.slab_mid, 0)
+        self.spare = x.fine - x.mid_all - x.coarse_all
+        self.pieces = -(-x.coarse_all // max(self.spare, 1))
+        if self.pieces * self.extra > self.slab_mid:
+            self.extra = 0
+        self.slab_sums = max(self.slab_mid, self.slab_coarse - self.extra)
+        self.slab_rows = up8(self.slab_fine + self.slab_sums)
         self.far_groups = x.fine // x.coarse_all
         self.far_planes = -(-z.coarse_all // self.far_groups)
         self.far_rows = up8(y.second * self.far_planes)
@@ -239,18 +248,18 @@
         turned = pltpu.roll(groups[g], (first - x.mid_all) % x.fine, 1)
         total = jnp.where((lane >= first) & (lane < first + x.coarse_all), turned, total)
     far[...] = total
-    is_side = iota((SPAN, x.fine), 1) < x.mid_all
     for message, route in zip((ahead, behind), s.y_routes):
         up = route.up()
         edge = jnp.where(up, charges[:, y.fine - RADIUS :, :], charges[:, :RADIUS, :])
         message[: s.y_fine] = edge.reshape(s.y_fine, x.fine)
+        packed[...] = jnp.zeros(packed.shape, F32)
         for p in range(z.mid_all):
-            last = jnp.where(is_side, own[p, y.mid_all - SPAN : y.mid_all], own[p, y.coarse_all - SPAN : y.coarse_all])
-            at = s.y_fine + p * SPAN
-            message[at : at + SPAN] = jnp.where(up, last, own[p, :SPAN])
-        filled = s.y_fine + SPAN * z.mid_all
-        if filled < s.y_rows:
-            message[filled:] = jnp.zeros((s.y_rows - filled, x.fine), F32)
+            packed[0, p * EDGE : (p + 1) * EDGE] = jnp.where(up, mid[p, y.mid_all - EDGE : y.mid_all], mid[p, :EDGE])
+        for p in range(z.coarse_all):
+            packed[1, p * SPAN : (p + 1) * SPAN] = coarse[p, :SPAN]
+        rows = s.y_rows - s.y_fine
+        is_mid = iota((rows, x.fine), 1) < x.mid_all
+        message[s.y_fine :] = jnp.where(is_mid, packed[0, :rows], packed[1, :rows])
     for message, route in zip(messages, s.z_routes):
         up = route.up().astype(jnp.int32)
         message[: s.z_fine] = charges[pl.ds(up * (z.fine - RADIUS), RADIUS)].reshape(s.z_fine, x.fine)
@@ -260,8 +269,9 @@
         for p in range(SPAN):
             plane = coarse[up * (z.coarse_all - SPAN) + p]
             packed[1, p * y.coarse_all : (p + 1) * y.coarse_all] = plane[: y.coarse_all]
-        is_mid = iota(packed.shape[1:], 1) < x.mid_all
-        message[s.z_fine :] = jnp.where(is_mid, packed[0], packed[1])
+        rows = s.z_rows - s.z_fine
+        is_mid = iota((rows, x.fine), 1) < x.mid_all
+        message[s.z_fine :] = jnp.where(is_mid, packed[0, :rows], packed[1, :rows])
     for message, route in zip(messages[nz:], s.z2_routes):
         up = route.up().astype(jnp.int32)
         message[...] = jnp.zeros(message.shape, F32)
@@ -273,6 +283,9 @@
 class Slab:
     def __init__(self, message, mid, coarse):
         self.message, self.mid, self.coarse = message, mid, coarse
+
+    def mid_rows(self, first, count):
+        return self.message[self.mid + first : self.mid + first + count]
 
     def coarse_rows(self, first, count):
         return self.message[self.coarse + first : self.coarse + first + count]
@@ -294,12 +307,21 @@
     return out
 
 
-def spread_kernel(s, nz, nz2, _, *rest):
+def spread_kernel(s, nz, nz2, _, __, *rest):
     z_messages, z2_messages = rest[:nz], rest[nz : nz + nz2]
-    ahead, behind = rest[-2:]
+    ahead, behind, packed = rest[-3:]
     z, y, x = s.z, s.y, s.x
-    is_mid = iota((SPAN, x.fine), 1) < x.mid_all
     planes = slabs(s, z_messages, z2_messages)
+    count = s.slab_rows - s.slab_fine
+    lane = iota((count, x.fine), 1)
+    packed[...] = jnp.zeros(packed.shape, F32)
+    for p, plane in enumerate(planes):
+        packed[1, p * SPAN : (p + 1) * SPAN] = plane.coarse_rows(0, SPAN)
+    for n in range(s.pieces if s.extra else 0):
+        first = x.mid_all + n * s.spare
+        turned = pltpu.roll(packed[1, s.slab_mid : s.slab_mid + up8(s.extra)], x.fine - s.spare - first, 1)
+        packed[2, n * s.extra : (n + 1) * s.extra] = turned[: s.extra]
+    coarse = jnp.where(lane < x.fine - s.spare, packed[1, :count], packed[2, :count])
     for message, route in zip((ahead, behind), s.y_routes):
         up = route.up()
         at = 0
@@ -308,12 +330,13 @@
             edge = jnp.where(up, slab[:, y.fine - RADIUS :], slab[:, :RADIUS])
             message[at : at + RADIUS * RADIUS] = edge.reshape(RADIUS * RADIUS, x.fine)
             at += RADIUS * RADIUS
+        at = 0
         for plane in planes:
-            last = plane.rows(is_mid, y.mid_all - SPAN, y.coarse_all - SPAN, SPAN)
-            message[at : at + SPAN] = jnp.where(up, last, plane.rows(is_mid, 0, 0, SPAN))
-            at += SPAN
-        if at < s.slab_rows:
-            message[at:] = jnp.zeros((s.slab_rows - at, x.fine), F32)
+            if plane.mid is not None:
+                first, last = plane.mid_rows(0, EDGE), plane.mid_rows(y.mid_all - EDGE, EDGE)
+                packed[0, at : at + EDGE] = jnp.where(up, last, first)
+                at += EDGE
+        message[s.slab_fine :] = jnp.where(lane < x.mid_all, packed[0, :count], coarse)
 
 
 def pass_kernel(s, far, out):
@@ -362,7 +385,7 @@
     rest = rest[nz + nz2 :]
     pairs = rest[:4]
     fars = rest[4 : 5 + nz + nz2]
-    fine, sums, first, second, raw, rows = rest[5 + nz + nz2 :]
+    fine, sums, first, second, raw, rows, near = rest[5 + nz + nz2 :]
     z, y, x = s.z, s.y, s.x
     below = s.y_routes[0].below()
     planes = slabs(s, z_messages, z2_messages)
@@ -386,27 +409,52 @@
                 rows[n, p, : y.second] = turned[at : at + y.second]
     is_mid = iota((y.second, x.fine), 1) < x.mid_all
 
-    def rows_of_plane(out, p, body, which, row, far_plane):
-        low, high = sides(which, row, SPAN)
+    lane = iota((up8(s.extra), x.fine), 1)
+    for side, got in enumerate(sides(1, s.slab_fine, s.slab_sums)):
+        near[side, : s.slab_sums] = got
+        if s.extra:
+            total = jnp.zeros(lane.shape, F32)
+            for n in range(s.pieces):
+                begin = x.mid_all + n * s.spare
+                piece = near[side, n * s.extra : n * s.extra + up8(s.extra)]
+                turned = pltpu.roll(piece, begin + s.spare, 1)
+                total = jnp.where(lane >= begin, turned, total)
+            near[side, s.slab_mid : s.slab_mid + s.extra] = total[: s.extra]
+    is_mid_edge = iota((EDGE, x.fine), 1) < x.mid_all
+    is_mid_span = iota((SPAN, x.fine), 1) < x.mid_all
+
+    def rows_of_plane(out, p, body, mids, coarses, far_plane):
         out[p, : y.mid_all] = body
-        out[p, s.low : s.low + SPAN] = low
-        out[p, s.high : s.high + SPAN] = high
+        for base, shift, n in ((s.low, SPAN - EDGE, 0), (s.high, 0, 1)):
+            if coarses is not None:
+                out[p, base : base + SPAN] = jnp.where(is_mid_span, 0.0, coarses[n])
+            if mids is not None:
+                at = slice(base + shift, base + shift + EDGE)
+                out[p, at] = jnp.where(is_mid_edge, mids[n], out[p, at])
         if far_plane is not None:
             at = slice(s.far, s.far + y.second)
             out[p, at] = jnp.where(is_mid, out[p, at], rows[far_plane][: y.second])
 
     for p in range(z.mid_all):
         far_plane = (0, p) if p < z.coarse_all else None
-        rows_of_plane(sums, s.place_of(p), own[p, : y.mid_all], 0, s.y_fine + p * SPAN, far_plane)
+        mids = sides(0, s.y_fine + p * EDGE, EDGE)
+        coarses = sides(0, s.y_fine + p * SPAN, SPAN) if p < z.coarse_all else None
+        rows_of_plane(sums, s.place_of(p), own[p, : y.mid_all], mids, coarses, far_plane)
     is_mid_row = iota((SPAN, x.fine), 1) < x.mid_all
     is_mid_rest = iota((y.mid_all - SPAN, x.fine), 1) < x.mid_all
     slab_far = [(1 + n, p) for n in range(nz) for p in range(SPAN)]
     for n, route in enumerate(s.z2_routes):
         at = jnp.where(route.below(), z.coarse_all - z.second, 0)
         slab_far += [(1 + nz + n, at + p) for p in range(z.second)]
+    held = 0
     for p, plane in enumerate(planes):
         body = [plane.rows(is_mid_row, 0, 0, SPAN), plane.rows(is_mid_rest, SPAN, None, y.mid_all - SPAN)]
-        rows_of_plane(raw, p, jnp.concatenate(body, axis=0), 1, s.slab_fine + p * SPAN, slab_far[p])
+        mids = None
+        if plane.mid is not None:
+            mids = sides(1, s.slab_fine + held * EDGE, EDGE)
+            held += 1
+        coarses = [near[side, p * SPAN : (p + 1) * SPAN] for side in range(2)]
+        rows_of_plane(raw, p, jnp.concatenate(body, axis=0), mids, coarses, slab_far[p])
     is_mid = iota((s.sum_rows, x.fine), 1) < x.mid_all
 
     def number(condition, a, b):
@@ -488,7 +536,7 @@
     return x.index() < x.count - 1
 
 
-def operator_kernel(s, taps, x_fine, x_sums, ends, y_own, y_edge, y_fine, y_mid, y_coarse, widen_x, widen_y, table):
+def later_kernel(s, taps, ends, table):
     y, x = s.y, s.x
     for level in range(2):
         for term in range(TERMS):
@@ -497,6 +545,30 @@
     is_second = iota((8, x.fine), 1) >= x.fine // TERMS
     for tap in range(TAPS):
         table[2 * TERMS * TAPS + tap] = jnp.where(is_second, taps[2, 1, tap], taps[2, 0, tap])
+
+    z, slots, wide = s.z, s.side * s.fine_groups, z_columns(s)
+    slot, column = iota((slots, wide), 0), iota((slots, wide), 1)
+    where, valid = slot, slot < z.fine
+    for n, route in enumerate(s.z_routes):
+        lower, i, first = route.below(), z.index(), z.fine + n * RADIUS
+        here = (slot >= first) & (slot < first + RADIUS)
+        where = jnp.where(here, slot - first + jnp.where(lower, -RADIUS, z.fine), where)
+        valid = choose(here, choose(lower, i >= 1, i + 1 < z.count), valid)
+    planes = band(taps, 0, where - column // RADIUS, valid)
+    r, c = iota((RADIUS, wide), 0), iota((RADIUS, wide), 1) % RADIUS
+    cells = (slots, RADIUS, wide)
+    for side, (offset, valid) in enumerate(((r - c - RADIUS, lower_x(x)), (r - c + RADIUS, higher_x(x)))):
+        columns = band(taps, 0, offset, choose(valid, r >= 0, r < 0))
+        for term in range(TERMS):
+            joint = jnp.broadcast_to(planes[term][:, None, :], cells) * jnp.broadcast_to(columns[term][None], cells)
+            high, low = split(joint.reshape(slots * RADIUS, wide))
+            at = 2 * term + side
+            ends[at, : slots * RADIUS] = high
+            ends[at, slots * RADIUS : 2 * slots * RADIUS] = high
+            ends[at, 2 * slots * RADIUS :] = low
+
+def operator_kernel(s, taps, x_fine, x_sums, y_own, y_edge, y_fine, y_mid, y_coarse, widen_x, widen_y):
+    y, x = s.y, s.x
     own, edge = x.fine, 64
     shape = (own + edge, x.fine)
     row, lane = iota(shape, 0), iota(shape, 1)
@@ -549,27 +621,6 @@
                 out[3 * own + n : 3 * own + 2 * n, cols] = high[own : own + n]
                 out[3 * own + 128 : 3 * own + 128 + n, cols] = low[own : own + n]
 
-    z, slots, wide = s.z, s.side * s.fine_groups, z_columns(s)
-    slot, column = iota((slots, wide), 0), iota((slots, wide), 1)
-    where, valid = slot, slot < z.fine
-    for n, route in enumerate(s.z_routes):
-        lower, i, first = route.below(), z.index(), z.fine + n * RADIUS
-        here = (slot >= first) & (slot < first + RADIUS)
-        where = jnp.where(here, slot - first + jnp.where(lower, -RADIUS, z.fine), where)
-        valid = choose(here, choose(lower, i >= 1, i + 1 < z.count), valid)
-    planes = band(taps, 0, where - column // RADIUS, valid)
-    r, c = iota((RADIUS, wide), 0), iota((RADIUS, wide), 1) % RADIUS
-    cells = (slots, RADIUS, wide)
-    for side, (offset, valid) in enumerate(((r - c - RADIUS, lower_x(x)), (r - c + RADIUS, higher_x(x)))):
-        columns = band(taps, 0, offset, choose(valid, r >= 0, r < 0))
-        for term in range(TERMS):
-            joint = jnp.broadcast_to(planes[term][:, None, :], cells) * jnp.broadcast_to(columns[term][None], cells)
-            high, low = split(joint.reshape(slots * RADIUS, wide))
-            at = 2 * term + side
-            ends[at, : slots * RADIUS] = high
-            ends[at, slots * RADIUS : 2 * slots * RADIUS] = high
-            ends[at, 2 * slots * RADIUS :] = low
-
     lower, higher = y.index() > 0, y.index() < y.count - 1
     far_below = s.y2_routes[0].below()
     n = up8(y.mid_all)
@@ -899,7 +950,7 @@
             pltpu.VMEM((z.mid_all, rows, n), F32),
             pltpu.VMEM((z.mid_all, up8(y.mid + 24), n), F32),
             pltpu.VMEM((z.mid_all, rows, n), F32),
-            pltpu.VMEM((2, s.z_rows - s.z_fine, n), F32),
+            pltpu.VMEM((2, max(s.z_rows - s.z_fine, s.y_rows - s.y_fine), n), F32),
             pltpu.VMEM((s.far_groups, s.far_rows, n), F32),
         ],
     )
@@ -912,7 +963,6 @@
         [
             array(3 * n, TERMS * n, dtype=BF16),
             array(3 * n + 256, (TERMS + 1) * n, dtype=BF16),
-            array(2 * TERMS, 3 * s.fine_groups * n, z_columns(s), dtype=BF16),
             array(TERMS * y.fine, 3 * y.fine, dtype=BF16),
             array(TERMS * y.fine, 6 * RADIUS, dtype=BF16),
             array(TERMS * y.fine, 3 * s.fine_rows, dtype=BF16),
@@ -920,18 +970,24 @@
             array(TERMS * s.coarse_rows, 3 * s.sum_rows, dtype=BF16),
             array(3 * n, n, dtype=BF16),
             array(y.fine, 3 * s.coarse_rows, dtype=BF16),
-            array((2 * TERMS + 1) * TAPS, 8, n),
         ],
         [kernel_taps],
     )
+    later = call(
+        bound(later_kernel),
+        [array(2 * TERMS, 3 * s.fine_groups * n, z_columns(s), dtype=BF16), array((2 * TERMS + 1) * TAPS, 8, n)],
+        [kernel_taps],
+    )
+    ends, table = later
     ahead, behind = call(
         bound(spread_kernel, nz, nz2),
         [array(s.slab_rows, n), array(s.slab_rows, n)],
-        [passed, *z_got],
+        [passed, later[1], *z_got],
+        [pltpu.VMEM((3, up8(max(s.slab_coarse, s.slab_rows - s.slab_fine)) + 8, n), F32)],
     )
     sides += [s.y_routes[0](ahead), s.y_routes[1](behind)]
     fars = [far] + [route(passed) for route in s.z_routes + s.z2_routes]
-    x_fine, x_sums, ends, y_own, y_edge, y_fine, y_mid, y_coarse, widen_x, widen_y, table = operators
+    x_fine, x_sums, y_own, y_edge, y_fine, y_mid, y_coarse, widen_x, widen_y = operators
     t_part, last, start = call(
         bound(early_kernel, nz),
         [array(z.fine + 2 * RADIUS, TERMS, y.fine, n)] + [array(s.fine_groups * y.fine, n)] * 2,
@@ -947,7 +1003,11 @@
             array(s.x_rows, n),
         ],
         [last, start, own, *z_got, *sides, *fars],
-        [pltpu.VMEM((s.slab_planes, s.sum_rows, n), F32), pltpu.VMEM((1 + nz + nz2, z.coarse_all, 8, n), F32)],
+        [
+            pltpu.VMEM((s.slab_planes, s.sum_rows, n), F32),
+            pltpu.VMEM((1 + nz + nz2, z.coarse_all, 8, n), F32),
+            pltpu.VMEM((2, up8(s.slab_coarse) + 8, n), F32),
+        ],
     )
     first, second = s.x_routes[0](first), s.x_routes[1](second)
     fine, sums = call(

time: 28.8 us -> 28.2 us (0.979)
  waiting for transfers between devices: 3.65 us -> 2.54 us
  Pallas kernels: 12.2 us -> 12.8 us
    ppermute x9, waiting for transfers between devices: 3.65 us -> 2.54 us  [__call__(): return lax.ppermute(x, self.names, self.pairs)]
    pallas_call x9 -> x10, Pallas kernels: 12.2 us -> 12.8 us  [call(): pl.pallas_call(kernel, out_shape=tuple(outs), in_specs=specs, out_specs=t...]
  transfers between devices with their start and end apart: 9 -> 9, of which waited for: 2 -> 2; matrix products, arithmetic and copies ran while one was open for 0% -> 0% of each run, Pallas kernels for 23% -> 25%
where the time goes in v10:
time: 28.2 us; the launch traced here: 28.1 us
  Pallas kernels  12.8 us (45%)
  starting transfers between devices  11.8 us (42%)
  waiting for transfers between devices  2.54 us (9%)
  local copies, waits for them, and re-layouts  0.8 us (3%)
    pallas_call x10, Pallas kernels, call(): pl.pallas_call(kernel, out_shape=tuple(outs), in_specs=specs, out_specs=t...  12.8 us
    ppermute x9, starting transfers between devices, __call__(): return lax.ppermute(x, self.names, self.pairs)  11.8 us
    ppermute x9, waiting for transfers between devices, __call__(): return lax.ppermute(x, self.names, self.pairs)  2.54 us
    unnamed x4, local copies, waits for them, and re-layouts  0.8 us
  transfers between devices with their start and end apart: 9, of which 2 were waited for; matrix products, arithmetic and copies ran while one was open for 0% of the time, Pallas kernels for 25%

profile of v10, /device:TPU:1, one launch (start us, length us, event | category | flops | bytes accessed | tf_op | source)
XLA Modules:
  0.0 28.1 jit_solution(14272976861573886362)
XLA Ops:
  0.0 0.0 copy-start
  0.0 0.0 copy-start.1
  0.0 0.2 shard_map.29.refs_1_
  0.2 0.8 %copy-done = f32[32,32,128]{2,1,0:T(8,128)S(1)} copy-done((f32[32,32,128]{2,1,0:T(8,128)S(1)}, f32[32,32,128]{2,1,0:T(8,128)}, u32[]{:S(2)}) %copy-start) | copy-done | bytes 524312
  1.0 0.9 %shard_map.30 = (f32[32,32,128]{2,1,0:T(8,128)S(1)}, f32[19,24,128]{2,1,0:T(8,128)S(1)}, f32[472,128]{1,0:T(8,128)S(1)}, f32[472,128]{1,0:T(8,128)S(1)}, f32[32,128]{1,0:T(8,128)S(1)}, /*index=5*/f32[472,128]{1,0:T(8,128)S(1)}) custom-call(f32[32,32,128]{2,1,0:T(8,128)S(1)} %copy-done, bf16[128,256]{1,0:T(8,128)(2,1)S(1)} %shard_map.29.refs_1_), custom_call_target="tpu_custom_call" | custom-call | flops 10000000 | bytes 2088960 | tf_op jit(solution)/shard_map/pallas_call | solution.py:918
  1.9 2.1 %collective-permute-start = (f32[472,128]{1,0:T(8,128)S(1)}, f32[472,128]{1,0:T(8,128)S(1)}, u32[]{:S(2)}, u32[]{:S(2)}) collective-permute-start(f32[472,128]{1,0:T(8,128)S(1)} %get-tuple-element.35), channel_id=1, source_target_pairs={{0,1},{1,0},{2,3},{3,2},{4,5},{5,4},{6,7},{7,6},{8,9},{9,8},{10,11... | collective-permute-start | bytes 725000 | tf_op jit(solution)/shard_map/ppermute | solution.py:64
  4.0 2.3 %collective-permute-start.3 = (f32[32,128]{1,0:T(8,128)S(1)}, f32[32,128]{1,0:T(8,128)S(1)}, u32[]{:S(2)}, u32[]{:S(2)}) collective-permute-start(f32[32,128]{1,0:T(8,128)S(1)} %get-tuple-element.44), channel_id=1, source_target_pairs={{0,4},{2,6},{4,0},{6,2},{1,5},{3,7},{5,1},{7,3},{8,12},{10,14},{12... | collective-permute-start | bytes 49160 | tf_op jit(solution)/shard_map/ppermute | solution.py:64
  6.3 1.2 %collective-permute-start.1 = (f32[472,128]{1,0:T(8,128)S(1)}, f32[472,128]{1,0:T(8,128)S(1)}, u32[]{:S(2)}, u32[]{:S(2)}) collective-permute-start(f32[472,128]{1,0:T(8,128)S(1)} %get-tuple-element.42), channel_id=1, source_target_pairs={{0,2},{2,4},{4,6},{6,14},{14,12},{12,10},{10,8},{8,0},{16,18},{18,... | collective-permute-start | bytes 725000 | tf_op jit(solution)/shard_map/ppermute | solution.py:64
  7.5 0.2 collective-permute-start.2
  7.8 0.0 copy-done.1
  7.8 1.1 %shard_map.28 = (bf16[4,1152,256]{2,1,0:T(8,128)(2,1)S(1)}, f32[85,8,128]{2,1,0:T(8,128)S(1)}) custom-call(f32[3,2,17]{2,1,0:T(2,128)S(1)} %copy-done.1), custom_call_target="tpu_custom_call" | custom-call | flops 10000000 | bytes 2707864 | tf_op jit(solution)/shard_map/pallas_call | solution.py:918
  8.9 0.0 collective-permute-done.3.refs_0_.refs_8_
  8.9 0.7 %collective-permute-done.refs_1_.refs_2_.refs_3_ = f32[472,128]{1,0:T(8,128)S(1)} collective-permute-done((f32[472,128]{1,0:T(8,128)S(1)}, f32[472,128]{1,0:T(8,128)S(1)}, u32[]{:S(2)}, u32[]{:S(2)}) %collective-permute-start) | collective-permute-done | bytes 241696 | tf_op jit(solution)/shard_map/ppermute | solution.py:64
  9.6 0.1 shard_map.34
  9.7 1.3 %collective-permute-start.4 = (f32[192,128]{1,0:T(8,128)S(1)}, f32[192,128]{1,0:T(8,128)S(1)}, u32[]{:S(2)}, u32[]{:S(2)}) collective-permute-start(f32[192,128]{1,0:T(8,128)S(1)} %get-tuple-element.45), channel_id=1, source_target_pairs={{0,2},{2,4},{4,6},{6,14},{14,12},{12,10},{10,8},{8,0},{16,18},{18,... | collective-permute-start | bytes 294920 | tf_op jit(solution)/shard_map/ppermute | solution.py:64
  10.9 0.2 collective-permute-start.5
  11.2 1.2 %collective-permute-start.6 = (f32[32,128]{1,0:T(8,128)S(1)}, f32[32,128]{1,0:T(8,128)S(1)}, u32[]{:S(2)}, u32[]{:S(2)}) collective-permute-start(f32[32,128]{1,0:T(8,128)S(1)} %shard_map.33.refs_0_), channel_id=1, source_target_pairs={{0,1},{1,0},{2,3},{3,2},{4,5},{5,4},{6,7},{7,6},{8,9},{9,8},{10,11... | collective-permute-start | bytes 49160 | tf_op jit(solution)/shard_map/ppermute | solution.py:64
  12.4 1.5 %shard_map.31 = (bf16[384,256]{1,0:T(8,128)(2,1)S(1)}, bf16[640,384]{1,0:T(8,128)(2,1)S(1)}, bf16[64,96]{1,0:T(8,128)(2,1)S(1)}, bf16[64,48]{1,0:T(8,128)(2,1)S(...) custom-call(f32[3,2,17]{2,1,0:T(2,128)S(1)} %copy-done.1), custom_call_target="tpu_custom_call" | custom-call | flops 10000000 | bytes 854424 | tf_op jit(solution)/shard_map/pallas_call | solution.py:918
  13.9 1.3 %shard_map.32 = (f32[48,2,32,128]{3,2,1,0:T(8,128)S(1)}, f32[96,128]{1,0:T(8,128)S(1)}, f32[96,128]{1,0:T(8,128)S(1)}) custom-call(f32[32,32,128]{2,1,0:T(8,128)S(1)} %get-tuple-element.34.refs_0_, f32[472,128]{1,0:T(8,128)S(1)} %collective-permute-done.refs_1_.refs_2_.refs_3_, bf16[384,256]{1,0:T(8,128)(2,1)S(1)} %get-tuple-element.36.refs_2_.refs_4_, ...), custom_call_target="tpu_custom_call" | custom-call | flops 10000000 | bytes 2646016 | tf_op jit(solution)/shard_map/pallas_call | solution.py:918
  15.2 0.0 collective-permute-done.6.refs_9_
  15.2 0.0 collective-permute-done.1.refs_4_
  15.2 0.0 collective-permute-done.2.refs_5_
  15.3 0.0 collective-permute-done.4.refs_6_
  15.3 0.0 collective-permute-done.5.refs_7_
  15.3 0.8 %shard_map.35 = (f32[40,16,128]{2,1,0:T(8,128)S(1)}, f32[27,48,128]{2,1,0:T(8,128)S(1)}, f32[360,128]{1,0:T(8,128)S(1)}, f32[360,128]{1,0:T(8,128)S(1)}) custom-call(f32[96,128]{1,0:T(8,128)S(1)} %get-tuple-element.39.refs_0_, f32[96,128]{1,0:T(8,128)S(1)} %get-tuple-element.40.refs_1_, f32[19,24,128]{2,1,0:T(8,128)S(1)} %get-tuple-element.41.refs_2_, ...), custom_call_target="tpu_custom_call" | custom-call | flops 10000000 | bytes 2646016 | tf_op jit(solution)/shard_map/pallas_call | solution.py:918
  16.0 3.3 %collective-permute-start.7 = (f32[360,128]{1,0:T(8,128)S(1)}, f32[360,128]{1,0:T(8,128)S(1)}, u32[]{:S(2)}, u32[]{:S(2)}) collective-permute-start(f32[360,128]{1,0:T(8,128)S(1)} %get-tuple-element.53), channel_id=1, source_target_pairs={{0,8},{8,16},{16,24},{24,25},{25,17},{17,9},{9,1},{1,0},{2,10},{10... | collective-permute-start | bytes 552968 | tf_op jit(solution)/shard_map/ppermute | solution.py:64
  19.3 0.0 collective-permute-start.8
  19.3 3.1 %shard_map.36 = (f32[32,32,128]{2,1,0:T(8,128)S(1)}, f32[1296,384]{1,0:T(8,128)S(1)}) custom-call(f32[85,8,128]{2,1,0:T(8,128)S(1)} %get-tuple-element.33.refs_1_.refs_0_, f32[48,2,32,128]{3,2,1,0:T(8,128)S(1)} %get-tuple-element.38.refs_1_, f32[40,16,128]{2,1,0:T(8,128)S(1)} %get-tuple-element.47.refs_2_, f32[27,48,128]{2,1,0:T(8,128)S(1)} %get-tuple-element.48.refs_3_, ...), custom_call_target="tpu_custom_call" | custom-call | flops 10000000 | bytes 6121472 | tf_op jit(solution)/shard_map/pallas_call | solution.py:918
  22.4 0.0 collective-permute-done.7.refs_3_
  22.4 1.8 %collective-permute-done.8.refs_4_ = f32[360,128]{1,0:T(8,128)S(1)} collective-permute-done((f32[360,128]{1,0:T(8,128)S(1)}, f32[360,128]{1,0:T(8,128)S(1)}, u32[]{:S(2)}, u32[]{:S(2)}) %collective-permute-start.8) | collective-permute-done | bytes 184352 | tf_op jit(solution)/shard_map/ppermute | solution.py:64
  24.3 3.8 %shard_map.37 = f32[32,32,128]{2,1,0:T(8,128)} custom-call(f32[85,8,128]{2,1,0:T(8,128)S(1)} %get-tuple-element.33.refs_1_.refs_0_, f32[32,32,128]{2,1,0:T(8,128)S(1)} %get-tuple-element.51.refs_1_, f32[1296,384]{1,0:T(8,128)S(1)} %get-tuple-element.52.refs_2_, f32[360,128]{1,0:T(8,128)S(1)} %collective-permute-done.7.refs_3_, ...), custom_call_target="tpu_custom_call" | custom-call | flops 10000000 | bytes 6754304 | tf_op jit(solution)/shard_map/pallas_call | solution.py:918
  (1 shorter events, 0.0 us)
Async XLA Ops:
  0.0 1.0 %copy-start = (f32[32,32,128]{2,1,0:T(8,128)S(1)}, f32[32,32,128]{2,1,0:T(8,128)}, u32[]{:S(2)}) copy-start(f32[32,32,128]{2,1,0:T(8,128)} %refs_0_.4) | copy-start | bytes 1572868
  0.0 7.8 %copy-start.1 = (f32[3,2,17]{2,1,0:T(2,128)S(1)}, f32[3,2,17]{2,1,0:T(2,128)}, u32[]{:S(2)}) copy-start(f32[3,2,17]{2,1,0:T(2,128)} %refs_0_.5) | copy-start | bytes 1228
  1.9 7.7 %collective-permute-start = (f32[472,128]{1,0:T(8,128)S(1)}, f32[472,128]{1,0:T(8,128)S(1)}, u32[]{:S(2)}, u32[]{:S(2)}) collective-permute-start(f32[472,128]{1,0:T(8,128)S(1)} %get-tuple-element.35), channel_id=1, source_target_pairs={{0,1},{1,0},{2,3},{3,2},{4,5},{5,4},{6,7},{7,6},{8,9},{9,8},{10,11... | collective-permute-start | bytes 725000 | tf_op jit(solution)/shard_map/ppermute | solution.py:64
  4.0 4.9 %collective-permute-start.3 = (f32[32,128]{1,0:T(8,128)S(1)}, f32[32,128]{1,0:T(8,128)S(1)}, u32[]{:S(2)}, u32[]{:S(2)}) collective-permute-start(f32[32,128]{1,0:T(8,128)S(1)} %get-tuple-element.44), channel_id=1, source_target_pairs={{0,4},{2,6},{4,0},{6,2},{1,5},{3,7},{5,1},{7,3},{8,12},{10,14},{12... | collective-permute-start | bytes 49160 | tf_op jit(solution)/shard_map/ppermute | solution.py:64
  6.3 8.9 %collective-permute-start.1 = (f32[472,128]{1,0:T(8,128)S(1)}, f32[472,128]{1,0:T(8,128)S(1)}, u32[]{:S(2)}, u32[]{:S(2)}) collective-permute-start(f32[472,128]{1,0:T(8,128)S(1)} %get-tuple-element.42), channel_id=1, source_target_pairs={{0,2},{2,4},{4,6},{6,14},{14,12},{12,10},{10,8},{8,0},{16,18},{18,... | collective-permute-start | bytes 725000 | tf_op jit(solution)/shard_map/ppermute | solution.py:64
  7.5 7.7 %collective-permute-start.2 = (f32[472,128]{1,0:T(8,128)S(1)}, f32[472,128]{1,0:T(8,128)S(1)}, u32[]{:S(2)}, u32[]{:S(2)}) collective-permute-start(f32[472,128]{1,0:T(8,128)S(1)} %get-tuple-element.43), channel_id=1, source_target_pairs={{2,0},{4,2},{6,4},{14,6},{12,14},{10,12},{8,10},{0,8},{18,16},{20,... | collective-permute-start | bytes 725000 | tf_op jit(solution)/shard_map/ppermute | solution.py:64
  9.7 5.6 %collective-permute-start.4 = (f32[192,128]{1,0:T(8,128)S(1)}, f32[192,128]{1,0:T(8,128)S(1)}, u32[]{:S(2)}, u32[]{:S(2)}) collective-permute-start(f32[192,128]{1,0:T(8,128)S(1)} %get-tuple-element.45), channel_id=1, source_target_pairs={{0,2},{2,4},{4,6},{6,14},{14,12},{12,10},{10,8},{8,0},{16,18},{18,... | collective-permute-start | bytes 294920 | tf_op jit(solution)/shard_map/ppermute | solution.py:64
  10.9 4.3 %collective-permute-start.5 = (f32[192,128]{1,0:T(8,128)S(1)}, f32[192,128]{1,0:T(8,128)S(1)}, u32[]{:S(2)}, u32[]{:S(2)}) collective-permute-start(f32[192,128]{1,0:T(8,128)S(1)} %get-tuple-element.46), channel_id=1, source_target_pairs={{2,0},{4,2},{6,4},{14,6},{12,14},{10,12},{8,10},{0,8},{18,16},{20,... | collective-permute-start | bytes 294920 | tf_op jit(solution)/shard_map/ppermute | solution.py:64
  11.2 4.1 %collective-permute-start.6 = (f32[32,128]{1,0:T(8,128)S(1)}, f32[32,128]{1,0:T(8,128)S(1)}, u32[]{:S(2)}, u32[]{:S(2)}) collective-permute-start(f32[32,128]{1,0:T(8,128)S(1)} %shard_map.33.refs_0_), channel_id=1, source_target_pairs={{0,1},{1,0},{2,3},{3,2},{4,5},{5,4},{6,7},{7,6},{8,9},{9,8},{10,11... | collective-permute-start | bytes 49160 | tf_op jit(solution)/shard_map/ppermute | solution.py:64
  16.0 6.4 %collective-permute-start.7 = (f32[360,128]{1,0:T(8,128)S(1)}, f32[360,128]{1,0:T(8,128)S(1)}, u32[]{:S(2)}, u32[]{:S(2)}) collective-permute-start(f32[360,128]{1,0:T(8,128)S(1)} %get-tuple-element.53), channel_id=1, source_target_pairs={{0,8},{8,16},{16,24},{24,25},{25,17},{17,9},{9,1},{1,0},{2,10},{10... | collective-permute-start | bytes 552968 | tf_op jit(solution)/shard_map/ppermute | solution.py:64
  19.3 5.0 %collective-permute-start.8 = (f32[360,128]{1,0:T(8,128)S(1)}, f32[360,128]{1,0:T(8,128)S(1)}, u32[]{:S(2)}, u32[]{:S(2)}) collective-permute-start(f32[360,128]{1,0:T(8,128)S(1)} %get-tuple-element.54), channel_id=1, source_target_pairs={{8,0},{16,8},{24,16},{25,24},{17,25},{9,17},{1,9},{0,1},{10,2},{18... | collective-permute-start | bytes 552968 | tf_op jit(solution)/shard_map/ppermute | solution.py:64

commit v11 on v10

--- a/solution.py
+++ b/solution.py
@@ -584,7 +584,8 @@
         return jnp.where(is_own, own_place, jnp.where(is_low, low_place + r, high_place + r)), valid
 
     half = s.edge_sums
-    fine = band(taps, 0, row - lane, is_own)
+    cell, column = iota((own, x.fine), 0), iota((own, x.fine), 1)
+    fine = band(taps, 0, cell - column, cell >= 0)
     where, valid = place(half, row - 1, row < x.mid_all, 0, EDGE, 2 - EDGE, x.mid - 1)
     mid = band(taps, 1, where - (lane - 1), valid & (lane < x.mid_all))
     first = x.mid_all
@@ -946,7 +947,7 @@
         [array(*charges.shape), array(z.mid_all, rows, n)] + [array(s.y_rows, n)] * 2 + [array(s.far_rows, n)] + [array(s.z_rows, n)] * nz + [array(s.z2_rows, n)] * nz2,
         [charges, weights],
         [
-            pltpu.VMEM((z.fine, y.fine + 16, n), F32),
+            pltpu.VMEM((z.fine, y.fine + 32, n), F32),
             pltpu.VMEM((z.mid_all, rows, n), F32),
             pltpu.VMEM((z.mid_all, up8(y.mid + 24), n), F32),
             pltpu.VMEM((z.mid_all, rows, n), F32),

time: 28.2 us -> 28.2 us (level)
  no operation moved by 1% of the time
where the time goes in v11:
time: 28.2 us; the launch traced here: 28.1 us
  Pallas kernels  12.8 us (45%)
  starting transfers between devices  11.8 us (42%)
  waiting for transfers between devices  2.54 us (9%)
  local copies, waits for them, and re-layouts  0.8 us (3%)
    pallas_call x10, Pallas kernels, call(): pl.pallas_call(kernel, out_shape=tuple(outs), in_specs=specs, out_specs=t...  12.8 us
    ppermute x9, starting transfers between devices, __call__(): return lax.ppermute(x, self.names, self.pairs)  11.8 us
    ppermute x9, waiting for transfers between devices, __call__(): return lax.ppermute(x, self.names, self.pairs)  2.54 us
    unnamed x4, local copies, waits for them, and re-layouts  0.8 us
  transfers between devices with their start and end apart: 9, of which 2 were waited for; matrix products, arithmetic and copies ran while one was open for 0% of the time, Pallas kernels for 25%

profile of v11, /device:TPU:1, one launch (start us, length us, event | category | flops | bytes accessed | tf_op | source)
XLA Modules:
  0.0 28.1 jit_solution(17105991588213558580)
XLA Ops:
  0.0 0.0 copy-start
  0.0 0.0 copy-start.1
  0.0 0.2 shard_map.29.refs_1_
  0.2 0.8 %copy-done = f32[32,32,128]{2,1,0:T(8,128)S(1)} copy-done((f32[32,32,128]{2,1,0:T(8,128)S(1)}, f32[32,32,128]{2,1,0:T(8,128)}, u32[]{:S(2)}) %copy-start) | copy-done | bytes 524312
  1.0 0.9 %shard_map.30 = (f32[32,32,128]{2,1,0:T(8,128)S(1)}, f32[19,24,128]{2,1,0:T(8,128)S(1)}, f32[472,128]{1,0:T(8,128)S(1)}, f32[472,128]{1,0:T(8,128)S(1)}, f32[32,128]{1,0:T(8,128)S(1)}, /*index=5*/f32[472,128]{1,0:T(8,128)S(1)}) custom-call(f32[32,32,128]{2,1,0:T(8,128)S(1)} %copy-done, bf16[128,256]{1,0:T(8,128)(2,1)S(1)} %shard_map.29.refs_1_), custom_call_target="tpu_custom_call" | custom-call | flops 10000000 | bytes 2088960 | tf_op jit(solution)/shard_map/pallas_call | solution.py:919
  1.9 2.1 %collective-permute-start = (f32[472,128]{1,0:T(8,128)S(1)}, f32[472,128]{1,0:T(8,128)S(1)}, u32[]{:S(2)}, u32[]{:S(2)}) collective-permute-start(f32[472,128]{1,0:T(8,128)S(1)} %get-tuple-element.35), channel_id=1, source_target_pairs={{0,1},{1,0},{2,3},{3,2},{4,5},{5,4},{6,7},{7,6},{8,9},{9,8},{10,11... | collective-permute-start | bytes 725000 | tf_op jit(solution)/shard_map/ppermute | solution.py:64
  4.0 2.3 %collective-permute-start.3 = (f32[32,128]{1,0:T(8,128)S(1)}, f32[32,128]{1,0:T(8,128)S(1)}, u32[]{:S(2)}, u32[]{:S(2)}) collective-permute-start(f32[32,128]{1,0:T(8,128)S(1)} %get-tuple-element.44), channel_id=1, source_target_pairs={{0,4},{2,6},{4,0},{6,2},{1,5},{3,7},{5,1},{7,3},{8,12},{10,14},{12... | collective-permute-start | bytes 49160 | tf_op jit(solution)/shard_map/ppermute | solution.py:64
  6.3 1.2 %collective-permute-start.1 = (f32[472,128]{1,0:T(8,128)S(1)}, f32[472,128]{1,0:T(8,128)S(1)}, u32[]{:S(2)}, u32[]{:S(2)}) collective-permute-start(f32[472,128]{1,0:T(8,128)S(1)} %get-tuple-element.42), channel_id=1, source_target_pairs={{0,2},{2,4},{4,6},{6,14},{14,12},{12,10},{10,8},{8,0},{16,18},{18,... | collective-permute-start | bytes 725000 | tf_op jit(solution)/shard_map/ppermute | solution.py:64
  7.5 0.2 collective-permute-start.2
  7.8 0.0 copy-done.1
  7.8 1.1 %shard_map.28 = (bf16[4,1152,256]{2,1,0:T(8,128)(2,1)S(1)}, f32[85,8,128]{2,1,0:T(8,128)S(1)}) custom-call(f32[3,2,17]{2,1,0:T(2,128)S(1)} %copy-done.1), custom_call_target="tpu_custom_call" | custom-call | flops 10000000 | bytes 2707864 | tf_op jit(solution)/shard_map/pallas_call | solution.py:919
  8.9 0.0 collective-permute-done.3.refs_0_.refs_8_
  8.9 0.7 %collective-permute-done.refs_1_.refs_2_.refs_3_ = f32[472,128]{1,0:T(8,128)S(1)} collective-permute-done((f32[472,128]{1,0:T(8,128)S(1)}, f32[472,128]{1,0:T(8,128)S(1)}, u32[]{:S(2)}, u32[]{:S(2)}) %collective-permute-start) | collective-permute-done | bytes 241696 | tf_op jit(solution)/shard_map/ppermute | solution.py:64
  9.6 0.1 shard_map.34
  9.7 1.2 %collective-permute-start.4 = (f32[192,128]{1,0:T(8,128)S(1)}, f32[192,128]{1,0:T(8,128)S(1)}, u32[]{:S(2)}, u32[]{:S(2)}) collective-permute-start(f32[192,128]{1,0:T(8,128)S(1)} %get-tuple-element.45), channel_id=1, source_target_pairs={{0,2},{2,4},{4,6},{6,14},{14,12},{12,10},{10,8},{8,0},{16,18},{18,... | collective-permute-start | bytes 294920 | tf_op jit(solution)/shard_map/ppermute | solution.py:64
  10.9 0.2 collective-permute-start.5
  11.2 1.2 %collective-permute-start.6 = (f32[32,128]{1,0:T(8,128)S(1)}, f32[32,128]{1,0:T(8,128)S(1)}, u32[]{:S(2)}, u32[]{:S(2)}) collective-permute-start(f32[32,128]{1,0:T(8,128)S(1)} %shard_map.33.refs_0_), channel_id=1, source_target_pairs={{0,1},{1,0},{2,3},{3,2},{4,5},{5,4},{6,7},{7,6},{8,9},{9,8},{10,11... | collective-permute-start | bytes 49160 | tf_op jit(solution)/shard_map/ppermute | solution.py:64
  12.4 1.5 %shard_map.31 = (bf16[384,256]{1,0:T(8,128)(2,1)S(1)}, bf16[640,384]{1,0:T(8,128)(2,1)S(1)}, bf16[64,96]{1,0:T(8,128)(2,1)S(1)}, bf16[64,48]{1,0:T(8,128)(2,1)S(...) custom-call(f32[3,2,17]{2,1,0:T(2,128)S(1)} %copy-done.1), custom_call_target="tpu_custom_call" | custom-call | flops 10000000 | bytes 854424 | tf_op jit(solution)/shard_map/pallas_call | solution.py:919
  13.9 1.3 %shard_map.32 = (f32[48,2,32,128]{3,2,1,0:T(8,128)S(1)}, f32[96,128]{1,0:T(8,128)S(1)}, f32[96,128]{1,0:T(8,128)S(1)}) custom-call(f32[32,32,128]{2,1,0:T(8,128)S(1)} %get-tuple-element.34.refs_0_, f32[472,128]{1,0:T(8,128)S(1)} %collective-permute-done.refs_1_.refs_2_.refs_3_, bf16[384,256]{1,0:T(8,128)(2,1)S(1)} %get-tuple-element.36.refs_2_.refs_4_, ...), custom_call_target="tpu_custom_call" | custom-call | flops 10000000 | bytes 2646016 | tf_op jit(solution)/shard_map/pallas_call | solution.py:919
  15.2 0.0 collective-permute-done.6.refs_9_
  15.2 0.0 collective-permute-done.1.refs_4_
  15.2 0.0 collective-permute-done.2.refs_5_
  15.2 0.0 collective-permute-done.4.refs_6_
  15.3 0.0 collective-permute-done.5.refs_7_
  15.3 0.8 %shard_map.35 = (f32[40,16,128]{2,1,0:T(8,128)S(1)}, f32[27,48,128]{2,1,0:T(8,128)S(1)}, f32[360,128]{1,0:T(8,128)S(1)}, f32[360,128]{1,0:T(8,128)S(1)}) custom-call(f32[96,128]{1,0:T(8,128)S(1)} %get-tuple-element.39.refs_0_, f32[96,128]{1,0:T(8,128)S(1)} %get-tuple-element.40.refs_1_, f32[19,24,128]{2,1,0:T(8,128)S(1)} %get-tuple-element.41.refs_2_, ...), custom_call_target="tpu_custom_call" | custom-call | flops 10000000 | bytes 2646016 | tf_op jit(solution)/shard_map/pallas_call | solution.py:919
  16.0 3.3 %collective-permute-start.7 = (f32[360,128]{1,0:T(8,128)S(1)}, f32[360,128]{1,0:T(8,128)S(1)}, u32[]{:S(2)}, u32[]{:S(2)}) collective-permute-start(f32[360,128]{1,0:T(8,128)S(1)} %get-tuple-element.53), channel_id=1, source_target_pairs={{0,8},{8,16},{16,24},{24,25},{25,17},{17,9},{9,1},{1,0},{2,10},{10... | collective-permute-start | bytes 552968 | tf_op jit(solution)/shard_map/ppermute | solution.py:64
  19.3 0.0 collective-permute-start.8
  19.3 3.1 %shard_map.36 = (f32[32,32,128]{2,1,0:T(8,128)S(1)}, f32[1296,384]{1,0:T(8,128)S(1)}) custom-call(f32[85,8,128]{2,1,0:T(8,128)S(1)} %get-tuple-element.33.refs_1_.refs_0_, f32[48,2,32,128]{3,2,1,0:T(8,128)S(1)} %get-tuple-element.38.refs_1_, f32[40,16,128]{2,1,0:T(8,128)S(1)} %get-tuple-element.47.refs_2_, f32[27,48,128]{2,1,0:T(8,128)S(1)} %get-tuple-element.48.refs_3_, ...), custom_call_target="tpu_custom_call" | custom-call | flops 10000000 | bytes 6121472 | tf_op jit(solution)/shard_map/pallas_call | solution.py:919
  22.4 0.0 collective-permute-done.7.refs_3_
  22.4 1.8 %collective-permute-done.8.refs_4_ = f32[360,128]{1,0:T(8,128)S(1)} collective-permute-done((f32[360,128]{1,0:T(8,128)S(1)}, f32[360,128]{1,0:T(8,128)S(1)}, u32[]{:S(2)}, u32[]{:S(2)}) %collective-permute-start.8) | collective-permute-done | bytes 184352 | tf_op jit(solution)/shard_map/ppermute | solution.py:64
  24.3 3.8 %shard_map.37 = f32[32,32,128]{2,1,0:T(8,128)} custom-call(f32[85,8,128]{2,1,0:T(8,128)S(1)} %get-tuple-element.33.refs_1_.refs_0_, f32[32,32,128]{2,1,0:T(8,128)S(1)} %get-tuple-element.51.refs_1_, f32[1296,384]{1,0:T(8,128)S(1)} %get-tuple-element.52.refs_2_, f32[360,128]{1,0:T(8,128)S(1)} %collective-permute-done.7.refs_3_, ...), custom_call_target="tpu_custom_call" | custom-call | flops 10000000 | bytes 6754304 | tf_op jit(solution)/shard_map/pallas_call | solution.py:919
  (1 shorter events, 0.0 us)
Async XLA Ops:
  0.0 1.0 %copy-start = (f32[32,32,128]{2,1,0:T(8,128)S(1)}, f32[32,32,128]{2,1,0:T(8,128)}, u32[]{:S(2)}) copy-start(f32[32,32,128]{2,1,0:T(8,128)} %refs_0_.4) | copy-start | bytes 1572868
  0.0 7.8 %copy-start.1 = (f32[3,2,17]{2,1,0:T(2,128)S(1)}, f32[3,2,17]{2,1,0:T(2,128)}, u32[]{:S(2)}) copy-start(f32[3,2,17]{2,1,0:T(2,128)} %refs_0_.5) | copy-start | bytes 1228
  1.9 7.7 %collective-permute-start = (f32[472,128]{1,0:T(8,128)S(1)}, f32[472,128]{1,0:T(8,128)S(1)}, u32[]{:S(2)}, u32[]{:S(2)}) collective-permute-start(f32[472,128]{1,0:T(8,128)S(1)} %get-tuple-element.35), channel_id=1, source_target_pairs={{0,1},{1,0},{2,3},{3,2},{4,5},{5,4},{6,7},{7,6},{8,9},{9,8},{10,11... | collective-permute-start | bytes 725000 | tf_op jit(solution)/shard_map/ppermute | solution.py:64
  4.0 4.9 %collective-permute-start.3 = (f32[32,128]{1,0:T(8,128)S(1)}, f32[32,128]{1,0:T(8,128)S(1)}, u32[]{:S(2)}, u32[]{:S(2)}) collective-permute-start(f32[32,128]{1,0:T(8,128)S(1)} %get-tuple-element.44), channel_id=1, source_target_pairs={{0,4},{2,6},{4,0},{6,2},{1,5},{3,7},{5,1},{7,3},{8,12},{10,14},{12... | collective-permute-start | bytes 49160 | tf_op jit(solution)/shard_map/ppermute | solution.py:64
  6.3 8.9 %collective-permute-start.1 = (f32[472,128]{1,0:T(8,128)S(1)}, f32[472,128]{1,0:T(8,128)S(1)}, u32[]{:S(2)}, u32[]{:S(2)}) collective-permute-start(f32[472,128]{1,0:T(8,128)S(1)} %get-tuple-element.42), channel_id=1, source_target_pairs={{0,2},{2,4},{4,6},{6,14},{14,12},{12,10},{10,8},{8,0},{16,18},{18,... | collective-permute-start | bytes 725000 | tf_op jit(solution)/shard_map/ppermute | solution.py:64
  7.5 7.7 %collective-permute-start.2 = (f32[472,128]{1,0:T(8,128)S(1)}, f32[472,128]{1,0:T(8,128)S(1)}, u32[]{:S(2)}, u32[]{:S(2)}) collective-permute-start(f32[472,128]{1,0:T(8,128)S(1)} %get-tuple-element.43), channel_id=1, source_target_pairs={{2,0},{4,2},{6,4},{14,6},{12,14},{10,12},{8,10},{0,8},{18,16},{20,... | collective-permute-start | bytes 725000 | tf_op jit(solution)/shard_map/ppermute | solution.py:64
  9.7 5.6 %collective-permute-start.4 = (f32[192,128]{1,0:T(8,128)S(1)}, f32[192,128]{1,0:T(8,128)S(1)}, u32[]{:S(2)}, u32[]{:S(2)}) collective-permute-start(f32[192,128]{1,0:T(8,128)S(1)} %get-tuple-element.45), channel_id=1, source_target_pairs={{0,2},{2,4},{4,6},{6,14},{14,12},{12,10},{10,8},{8,0},{16,18},{18,... | collective-permute-start | bytes 294920 | tf_op jit(solution)/shard_map/ppermute | solution.py:64
  10.9 4.3 %collective-permute-start.5 = (f32[192,128]{1,0:T(8,128)S(1)}, f32[192,128]{1,0:T(8,128)S(1)}, u32[]{:S(2)}, u32[]{:S(2)}) collective-permute-start(f32[192,128]{1,0:T(8,128)S(1)} %get-tuple-element.46), channel_id=1, source_target_pairs={{2,0},{4,2},{6,4},{14,6},{12,14},{10,12},{8,10},{0,8},{18,16},{20,... | collective-permute-start | bytes 294920 | tf_op jit(solution)/shard_map/ppermute | solution.py:64
  11.2 4.0 %collective-permute-start.6 = (f32[32,128]{1,0:T(8,128)S(1)}, f32[32,128]{1,0:T(8,128)S(1)}, u32[]{:S(2)}, u32[]{:S(2)}) collective-permute-start(f32[32,128]{1,0:T(8,128)S(1)} %shard_map.33.refs_0_), channel_id=1, source_target_pairs={{0,1},{1,0},{2,3},{3,2},{4,5},{5,4},{6,7},{7,6},{8,9},{9,8},{10,11... | collective-permute-start | bytes 49160 | tf_op jit(solution)/shard_map/ppermute | solution.py:64
  16.0 6.4 %collective-permute-start.7 = (f32[360,128]{1,0:T(8,128)S(1)}, f32[360,128]{1,0:T(8,128)S(1)}, u32[]{:S(2)}, u32[]{:S(2)}) collective-permute-start(f32[360,128]{1,0:T(8,128)S(1)} %get-tuple-element.53), channel_id=1, source_target_pairs={{0,8},{8,16},{16,24},{24,25},{25,17},{17,9},{9,1},{1,0},{2,10},{10... | collective-permute-start | bytes 552968 | tf_op jit(solution)/shard_map/ppermute | solution.py:64
  19.3 5.0 %collective-permute-start.8 = (f32[360,128]{1,0:T(8,128)S(1)}, f32[360,128]{1,0:T(8,128)S(1)}, u32[]{:S(2)}, u32[]{:S(2)}) collective-permute-start(f32[360,128]{1,0:T(8,128)S(1)} %get-tuple-element.54), channel_id=1, source_target_pairs={{8,0},{16,8},{24,16},{25,24},{17,25},{9,17},{1,9},{0,1},{10,2},{18... | collective-permute-start | bytes 552968 | tf_op jit(solution)/shard_map/ppermute | solution.py:64

commit v12 on v11

--- a/solution.py
+++ b/solution.py
@@ -130,7 +130,8 @@
         self.y_routes = folded(y, x.name, (x.name, y.name))
         self.y2_routes = swap(y, 2)
         self.x_routes = folded(x, z.name, (x.name, z.name))
-        self.z_fine = RADIUS * y.fine
+        self.inner = y.fine - 2 * RADIUS
+        self.z_fine = RADIUS * 2 * RADIUS
         self.z_sums = max(EDGE * y.mid_all, SPAN * y.coarse_all)
         self.z_rows = up8(self.z_fine + self.z_sums)
         self.z2_rows = up8(z.second * y.coarse_all)
@@ -164,6 +165,8 @@
         self.edge_sums = EDGE + SPAN
         self.side = x.fine // RADIUS
         self.fine_groups = -(-self.fine_planes // self.side)
+        assert z.fine % self.side == 0
+        self.own_groups = z.fine // self.side
         self.folded = 0 < self.fine_planes % self.side <= self.side // 2
         self.fine_ends = self.fine_groups * self.fine_rows - (self.fine_rows // 2 if self.folded else 0)
         self.sum_blocks = -(-self.sum_planes * self.sum_rows // 128)
@@ -262,7 +265,9 @@
         message[s.y_fine :] = jnp.where(is_mid, packed[0, :rows], packed[1, :rows])
     for message, route in zip(messages, s.z_routes):
         up = route.up().astype(jnp.int32)
-        message[: s.z_fine] = charges[pl.ds(up * (z.fine - RADIUS), RADIUS)].reshape(s.z_fine, x.fine)
+        planes = charges[pl.ds(up * (z.fine - RADIUS), RADIUS)]
+        outer = jnp.concatenate([planes[:, :RADIUS], planes[:, y.fine - RADIUS :]], axis=1)
+        message[: s.z_fine] = outer.reshape(s.z_fine, x.fine)
         packed[...] = jnp.zeros(packed.shape, F32)
         for p in range(EDGE):
             packed[0, p * y.mid_all : (p + 1) * y.mid_all] = mid[up * (z.mid_all - EDGE) + p][: y.mid_all]
@@ -326,8 +331,8 @@
         up = route.up()
         at = 0
         for z_message in z_messages:
-            slab = z_message[: s.z_fine].reshape(RADIUS, y.fine, x.fine)
-            edge = jnp.where(up, slab[:, y.fine - RADIUS :], slab[:, :RADIUS])
+            slab = z_message[: s.z_fine].reshape(RADIUS, 2 * RADIUS, x.fine)
+            edge = jnp.where(up, slab[:, RADIUS:], slab[:, :RADIUS])
             message[at : at + RADIUS * RADIUS] = edge.reshape(RADIUS * RADIUS, x.fine)
             at += RADIUS * RADIUS
         at = 0
@@ -339,14 +344,21 @@
         message[s.slab_fine :] = jnp.where(lane < x.mid_all, packed[0, :count], coarse)
 
 
-def pass_kernel(s, far, out):
-    out[...] = far[...]
-
-
-def roll_ends(s, plane_rows, count):
+def pass_kernel(s, nz, far, charges, *outs):
+    z, x = s.z, s.x
+    rows = RADIUS * s.inner
+    for out, route in zip(outs, s.z_routes):
+        planes = charges[pl.ds(route.up().astype(jnp.int32) * (z.fine - RADIUS), RADIUS)]
+        out[:rows] = planes[:, RADIUS : RADIUS + s.inner].reshape(rows, x.fine)
+        out[rows:] = far[...]
+    for out in outs[nz:]:
+        out[...] = far[...]
+
+
+def roll_ends(s, plane_rows, count, groups):
     x = s.x
     lane = iota((count, x.fine), 1)
-    for g in range(s.fine_groups):
+    for g in groups:
         ends = [jnp.zeros(lane.shape, F32)] * 2
         for j in range(min(s.side, s.fine_planes - g * s.side)):
             plane = plane_rows(g * s.side + j)
@@ -357,25 +369,15 @@
         yield g, ends
 
 
-def early_kernel(s, nz, charges, *rest):
-    z_messages = rest[:nz]
-    x_fine, y_own, t_part, last, start, slab = rest[nz:]
+def early_kernel(s, charges, x_fine, y_own, t_part, last, start):
     z, y, x = s.z, s.y, s.x
-    for n, message in enumerate(z_messages):
-        slab[n * RADIUS : (n + 1) * RADIUS] = message[: s.z_fine].reshape(RADIUS, y.fine, x.fine)
-
-    def rows_of(p):
-        return charges[p] if p < z.fine else slab[p - z.fine]
-
     t_part[...] = jnp.zeros(t_part.shape, F32)
-    fine_at = fine_places(s)
-    for g in range(0, s.fine_planes, 8):
-        planes = charges[g : g + 8] if g < z.fine else slab[g - z.fine : g - z.fine + 8]
-        a, b = split(contract_x(s, planes.reshape(8 * y.fine, x.fine), x_fine))
+    for g in range(0, z.fine, 8):
+        a, b = split(contract_x(s, charges[g : g + 8].reshape(8 * y.fine, x.fine), x_fine))
         for p in range(8):
             rows = slice(p * y.fine, (p + 1) * y.fine)
-            store_terms(t_part, *fine_at[g + p], contract_y(s, y_own, a[rows], b[rows]))
-    for g, ends in roll_ends(s, rows_of, y.fine):
+            store_terms(t_part, RADIUS + g + p, None, contract_y(s, y_own, a[rows], b[rows]))
+    for g, ends in roll_ends(s, lambda p: charges[p], y.fine, range(s.own_groups)):
         rows = slice(g * y.fine, (g + 1) * y.fine)
         last[rows], start[rows] = ends
 
@@ -385,7 +387,7 @@
     rest = rest[nz + nz2 :]
     pairs = rest[:4]
     fars = rest[4 : 5 + nz + nz2]
-    fine, sums, first, second, raw, rows, near = rest[5 + nz + nz2 :]
+    fine, slab, sums, first, second, raw, rows, near = rest[5 + nz + nz2 :]
     z, y, x = s.z, s.y, s.x
     below = s.y_routes[0].below()
     planes = slabs(s, z_messages, z2_messages)
@@ -401,9 +403,18 @@
         fine[at : at + count, RADIUS:] = high.reshape(count, RADIUS, x.fine)
     sums[...] = jnp.zeros(sums.shape, F32)
     raw[...] = jnp.zeros(raw.shape, F32)
+    inner_rows = RADIUS * s.inner
     for n, far in enumerate(fars):
+        is_joint = 0 < n <= nz
+        if is_joint:
+            outer = z_messages[n - 1][: s.z_fine].reshape(RADIUS, 2 * RADIUS, x.fine)
+            planes_here = slice((n - 1) * RADIUS, n * RADIUS)
+            slab[planes_here, :RADIUS] = outer[:, :RADIUS]
+            slab[planes_here, RADIUS : RADIUS + s.inner] = far[:inner_rows].reshape(RADIUS, s.inner, x.fine)
+            slab[planes_here, RADIUS + s.inner :] = outer[:, RADIUS:]
+        two_away = far[inner_rows:] if is_joint else far[...]
         for g in range(s.far_groups):
-            turned = pltpu.roll(far[...], (x.mid_all - g * x.coarse_all) % x.fine, 1)
+            turned = pltpu.roll(two_away, (x.mid_all - g * x.coarse_all) % x.fine, 1)
             for p in range(g * s.far_planes, min((g + 1) * s.far_planes, z.coarse_all)):
                 at = p % s.far_planes * y.second
                 rows[n, p, : y.second] = turned[at : at + y.second]
@@ -481,9 +492,14 @@
     up = s.x_routes[0].up()
     half, shift = s.fine_rows // 2, x.fine // 2
     is_first_half = iota((half, x.fine), 1) < shift
-    for g, ends in roll_ends(s, lambda p: fine[p], 2 * RADIUS):
-        rows = slice(g * y.fine, (g + 1) * y.fine)
-        both = [jnp.concatenate([old[rows], new], axis=0) for old, new in zip((last, start), ends)]
+    own_ends = roll_ends(s, lambda p: fine[p], 2 * RADIUS, range(s.own_groups))
+    slab_rows = [jnp.concatenate([slab[p], fine[z.fine + p]], axis=0) for p in range(nz * RADIUS)]
+    slab_ends = roll_ends(s, lambda p: slab_rows[p - z.fine], s.fine_rows, range(s.own_groups, s.fine_groups))
+    for g, ends in list(own_ends) + list(slab_ends):
+        both = ends
+        if g < s.own_groups:
+            rows = slice(g * y.fine, (g + 1) * y.fine)
+            both = [jnp.concatenate([old[rows], new], axis=0) for old, new in zip((last, start), ends)]
         if s.folded and g == s.fine_groups - 1:
             both = [jnp.where(is_first_half, e[:half], pltpu.roll(e[half:], shift, 1)) for e in both]
         at = slice(g * s.fine_rows, g * s.fine_rows + both[0].shape[0])
@@ -722,10 +738,18 @@
     return jnp.dot(joined, weights[: 3 * s.x.fine], preferred_element_type=F32)
 
 
-def own_kernel(s, table, t_part, fine, sums, x_fine, x_sums, y_edge, fine_part, sums_part, t_fine):
+def own_kernel(s, table, t_part, fine, slab, sums, x_fine, x_sums, y_edge, y_fine, fine_part, sums_part, t_fine):
     z, x = s.z, s.x
     t_fine[...] = t_part[...]
     fine_at = fine_places(s)
+
+    def slab_group(g, count):
+        n = s.fine_rows
+        planes = jnp.concatenate([slab[g : g + count], fine[z.fine + g : z.fine + g + count]], axis=1)
+        a, b = split(contract_x(s, planes.reshape(count * n, x.fine), x_fine))
+        for p in range(count):
+            rows = slice(p * n, (p + 1) * n)
+            store_terms(t_fine, *fine_at[z.fine + g + p], contract_y(s, y_fine, a[rows], b[rows]))
 
     def fine_group(g, count):
         n = 2 * RADIUS
@@ -747,11 +771,13 @@
 
     later = []
     done = 0
-    for g in list(range(z.fine, s.fine_planes, 8)) + list(range(0, z.fine, 8)):
+    for g in range(0, s.fine_planes - z.fine, 8):
+        slab_group(g, 8)
+    for g in range(0, z.fine, 8):
         fine_group(g, 8)
         while later:
             later.pop(0)()
-        if g < z.fine:
+        if g >= 0:
             ready = g if g + 8 < z.fine else z.fine
             later += [lambda k=k: fine_block(k) for k in range(done, ready, BLOCK)]
             done = max(done, ready)
@@ -958,7 +984,12 @@
     z_got = [route(m) for route, m in zip(s.z_routes + s.z2_routes, messages)]
     sides = [s.y_routes[0](ahead), s.y_routes[1](behind)]
     far = s.y2_routes[0](far)
-    (passed,) = call(bound(pass_kernel), [array(s.far_rows, n)], [far], flops=2*10**9)
+    passed = call(
+        bound(pass_kernel, nz),
+        [array(RADIUS * s.inner + s.far_rows, n)] * nz + [array(s.far_rows, n)] * nz2,
+        [far, held],
+        flops=15 * 10**8,
+    )
     operators = call(
         bound(operator_kernel),
         [
@@ -983,22 +1014,22 @@
     ahead, behind = call(
         bound(spread_kernel, nz, nz2),
         [array(s.slab_rows, n), array(s.slab_rows, n)],
-        [passed, later[1], *z_got],
+        [passed[0], later[1], *z_got],
         [pltpu.VMEM((3, up8(max(s.slab_coarse, s.slab_rows - s.slab_fine)) + 8, n), F32)],
     )
     sides += [s.y_routes[0](ahead), s.y_routes[1](behind)]
-    fars = [far] + [route(passed) for route in s.z_routes + s.z2_routes]
+    fars = [far] + [route(m) for route, m in zip(s.z_routes + s.z2_routes, passed)]
     x_fine, x_sums, y_own, y_edge, y_fine, y_mid, y_coarse, widen_x, widen_y = operators
     t_part, last, start = call(
-        bound(early_kernel, nz),
-        [array(z.fine + 2 * RADIUS, TERMS, y.fine, n)] + [array(s.fine_groups * y.fine, n)] * 2,
-        [held, *z_got[:nz], x_fine, y_own],
-        [pltpu.VMEM((nz * RADIUS, y.fine, n), F32)],
+        bound(early_kernel),
+        [array(z.fine + 2 * RADIUS, TERMS, y.fine, n)] + [array(s.own_groups * y.fine, n)] * 2,
+        [held, x_fine, y_own],
     )
-    fine, sums, first, second = call(
+    fine, slab, sums, first, second = call(
         bound(collect_kernel, nz, nz2),
         [
             array(s.fine_planes, 2 * RADIUS, n),
+            array(nz * RADIUS, y.fine, n),
             array(s.sum_planes, s.sum_rows, n),
             array(s.x_rows, n),
             array(s.x_rows, n),
@@ -1014,7 +1045,7 @@
     fine, sums = call(
         bound(own_kernel),
         [array(z.fine, y.fine, n), array(s.sum_planes * s.sum_rows, (TERMS + 1) * n)],
-        [table, t_part, fine, sums, x_fine, x_sums, y_edge],
+        [table, t_part, fine, slab, sums, x_fine, x_sums, y_edge, y_fine],
         [pltpu.VMEM((z.fine + 2 * RADIUS, TERMS, y.fine, n), F32)],
     )
     (out,) = call(

time: 28.2 us -> 27.9 us (0.989)
  transfers between devices with their start and end apart: 9 -> 9, of which waited for: 2 -> 3; matrix products, arithmetic and copies ran while one was open for 0% -> 0% of each run, Pallas kernels for 25% -> 26%
where the time goes in v12:
time: 27.9 us; the launch traced here: 27.8 us
  Pallas kernels  12.8 us (46%)
  starting transfers between devices  11.8 us (42%)
  waiting for transfers between devices  2.29 us (8%)
  local copies, waits for them, and re-layouts  0.8 us (3%)
    pallas_call x10, Pallas kernels, call(): pl.pallas_call(kernel, out_shape=tuple(outs), in_specs=specs, out_specs=t...  12.8 us
    ppermute x9, starting transfers between devices, __call__(): return lax.ppermute(x, self.names, self.pairs)  11.8 us
    ppermute x9, waiting for transfers between devices, __call__(): return lax.ppermute(x, self.names, self.pairs)  2.29 us
    unnamed x4, local copies, waits for them, and re-layouts  0.8 us
  transfers between devices with their start and end apart: 9, of which 3 were waited for; matrix products, arithmetic and copies ran while one was open for 0% of the time, Pallas kernels for 26%

profile of v12, /device:TPU:1, one launch (start us, length us, event | category | flops | bytes accessed | tf_op | source)
XLA Modules:
  0.0 27.8 jit_solution(9972476041343226863)
XLA Ops:
  0.0 0.0 copy-start
  0.0 0.0 copy-start.1
  0.0 0.2 shard_map.29.refs_1_
  0.2 0.8 %copy-done = f32[32,32,128]{2,1,0:T(8,128)S(1)} copy-done((f32[32,32,128]{2,1,0:T(8,128)S(1)}, f32[32,32,128]{2,1,0:T(8,128)}, u32[]{:S(2)}) %copy-start) | copy-done | bytes 524312
  1.0 0.9 %shard_map.30 = (f32[32,32,128]{2,1,0:T(8,128)S(1)}, f32[19,24,128]{2,1,0:T(8,128)S(1)}, f32[472,128]{1,0:T(8,128)S(1)}, f32[472,128]{1,0:T(8,128)S(1)}, f32[32,128]{1,0:T(8,128)S(1)}, /*index=5*/f32[344,128]{1,0:T(8,128)S(1)}) custom-call(f32[32,32,128]{2,1,0:T(8,128)S(1)} %copy-done, bf16[128,256]{1,0:T(8,128)(2,1)S(1)} %shard_map.29.refs_1_), custom_call_target="tpu_custom_call" | custom-call | flops 10000000 | bytes 2023424 | tf_op jit(solution)/shard_map/pallas_call | solution.py:945
  1.9 2.1 %collective-permute-start = (f32[344,128]{1,0:T(8,128)S(1)}, f32[344,128]{1,0:T(8,128)S(1)}, u32[]{:S(2)}, u32[]{:S(2)}) collective-permute-start(f32[344,128]{1,0:T(8,128)S(1)} %get-tuple-element.42), channel_id=1, source_target_pairs={{0,1},{1,0},{2,3},{3,2},{4,5},{5,4},{6,7},{7,6},{8,9},{9,8},{10,11... | collective-permute-start | bytes 528392 | tf_op jit(solution)/shard_map/ppermute | solution.py:64
  4.0 2.3 %collective-permute-start.3 = (f32[32,128]{1,0:T(8,128)S(1)}, f32[32,128]{1,0:T(8,128)S(1)}, u32[]{:S(2)}, u32[]{:S(2)}) collective-permute-start(f32[32,128]{1,0:T(8,128)S(1)} %get-tuple-element.45), channel_id=1, source_target_pairs={{0,4},{2,6},{4,0},{6,2},{1,5},{3,7},{5,1},{7,3},{8,12},{10,14},{12... | collective-permute-start | bytes 49160 | tf_op jit(solution)/shard_map/ppermute | solution.py:64
  6.3 1.2 %collective-permute-start.1 = (f32[472,128]{1,0:T(8,128)S(1)}, f32[472,128]{1,0:T(8,128)S(1)}, u32[]{:S(2)}, u32[]{:S(2)}) collective-permute-start(f32[472,128]{1,0:T(8,128)S(1)} %get-tuple-element.43), channel_id=1, source_target_pairs={{0,2},{2,4},{4,6},{6,14},{14,12},{12,10},{10,8},{8,0},{16,18},{18,... | collective-permute-start | bytes 725000 | tf_op jit(solution)/shard_map/ppermute | solution.py:64
  7.5 0.2 collective-permute-start.2
  7.8 0.0 copy-done.1
  7.8 1.1 %shard_map.28 = (bf16[4,1152,256]{2,1,0:T(8,128)(2,1)S(1)}, f32[85,8,128]{2,1,0:T(8,128)S(1)}) custom-call(f32[3,2,17]{2,1,0:T(2,128)S(1)} %copy-done.1), custom_call_target="tpu_custom_call" | custom-call | flops 10000000 | bytes 2707864 | tf_op jit(solution)/shard_map/pallas_call | solution.py:945
  8.9 0.0 collective-permute-done.3.refs_0_.refs_8_
  8.9 0.0 collective-permute-done.refs_2_.refs_3_
  8.9 0.1 shard_map.34
  9.0 1.4 %collective-permute-start.4 = (f32[192,128]{1,0:T(8,128)S(1)}, f32[192,128]{1,0:T(8,128)S(1)}, u32[]{:S(2)}, u32[]{:S(2)}) collective-permute-start(f32[192,128]{1,0:T(8,128)S(1)} %get-tuple-element.46), channel_id=1, source_target_pairs={{0,2},{2,4},{4,6},{6,14},{14,12},{12,10},{10,8},{8,0},{16,18},{18,... | collective-permute-start | bytes 294920 | tf_op jit(solution)/shard_map/ppermute | solution.py:64
  10.4 0.1 collective-permute-start.5
  10.5 0.5 %collective-permute-start.6 = (f32[160,128]{1,0:T(8,128)S(1)}, f32[160,128]{1,0:T(8,128)S(1)}, u32[]{:S(2)}, u32[]{:S(2)}) collective-permute-start(f32[160,128]{1,0:T(8,128)S(1)} %shard_map.33.refs_0_), channel_id=1, source_target_pairs={{0,1},{1,0},{2,3},{3,2},{4,5},{5,4},{6,7},{7,6},{8,9},{9,8},{10,11... | collective-permute-start | bytes 245768 | tf_op jit(solution)/shard_map/ppermute | solution.py:64
  11.0 1.5 %shard_map.31 = (bf16[384,256]{1,0:T(8,128)(2,1)S(1)}, bf16[640,384]{1,0:T(8,128)(2,1)S(1)}, bf16[64,96]{1,0:T(8,128)(2,1)S(1)}, bf16[64,48]{1,0:T(8,128)(2,1)S(...) custom-call(f32[3,2,17]{2,1,0:T(2,128)S(1)} %copy-done.1), custom_call_target="tpu_custom_call" | custom-call | flops 10000000 | bytes 854424 | tf_op jit(solution)/shard_map/pallas_call | solution.py:945
  12.5 1.1 %shard_map.32 = (f32[48,2,32,128]{3,2,1,0:T(8,128)S(1)}, f32[64,128]{1,0:T(8,128)S(1)}, f32[64,128]{1,0:T(8,128)S(1)}) custom-call(f32[32,32,128]{2,1,0:T(8,128)S(1)} %get-tuple-element.35.refs_0_.refs_1_, bf16[384,256]{1,0:T(8,128)(2,1)S(1)} %get-tuple-element.36.refs_1_.refs_5_, bf16[64,96]{1,0:T(8,128)(2,1)S(1)} %get-tuple-element.37.refs_2_), custom_call_target="tpu_custom_call" | custom-call | flops 10000000 | bytes 2371584 | tf_op jit(solution)/shard_map/pallas_call | solution.py:945
  13.7 0.4 %collective-permute-done.6.refs_9_ = f32[160,128]{1,0:T(8,128)S(1)} collective-permute-done((f32[160,128]{1,0:T(8,128)S(1)}, f32[160,128]{1,0:T(8,128)S(1)}, u32[]{:S(2)}, u32[]{:S(2)}) %collective-permute-start.6) | collective-permute-done | bytes 81952 | tf_op jit(solution)/shard_map/ppermute | solution.py:64
  14.1 0.0 collective-permute-done.1.refs_4_
  14.1 0.0 collective-permute-done.2.refs_5_
  14.1 0.0 collective-permute-done.4.refs_6_
  14.1 0.1 collective-permute-done.5.refs_7_
  14.2 0.8 %shard_map.35 = (f32[40,16,128]{2,1,0:T(8,128)S(1)}, f32[8,32,128]{2,1,0:T(8,128)S(1)}, f32[27,48,128]{2,1,0:T(8,128)S(1)}, f32[360,128]{1,0:T(8,128)S(1)}, f32[360,128]{1,0:T(8,128)S(1)}) custom-call(f32[64,128]{1,0:T(8,128)S(1)} %get-tuple-element.39.refs_0_, f32[64,128]{1,0:T(8,128)S(1)} %get-tuple-element.40.refs_1_, ...), custom_call_target="tpu_custom_call" | custom-call | flops 10000000 | bytes 2744320 | tf_op jit(solution)/shard_map/pallas_call | solution.py:945
  15.0 4.0 %collective-permute-start.7 = (f32[360,128]{1,0:T(8,128)S(1)}, f32[360,128]{1,0:T(8,128)S(1)}, u32[]{:S(2)}, u32[]{:S(2)}) collective-permute-start(f32[360,128]{1,0:T(8,128)S(1)} %get-tuple-element.56), channel_id=1, source_target_pairs={{0,8},{8,16},{16,24},{24,25},{25,17},{17,9},{9,1},{1,0},{2,10},{10... | collective-permute-start | bytes 552968 | tf_op jit(solution)/shard_map/ppermute | solution.py:64
  19.0 0.0 collective-permute-start.8
  19.0 3.2 %shard_map.36 = (f32[32,32,128]{2,1,0:T(8,128)S(1)}, f32[1296,384]{1,0:T(8,128)S(1)}) custom-call(f32[85,8,128]{2,1,0:T(8,128)S(1)} %get-tuple-element.34.refs_1_.refs_0_, f32[48,2,32,128]{3,2,1,0:T(8,128)S(1)} %get-tuple-element.38.refs_1_, f32[40,16,128]{2,1,0:T(8,128)S(1)} %get-tuple-element.48.refs_2_, f32[8,32,128]{2,1,0:T(8,128)S(1)} %get-tuple-element.49.refs_3_, ...), custom_call_target="tpu_custom_call" | custom-call | flops 10000000 | bytes 6270976 | tf_op jit(solution)/shard_map/pallas_call | solution.py:945
  22.2 0.0 collective-permute-done.7.refs_3_
  22.2 1.7 %collective-permute-done.8.refs_4_ = f32[360,128]{1,0:T(8,128)S(1)} collective-permute-done((f32[360,128]{1,0:T(8,128)S(1)}, f32[360,128]{1,0:T(8,128)S(1)}, u32[]{:S(2)}, u32[]{:S(2)}) %collective-permute-start.8) | collective-permute-done | bytes 184352 | tf_op jit(solution)/shard_map/ppermute | solution.py:64
  24.0 3.8 %shard_map.37 = f32[32,32,128]{2,1,0:T(8,128)} custom-call(f32[85,8,128]{2,1,0:T(8,128)S(1)} %get-tuple-element.34.refs_1_.refs_0_, f32[32,32,128]{2,1,0:T(8,128)S(1)} %get-tuple-element.54.refs_1_, f32[1296,384]{1,0:T(8,128)S(1)} %get-tuple-element.55.refs_2_, f32[360,128]{1,0:T(8,128)S(1)} %collective-permute-done.7.refs_3_, ...), custom_call_target="tpu_custom_call" | custom-call | flops 10000000 | bytes 6754304 | tf_op jit(solution)/shard_map/pallas_call | solution.py:945
  (1 shorter events, 0.0 us)
Async XLA Ops:
  0.0 1.0 %copy-start = (f32[32,32,128]{2,1,0:T(8,128)S(1)}, f32[32,32,128]{2,1,0:T(8,128)}, u32[]{:S(2)}) copy-start(f32[32,32,128]{2,1,0:T(8,128)} %refs_0_.4) | copy-start | bytes 1572868
  0.0 7.8 %copy-start.1 = (f32[3,2,17]{2,1,0:T(2,128)S(1)}, f32[3,2,17]{2,1,0:T(2,128)}, u32[]{:S(2)}) copy-start(f32[3,2,17]{2,1,0:T(2,128)} %refs_0_.5) | copy-start | bytes 1228
  1.9 7.0 %collective-permute-start = (f32[344,128]{1,0:T(8,128)S(1)}, f32[344,128]{1,0:T(8,128)S(1)}, u32[]{:S(2)}, u32[]{:S(2)}) collective-permute-start(f32[344,128]{1,0:T(8,128)S(1)} %get-tuple-element.42), channel_id=1, source_target_pairs={{0,1},{1,0},{2,3},{3,2},{4,5},{5,4},{6,7},{7,6},{8,9},{9,8},{10,11... | collective-permute-start | bytes 528392 | tf_op jit(solution)/shard_map/ppermute | solution.py:64
  4.0 4.9 %collective-permute-start.3 = (f32[32,128]{1,0:T(8,128)S(1)}, f32[32,128]{1,0:T(8,128)S(1)}, u32[]{:S(2)}, u32[]{:S(2)}) collective-permute-start(f32[32,128]{1,0:T(8,128)S(1)} %get-tuple-element.45), channel_id=1, source_target_pairs={{0,4},{2,6},{4,0},{6,2},{1,5},{3,7},{5,1},{7,3},{8,12},{10,14},{12... | collective-permute-start | bytes 49160 | tf_op jit(solution)/shard_map/ppermute | solution.py:64
  6.3 7.8 %collective-permute-start.1 = (f32[472,128]{1,0:T(8,128)S(1)}, f32[472,128]{1,0:T(8,128)S(1)}, u32[]{:S(2)}, u32[]{:S(2)}) collective-permute-start(f32[472,128]{1,0:T(8,128)S(1)} %get-tuple-element.43), channel_id=1, source_target_pairs={{0,2},{2,4},{4,6},{6,14},{14,12},{12,10},{10,8},{8,0},{16,18},{18,... | collective-permute-start | bytes 725000 | tf_op jit(solution)/shard_map/ppermute | solution.py:64
  7.5 6.6 %collective-permute-start.2 = (f32[472,128]{1,0:T(8,128)S(1)}, f32[472,128]{1,0:T(8,128)S(1)}, u32[]{:S(2)}, u32[]{:S(2)}) collective-permute-start(f32[472,128]{1,0:T(8,128)S(1)} %get-tuple-element.44), channel_id=1, source_target_pairs={{2,0},{4,2},{6,4},{14,6},{12,14},{10,12},{8,10},{0,8},{18,16},{20,... | collective-permute-start | bytes 725000 | tf_op jit(solution)/shard_map/ppermute | solution.py:64
  9.0 5.1 %collective-permute-start.4 = (f32[192,128]{1,0:T(8,128)S(1)}, f32[192,128]{1,0:T(8,128)S(1)}, u32[]{:S(2)}, u32[]{:S(2)}) collective-permute-start(f32[192,128]{1,0:T(8,128)S(1)} %get-tuple-element.46), channel_id=1, source_target_pairs={{0,2},{2,4},{4,6},{6,14},{14,12},{12,10},{10,8},{8,0},{16,18},{18,... | collective-permute-start | bytes 294920 | tf_op jit(solution)/shard_map/ppermute | solution.py:64
  10.4 3.8 %collective-permute-start.5 = (f32[192,128]{1,0:T(8,128)S(1)}, f32[192,128]{1,0:T(8,128)S(1)}, u32[]{:S(2)}, u32[]{:S(2)}) collective-permute-start(f32[192,128]{1,0:T(8,128)S(1)} %get-tuple-element.47), channel_id=1, source_target_pairs={{2,0},{4,2},{6,4},{14,6},{12,14},{10,12},{8,10},{0,8},{18,16},{20,... | collective-permute-start | bytes 294920 | tf_op jit(solution)/shard_map/ppermute | solution.py:64
  10.5 3.6 %collective-permute-start.6 = (f32[160,128]{1,0:T(8,128)S(1)}, f32[160,128]{1,0:T(8,128)S(1)}, u32[]{:S(2)}, u32[]{:S(2)}) collective-permute-start(f32[160,128]{1,0:T(8,128)S(1)} %shard_map.33.refs_0_), channel_id=1, source_target_pairs={{0,1},{1,0},{2,3},{3,2},{4,5},{5,4},{6,7},{7,6},{8,9},{9,8},{10,11... | collective-permute-start | bytes 245768 | tf_op jit(solution)/shard_map/ppermute | solution.py:64
  15.0 7.2 %collective-permute-start.7 = (f32[360,128]{1,0:T(8,128)S(1)}, f32[360,128]{1,0:T(8,128)S(1)}, u32[]{:S(2)}, u32[]{:S(2)}) collective-permute-start(f32[360,128]{1,0:T(8,128)S(1)} %get-tuple-element.56), channel_id=1, source_target_pairs={{0,8},{8,16},{16,24},{24,25},{25,17},{17,9},{9,1},{1,0},{2,10},{10... | collective-permute-start | bytes 552968 | tf_op jit(solution)/shard_map/ppermute | solution.py:64
  19.0 5.0 %collective-permute-start.8 = (f32[360,128]{1,0:T(8,128)S(1)}, f32[360,128]{1,0:T(8,128)S(1)}, u32[]{:S(2)}, u32[]{:S(2)}) collective-permute-start(f32[360,128]{1,0:T(8,128)S(1)} %get-tuple-element.57), channel_id=1, source_target_pairs={{8,0},{16,8},{24,16},{25,24},{17,25},{9,17},{1,9},{0,1},{10,2},{18... | collective-permute-start | bytes 552968 | tf_op jit(solution)/shard_map/ppermute | solution.py:64

commit v13 on v12

--- a/solution.py
+++ b/solution.py
@@ -915,10 +915,10 @@
                 total = total + weight * p_mid[(k - offset) // 2 + 1]
         out[k] = total
 
-    groups = list(range(0, s.sum_planes, 4))
+    groups = list(range(0, s.sum_planes, 14))
     share = -(-z.fine // len(groups))
     for n, g in enumerate(groups):
-        sum_group(g, min(4, s.sum_planes - g))
+        sum_group(g, min(14, s.sum_planes - g))
         for k in range(n * share, min((n + 1) * share, z.fine)):
             begin(k)
     for k in range(0, z.coarse_all, BLOCK):

time: 27.9 us -> 27.5 us (0.986)
  Pallas kernels: 12.8 us -> 12.4 us
    pallas_call x10, Pallas kernels: 12.8 us -> 12.4 us  [call(): pl.pallas_call(kernel, out_shape=tuple(outs), in_specs=specs, out_specs=t...]
where the time goes in v13:
time: 27.5 us; the launch traced here: 27.4 us
  Pallas kernels  12.4 us (45%)
  starting transfers between devices  11.8 us (43%)
  waiting for transfers between devices  2.29 us (8%)
  local copies, waits for them, and re-layouts  0.8 us (3%)
    pallas_call x10, Pallas kernels, call(): pl.pallas_call(kernel, out_shape=tuple(outs), in_specs=specs, out_specs=t...  12.4 us
    ppermute x9, starting transfers between devices, __call__(): return lax.ppermute(x, self.names, self.pairs)  11.8 us
    ppermute x9, waiting for transfers between devices, __call__(): return lax.ppermute(x, self.names, self.pairs)  2.29 us
    unnamed x4, local copies, waits for them, and re-layouts  0.8 us
  transfers between devices with their start and end apart: 9, of which 3 were waited for; matrix products, arithmetic and copies ran while one was open for 0% of the time, Pallas kernels for 26%

profile of v13, /device:TPU:1, one launch (start us, length us, event | category | flops | bytes accessed | tf_op | source)
XLA Modules:
  0.0 27.4 jit_solution(16184271915860753630)
XLA Ops:
  0.0 0.0 copy-start
  0.0 0.0 copy-start.1
  0.0 0.2 shard_map.29.refs_1_
  0.2 0.8 %copy-done = f32[32,32,128]{2,1,0:T(8,128)S(1)} copy-done((f32[32,32,128]{2,1,0:T(8,128)S(1)}, f32[32,32,128]{2,1,0:T(8,128)}, u32[]{:S(2)}) %copy-start) | copy-done | bytes 524312
  1.0 0.9 %shard_map.30 = (f32[32,32,128]{2,1,0:T(8,128)S(1)}, f32[19,24,128]{2,1,0:T(8,128)S(1)}, f32[472,128]{1,0:T(8,128)S(1)}, f32[472,128]{1,0:T(8,128)S(1)}, f32[32,128]{1,0:T(8,128)S(1)}, /*index=5*/f32[344,128]{1,0:T(8,128)S(1)}) custom-call(f32[32,32,128]{2,1,0:T(8,128)S(1)} %copy-done, bf16[128,256]{1,0:T(8,128)(2,1)S(1)} %shard_map.29.refs_1_), custom_call_target="tpu_custom_call" | custom-call | flops 10000000 | bytes 2023424 | tf_op jit(solution)/shard_map/pallas_call | solution.py:945
  1.9 2.1 %collective-permute-start = (f32[344,128]{1,0:T(8,128)S(1)}, f32[344,128]{1,0:T(8,128)S(1)}, u32[]{:S(2)}, u32[]{:S(2)}) collective-permute-start(f32[344,128]{1,0:T(8,128)S(1)} %get-tuple-element.42), channel_id=1, source_target_pairs={{0,1},{1,0},{2,3},{3,2},{4,5},{5,4},{6,7},{7,6},{8,9},{9,8},{10,11... | collective-permute-start | bytes 528392 | tf_op jit(solution)/shard_map/ppermute | solution.py:64
  4.0 2.3 %collective-permute-start.3 = (f32[32,128]{1,0:T(8,128)S(1)}, f32[32,128]{1,0:T(8,128)S(1)}, u32[]{:S(2)}, u32[]{:S(2)}) collective-permute-start(f32[32,128]{1,0:T(8,128)S(1)} %get-tuple-element.45), channel_id=1, source_target_pairs={{0,4},{2,6},{4,0},{6,2},{1,5},{3,7},{5,1},{7,3},{8,12},{10,14},{12... | collective-permute-start | bytes 49160 | tf_op jit(solution)/shard_map/ppermute | solution.py:64
  6.3 1.2 %collective-permute-start.1 = (f32[472,128]{1,0:T(8,128)S(1)}, f32[472,128]{1,0:T(8,128)S(1)}, u32[]{:S(2)}, u32[]{:S(2)}) collective-permute-start(f32[472,128]{1,0:T(8,128)S(1)} %get-tuple-element.43), channel_id=1, source_target_pairs={{0,2},{2,4},{4,6},{6,14},{14,12},{12,10},{10,8},{8,0},{16,18},{18,... | collective-permute-start | bytes 725000 | tf_op jit(solution)/shard_map/ppermute | solution.py:64
  7.5 0.2 collective-permute-start.2
  7.8 0.0 copy-done.1
  7.8 1.1 %shard_map.28 = (bf16[4,1152,256]{2,1,0:T(8,128)(2,1)S(1)}, f32[85,8,128]{2,1,0:T(8,128)S(1)}) custom-call(f32[3,2,17]{2,1,0:T(2,128)S(1)} %copy-done.1), custom_call_target="tpu_custom_call" | custom-call | flops 10000000 | bytes 2707864 | tf_op jit(solution)/shard_map/pallas_call | solution.py:945
  8.9 0.0 collective-permute-done.3.refs_0_.refs_8_
  8.9 0.0 collective-permute-done.refs_2_.refs_3_
  8.9 0.1 shard_map.34
  9.0 1.4 %collective-permute-start.4 = (f32[192,128]{1,0:T(8,128)S(1)}, f32[192,128]{1,0:T(8,128)S(1)}, u32[]{:S(2)}, u32[]{:S(2)}) collective-permute-start(f32[192,128]{1,0:T(8,128)S(1)} %get-tuple-element.46), channel_id=1, source_target_pairs={{0,2},{2,4},{4,6},{6,14},{14,12},{12,10},{10,8},{8,0},{16,18},{18,... | collective-permute-start | bytes 294920 | tf_op jit(solution)/shard_map/ppermute | solution.py:64
  10.4 0.1 collective-permute-start.5
  10.5 0.5 %collective-permute-start.6 = (f32[160,128]{1,0:T(8,128)S(1)}, f32[160,128]{1,0:T(8,128)S(1)}, u32[]{:S(2)}, u32[]{:S(2)}) collective-permute-start(f32[160,128]{1,0:T(8,128)S(1)} %shard_map.33.refs_0_), channel_id=1, source_target_pairs={{0,1},{1,0},{2,3},{3,2},{4,5},{5,4},{6,7},{7,6},{8,9},{9,8},{10,11... | collective-permute-start | bytes 245768 | tf_op jit(solution)/shard_map/ppermute | solution.py:64
  11.0 1.5 %shard_map.31 = (bf16[384,256]{1,0:T(8,128)(2,1)S(1)}, bf16[640,384]{1,0:T(8,128)(2,1)S(1)}, bf16[64,96]{1,0:T(8,128)(2,1)S(1)}, bf16[64,48]{1,0:T(8,128)(2,1)S(...) custom-call(f32[3,2,17]{2,1,0:T(2,128)S(1)} %copy-done.1), custom_call_target="tpu_custom_call" | custom-call | flops 10000000 | bytes 854424 | tf_op jit(solution)/shard_map/pallas_call | solution.py:945
  12.5 1.1 %shard_map.32 = (f32[48,2,32,128]{3,2,1,0:T(8,128)S(1)}, f32[64,128]{1,0:T(8,128)S(1)}, f32[64,128]{1,0:T(8,128)S(1)}) custom-call(f32[32,32,128]{2,1,0:T(8,128)S(1)} %get-tuple-element.35.refs_0_.refs_1_, bf16[384,256]{1,0:T(8,128)(2,1)S(1)} %get-tuple-element.36.refs_1_.refs_5_, bf16[64,96]{1,0:T(8,128)(2,1)S(1)} %get-tuple-element.37.refs_2_), custom_call_target="tpu_custom_call" | custom-call | flops 10000000 | bytes 2371584 | tf_op jit(solution)/shard_map/pallas_call | solution.py:945
  13.7 0.4 %collective-permute-done.6.refs_9_ = f32[160,128]{1,0:T(8,128)S(1)} collective-permute-done((f32[160,128]{1,0:T(8,128)S(1)}, f32[160,128]{1,0:T(8,128)S(1)}, u32[]{:S(2)}, u32[]{:S(2)}) %collective-permute-start.6) | collective-permute-done | bytes 81952 | tf_op jit(solution)/shard_map/ppermute | solution.py:64
  14.1 0.0 collective-permute-done.1.refs_4_
  14.1 0.0 collective-permute-done.2.refs_5_
  14.1 0.0 collective-permute-done.4.refs_6_
  14.1 0.1 collective-permute-done.5.refs_7_
  14.2 0.8 %shard_map.35 = (f32[40,16,128]{2,1,0:T(8,128)S(1)}, f32[8,32,128]{2,1,0:T(8,128)S(1)}, f32[27,48,128]{2,1,0:T(8,128)S(1)}, f32[360,128]{1,0:T(8,128)S(1)}, f32[360,128]{1,0:T(8,128)S(1)}) custom-call(f32[64,128]{1,0:T(8,128)S(1)} %get-tuple-element.39.refs_0_, f32[64,128]{1,0:T(8,128)S(1)} %get-tuple-element.40.refs_1_, ...), custom_call_target="tpu_custom_call" | custom-call | flops 10000000 | bytes 2744320 | tf_op jit(solution)/shard_map/pallas_call | solution.py:945
  15.0 4.0 %collective-permute-start.7 = (f32[360,128]{1,0:T(8,128)S(1)}, f32[360,128]{1,0:T(8,128)S(1)}, u32[]{:S(2)}, u32[]{:S(2)}) collective-permute-start(f32[360,128]{1,0:T(8,128)S(1)} %get-tuple-element.56), channel_id=1, source_target_pairs={{0,8},{8,16},{16,24},{24,25},{25,17},{17,9},{9,1},{1,0},{2,10},{10... | collective-permute-start | bytes 552968 | tf_op jit(solution)/shard_map/ppermute | solution.py:64
  19.0 0.0 collective-permute-start.8
  19.0 3.2 %shard_map.36 = (f32[32,32,128]{2,1,0:T(8,128)S(1)}, f32[1296,384]{1,0:T(8,128)S(1)}) custom-call(f32[85,8,128]{2,1,0:T(8,128)S(1)} %get-tuple-element.34.refs_1_.refs_0_, f32[48,2,32,128]{3,2,1,0:T(8,128)S(1)} %get-tuple-element.38.refs_1_, f32[40,16,128]{2,1,0:T(8,128)S(1)} %get-tuple-element.48.refs_2_, f32[8,32,128]{2,1,0:T(8,128)S(1)} %get-tuple-element.49.refs_3_, ...), custom_call_target="tpu_custom_call" | custom-call | flops 10000000 | bytes 6270976 | tf_op jit(solution)/shard_map/pallas_call | solution.py:945
  22.2 0.0 collective-permute-done.7.refs_3_
  22.2 1.7 %collective-permute-done.8.refs_4_ = f32[360,128]{1,0:T(8,128)S(1)} collective-permute-done((f32[360,128]{1,0:T(8,128)S(1)}, f32[360,128]{1,0:T(8,128)S(1)}, u32[]{:S(2)}, u32[]{:S(2)}) %collective-permute-start.8) | collective-permute-done | bytes 184352 | tf_op jit(solution)/shard_map/ppermute | solution.py:64
  24.0 3.4 %shard_map.37 = f32[32,32,128]{2,1,0:T(8,128)} custom-call(f32[85,8,128]{2,1,0:T(8,128)S(1)} %get-tuple-element.34.refs_1_.refs_0_, f32[32,32,128]{2,1,0:T(8,128)S(1)} %get-tuple-element.54.refs_1_, f32[1296,384]{1,0:T(8,128)S(1)} %get-tuple-element.55.refs_2_, f32[360,128]{1,0:T(8,128)S(1)} %collective-permute-done.7.refs_3_, ...), custom_call_target="tpu_custom_call" | custom-call | flops 10000000 | bytes 6754304 | tf_op jit(solution)/shard_map/pallas_call | solution.py:945
  (1 shorter events, 0.0 us)
Async XLA Ops:
  0.0 1.0 %copy-start = (f32[32,32,128]{2,1,0:T(8,128)S(1)}, f32[32,32,128]{2,1,0:T(8,128)}, u32[]{:S(2)}) copy-start(f32[32,32,128]{2,1,0:T(8,128)} %refs_0_.4) | copy-start | bytes 1572868
  0.0 7.8 %copy-start.1 = (f32[3,2,17]{2,1,0:T(2,128)S(1)}, f32[3,2,17]{2,1,0:T(2,128)}, u32[]{:S(2)}) copy-start(f32[3,2,17]{2,1,0:T(2,128)} %refs_0_.5) | copy-start | bytes 1228
  1.9 7.0 %collective-permute-start = (f32[344,128]{1,0:T(8,128)S(1)}, f32[344,128]{1,0:T(8,128)S(1)}, u32[]{:S(2)}, u32[]{:S(2)}) collective-permute-start(f32[344,128]{1,0:T(8,128)S(1)} %get-tuple-element.42), channel_id=1, source_target_pairs={{0,1},{1,0},{2,3},{3,2},{4,5},{5,4},{6,7},{7,6},{8,9},{9,8},{10,11... | collective-permute-start | bytes 528392 | tf_op jit(solution)/shard_map/ppermute | solution.py:64
  4.0 4.9 %collective-permute-start.3 = (f32[32,128]{1,0:T(8,128)S(1)}, f32[32,128]{1,0:T(8,128)S(1)}, u32[]{:S(2)}, u32[]{:S(2)}) collective-permute-start(f32[32,128]{1,0:T(8,128)S(1)} %get-tuple-element.45), channel_id=1, source_target_pairs={{0,4},{2,6},{4,0},{6,2},{1,5},{3,7},{5,1},{7,3},{8,12},{10,14},{12... | collective-permute-start | bytes 49160 | tf_op jit(solution)/shard_map/ppermute | solution.py:64
  6.3 7.8 %collective-permute-start.1 = (f32[472,128]{1,0:T(8,128)S(1)}, f32[472,128]{1,0:T(8,128)S(1)}, u32[]{:S(2)}, u32[]{:S(2)}) collective-permute-start(f32[472,128]{1,0:T(8,128)S(1)} %get-tuple-element.43), channel_id=1, source_target_pairs={{0,2},{2,4},{4,6},{6,14},{14,12},{12,10},{10,8},{8,0},{16,18},{18,... | collective-permute-start | bytes 725000 | tf_op jit(solution)/shard_map/ppermute | solution.py:64
  7.5 6.6 %collective-permute-start.2 = (f32[472,128]{1,0:T(8,128)S(1)}, f32[472,128]{1,0:T(8,128)S(1)}, u32[]{:S(2)}, u32[]{:S(2)}) collective-permute-start(f32[472,128]{1,0:T(8,128)S(1)} %get-tuple-element.44), channel_id=1, source_target_pairs={{2,0},{4,2},{6,4},{14,6},{12,14},{10,12},{8,10},{0,8},{18,16},{20,... | collective-permute-start | bytes 725000 | tf_op jit(solution)/shard_map/ppermute | solution.py:64
  9.0 5.1 %collective-permute-start.4 = (f32[192,128]{1,0:T(8,128)S(1)}, f32[192,128]{1,0:T(8,128)S(1)}, u32[]{:S(2)}, u32[]{:S(2)}) collective-permute-start(f32[192,128]{1,0:T(8,128)S(1)} %get-tuple-element.46), channel_id=1, source_target_pairs={{0,2},{2,4},{4,6},{6,14},{14,12},{12,10},{10,8},{8,0},{16,18},{18,... | collective-permute-start | bytes 294920 | tf_op jit(solution)/shard_map/ppermute | solution.py:64
  10.4 3.8 %collective-permute-start.5 = (f32[192,128]{1,0:T(8,128)S(1)}, f32[192,128]{1,0:T(8,128)S(1)}, u32[]{:S(2)}, u32[]{:S(2)}) collective-permute-start(f32[192,128]{1,0:T(8,128)S(1)} %get-tuple-element.47), channel_id=1, source_target_pairs={{2,0},{4,2},{6,4},{14,6},{12,14},{10,12},{8,10},{0,8},{18,16},{20,... | collective-permute-start | bytes 294920 | tf_op jit(solution)/shard_map/ppermute | solution.py:64
  10.5 3.6 %collective-permute-start.6 = (f32[160,128]{1,0:T(8,128)S(1)}, f32[160,128]{1,0:T(8,128)S(1)}, u32[]{:S(2)}, u32[]{:S(2)}) collective-permute-start(f32[160,128]{1,0:T(8,128)S(1)} %shard_map.33.refs_0_), channel_id=1, source_target_pairs={{0,1},{1,0},{2,3},{3,2},{4,5},{5,4},{6,7},{7,6},{8,9},{9,8},{10,11... | collective-permute-start | bytes 245768 | tf_op jit(solution)/shard_map/ppermute | solution.py:64
  15.0 7.2 %collective-permute-start.7 = (f32[360,128]{1,0:T(8,128)S(1)}, f32[360,128]{1,0:T(8,128)S(1)}, u32[]{:S(2)}, u32[]{:S(2)}) collective-permute-start(f32[360,128]{1,0:T(8,128)S(1)} %get-tuple-element.56), channel_id=1, source_target_pairs={{0,8},{8,16},{16,24},{24,25},{25,17},{17,9},{9,1},{1,0},{2,10},{10... | collective-permute-start | bytes 552968 | tf_op jit(solution)/shard_map/ppermute | solution.py:64
  19.0 5.0 %collective-permute-start.8 = (f32[360,128]{1,0:T(8,128)S(1)}, f32[360,128]{1,0:T(8,128)S(1)}, u32[]{:S(2)}, u32[]{:S(2)}) collective-permute-start(f32[360,128]{1,0:T(8,128)S(1)} %get-tuple-element.57), channel_id=1, source_target_pairs={{8,0},{16,8},{24,16},{25,24},{17,25},{9,17},{1,9},{0,1},{10,2},{18... | collective-permute-start | bytes 552968 | tf_op jit(solution)/shard_map/ppermute | solution.py:64

commit v14 on v13

--- a/solution.py
+++ b/solution.py
@@ -312,7 +312,7 @@
     return out
 
 
-def spread_kernel(s, nz, nz2, _, __, *rest):
+def spread_kernel(s, nz, nz2, _, *rest):
     z_messages, z2_messages = rest[:nz], rest[nz : nz + nz2]
     ahead, behind, packed = rest[-3:]
     z, y, x = s.z, s.y, s.x
@@ -369,7 +369,7 @@
         yield g, ends
 
 
-def early_kernel(s, charges, x_fine, y_own, t_part, last, start):
+def early_kernel(s, charges, x_fine, y_own, _, t_part, last, start):
     z, y, x = s.z, s.y, s.x
     t_part[...] = jnp.zeros(t_part.shape, F32)
     for g in range(0, z.fine, 8):
@@ -1014,7 +1014,7 @@
     ahead, behind = call(
         bound(spread_kernel, nz, nz2),
         [array(s.slab_rows, n), array(s.slab_rows, n)],
-        [passed[0], later[1], *z_got],
+        [passed[0], *z_got],
         [pltpu.VMEM((3, up8(max(s.slab_coarse, s.slab_rows - s.slab_fine)) + 8, n), F32)],
     )
     sides += [s.y_routes[0](ahead), s.y_routes[1](behind)]
@@ -1023,7 +1023,7 @@
     t_part, last, start = call(
         bound(early_kernel),
         [array(z.fine + 2 * RADIUS, TERMS, y.fine, n)] + [array(s.own_groups * y.fine, n)] * 2,
-        [held, x_fine, y_own],
+        [held, x_fine, y_own, table],
     )
     fine, slab, sums, first, second = call(
         bound(collect_kernel, nz, nz2),

time: 27.5 us -> 27.4 us (level)
  transfers between devices with their start and end apart: 9 -> 9, of which waited for: 3 -> 2; matrix products, arithmetic and copies ran while one was open for 0% -> 0% of each run, Pallas kernels for 26% -> 26%
where the time goes in v14:
time: 27.4 us; the launch traced here: 27.2 us
  Pallas kernels  12.4 us (45%)
  starting transfers between devices  11.8 us (43%)
  waiting for transfers between devices  2.15 us (8%)
  local copies, waits for them, and re-layouts  0.8 us (3%)
    pallas_call x10, Pallas kernels, call(): pl.pallas_call(kernel, out_shape=tuple(outs), in_specs=specs, out_specs=t...  12.4 us
    ppermute x9, starting transfers between devices, __call__(): return lax.ppermute(x, self.names, self.pairs)  11.8 us
    ppermute x9, waiting for transfers between devices, __call__(): return lax.ppermute(x, self.names, self.pairs)  2.15 us
    unnamed x4, local copies, waits for them, and re-layouts  0.8 us
  transfers between devices with their start and end apart: 9, of which 2 were waited for; matrix products, arithmetic and copies ran while one was open for 0% of the time, Pallas kernels for 26%

profile of v14, /device:TPU:1, one launch (start us, length us, event | category | flops | bytes accessed | tf_op | source)
XLA Modules:
  0.0 27.2 jit_solution(8867307773279940357)
XLA Ops:
  0.0 0.0 copy-start
  0.0 0.2 shard_map.29.refs_1_
  0.2 0.8 %copy-done = f32[32,32,128]{2,1,0:T(8,128)S(1)} copy-done((f32[32,32,128]{2,1,0:T(8,128)S(1)}, f32[32,32,128]{2,1,0:T(8,128)}, u32[]{:S(2)}) %copy-start) | copy-done | bytes 524312
  1.0 0.9 %shard_map.30 = (f32[32,32,128]{2,1,0:T(8,128)S(1)}, f32[19,24,128]{2,1,0:T(8,128)S(1)}, f32[472,128]{1,0:T(8,128)S(1)}, f32[472,128]{1,0:T(8,128)S(1)}, f32[32,128]{1,0:T(8,128)S(1)}, /*index=5*/f32[344,128]{1,0:T(8,128)S(1)}) custom-call(f32[32,32,128]{2,1,0:T(8,128)S(1)} %copy-done, bf16[128,256]{1,0:T(8,128)(2,1)S(1)} %shard_map.29.refs_1_), custom_call_target="tpu_custom_call" | custom-call | flops 10000000 | bytes 2023424 | tf_op jit(solution)/shard_map/pallas_call | solution.py:945
  1.9 2.1 %collective-permute-start = (f32[344,128]{1,0:T(8,128)S(1)}, f32[344,128]{1,0:T(8,128)S(1)}, u32[]{:S(2)}, u32[]{:S(2)}) collective-permute-start(f32[344,128]{1,0:T(8,128)S(1)} %get-tuple-element.42), channel_id=1, source_target_pairs={{0,1},{1,0},{2,3},{3,2},{4,5},{5,4},{6,7},{7,6},{8,9},{9,8},{10,11... | collective-permute-start | bytes 528392 | tf_op jit(solution)/shard_map/ppermute | solution.py:64
  4.0 2.3 %collective-permute-start.3 = (f32[32,128]{1,0:T(8,128)S(1)}, f32[32,128]{1,0:T(8,128)S(1)}, u32[]{:S(2)}, u32[]{:S(2)}) collective-permute-start(f32[32,128]{1,0:T(8,128)S(1)} %get-tuple-element.45), channel_id=1, source_target_pairs={{0,4},{2,6},{4,0},{6,2},{1,5},{3,7},{5,1},{7,3},{8,12},{10,14},{12... | collective-permute-start | bytes 49160 | tf_op jit(solution)/shard_map/ppermute | solution.py:64
  6.3 1.2 %collective-permute-start.1 = (f32[472,128]{1,0:T(8,128)S(1)}, f32[472,128]{1,0:T(8,128)S(1)}, u32[]{:S(2)}, u32[]{:S(2)}) collective-permute-start(f32[472,128]{1,0:T(8,128)S(1)} %get-tuple-element.43), channel_id=1, source_target_pairs={{0,2},{2,4},{4,6},{6,14},{14,12},{12,10},{10,8},{8,0},{16,18},{18,... | collective-permute-start | bytes 725000 | tf_op jit(solution)/shard_map/ppermute | solution.py:64
  7.5 0.2 collective-permute-start.2
  7.8 0.0 collective-permute-done.3.refs_0_.refs_8_
  7.8 0.0 copy-start.1
  7.8 0.4 %collective-permute-done.refs_1_.refs_3_ = f32[344,128]{1,0:T(8,128)S(1)} collective-permute-done((f32[344,128]{1,0:T(8,128)S(1)}, f32[344,128]{1,0:T(8,128)S(1)}, u32[]{:S(2)}, u32[]{:S(2)}) %collective-permute-start) | collective-permute-done | bytes 176160 | tf_op jit(solution)/shard_map/ppermute | solution.py:64
  8.2 0.1 shard_map.34
  8.3 1.6 %collective-permute-start.4 = (f32[192,128]{1,0:T(8,128)S(1)}, f32[192,128]{1,0:T(8,128)S(1)}, u32[]{:S(2)}, u32[]{:S(2)}) collective-permute-start(f32[192,128]{1,0:T(8,128)S(1)} %get-tuple-element.46), channel_id=1, source_target_pairs={{0,2},{2,4},{4,6},{6,14},{14,12},{12,10},{10,8},{8,0},{16,18},{18,... | collective-permute-start | bytes 294920 | tf_op jit(solution)/shard_map/ppermute | solution.py:64
  9.8 0.0 collective-permute-start.5
  9.8 1.2 %collective-permute-start.6 = (f32[160,128]{1,0:T(8,128)S(1)}, f32[160,128]{1,0:T(8,128)S(1)}, u32[]{:S(2)}, u32[]{:S(2)}) collective-permute-start(f32[160,128]{1,0:T(8,128)S(1)} %shard_map.33.refs_0_), channel_id=1, source_target_pairs={{0,1},{1,0},{2,3},{3,2},{4,5},{5,4},{6,7},{7,6},{8,9},{9,8},{10,11... | collective-permute-start | bytes 245768 | tf_op jit(solution)/shard_map/ppermute | solution.py:64
  11.0 0.0 copy-done.1
  11.0 1.5 %shard_map.31 = (bf16[384,256]{1,0:T(8,128)(2,1)S(1)}, bf16[640,384]{1,0:T(8,128)(2,1)S(1)}, bf16[64,96]{1,0:T(8,128)(2,1)S(1)}, bf16[64,48]{1,0:T(8,128)(2,1)S(...) custom-call(f32[3,2,17]{2,1,0:T(2,128)S(1)} %copy-done.1), custom_call_target="tpu_custom_call" | custom-call | flops 10000000 | bytes 854424 | tf_op jit(solution)/shard_map/pallas_call | solution.py:945
  12.5 1.1 %shard_map.28 = (bf16[4,1152,256]{2,1,0:T(8,128)(2,1)S(1)}, f32[85,8,128]{2,1,0:T(8,128)S(1)}) custom-call(f32[3,2,17]{2,1,0:T(2,128)S(1)} %copy-done.1), custom_call_target="tpu_custom_call" | custom-call | flops 10000000 | bytes 2707864 | tf_op jit(solution)/shard_map/pallas_call | solution.py:945
  13.6 1.1 %shard_map.32 = (f32[48,2,32,128]{3,2,1,0:T(8,128)S(1)}, f32[64,128]{1,0:T(8,128)S(1)}, f32[64,128]{1,0:T(8,128)S(1)}) custom-call(f32[32,32,128]{2,1,0:T(8,128)S(1)} %get-tuple-element.35.refs_0_.refs_1_, bf16[384,256]{1,0:T(8,128)(2,1)S(1)} %get-tuple-element.36.refs_1_.refs_5_, bf16[64,96]{1,0:T(8,128)(2,1)S(1)} %get-tuple-element.37.refs_2_, ...), custom_call_target="tpu_custom_call" | custom-call | flops 10000000 | bytes 2719744 | tf_op jit(solution)/shard_map/pallas_call | solution.py:945
  14.8 0.0 collective-permute-done.6.refs_9_
  14.8 0.0 collective-permute-done.1.refs_4_
  14.8 0.0 collective-permute-done.2.refs_5_
  14.8 0.0 collective-permute-done.4.refs_6_
  14.8 0.0 collective-permute-done.5.refs_7_
  14.8 0.8 %shard_map.35 = (f32[40,16,128]{2,1,0:T(8,128)S(1)}, f32[8,32,128]{2,1,0:T(8,128)S(1)}, f32[27,48,128]{2,1,0:T(8,128)S(1)}, f32[360,128]{1,0:T(8,128)S(1)}, f32[360,128]{1,0:T(8,128)S(1)}) custom-call(f32[64,128]{1,0:T(8,128)S(1)} %get-tuple-element.39.refs_0_, f32[64,128]{1,0:T(8,128)S(1)} %get-tuple-element.40.refs_1_, ...), custom_call_target="tpu_custom_call" | custom-call | flops 10000000 | bytes 2744320 | tf_op jit(solution)/shard_map/pallas_call | solution.py:945
  15.7 3.2 %collective-permute-start.7 = (f32[360,128]{1,0:T(8,128)S(1)}, f32[360,128]{1,0:T(8,128)S(1)}, u32[]{:S(2)}, u32[]{:S(2)}) collective-permute-start(f32[360,128]{1,0:T(8,128)S(1)} %get-tuple-element.56), channel_id=1, source_target_pairs={{0,8},{8,16},{16,24},{24,25},{25,17},{17,9},{9,1},{1,0},{2,10},{10... | collective-permute-start | bytes 552968 | tf_op jit(solution)/shard_map/ppermute | solution.py:64
  18.8 0.0 collective-permute-start.8
  18.8 3.2 %shard_map.36 = (f32[32,32,128]{2,1,0:T(8,128)S(1)}, f32[1296,384]{1,0:T(8,128)S(1)}) custom-call(f32[85,8,128]{2,1,0:T(8,128)S(1)} %get-tuple-element.34.refs_3_.refs_0_, f32[48,2,32,128]{3,2,1,0:T(8,128)S(1)} %get-tuple-element.38.refs_1_, f32[40,16,128]{2,1,0:T(8,128)S(1)} %get-tuple-element.48.refs_2_, f32[8,32,128]{2,1,0:T(8,128)S(1)} %get-tuple-element.49.refs_3_, ...), custom_call_target="tpu_custom_call" | custom-call | flops 10000000 | bytes 6270976 | tf_op jit(solution)/shard_map/pallas_call | solution.py:945
  22.1 0.0 collective-permute-done.7.refs_3_
  22.1 1.7 %collective-permute-done.8.refs_4_ = f32[360,128]{1,0:T(8,128)S(1)} collective-permute-done((f32[360,128]{1,0:T(8,128)S(1)}, f32[360,128]{1,0:T(8,128)S(1)}, u32[]{:S(2)}, u32[]{:S(2)}) %collective-permute-start.8) | collective-permute-done | bytes 184352 | tf_op jit(solution)/shard_map/ppermute | solution.py:64
  23.8 3.4 %shard_map.37 = f32[32,32,128]{2,1,0:T(8,128)} custom-call(f32[85,8,128]{2,1,0:T(8,128)S(1)} %get-tuple-element.34.refs_3_.refs_0_, f32[32,32,128]{2,1,0:T(8,128)S(1)} %get-tuple-element.54.refs_1_, f32[1296,384]{1,0:T(8,128)S(1)} %get-tuple-element.55.refs_2_, f32[360,128]{1,0:T(8,128)S(1)} %collective-permute-done.7.refs_3_, ...), custom_call_target="tpu_custom_call" | custom-call | flops 10000000 | bytes 6754304 | tf_op jit(solution)/shard_map/pallas_call | solution.py:945
  (1 shorter events, 0.0 us)
Async XLA Ops:
  0.0 1.0 %copy-start = (f32[32,32,128]{2,1,0:T(8,128)S(1)}, f32[32,32,128]{2,1,0:T(8,128)}, u32[]{:S(2)}) copy-start(f32[32,32,128]{2,1,0:T(8,128)} %refs_0_.4) | copy-start | bytes 1572868
  1.9 6.3 %collective-permute-start = (f32[344,128]{1,0:T(8,128)S(1)}, f32[344,128]{1,0:T(8,128)S(1)}, u32[]{:S(2)}, u32[]{:S(2)}) collective-permute-start(f32[344,128]{1,0:T(8,128)S(1)} %get-tuple-element.42), channel_id=1, source_target_pairs={{0,1},{1,0},{2,3},{3,2},{4,5},{5,4},{6,7},{7,6},{8,9},{9,8},{10,11... | collective-permute-start | bytes 528392 | tf_op jit(solution)/shard_map/ppermute | solution.py:64
  4.0 3.8 %collective-permute-start.3 = (f32[32,128]{1,0:T(8,128)S(1)}, f32[32,128]{1,0:T(8,128)S(1)}, u32[]{:S(2)}, u32[]{:S(2)}) collective-permute-start(f32[32,128]{1,0:T(8,128)S(1)} %get-tuple-element.45), channel_id=1, source_target_pairs={{0,4},{2,6},{4,0},{6,2},{1,5},{3,7},{5,1},{7,3},{8,12},{10,14},{12... | collective-permute-start | bytes 49160 | tf_op jit(solution)/shard_map/ppermute | solution.py:64
  6.3 8.5 %collective-permute-start.1 = (f32[472,128]{1,0:T(8,128)S(1)}, f32[472,128]{1,0:T(8,128)S(1)}, u32[]{:S(2)}, u32[]{:S(2)}) collective-permute-start(f32[472,128]{1,0:T(8,128)S(1)} %get-tuple-element.43), channel_id=1, source_target_pairs={{0,2},{2,4},{4,6},{6,14},{14,12},{12,10},{10,8},{8,0},{16,18},{18,... | collective-permute-start | bytes 725000 | tf_op jit(solution)/shard_map/ppermute | solution.py:64
  7.5 7.3 %collective-permute-start.2 = (f32[472,128]{1,0:T(8,128)S(1)}, f32[472,128]{1,0:T(8,128)S(1)}, u32[]{:S(2)}, u32[]{:S(2)}) collective-permute-start(f32[472,128]{1,0:T(8,128)S(1)} %get-tuple-element.44), channel_id=1, source_target_pairs={{2,0},{4,2},{6,4},{14,6},{12,14},{10,12},{8,10},{0,8},{18,16},{20,... | collective-permute-start | bytes 725000 | tf_op jit(solution)/shard_map/ppermute | solution.py:64
  7.8 3.2 %copy-start.1 = (f32[3,2,17]{2,1,0:T(2,128)S(1)}, f32[3,2,17]{2,1,0:T(2,128)}, u32[]{:S(2)}) copy-start(f32[3,2,17]{2,1,0:T(2,128)} %refs_0_.5) | copy-start | bytes 1228
  8.3 6.5 %collective-permute-start.4 = (f32[192,128]{1,0:T(8,128)S(1)}, f32[192,128]{1,0:T(8,128)S(1)}, u32[]{:S(2)}, u32[]{:S(2)}) collective-permute-start(f32[192,128]{1,0:T(8,128)S(1)} %get-tuple-element.46), channel_id=1, source_target_pairs={{0,2},{2,4},{4,6},{6,14},{14,12},{12,10},{10,8},{8,0},{16,18},{18,... | collective-permute-start | bytes 294920 | tf_op jit(solution)/shard_map/ppermute | solution.py:64
  9.8 5.0 %collective-permute-start.5 = (f32[192,128]{1,0:T(8,128)S(1)}, f32[192,128]{1,0:T(8,128)S(1)}, u32[]{:S(2)}, u32[]{:S(2)}) collective-permute-start(f32[192,128]{1,0:T(8,128)S(1)} %get-tuple-element.47), channel_id=1, source_target_pairs={{2,0},{4,2},{6,4},{14,6},{12,14},{10,12},{8,10},{0,8},{18,16},{20,... | collective-permute-start | bytes 294920 | tf_op jit(solution)/shard_map/ppermute | solution.py:64
  9.8 5.0 %collective-permute-start.6 = (f32[160,128]{1,0:T(8,128)S(1)}, f32[160,128]{1,0:T(8,128)S(1)}, u32[]{:S(2)}, u32[]{:S(2)}) collective-permute-start(f32[160,128]{1,0:T(8,128)S(1)} %shard_map.33.refs_0_), channel_id=1, source_target_pairs={{0,1},{1,0},{2,3},{3,2},{4,5},{5,4},{6,7},{7,6},{8,9},{9,8},{10,11... | collective-permute-start | bytes 245768 | tf_op jit(solution)/shard_map/ppermute | solution.py:64
  15.7 6.4 %collective-permute-start.7 = (f32[360,128]{1,0:T(8,128)S(1)}, f32[360,128]{1,0:T(8,128)S(1)}, u32[]{:S(2)}, u32[]{:S(2)}) collective-permute-start(f32[360,128]{1,0:T(8,128)S(1)} %get-tuple-element.56), channel_id=1, source_target_pairs={{0,8},{8,16},{16,24},{24,25},{25,17},{17,9},{9,1},{1,0},{2,10},{10... | collective-permute-start | bytes 552968 | tf_op jit(solution)/shard_map/ppermute | solution.py:64
  18.8 5.0 %collective-permute-start.8 = (f32[360,128]{1,0:T(8,128)S(1)}, f32[360,128]{1,0:T(8,128)S(1)}, u32[]{:S(2)}, u32[]{:S(2)}) collective-permute-start(f32[360,128]{1,0:T(8,128)S(1)} %get-tuple-element.57), channel_id=1, source_target_pairs={{8,0},{16,8},{24,16},{25,24},{17,25},{9,17},{1,9},{0,1},{10,2},{18... | collective-permute-start | bytes 552968 | tf_op jit(solution)/shard_map/ppermute | solution.py:64

commit v15 on v14

--- a/solution.py
+++ b/solution.py
@@ -371,7 +371,7 @@
 
 def early_kernel(s, charges, x_fine, y_own, _, t_part, last, start):
     z, y, x = s.z, s.y, s.x
-    t_part[...] = jnp.zeros(t_part.shape, F32)
+    clear_ends(t_part, z.fine)
     for g in range(0, z.fine, 8):
         a, b = split(contract_x(s, charges[g : g + 8].reshape(8 * y.fine, x.fine), x_fine))
         for p in range(8):
@@ -725,6 +725,12 @@
 BLOCK = 4
 
 
+def clear_ends(held, own):
+    zeros = jnp.zeros((RADIUS,) + held.shape[1:], F32)
+    held[:RADIUS] = zeros
+    held[RADIUS + own :] = zeros
+
+
 def fine_places(s):
     places = [(RADIUS + p, None) for p in range(s.z.fine)]
     for start, valid in slab_starts(s, 0, s.z.fine + RADIUS):
@@ -811,9 +817,10 @@
         sums_ends[b * 128 : (b + 1) * 128] = jnp.concatenate([rows, rows, zeros], axis=0).T
 
     def along_x(start, rows):
-        edge_high, edge_low = split(sums_ends[start : start + rows])
-        is_high = iota(edge_high.shape, 1) < 2 * half
-        packed = jnp.where(is_high, edge_high.astype(F32), edge_low.astype(F32)).astype(BF16)
+        edge = sums_ends[start : start + rows]
+        edge_high = edge.astype(BF16)
+        is_high = iota(edge.shape, 1) < 2 * half
+        packed = jnp.where(is_high, edge, edge - edge_high.astype(F32)).astype(BF16)
         joined = jnp.concatenate([packed, edge_high], axis=1)
         part = jnp.dot(joined, x_sums[3 * x.fine :], preferred_element_type=F32)
         return split(sums[start : start + rows] + part)
@@ -844,8 +851,8 @@
             result.append(total)
         return result
 
-    t_mid[...] = jnp.zeros(t_mid.shape, F32)
-    t_coarse[...] = jnp.zeros(t_coarse.shape, F32)
+    clear_ends(t_mid, z.mid_all)
+    clear_ends(t_coarse, z.coarse_all)
     mid_at = [(RADIUS + p, None) for p in range(z.mid_all)]
     mid_at, rest_at = mid_at[: z.coarse_all], mid_at[z.coarse_all :]
     coarse_at = [(RADIUS + p, None) for p in range(z.coarse_all)]

time: 27.4 us -> 27.4 us (level)
  no operation moved by 1% of the time
where the time goes in v15:
time: 27.4 us; the launch traced here: 27.2 us
  Pallas kernels  12.4 us (45%)
  starting transfers between devices  11.8 us (43%)
  waiting for transfers between devices  2.15 us (8%)
  local copies, waits for them, and re-layouts  0.8 us (3%)
    pallas_call x10, Pallas kernels, call(): pl.pallas_call(kernel, out_shape=tuple(outs), in_specs=specs, out_specs=t...  12.4 us
    ppermute x9, starting transfers between devices, __call__(): return lax.ppermute(x, self.names, self.pairs)  11.8 us
    ppermute x9, waiting for transfers between devices, __call__(): return lax.ppermute(x, self.names, self.pairs)  2.15 us
    unnamed x4, local copies, waits for them, and re-layouts  0.8 us
  transfers between devices with their start and end apart: 9, of which 2 were waited for; matrix products, arithmetic and copies ran while one was open for 0% of the time, Pallas kernels for 26%

profile of v15, /device:TPU:1, one launch (start us, length us, event | category | flops | bytes accessed | tf_op | source)
XLA Modules:
  0.0 27.2 jit_solution(15814243196405073682)
XLA Ops:
  0.0 0.0 copy-start
  0.0 0.2 shard_map.29.refs_1_
  0.2 0.8 %copy-done = f32[32,32,128]{2,1,0:T(8,128)S(1)} copy-done((f32[32,32,128]{2,1,0:T(8,128)S(1)}, f32[32,32,128]{2,1,0:T(8,128)}, u32[]{:S(2)}) %copy-start) | copy-done | bytes 524312
  1.0 0.9 %shard_map.30 = (f32[32,32,128]{2,1,0:T(8,128)S(1)}, f32[19,24,128]{2,1,0:T(8,128)S(1)}, f32[472,128]{1,0:T(8,128)S(1)}, f32[472,128]{1,0:T(8,128)S(1)}, f32[32,128]{1,0:T(8,128)S(1)}, /*index=5*/f32[344,128]{1,0:T(8,128)S(1)}) custom-call(f32[32,32,128]{2,1,0:T(8,128)S(1)} %copy-done, bf16[128,256]{1,0:T(8,128)(2,1)S(1)} %shard_map.29.refs_1_), custom_call_target="tpu_custom_call" | custom-call | flops 10000000 | bytes 2023424 | tf_op jit(solution)/shard_map/pallas_call | solution.py:952
  1.9 2.1 %collective-permute-start = (f32[344,128]{1,0:T(8,128)S(1)}, f32[344,128]{1,0:T(8,128)S(1)}, u32[]{:S(2)}, u32[]{:S(2)}) collective-permute-start(f32[344,128]{1,0:T(8,128)S(1)} %get-tuple-element.42), channel_id=1, source_target_pairs={{0,1},{1,0},{2,3},{3,2},{4,5},{5,4},{6,7},{7,6},{8,9},{9,8},{10,11... | collective-permute-start | bytes 528392 | tf_op jit(solution)/shard_map/ppermute | solution.py:64
  4.0 2.3 %collective-permute-start.3 = (f32[32,128]{1,0:T(8,128)S(1)}, f32[32,128]{1,0:T(8,128)S(1)}, u32[]{:S(2)}, u32[]{:S(2)}) collective-permute-start(f32[32,128]{1,0:T(8,128)S(1)} %get-tuple-element.45), channel_id=1, source_target_pairs={{0,4},{2,6},{4,0},{6,2},{1,5},{3,7},{5,1},{7,3},{8,12},{10,14},{12... | collective-permute-start | bytes 49160 | tf_op jit(solution)/shard_map/ppermute | solution.py:64
  6.3 1.2 %collective-permute-start.1 = (f32[472,128]{1,0:T(8,128)S(1)}, f32[472,128]{1,0:T(8,128)S(1)}, u32[]{:S(2)}, u32[]{:S(2)}) collective-permute-start(f32[472,128]{1,0:T(8,128)S(1)} %get-tuple-element.43), channel_id=1, source_target_pairs={{0,2},{2,4},{4,6},{6,14},{14,12},{12,10},{10,8},{8,0},{16,18},{18,... | collective-permute-start | bytes 725000 | tf_op jit(solution)/shard_map/ppermute | solution.py:64
  7.5 0.2 collective-permute-start.2
  7.8 0.0 collective-permute-done.3.refs_0_.refs_8_
  7.8 0.0 copy-start.1
  7.8 0.4 %collective-permute-done.refs_1_.refs_3_ = f32[344,128]{1,0:T(8,128)S(1)} collective-permute-done((f32[344,128]{1,0:T(8,128)S(1)}, f32[344,128]{1,0:T(8,128)S(1)}, u32[]{:S(2)}, u32[]{:S(2)}) %collective-permute-start) | collective-permute-done | bytes 176160 | tf_op jit(solution)/shard_map/ppermute | solution.py:64
  8.2 0.1 shard_map.34
  8.3 1.6 %collective-permute-start.4 = (f32[192,128]{1,0:T(8,128)S(1)}, f32[192,128]{1,0:T(8,128)S(1)}, u32[]{:S(2)}, u32[]{:S(2)}) collective-permute-start(f32[192,128]{1,0:T(8,128)S(1)} %get-tuple-element.46), channel_id=1, source_target_pairs={{0,2},{2,4},{4,6},{6,14},{14,12},{12,10},{10,8},{8,0},{16,18},{18,... | collective-permute-start | bytes 294920 | tf_op jit(solution)/shard_map/ppermute | solution.py:64
  9.8 0.0 collective-permute-start.5
  9.8 1.2 %collective-permute-start.6 = (f32[160,128]{1,0:T(8,128)S(1)}, f32[160,128]{1,0:T(8,128)S(1)}, u32[]{:S(2)}, u32[]{:S(2)}) collective-permute-start(f32[160,128]{1,0:T(8,128)S(1)} %shard_map.33.refs_0_), channel_id=1, source_target_pairs={{0,1},{1,0},{2,3},{3,2},{4,5},{5,4},{6,7},{7,6},{8,9},{9,8},{10,11... | collective-permute-start | bytes 245768 | tf_op jit(solution)/shard_map/ppermute | solution.py:64
  11.0 0.0 copy-done.1
  11.0 1.5 %shard_map.31 = (bf16[384,256]{1,0:T(8,128)(2,1)S(1)}, bf16[640,384]{1,0:T(8,128)(2,1)S(1)}, bf16[64,96]{1,0:T(8,128)(2,1)S(1)}, bf16[64,48]{1,0:T(8,128)(2,1)S(...) custom-call(f32[3,2,17]{2,1,0:T(2,128)S(1)} %copy-done.1), custom_call_target="tpu_custom_call" | custom-call | flops 10000000 | bytes 854424 | tf_op jit(solution)/shard_map/pallas_call | solution.py:952
  12.5 1.1 %shard_map.28 = (bf16[4,1152,256]{2,1,0:T(8,128)(2,1)S(1)}, f32[85,8,128]{2,1,0:T(8,128)S(1)}) custom-call(f32[3,2,17]{2,1,0:T(2,128)S(1)} %copy-done.1), custom_call_target="tpu_custom_call" | custom-call | flops 10000000 | bytes 2707864 | tf_op jit(solution)/shard_map/pallas_call | solution.py:952
  13.6 1.1 %shard_map.32 = (f32[48,2,32,128]{3,2,1,0:T(8,128)S(1)}, f32[64,128]{1,0:T(8,128)S(1)}, f32[64,128]{1,0:T(8,128)S(1)}) custom-call(f32[32,32,128]{2,1,0:T(8,128)S(1)} %get-tuple-element.35.refs_0_.refs_1_, bf16[384,256]{1,0:T(8,128)(2,1)S(1)} %get-tuple-element.36.refs_1_.refs_5_, bf16[64,96]{1,0:T(8,128)(2,1)S(1)} %get-tuple-element.37.refs_2_, ...), custom_call_target="tpu_custom_call" | custom-call | flops 10000000 | bytes 2719744 | tf_op jit(solution)/shard_map/pallas_call | solution.py:952
  14.8 0.0 collective-permute-done.6.refs_9_
  14.8 0.0 collective-permute-done.1.refs_4_
  14.8 0.0 collective-permute-done.2.refs_5_
  14.8 0.0 collective-permute-done.4.refs_6_
  14.8 0.0 collective-permute-done.5.refs_7_
  14.8 0.8 %shard_map.35 = (f32[40,16,128]{2,1,0:T(8,128)S(1)}, f32[8,32,128]{2,1,0:T(8,128)S(1)}, f32[27,48,128]{2,1,0:T(8,128)S(1)}, f32[360,128]{1,0:T(8,128)S(1)}, f32[360,128]{1,0:T(8,128)S(1)}) custom-call(f32[64,128]{1,0:T(8,128)S(1)} %get-tuple-element.39.refs_0_, f32[64,128]{1,0:T(8,128)S(1)} %get-tuple-element.40.refs_1_, ...), custom_call_target="tpu_custom_call" | custom-call | flops 10000000 | bytes 2744320 | tf_op jit(solution)/shard_map/pallas_call | solution.py:952
  15.7 3.2 %collective-permute-start.7 = (f32[360,128]{1,0:T(8,128)S(1)}, f32[360,128]{1,0:T(8,128)S(1)}, u32[]{:S(2)}, u32[]{:S(2)}) collective-permute-start(f32[360,128]{1,0:T(8,128)S(1)} %get-tuple-element.56), channel_id=1, source_target_pairs={{0,8},{8,16},{16,24},{24,25},{25,17},{17,9},{9,1},{1,0},{2,10},{10... | collective-permute-start | bytes 552968 | tf_op jit(solution)/shard_map/ppermute | solution.py:64
  18.8 0.0 collective-permute-start.8
  18.8 3.2 %shard_map.36 = (f32[32,32,128]{2,1,0:T(8,128)S(1)}, f32[1296,384]{1,0:T(8,128)S(1)}) custom-call(f32[85,8,128]{2,1,0:T(8,128)S(1)} %get-tuple-element.34.refs_3_.refs_0_, f32[48,2,32,128]{3,2,1,0:T(8,128)S(1)} %get-tuple-element.38.refs_1_, f32[40,16,128]{2,1,0:T(8,128)S(1)} %get-tuple-element.48.refs_2_, f32[8,32,128]{2,1,0:T(8,128)S(1)} %get-tuple-element.49.refs_3_, ...), custom_call_target="tpu_custom_call" | custom-call | flops 10000000 | bytes 6270976 | tf_op jit(solution)/shard_map/pallas_call | solution.py:952
  22.1 0.0 collective-permute-done.7.refs_3_
  22.1 1.7 %collective-permute-done.8.refs_4_ = f32[360,128]{1,0:T(8,128)S(1)} collective-permute-done((f32[360,128]{1,0:T(8,128)S(1)}, f32[360,128]{1,0:T(8,128)S(1)}, u32[]{:S(2)}, u32[]{:S(2)}) %collective-permute-start.8) | collective-permute-done | bytes 184352 | tf_op jit(solution)/shard_map/ppermute | solution.py:64
  23.8 3.4 %shard_map.37 = f32[32,32,128]{2,1,0:T(8,128)} custom-call(f32[85,8,128]{2,1,0:T(8,128)S(1)} %get-tuple-element.34.refs_3_.refs_0_, f32[32,32,128]{2,1,0:T(8,128)S(1)} %get-tuple-element.54.refs_1_, f32[1296,384]{1,0:T(8,128)S(1)} %get-tuple-element.55.refs_2_, f32[360,128]{1,0:T(8,128)S(1)} %collective-permute-done.7.refs_3_, ...), custom_call_target="tpu_custom_call" | custom-call | flops 10000000 | bytes 6754304 | tf_op jit(solution)/shard_map/pallas_call | solution.py:952
  (1 shorter events, 0.0 us)
Async XLA Ops:
  0.0 1.0 %copy-start = (f32[32,32,128]{2,1,0:T(8,128)S(1)}, f32[32,32,128]{2,1,0:T(8,128)}, u32[]{:S(2)}) copy-start(f32[32,32,128]{2,1,0:T(8,128)} %refs_0_.4) | copy-start | bytes 1572868
  1.9 6.3 %collective-permute-start = (f32[344,128]{1,0:T(8,128)S(1)}, f32[344,128]{1,0:T(8,128)S(1)}, u32[]{:S(2)}, u32[]{:S(2)}) collective-permute-start(f32[344,128]{1,0:T(8,128)S(1)} %get-tuple-element.42), channel_id=1, source_target_pairs={{0,1},{1,0},{2,3},{3,2},{4,5},{5,4},{6,7},{7,6},{8,9},{9,8},{10,11... | collective-permute-start | bytes 528392 | tf_op jit(solution)/shard_map/ppermute | solution.py:64
  4.0 3.8 %collective-permute-start.3 = (f32[32,128]{1,0:T(8,128)S(1)}, f32[32,128]{1,0:T(8,128)S(1)}, u32[]{:S(2)}, u32[]{:S(2)}) collective-permute-start(f32[32,128]{1,0:T(8,128)S(1)} %get-tuple-element.45), channel_id=1, source_target_pairs={{0,4},{2,6},{4,0},{6,2},{1,5},{3,7},{5,1},{7,3},{8,12},{10,14},{12... | collective-permute-start | bytes 49160 | tf_op jit(solution)/shard_map/ppermute | solution.py:64
  6.3 8.5 %collective-permute-start.1 = (f32[472,128]{1,0:T(8,128)S(1)}, f32[472,128]{1,0:T(8,128)S(1)}, u32[]{:S(2)}, u32[]{:S(2)}) collective-permute-start(f32[472,128]{1,0:T(8,128)S(1)} %get-tuple-element.43), channel_id=1, source_target_pairs={{0,2},{2,4},{4,6},{6,14},{14,12},{12,10},{10,8},{8,0},{16,18},{18,... | collective-permute-start | bytes 725000 | tf_op jit(solution)/shard_map/ppermute | solution.py:64
  7.5 7.3 %collective-permute-start.2 = (f32[472,128]{1,0:T(8,128)S(1)}, f32[472,128]{1,0:T(8,128)S(1)}, u32[]{:S(2)}, u32[]{:S(2)}) collective-permute-start(f32[472,128]{1,0:T(8,128)S(1)} %get-tuple-element.44), channel_id=1, source_target_pairs={{2,0},{4,2},{6,4},{14,6},{12,14},{10,12},{8,10},{0,8},{18,16},{20,... | collective-permute-start | bytes 725000 | tf_op jit(solution)/shard_map/ppermute | solution.py:64
  7.8 3.2 %copy-start.1 = (f32[3,2,17]{2,1,0:T(2,128)S(1)}, f32[3,2,17]{2,1,0:T(2,128)}, u32[]{:S(2)}) copy-start(f32[3,2,17]{2,1,0:T(2,128)} %refs_0_.5) | copy-start | bytes 1228
  8.3 6.5 %collective-permute-start.4 = (f32[192,128]{1,0:T(8,128)S(1)}, f32[192,128]{1,0:T(8,128)S(1)}, u32[]{:S(2)}, u32[]{:S(2)}) collective-permute-start(f32[192,128]{1,0:T(8,128)S(1)} %get-tuple-element.46), channel_id=1, source_target_pairs={{0,2},{2,4},{4,6},{6,14},{14,12},{12,10},{10,8},{8,0},{16,18},{18,... | collective-permute-start | bytes 294920 | tf_op jit(solution)/shard_map/ppermute | solution.py:64
  9.8 5.0 %collective-permute-start.5 = (f32[192,128]{1,0:T(8,128)S(1)}, f32[192,128]{1,0:T(8,128)S(1)}, u32[]{:S(2)}, u32[]{:S(2)}) collective-permute-start(f32[192,128]{1,0:T(8,128)S(1)} %get-tuple-element.47), channel_id=1, source_target_pairs={{2,0},{4,2},{6,4},{14,6},{12,14},{10,12},{8,10},{0,8},{18,16},{20,... | collective-permute-start | bytes 294920 | tf_op jit(solution)/shard_map/ppermute | solution.py:64
  9.8 5.0 %collective-permute-start.6 = (f32[160,128]{1,0:T(8,128)S(1)}, f32[160,128]{1,0:T(8,128)S(1)}, u32[]{:S(2)}, u32[]{:S(2)}) collective-permute-start(f32[160,128]{1,0:T(8,128)S(1)} %shard_map.33.refs_0_), channel_id=1, source_target_pairs={{0,1},{1,0},{2,3},{3,2},{4,5},{5,4},{6,7},{7,6},{8,9},{9,8},{10,11... | collective-permute-start | bytes 245768 | tf_op jit(solution)/shard_map/ppermute | solution.py:64
  15.7 6.4 %collective-permute-start.7 = (f32[360,128]{1,0:T(8,128)S(1)}, f32[360,128]{1,0:T(8,128)S(1)}, u32[]{:S(2)}, u32[]{:S(2)}) collective-permute-start(f32[360,128]{1,0:T(8,128)S(1)} %get-tuple-element.56), channel_id=1, source_target_pairs={{0,8},{8,16},{16,24},{24,25},{25,17},{17,9},{9,1},{1,0},{2,10},{10... | collective-permute-start | bytes 552968 | tf_op jit(solution)/shard_map/ppermute | solution.py:64
  18.8 5.0 %collective-permute-start.8 = (f32[360,128]{1,0:T(8,128)S(1)}, f32[360,128]{1,0:T(8,128)S(1)}, u32[]{:S(2)}, u32[]{:S(2)}) collective-permute-start(f32[360,128]{1,0:T(8,128)S(1)} %get-tuple-element.57), channel_id=1, source_target_pairs={{8,0},{16,8},{24,16},{25,24},{17,25},{9,17},{1,9},{0,1},{10,2},{18... | collective-permute-start | bytes 552968 | tf_op jit(solution)/shard_map/ppermute | solution.py:64

commit v16 on v14

--- a/solution.py
+++ b/solution.py
@@ -194,7 +194,8 @@
 def restrict_kernel(s, nz, source, narrow, charges, own, ahead, behind, far, *rest):
     messages, (wide, mid, high, coarse, packed, groups) = rest[:-6], rest[-6:]
     z, y, x = s.z, s.y, s.x
-    wide[...] = jnp.zeros(wide.shape, F32)
+    wide[:, :8] = jnp.zeros((z.fine, 8, x.fine), F32)
+    wide[:, 8 + y.fine :] = jnp.zeros((z.fine, wide.shape[1] - 8 - y.fine, x.fine), F32)
     charges[...] = source[...]
     cells = source[...].reshape(z.fine * y.fine, x.fine)
     top, rest = cells.astype(BF16), cells

time: 27.4 us -> 27.4 us (level)
  no operation moved by 1% of the time
where the time goes in v16:
time: 27.4 us; the launch traced here: 27.2 us
  Pallas kernels  12.4 us (45%)
  starting transfers between devices  11.8 us (43%)
  waiting for transfers between devices  2.15 us (8%)
  local copies, waits for them, and re-layouts  0.8 us (3%)
    pallas_call x10, Pallas kernels, call(): pl.pallas_call(kernel, out_shape=tuple(outs), in_specs=specs, out_specs=t...  12.4 us
    ppermute x9, starting transfers between devices, __call__(): return lax.ppermute(x, self.names, self.pairs)  11.8 us
    ppermute x9, waiting for transfers between devices, __call__(): return lax.ppermute(x, self.names, self.pairs)  2.15 us
    unnamed x4, local copies, waits for them, and re-layouts  0.8 us
  transfers between devices with their start and end apart: 9, of which 2 were waited for; matrix products, arithmetic and copies ran while one was open for 0% of the time, Pallas kernels for 26%

profile of v16, /device:TPU:1, one launch (start us, length us, event | category | flops | bytes accessed | tf_op | source)
XLA Modules:
  0.0 27.2 jit_solution(4115412284297175135)
XLA Ops:
  0.0 0.0 copy-start
  0.0 0.2 shard_map.29.refs_1_
  0.2 0.8 %copy-done = f32[32,32,128]{2,1,0:T(8,128)S(1)} copy-done((f32[32,32,128]{2,1,0:T(8,128)S(1)}, f32[32,32,128]{2,1,0:T(8,128)}, u32[]{:S(2)}) %copy-start) | copy-done | bytes 524312
  1.0 0.9 %shard_map.30 = (f32[32,32,128]{2,1,0:T(8,128)S(1)}, f32[19,24,128]{2,1,0:T(8,128)S(1)}, f32[472,128]{1,0:T(8,128)S(1)}, f32[472,128]{1,0:T(8,128)S(1)}, f32[32,128]{1,0:T(8,128)S(1)}, /*index=5*/f32[344,128]{1,0:T(8,128)S(1)}) custom-call(f32[32,32,128]{2,1,0:T(8,128)S(1)} %copy-done, bf16[128,256]{1,0:T(8,128)(2,1)S(1)} %shard_map.29.refs_1_), custom_call_target="tpu_custom_call" | custom-call | flops 10000000 | bytes 2023424 | tf_op jit(solution)/shard_map/pallas_call | solution.py:946
  1.9 2.1 %collective-permute-start = (f32[344,128]{1,0:T(8,128)S(1)}, f32[344,128]{1,0:T(8,128)S(1)}, u32[]{:S(2)}, u32[]{:S(2)}) collective-permute-start(f32[344,128]{1,0:T(8,128)S(1)} %get-tuple-element.42), channel_id=1, source_target_pairs={{0,1},{1,0},{2,3},{3,2},{4,5},{5,4},{6,7},{7,6},{8,9},{9,8},{10,11... | collective-permute-start | bytes 528392 | tf_op jit(solution)/shard_map/ppermute | solution.py:64
  4.0 2.3 %collective-permute-start.3 = (f32[32,128]{1,0:T(8,128)S(1)}, f32[32,128]{1,0:T(8,128)S(1)}, u32[]{:S(2)}, u32[]{:S(2)}) collective-permute-start(f32[32,128]{1,0:T(8,128)S(1)} %get-tuple-element.45), channel_id=1, source_target_pairs={{0,4},{2,6},{4,0},{6,2},{1,5},{3,7},{5,1},{7,3},{8,12},{10,14},{12... | collective-permute-start | bytes 49160 | tf_op jit(solution)/shard_map/ppermute | solution.py:64
  6.3 1.2 %collective-permute-start.1 = (f32[472,128]{1,0:T(8,128)S(1)}, f32[472,128]{1,0:T(8,128)S(1)}, u32[]{:S(2)}, u32[]{:S(2)}) collective-permute-start(f32[472,128]{1,0:T(8,128)S(1)} %get-tuple-element.43), channel_id=1, source_target_pairs={{0,2},{2,4},{4,6},{6,14},{14,12},{12,10},{10,8},{8,0},{16,18},{18,... | collective-permute-start | bytes 725000 | tf_op jit(solution)/shard_map/ppermute | solution.py:64
  7.6 0.2 collective-permute-start.2
  7.8 0.0 collective-permute-done.3.refs_0_.refs_8_
  7.8 0.0 copy-start.1
  7.8 0.4 %collective-permute-done.refs_1_.refs_3_ = f32[344,128]{1,0:T(8,128)S(1)} collective-permute-done((f32[344,128]{1,0:T(8,128)S(1)}, f32[344,128]{1,0:T(8,128)S(1)}, u32[]{:S(2)}, u32[]{:S(2)}) %collective-permute-start) | collective-permute-done | bytes 176160 | tf_op jit(solution)/shard_map/ppermute | solution.py:64
  8.2 0.1 shard_map.34
  8.3 1.5 %collective-permute-start.4 = (f32[192,128]{1,0:T(8,128)S(1)}, f32[192,128]{1,0:T(8,128)S(1)}, u32[]{:S(2)}, u32[]{:S(2)}) collective-permute-start(f32[192,128]{1,0:T(8,128)S(1)} %get-tuple-element.46), channel_id=1, source_target_pairs={{0,2},{2,4},{4,6},{6,14},{14,12},{12,10},{10,8},{8,0},{16,18},{18,... | collective-permute-start | bytes 294920 | tf_op jit(solution)/shard_map/ppermute | solution.py:64
  9.9 0.0 collective-permute-start.5
  9.9 1.2 %collective-permute-start.6 = (f32[160,128]{1,0:T(8,128)S(1)}, f32[160,128]{1,0:T(8,128)S(1)}, u32[]{:S(2)}, u32[]{:S(2)}) collective-permute-start(f32[160,128]{1,0:T(8,128)S(1)} %shard_map.33.refs_0_), channel_id=1, source_target_pairs={{0,1},{1,0},{2,3},{3,2},{4,5},{5,4},{6,7},{7,6},{8,9},{9,8},{10,11... | collective-permute-start | bytes 245768 | tf_op jit(solution)/shard_map/ppermute | solution.py:64
  11.0 0.0 copy-done.1
  11.0 1.5 %shard_map.31 = (bf16[384,256]{1,0:T(8,128)(2,1)S(1)}, bf16[640,384]{1,0:T(8,128)(2,1)S(1)}, bf16[64,96]{1,0:T(8,128)(2,1)S(1)}, bf16[64,48]{1,0:T(8,128)(2,1)S(...) custom-call(f32[3,2,17]{2,1,0:T(2,128)S(1)} %copy-done.1), custom_call_target="tpu_custom_call" | custom-call | flops 10000000 | bytes 854424 | tf_op jit(solution)/shard_map/pallas_call | solution.py:946
  12.6 1.1 %shard_map.28 = (bf16[4,1152,256]{2,1,0:T(8,128)(2,1)S(1)}, f32[85,8,128]{2,1,0:T(8,128)S(1)}) custom-call(f32[3,2,17]{2,1,0:T(2,128)S(1)} %copy-done.1), custom_call_target="tpu_custom_call" | custom-call | flops 10000000 | bytes 2707864 | tf_op jit(solution)/shard_map/pallas_call | solution.py:946
  13.7 1.1 %shard_map.32 = (f32[48,2,32,128]{3,2,1,0:T(8,128)S(1)}, f32[64,128]{1,0:T(8,128)S(1)}, f32[64,128]{1,0:T(8,128)S(1)}) custom-call(f32[32,32,128]{2,1,0:T(8,128)S(1)} %get-tuple-element.35.refs_0_.refs_1_, bf16[384,256]{1,0:T(8,128)(2,1)S(1)} %get-tuple-element.36.refs_1_.refs_5_, bf16[64,96]{1,0:T(8,128)(2,1)S(1)} %get-tuple-element.37.refs_2_, ...), custom_call_target="tpu_custom_call" | custom-call | flops 10000000 | bytes 2719744 | tf_op jit(solution)/shard_map/pallas_call | solution.py:946
  14.8 0.0 collective-permute-done.6.refs_9_
  14.8 0.0 collective-permute-done.1.refs_4_
  14.8 0.0 collective-permute-done.2.refs_5_
  14.8 0.0 collective-permute-done.4.refs_6_
  14.9 0.0 collective-permute-done.5.refs_7_
  14.9 0.8 %shard_map.35 = (f32[40,16,128]{2,1,0:T(8,128)S(1)}, f32[8,32,128]{2,1,0:T(8,128)S(1)}, f32[27,48,128]{2,1,0:T(8,128)S(1)}, f32[360,128]{1,0:T(8,128)S(1)}, f32[360,128]{1,0:T(8,128)S(1)}) custom-call(f32[64,128]{1,0:T(8,128)S(1)} %get-tuple-element.39.refs_0_, f32[64,128]{1,0:T(8,128)S(1)} %get-tuple-element.40.refs_1_, ...), custom_call_target="tpu_custom_call" | custom-call | flops 10000000 | bytes 2744320 | tf_op jit(solution)/shard_map/pallas_call | solution.py:946
  15.7 3.2 %collective-permute-start.7 = (f32[360,128]{1,0:T(8,128)S(1)}, f32[360,128]{1,0:T(8,128)S(1)}, u32[]{:S(2)}, u32[]{:S(2)}) collective-permute-start(f32[360,128]{1,0:T(8,128)S(1)} %get-tuple-element.56), channel_id=1, source_target_pairs={{0,8},{8,16},{16,24},{24,25},{25,17},{17,9},{9,1},{1,0},{2,10},{10... | collective-permute-start | bytes 552968 | tf_op jit(solution)/shard_map/ppermute | solution.py:64
  18.9 0.0 collective-permute-start.8
  18.9 3.2 %shard_map.36 = (f32[32,32,128]{2,1,0:T(8,128)S(1)}, f32[1296,384]{1,0:T(8,128)S(1)}) custom-call(f32[85,8,128]{2,1,0:T(8,128)S(1)} %get-tuple-element.34.refs_3_.refs_0_, f32[48,2,32,128]{3,2,1,0:T(8,128)S(1)} %get-tuple-element.38.refs_1_, f32[40,16,128]{2,1,0:T(8,128)S(1)} %get-tuple-element.48.refs_2_, f32[8,32,128]{2,1,0:T(8,128)S(1)} %get-tuple-element.49.refs_3_, ...), custom_call_target="tpu_custom_call" | custom-call | flops 10000000 | bytes 6270976 | tf_op jit(solution)/shard_map/pallas_call | solution.py:946
  22.1 0.0 collective-permute-done.7.refs_3_
  22.1 1.7 %collective-permute-done.8.refs_4_ = f32[360,128]{1,0:T(8,128)S(1)} collective-permute-done((f32[360,128]{1,0:T(8,128)S(1)}, f32[360,128]{1,0:T(8,128)S(1)}, u32[]{:S(2)}, u32[]{:S(2)}) %collective-permute-start.8) | collective-permute-done | bytes 184352 | tf_op jit(solution)/shard_map/ppermute | solution.py:64
  23.8 3.4 %shard_map.37 = f32[32,32,128]{2,1,0:T(8,128)} custom-call(f32[85,8,128]{2,1,0:T(8,128)S(1)} %get-tuple-element.34.refs_3_.refs_0_, f32[32,32,128]{2,1,0:T(8,128)S(1)} %get-tuple-element.54.refs_1_, f32[1296,384]{1,0:T(8,128)S(1)} %get-tuple-element.55.refs_2_, f32[360,128]{1,0:T(8,128)S(1)} %collective-permute-done.7.refs_3_, ...), custom_call_target="tpu_custom_call" | custom-call | flops 10000000 | bytes 6754304 | tf_op jit(solution)/shard_map/pallas_call | solution.py:946
  (1 shorter events, 0.0 us)
Async XLA Ops:
  0.0 1.0 %copy-start = (f32[32,32,128]{2,1,0:T(8,128)S(1)}, f32[32,32,128]{2,1,0:T(8,128)}, u32[]{:S(2)}) copy-start(f32[32,32,128]{2,1,0:T(8,128)} %refs_0_.4) | copy-start | bytes 1572868
  1.9 6.3 %collective-permute-start = (f32[344,128]{1,0:T(8,128)S(1)}, f32[344,128]{1,0:T(8,128)S(1)}, u32[]{:S(2)}, u32[]{:S(2)}) collective-permute-start(f32[344,128]{1,0:T(8,128)S(1)} %get-tuple-element.42), channel_id=1, source_target_pairs={{0,1},{1,0},{2,3},{3,2},{4,5},{5,4},{6,7},{7,6},{8,9},{9,8},{10,11... | collective-permute-start | bytes 528392 | tf_op jit(solution)/shard_map/ppermute | solution.py:64
  4.0 3.8 %collective-permute-start.3 = (f32[32,128]{1,0:T(8,128)S(1)}, f32[32,128]{1,0:T(8,128)S(1)}, u32[]{:S(2)}, u32[]{:S(2)}) collective-permute-start(f32[32,128]{1,0:T(8,128)S(1)} %get-tuple-element.45), channel_id=1, source_target_pairs={{0,4},{2,6},{4,0},{6,2},{1,5},{3,7},{5,1},{7,3},{8,12},{10,14},{12... | collective-permute-start | bytes 49160 | tf_op jit(solution)/shard_map/ppermute | solution.py:64
  6.3 8.5 %collective-permute-start.1 = (f32[472,128]{1,0:T(8,128)S(1)}, f32[472,128]{1,0:T(8,128)S(1)}, u32[]{:S(2)}, u32[]{:S(2)}) collective-permute-start(f32[472,128]{1,0:T(8,128)S(1)} %get-tuple-element.43), channel_id=1, source_target_pairs={{0,2},{2,4},{4,6},{6,14},{14,12},{12,10},{10,8},{8,0},{16,18},{18,... | collective-permute-start | bytes 725000 | tf_op jit(solution)/shard_map/ppermute | solution.py:64
  7.6 7.3 %collective-permute-start.2 = (f32[472,128]{1,0:T(8,128)S(1)}, f32[472,128]{1,0:T(8,128)S(1)}, u32[]{:S(2)}, u32[]{:S(2)}) collective-permute-start(f32[472,128]{1,0:T(8,128)S(1)} %get-tuple-element.44), channel_id=1, source_target_pairs={{2,0},{4,2},{6,4},{14,6},{12,14},{10,12},{8,10},{0,8},{18,16},{20,... | collective-permute-start | bytes 725000 | tf_op jit(solution)/shard_map/ppermute | solution.py:64
  7.8 3.2 %copy-start.1 = (f32[3,2,17]{2,1,0:T(2,128)S(1)}, f32[3,2,17]{2,1,0:T(2,128)}, u32[]{:S(2)}) copy-start(f32[3,2,17]{2,1,0:T(2,128)} %refs_0_.5) | copy-start | bytes 1228
  8.3 6.5 %collective-permute-start.4 = (f32[192,128]{1,0:T(8,128)S(1)}, f32[192,128]{1,0:T(8,128)S(1)}, u32[]{:S(2)}, u32[]{:S(2)}) collective-permute-start(f32[192,128]{1,0:T(8,128)S(1)} %get-tuple-element.46), channel_id=1, source_target_pairs={{0,2},{2,4},{4,6},{6,14},{14,12},{12,10},{10,8},{8,0},{16,18},{18,... | collective-permute-start | bytes 294920 | tf_op jit(solution)/shard_map/ppermute | solution.py:64
  9.9 5.0 %collective-permute-start.5 = (f32[192,128]{1,0:T(8,128)S(1)}, f32[192,128]{1,0:T(8,128)S(1)}, u32[]{:S(2)}, u32[]{:S(2)}) collective-permute-start(f32[192,128]{1,0:T(8,128)S(1)} %get-tuple-element.47), channel_id=1, source_target_pairs={{2,0},{4,2},{6,4},{14,6},{12,14},{10,12},{8,10},{0,8},{18,16},{20,... | collective-permute-start | bytes 294920 | tf_op jit(solution)/shard_map/ppermute | solution.py:64
  9.9 5.0 %collective-permute-start.6 = (f32[160,128]{1,0:T(8,128)S(1)}, f32[160,128]{1,0:T(8,128)S(1)}, u32[]{:S(2)}, u32[]{:S(2)}) collective-permute-start(f32[160,128]{1,0:T(8,128)S(1)} %shard_map.33.refs_0_), channel_id=1, source_target_pairs={{0,1},{1,0},{2,3},{3,2},{4,5},{5,4},{6,7},{7,6},{8,9},{9,8},{10,11... | collective-permute-start | bytes 245768 | tf_op jit(solution)/shard_map/ppermute | solution.py:64
  15.7 6.4 %collective-permute-start.7 = (f32[360,128]{1,0:T(8,128)S(1)}, f32[360,128]{1,0:T(8,128)S(1)}, u32[]{:S(2)}, u32[]{:S(2)}) collective-permute-start(f32[360,128]{1,0:T(8,128)S(1)} %get-tuple-element.56), channel_id=1, source_target_pairs={{0,8},{8,16},{16,24},{24,25},{25,17},{17,9},{9,1},{1,0},{2,10},{10... | collective-permute-start | bytes 552968 | tf_op jit(solution)/shard_map/ppermute | solution.py:64
  18.9 5.0 %collective-permute-start.8 = (f32[360,128]{1,0:T(8,128)S(1)}, f32[360,128]{1,0:T(8,128)S(1)}, u32[]{:S(2)}, u32[]{:S(2)}) collective-permute-start(f32[360,128]{1,0:T(8,128)S(1)} %get-tuple-element.57), channel_id=1, source_target_pairs={{8,0},{16,8},{24,16},{25,24},{17,25},{9,17},{1,9},{0,1},{10,2},{18... | collective-permute-start | bytes 552968 | tf_op jit(solution)/shard_map/ppermute | solution.py:64
